TPU v7x, 32 devices: a whole 2x2x4 slice. The times are simulated.
32 devices in a mesh: frame: 8 (over z, x), batch: 4 (over y, core).
Axes of the slice: x: 2, y: 2, z: 4, core: 2. Of those that a mesh axis runs over, the one named last changes fastest.
Arguments:
- tokens: bfloat16 [4, 3136, 768], P('batch', 'frame'), may hold values from -6 to 6
- cotangent: bfloat16 [4, 128, 768], P('batch', 'frame'), may hold values from -6 to 6
- clip_lengths: int32 [4, 8], P('batch'), may hold values from 1 to 8, 16 in all within a row
- clip_order: int32 [4, 8], P('batch'), may hold values from 0 to 7, each once within a row
- block_owner: int32 [448], replicated, may hold values from 0 to 447, as said below
- master: float32 [448, 128, 128], P(('frame', 'batch'))
- moment1: float32 [448, 128, 128], P(('frame', 'batch'))
- moment2: float32 [448, 128, 128], P(('frame', 'batch')), as said below
- stat_left: float32 [448, 128, 128], P(('frame', 'batch')), as said below
- stat_right: float32 [448, 128, 128], P(('frame', 'batch')), as said below
- basis_left: float32 [448, 128, 128], P(('frame', 'batch')), as said below
- basis_right: float32 [448, 128, 128], P(('frame', 'batch')), as said below
- small_params: float32 [67808], replicated
- small_moment1: float32 [67808], replicated
- small_moment2: float32 [67808], replicated, as said below
Outputs:
- learned: float32 [4, 128, 768], P('batch', 'frame')
- grad_input: float32 [4, 3136, 768], P('batch', 'frame')
- new_master: float32 [448, 128, 128], P(('frame', 'batch'))
- new_moment1: float32 [448, 128, 128], P(('frame', 'batch'))
- new_moment2: float32 [448, 128, 128], P(('frame', 'batch'))
- new_left: float32 [448, 128, 128], P(('frame', 'batch'))
- new_right: float32 [448, 128, 128], P(('frame', 'batch'))
- new_basis_left: float32 [448, 128, 128], P(('frame', 'batch'))
- new_basis_right: float32 [448, 128, 128], P(('frame', 'batch'))
- small_first: float32 [67808], replicated
- small_second: float32 [67808], replicated
- small_new: float32 [67808], replicated
- grad_norm: float32 [], replicated
Inputs may be any that keep to these rules, and one draw needn't show every extreme that they name: `clip_lengths`: in each group the lengths sum to 16; the longest is exactly 8. `clip_order`: each row is a permutation of the clip numbers. `block_owner`: a permutation of the slot numbers; values of 432 or more mark empty slots. `basis_left`: each block is orthogonal. `basis_right`: each block is orthogonal. `stat_left`: each block is symmetric positive definite. `stat_right`: each block is symmetric positive definite. `moment2`: positive. `small_moment2`: positive.
All inputs are finite; a program needn't handle non-finite values.
Results may differ from a plain program's by a relative error of at most 0.012.
Values may be sent and summed in bfloat16 or wider, within the bound.
No kernel may reach another device: no remote copies, remote signals or barrier semaphores. Data moves between devices by JAX's collectives and lax.ppermute only.
A program may use at most 256 MiB of HBM per device.

v0:
```python
import math

import jax
import jax.numpy as jnp
from jax import lax
from jax.sharding import PartitionSpec as P

D = 768
HEADS = 12
HD = 64
FF = 3072
GRID = 14
NT = 8
BLOCK_SIDE = 128
STEP = 10
MATRIX_BLOCKS = 432


FULL_PRECISION = lax.Precision.HIGHEST
NORM_EPSILON = 1e-06
BETA_ONE = 0.9
BETA_TWO = 0.95
STAT_DECAY = 0.95
LEARN_RATE = 0.1
WEIGHT_DECAY = 0.01
ADAM_EPSILON = 1e-08
CLIP_NORM = 1.0
MASK_FLOOR = -1e30


def layout():
    return [
        ("gain_one", (D,)),
        ("shift_one", (D,)),
        ("gain_two", (D,)),
        ("shift_two", (D,)),
        ("gain_three", (D,)),
        ("shift_three", (D,)),
        ("bias_query", (D,)),
        ("bias_value", (D,)),
        ("bias_out", (D,)),
        ("bias_up", (FF,)),
        ("bias_down", (D,)),
        ("conv_first", (D, 9, NT)),
        ("conv_second", (9, NT, NT)),
        ("conv_third", (9, NT, NT)),
        ("conv_fourth", (9, NT, NT)),
        ("conv_bias", (4, NT)),
    ]


def unpack(vector):
    params_split = {}
    offset = 0
    for part_name, part_shape in layout():
        entries = math.prod(part_shape)
        params_split[part_name] = vector[offset : offset + entries].reshape(part_shape)
        offset = offset + entries
    return params_split


def matrix_shapes():
    return [(D, 3 * D), (D, D), (D, FF), (FF, D)]


def to_blocks(matrix):
    row_count, col_count = matrix.shape
    tiled = matrix.reshape(row_count // BLOCK_SIDE, BLOCK_SIDE, col_count // BLOCK_SIDE, BLOCK_SIDE)
    return tiled.transpose(0, 2, 1, 3).reshape(-1, BLOCK_SIDE, BLOCK_SIDE)


def from_blocks(blocks):
    matrices = []
    offset = 0
    for row_count, col_count in matrix_shapes():
        tiles = row_count // BLOCK_SIDE * (col_count // BLOCK_SIDE)
        piece_tiles = blocks[offset : offset + tiles].reshape(
            row_count // BLOCK_SIDE, col_count // BLOCK_SIDE, BLOCK_SIDE, BLOCK_SIDE
        )
        matrices.append(piece_tiles.transpose(0, 2, 1, 3).reshape(row_count, col_count))
        offset = offset + tiles
    return matrices


def layer_norm(values, gain_vec, shift_vec):
    centre = jnp.mean(values, -1, keepdims=True)
    centered = values - centre
    spread = jnp.mean(centered * centered, -1, keepdims=True)
    return centered * lax.rsqrt(spread + NORM_EPSILON) * gain_vec + shift_vec


def gelu_exact(values):
    return jax.nn.gelu(values, approximate=False)


def taps_sum(taps):
    padded = jnp.pad(taps, ((0, 0), (1, 1), (1, 1), (0, 0), (0, 0)))
    summed = jnp.zeros(taps.shape[:3] + taps.shape[4:], taps.dtype)
    for tap_index in range(9):
        row_off = tap_index // 3 - 1
        col_off = tap_index % 3 - 1
        summed = (
            summed
            + padded[
                :, 1 + row_off : 1 + row_off + GRID, 1 + col_off : 1 + col_off + GRID, tap_index
            ]
        )
    return summed


def taps_back(grads):
    padded = jnp.pad(grads, ((0, 0), (1, 1), (1, 1), (0, 0)))
    shifted = []
    for tap_index in range(9):
        row_off = tap_index // 3 - 1
        col_off = tap_index % 3 - 1
        shifted.append(
            padded[:, 1 - row_off : 1 - row_off + GRID, 1 - col_off : 1 - col_off + GRID]
        )
    return jnp.stack(shifted, axis=3)


def conv_small(values, weight):
    taps = jnp.einsum("fyxc,tco->fyxto", values, weight, precision=FULL_PRECISION)
    return taps_sum(taps)


def learner_tail(first_pre, values, second_w, third_w, fourth_w, tail_bias):
    frames = first_pre.shape[0]
    act_one = gelu_exact(first_pre)
    act_two = gelu_exact(conv_small(act_one, second_w) + tail_bias[0])
    act_three = gelu_exact(conv_small(act_two, third_w) + tail_bias[1])
    maps = jax.nn.sigmoid(conv_small(act_three, fourth_w) + tail_bias[2])
    grid_values = values.reshape(frames, GRID, GRID, values.shape[-1])
    pooled = jnp.einsum("fyxk,fyxd->fkd", maps, grid_values, precision=FULL_PRECISION)
    return pooled.reshape(frames * NT, values.shape[-1])


def clip_segments(lengths, order_row, group_frames, frames_dev, frame_count):
    clip_ids = jnp.arange(lengths.shape[0], dtype=jnp.int32)
    ordered_len = jnp.sum(
        jnp.where(order_row[:, None] == clip_ids[None, :], lengths[None, :], 0), 1
    )
    ends = jnp.cumsum(ordered_len)
    slots = jnp.arange(group_frames, dtype=jnp.int32)
    places = slots % frames_dev * frame_count + slots // frames_dev
    return jnp.sum((ends[None, :] <= places[:, None]).astype(jnp.int32), 1)


def cholesky_basis(product):
    gram_matrix = jnp.einsum("sji,sjk->sik", product, product, precision=FULL_PRECISION)
    lower_factor = jnp.linalg.cholesky(gram_matrix)
    solved = jax.scipy.linalg.solve_triangular(
        lower_factor, jnp.swapaxes(product, 1, 2), lower=True
    )
    return jnp.swapaxes(solved, 1, 2)


def soap_update(clipped, master, moment1, moment2, stat_left, stat_right, basis_left, basis_right):
    rotated = jnp.einsum("sji,sjk->sik", basis_left, clipped, precision=FULL_PRECISION)
    rotated = jnp.einsum("sik,skl->sil", rotated, basis_right, precision=FULL_PRECISION)
    first_new = BETA_ONE * moment1 + (1.0 - BETA_ONE) * rotated
    second_new = BETA_TWO * moment2 + (1.0 - BETA_TWO) * rotated * rotated
    direction = (
        first_new
        / (1.0 - BETA_ONE**STEP)
        / (jnp.sqrt(second_new / (1.0 - BETA_TWO**STEP)) + ADAM_EPSILON)
    )
    returned = jnp.einsum("sij,sjk->sik", basis_left, direction, precision=FULL_PRECISION)
    returned = jnp.einsum("sik,slk->sil", returned, basis_right, precision=FULL_PRECISION)
    new_master = master - LEARN_RATE * (returned + WEIGHT_DECAY * master)
    new_left = STAT_DECAY * stat_left + (1.0 - STAT_DECAY) * jnp.einsum(
        "sij,skj->sik", clipped, clipped, precision=FULL_PRECISION
    )
    new_right = STAT_DECAY * stat_right + (1.0 - STAT_DECAY) * jnp.einsum(
        "sji,sjk->sik", clipped, clipped, precision=FULL_PRECISION
    )
    new_basis_left = cholesky_basis(
        jnp.einsum("sij,sjk->sik", new_left, basis_left, precision=FULL_PRECISION)
    )
    new_basis_right = cholesky_basis(
        jnp.einsum("sij,sjk->sik", new_right, basis_right, precision=FULL_PRECISION)
    )
    turn_left = jnp.einsum("sji,sjk->sik", new_basis_left, basis_left, precision=FULL_PRECISION)
    turn_right = jnp.einsum("sji,sjk->sik", basis_right, new_basis_right, precision=FULL_PRECISION)
    moved = jnp.einsum("sij,sjk->sik", turn_left, first_new, precision=FULL_PRECISION)
    moved = jnp.einsum("sij,sjk->sik", moved, turn_right, precision=FULL_PRECISION)
    return (new_master, moved, second_new, new_left, new_right, new_basis_left, new_basis_right)


def adam_update(clipped, params_old, first_old, second_old):
    first_new = BETA_ONE * first_old + (1.0 - BETA_ONE) * clipped
    second_new = BETA_TWO * second_old + (1.0 - BETA_TWO) * clipped * clipped
    stepped = (
        first_new
        / (1.0 - BETA_ONE**STEP)
        / (jnp.sqrt(second_new / (1.0 - BETA_TWO**STEP)) + ADAM_EPSILON)
    )
    return (first_new, second_new, params_old - LEARN_RATE * stepped)


def block_length(rows_total):
    length = rows_total
    while length > 512 and length % 2 == 0:
        length = length // 2
    return length


def masked_scores(query_heads, key_block, seg_query, seg_key):
    score_scale = 1.0 / math.sqrt(HD)
    scores = (
        jnp.einsum("qhd,khd->hqk", query_heads, key_block, preferred_element_type=jnp.float32)
        * score_scale
    )
    allowed = (seg_query[:, None] == seg_key[None, :])[None]
    return (jnp.where(allowed, scores, MASK_FLOOR), allowed)


def block_grads(
    query_heads, key_block, value_block, grad_heads, log_rows, delta_rows, seg_query, seg_key
):
    scores, allowed = masked_scores(query_heads, key_block, seg_query, seg_key)
    soft = jnp.where(allowed, jnp.exp(scores - log_rows[:, :, None]), 0.0)
    grad_soft = jnp.einsum(
        "qhd,khd->hqk", grad_heads, value_block, preferred_element_type=jnp.float32
    )
    grad_scores = (soft * (grad_soft - delta_rows[:, :, None])).astype(jnp.bfloat16)
    return (soft.astype(jnp.bfloat16), grad_scores)


def on_device(
    tokens,
    cotangent,
    clip_lengths,
    clip_order,
    block_owner,
    master,
    moment1,
    moment2,
    stat_left,
    stat_right,
    basis_left,
    basis_right,
    small_params,
    small_moment1,
    small_moment2,
):
    frame_count = lax.axis_size("frame")
    frame_index = lax.axis_index("frame")
    local_rows = tokens.shape[1]
    frames_dev = local_rows // (GRID * GRID)
    group_rows = local_rows * frame_count
    slot_total = block_owner.shape[0]
    params_split = unpack(small_params)
    gathered = lax.all_gather(master.astype(jnp.bfloat16), ("frame", "batch"), axis=0, tiled=True)
    ordered = jnp.zeros_like(gathered).at[block_owner].set(gathered)
    w_qkv, w_out, w_up, w_down = from_blocks(ordered)
    segment_slots = clip_segments(
        clip_lengths[0], clip_order[0], frames_dev * frame_count, frames_dev, frame_count
    )
    seg_tokens = jnp.repeat(segment_slots, GRID * GRID)
    seg_local = lax.dynamic_slice_in_dim(seg_tokens, frame_index * local_rows, local_rows)
    inputs = tokens[0].astype(jnp.float32)
    normed_one, norm_one_back = jax.vjp(
        layer_norm, inputs, params_split["gain_one"], params_split["shift_one"]
    )
    normed_one_low = normed_one.astype(jnp.bfloat16)
    qkv_bias = jnp.concatenate(
        [
            params_split["bias_query"],
            jnp.zeros_like(params_split["bias_query"]),
            params_split["bias_value"],
        ]
    )
    projected = (
        jnp.dot(normed_one_low, w_qkv, preferred_element_type=jnp.float32) + qkv_bias
    ).astype(jnp.bfloat16)
    query_rows = projected[:, :D]
    key_rows = projected[:, D : 2 * D]
    value_rows = projected[:, 2 * D :]
    query_heads = query_rows.reshape(local_rows, HEADS, HD)
    start_state = (
        jnp.full((HEADS, local_rows), MASK_FLOOR, jnp.float32),
        jnp.zeros((HEADS, local_rows), jnp.float32),
        jnp.zeros((HEADS, local_rows, HD), jnp.float32),
    )
    key_piece = lax.all_gather(key_rows, "frame", axis=0, tiled=True)
    value_piece = lax.all_gather(value_rows, "frame", axis=0, tiled=True)
    piece_rows = key_piece.shape[0]
    length = block_length(piece_rows)

    def forward_one_block(block_step, block_state):
        run_max, run_sum, weighted = block_state
        offset = block_step * length
        key_block = lax.dynamic_slice_in_dim(key_piece, offset, length).reshape(length, HEADS, HD)
        value_block = lax.dynamic_slice_in_dim(value_piece, offset, length).reshape(
            length, HEADS, HD
        )
        seg_key = lax.dynamic_slice_in_dim(seg_tokens, offset, length)
        scores, allowed = masked_scores(query_heads, key_block, seg_local, seg_key)
        new_max = jnp.maximum(run_max, jnp.max(scores, -1))
        weights = jnp.where(allowed, jnp.exp(scores - new_max[:, :, None]), 0.0)
        rescale = jnp.exp(run_max - new_max)
        run_sum = run_sum * rescale + jnp.sum(weights, -1)
        weighted = weighted * rescale[:, :, None] + jnp.einsum(
            "hqk,khd->hqd",
            weights.astype(jnp.bfloat16),
            value_block,
            preferred_element_type=jnp.float32,
        )
        return (new_max, run_sum, weighted)

    run_max, run_sum, weighted = lax.fori_loop(
        0, piece_rows // length, forward_one_block, start_state
    )
    attended_heads = (weighted / run_sum[:, :, None]).transpose(1, 0, 2)
    attended = attended_heads.reshape(local_rows, D)
    log_total = run_max + jnp.log(run_sum)
    attended_low = attended.astype(jnp.bfloat16)
    mixed_sum = (
        inputs
        + jnp.dot(attended_low, w_out, preferred_element_type=jnp.float32)
        + params_split["bias_out"]
    )
    normed_two, norm_two_back = jax.vjp(
        layer_norm, mixed_sum, params_split["gain_two"], params_split["shift_two"]
    )
    normed_two_low = normed_two.astype(jnp.bfloat16)
    hidden = (
        jnp.dot(normed_two_low, w_up, preferred_element_type=jnp.float32) + params_split["bias_up"]
    )
    activated, gelu_back = jax.vjp(gelu_exact, hidden)
    activated_low = activated.astype(jnp.bfloat16)
    output_two = (
        mixed_sum
        + jnp.dot(activated_low, w_down, preferred_element_type=jnp.float32)
        + params_split["bias_down"]
    )
    normed_three, norm_three_back = jax.vjp(
        layer_norm, output_two, params_split["gain_three"], params_split["shift_three"]
    )
    normed_three_low = normed_three.astype(jnp.bfloat16)
    conv_low = params_split["conv_first"].astype(jnp.bfloat16).reshape(D, 9 * NT)
    taps = jnp.dot(normed_three_low, conv_low, preferred_element_type=jnp.float32).reshape(
        frames_dev, GRID, GRID, 9, NT
    )
    first_pre = taps_sum(taps) + params_split["conv_bias"][0]
    learned, tail_back = jax.vjp(
        learner_tail,
        first_pre,
        output_two,
        params_split["conv_second"],
        params_split["conv_third"],
        params_split["conv_fourth"],
        params_split["conv_bias"][1:],
    )
    grad_first, grad_values, grad_second_w, grad_third_w, grad_fourth_w, grad_tail_bias = tail_back(
        cotangent[0].astype(jnp.float32)
    )
    grad_first_low = grad_first.astype(jnp.bfloat16)
    grad_bias_first = jnp.sum(grad_first_low, axis=(0, 1, 2), dtype=jnp.float32)
    grad_taps = taps_back(grad_first_low).reshape(local_rows, 9 * NT)
    grad_conv_first = jnp.einsum(
        "nd,nt->dt", normed_three_low, grad_taps, preferred_element_type=jnp.float32
    )
    grad_normed_three = jnp.einsum(
        "nt,dt->nd", grad_taps, conv_low, preferred_element_type=jnp.float32
    )
    grad_output_norm, grad_gain_three, grad_shift_three = norm_three_back(grad_normed_three)
    grad_output_two = grad_values + grad_output_norm
    grad_down_out = grad_output_two.astype(jnp.bfloat16)
    grad_bias_down = jnp.sum(grad_down_out, 0, dtype=jnp.float32)
    grad_w_down = jnp.einsum(
        "nf,nd->fd", activated_low, grad_down_out, preferred_element_type=jnp.float32
    )
    grad_activated = jnp.einsum(
        "nd,fd->nf", grad_down_out, w_down, preferred_element_type=jnp.float32
    )
    (grad_hidden,) = gelu_back(grad_activated)
    grad_hidden_low = grad_hidden.astype(jnp.bfloat16)
    grad_bias_up = jnp.sum(grad_hidden_low, 0, dtype=jnp.float32)
    grad_w_up = jnp.einsum(
        "nd,nf->df", normed_two_low, grad_hidden_low, preferred_element_type=jnp.float32
    )
    grad_normed_two = jnp.einsum(
        "nf,df->nd", grad_hidden_low, w_up, preferred_element_type=jnp.float32
    )
    grad_mixed_norm, grad_gain_two, grad_shift_two = norm_two_back(grad_normed_two)
    grad_mixed = grad_output_two + grad_mixed_norm
    grad_branch = grad_mixed.astype(jnp.bfloat16)
    grad_bias_out = jnp.sum(grad_branch, 0, dtype=jnp.float32)
    grad_w_out = jnp.einsum(
        "nc,nd->cd", attended_low, grad_branch, preferred_element_type=jnp.float32
    )
    grad_attended = jnp.einsum(
        "nd,cd->nc", grad_branch, w_out, preferred_element_type=jnp.float32
    ).astype(jnp.bfloat16)
    grad_heads = grad_attended.reshape(local_rows, HEADS, HD)
    delta = jnp.einsum(
        "qhd,qhd->hq", grad_heads, attended_heads, preferred_element_type=jnp.float32
    )
    empty_query = jnp.zeros((HEADS, local_rows, HD), jnp.float32)
    empty_total = jnp.zeros((group_rows, D), jnp.float32)
    backward_key_piece = lax.all_gather(key_rows, "frame", axis=0, tiled=True)
    backward_value_piece = lax.all_gather(value_rows, "frame", axis=0, tiled=True)
    piece_rows = backward_key_piece.shape[0]
    backward_length = block_length(piece_rows)

    def backward_one_block(block_step, block_state):
        query_acc, key_total, value_total = block_state
        offset = block_step * backward_length
        key_block = lax.dynamic_slice_in_dim(backward_key_piece, offset, backward_length).reshape(
            backward_length, HEADS, HD
        )
        value_block = lax.dynamic_slice_in_dim(
            backward_value_piece, offset, backward_length
        ).reshape(backward_length, HEADS, HD)
        seg_key = lax.dynamic_slice_in_dim(seg_tokens, offset, backward_length)
        soft_low, grad_scores = block_grads(
            query_heads, key_block, value_block, grad_heads, log_total, delta, seg_local, seg_key
        )
        query_acc = query_acc + jnp.einsum(
            "hqk,khd->hqd", grad_scores, key_block, preferred_element_type=jnp.float32
        )
        key_part = jnp.einsum(
            "hqk,qhd->khd", grad_scores, query_heads, preferred_element_type=jnp.float32
        ).reshape(backward_length, D)
        value_part = jnp.einsum(
            "hqk,qhd->khd", soft_low, grad_heads, preferred_element_type=jnp.float32
        ).reshape(backward_length, D)
        key_total = lax.dynamic_update_slice_in_dim(
            key_total,
            lax.dynamic_slice_in_dim(key_total, offset, backward_length) + key_part,
            offset,
            0,
        )
        value_total = lax.dynamic_update_slice_in_dim(
            value_total,
            lax.dynamic_slice_in_dim(value_total, offset, backward_length) + value_part,
            offset,
            0,
        )
        return (query_acc, key_total, value_total)

    query_acc, key_total, value_total = lax.fori_loop(
        0,
        piece_rows // backward_length,
        backward_one_block,
        (empty_query, empty_total, empty_total),
    )
    grad_key, grad_value = (
        lax.psum_scatter(
            key_total.astype(jnp.bfloat16), "frame", scatter_dimension=0, tiled=True
        ).astype(jnp.float32),
        lax.psum_scatter(
            value_total.astype(jnp.bfloat16), "frame", scatter_dimension=0, tiled=True
        ).astype(jnp.float32),
    )
    score_scale = 1.0 / math.sqrt(HD)
    grad_query = (query_acc * score_scale).transpose(1, 0, 2).reshape(local_rows, D)
    grad_qkv = jnp.concatenate([grad_query, grad_key * score_scale, grad_value], 1).astype(
        jnp.bfloat16
    )
    grad_bias_query = jnp.sum(grad_qkv[:, :D], 0, dtype=jnp.float32)
    grad_bias_value = jnp.sum(grad_qkv[:, 2 * D :], 0, dtype=jnp.float32)
    grad_w_qkv = jnp.einsum(
        "nd,ne->de", normed_one_low, grad_qkv, preferred_element_type=jnp.float32
    )
    grad_normed_one = jnp.einsum("ne,de->nd", grad_qkv, w_qkv, preferred_element_type=jnp.float32)
    grad_inputs_norm, grad_gain_one, grad_shift_one = norm_one_back(grad_normed_one)
    grad_inputs = grad_mixed + grad_inputs_norm
    conv_bias_grad = jnp.concatenate([grad_bias_first[None, :], grad_tail_bias], 0)
    small_local = jnp.concatenate(
        [
            grad_gain_one,
            grad_shift_one,
            grad_gain_two,
            grad_shift_two,
            grad_gain_three,
            grad_shift_three,
            grad_bias_query,
            grad_bias_value,
            grad_bias_out,
            grad_bias_up,
            grad_bias_down,
            grad_conv_first.reshape(-1),
            grad_second_w.reshape(-1),
            grad_third_w.reshape(-1),
            grad_fourth_w.reshape(-1),
            conv_bias_grad.reshape(-1),
        ]
    )
    padding_amount = jnp.zeros((slot_total - MATRIX_BLOCKS, BLOCK_SIDE, BLOCK_SIDE), jnp.float32)
    grad_blocks = jnp.concatenate(
        [
            to_blocks(grad_w_qkv),
            to_blocks(grad_w_out),
            to_blocks(grad_w_up),
            to_blocks(grad_w_down),
            padding_amount,
        ]
    )
    owned_grads = lax.psum_scatter(
        grad_blocks[block_owner], ("frame", "batch"), scatter_dimension=0, tiled=True
    )
    small_grad, owned_square = lax.psum(
        (small_local, jnp.sum(owned_grads * owned_grads)), ("frame", "batch")
    )
    grad_norm = jnp.sqrt(owned_square + jnp.sum(small_grad * small_grad))
    factor = 1.0 / jnp.maximum(grad_norm, CLIP_NORM)
    soap_out = soap_update(
        owned_grads * factor,
        master,
        moment1,
        moment2,
        stat_left,
        stat_right,
        basis_left,
        basis_right,
    )
    small_first, small_second, small_new = adam_update(
        small_grad * factor, small_params, small_moment1, small_moment2
    )
    return (
        learned[None],
        grad_inputs[None],
        soap_out[0],
        soap_out[1],
        soap_out[2],
        soap_out[3],
        soap_out[4],
        soap_out[5],
        soap_out[6],
        small_first,
        small_second,
        small_new,
        grad_norm,
    )


def solution(mesh):
    placed = (
        P("batch", "frame", None),
        P("batch", "frame", None),
        P("batch", None),
        P("batch", None),
        P(),
        P(("frame", "batch"), None, None),
        P(("frame", "batch"), None, None),
        P(("frame", "batch"), None, None),
        P(("frame", "batch"), None, None),
        P(("frame", "batch"), None, None),
        P(("frame", "batch"), None, None),
        P(("frame", "batch"), None, None),
        P(),
        P(),
        P(),
    )
    return jax.shard_map(
        on_device,
        mesh=mesh,
        in_specs=placed,
        out_specs=(
            P("batch", "frame", None),
            P("batch", "frame", None),
            P(("frame", "batch"), None, None),
            P(("frame", "batch"), None, None),
            P(("frame", "batch"), None, None),
            P(("frame", "batch"), None, None),
            P(("frame", "batch"), None, None),
            P(("frame", "batch"), None, None),
            P(("frame", "batch"), None, None),
            P(),
            P(),
            P(),
            P(),
        ),
        check_vma=False,
    )
```

profile of v0, /device:TPU:15, one launch (start us, length us, event | category | flops | bytes accessed | tf_op | source)
XLA Modules:
  0.0 2399.5 jit_solution(4890429496885949791)
XLA Ops:
  12.6 104.0 %all-gather.4.cloned.1.call-done = bf16[448,128,128]{2,1,0:T(8,128)(2,1)} async-done(((bf16[14,128,128]{2,1,0:T(8,128)(2,1)}), bf16[448,128,128]{2,1,0:T(8,128)(2,1)}) %all-gather.4.cloned.1.call-update) | async-done | bytes 14680080 | tf_op jit(solution)/shard_map/all_gather | solution.py:255
  116.6 8.9 broadcast_in_dim.233
  125.5 66.3 %scatter_fusion = bf16[448,128,128]{2,1,0:T(8,128)(2,1)} fusion(bf16[448,128,128]{2,1,0:T(8,128)(2,1)} %broadcast_in_dim.233, s32[448]{0:T(512)S(1)} %compare_select_fusion, bf16[448,128,128]{2,1,0:T(8,128)(2,1)} %all-gather.4.cloned.1.call-done), kind=kCustom, calls=%fused_computation.1 | custom fusion | bytes 44041984 | tf_op jit(solution)/shard_map/scatter | solution.py:256
  214.7 9.2 fusion.629
  229.0 7.1 copy.208
  236.1 41.7 %all-gather.6.cloned.1.call-done = bf16[3136,768]{1,0:T(8,128)(2,1)} async-done(((bf16[392,768]{1,0:T(8,128)(2,1)}), bf16[3136,768]{1,0:T(8,128)(2,1)}) %all-gather.6.cloned.1.call-update) | async-done | bytes 4816912 | tf_op jit(solution)/shard_map/all_gather | solution.py:287
  277.8 7.3 copy.204
  285.1 74.7 %all-gather.8.cloned.1.call-done = bf16[3136,768]{1,0:T(8,128)(2,1)} async-done(((bf16[392,768]{1,0:T(8,128)(2,1)}), bf16[3136,768]{1,0:T(8,128)(2,1)}) %all-gather.8.cloned.1.call-update) | async-done | bytes 4816912 | tf_op jit(solution)/shard_map/all_gather | solution.py:288
  359.9 7.2 copy.205
  367.1 152.5 %while.36 = (s32[]{:T(128)}, f32[12,392]{1,0:T(8,128)S(1)}, f32[12,392]{1,0:T(8,128)S(1)}, f32[12,392,64]{1,2,0:T(8,128)}, s32[392]{0:T(512)S(1)}, /*index=5*/s3...) while((s32[]{:T(128)}, f32[12,392]{1,0:T(8,128)S(1)}, ...), condition=%wide.region_9.10_spmd.clone, body=%wide.region_6.9_spmd.clone.sunk | while | flops 497107744 | bytes 59176536 | solution.py:313
  375.2 6.2 fusion.726
  524.2 16.1 multiply_convert_fusion
  576.9 8.6 convert_reduce_fusion
  609.0 352.2 %while.37 = (s32[]{:T(128)}, f32[12,392,64]{1,2,0:T(8,128)}, f32[3136,768]{0,1:T(8,128)}, f32[3136,768]{0,1:T(8,128)}, s32[392]{0:T(512)S(1)}, /*index=5*/s32[31...) while((s32[]{:T(128)}, f32[12,392,64]{1,2,0:T(8,128)}, ...), condition=%wide.region_19.20_spmd.clone, body=%wide.region_18.19_spmd.clone.sunk | while | flops 1203624960 | bytes 71949496 | solution.py:445
  630.1 8.5 dynamic_update_slice.19
  638.5 8.5 dynamic_update_slice.18
  672.3 9.4 dynamic_update_slice.19
  681.7 9.4 dynamic_update_slice.18
  716.7 9.4 dynamic_update_slice.19
  726.1 9.4 dynamic_update_slice.18
  761.2 9.4 dynamic_update_slice.19
  770.6 9.4 dynamic_update_slice.18
  805.7 9.4 dynamic_update_slice.19
  815.1 9.4 dynamic_update_slice.18
  850.2 9.4 dynamic_update_slice.19
  859.6 9.4 dynamic_update_slice.18
  894.7 9.4 dynamic_update_slice.19
  904.0 9.3 dynamic_update_slice.18
  938.7 8.7 dynamic_update_slice.19
  947.4 8.7 dynamic_update_slice.18
  961.1 6.5 convert_element_type.147
  967.7 7.4 copy.322
  975.1 6.5 convert_element_type.149
  981.6 7.5 copy.324
  990.6 7.2 convolution_bitcast_fusion.1
  1020.8 10.0 copy.233
  1031.1 41.5 %reduce-scatter.10.cloned.1.call-done = bf16[392,768]{1,0:T(8,128)(2,1)} async-done(((bf16[3136,768]{1,0:T(8,128)(2,1)}), bf16[392,768]{1,0:T(8,128)(2,1)}) %reduce-scatter.10.cloned.1.call-update) | async-done | bytes 602128
  1074.9 97.4 %reduce-scatter.12.cloned.1.call-done = bf16[392,768]{1,0:T(8,128)(2,1)} async-done(((bf16[3136,768]{1,0:T(8,128)(2,1)}), bf16[392,768]{1,0:T(8,128)(2,1)}) %reduce-scatter.12.cloned.1.call-update) | async-done | bytes 602128
  1202.5 8.6 constant_dynamic-update-slice_fusion
  1212.1 23.7 gather_fusion
  1252.2 19.4 concatenate.20
  1271.6 273.7 %reduce-scatter.8.cloned.1.call-done = f32[14,128,128]{2,1,0:T(8,128)} async-done(((f32[448,128,128]{2,1,0:T(8,128)}), f32[14,128,128]{2,1,0:T(8,128)}) %reduce-scatter.8.cloned.1.call-update) | async-done | bytes 917520 | tf_op jit(solution)/shard_map/reduce_scatter | solution.py:503
  1547.3 132.9 %all-reduce.37.cloned.1.call-done = f32[67808]{0:T(1024)} async-done(((f32[67808]{0:T(1024)}), f32[67808]{0:T(1024)}) %all-reduce.37.cloned.1.call-update) | async-done | bytes 271248 | tf_op jit(solution)/shard_map/psum | solution.py:506
  1681.8 41.3 %psum.14 = f32[]{:T(128)} all-reduce(f32[]{:T(128)} %multiply_reduce_fusion.6), channel_id=1, replica_groups=mesh['frame'=8,'batch'=4] {'frame','batch'}, use_global_device_ids=true, to_apply=%region_26.27 | all-reduce | flops 1 | bytes 8 | tf_op jit(solution)/shard_map/psum | solution.py:506
  1736.6 166.0 %custom-call.12 = f32[14,128,128]{2,1,0:T(8,128)} custom-call(f32[14,128,128]{2,1,0:T(8,128)} %fusion.95), custom_call_target="Cholesky" | custom-call | tf_op jit(solution)/shard_map/jit(cholesky)/cholesky | solution.py:152
  1915.9 165.6 %custom-call.14 = f32[14,128,128]{2,1,0:T(8,128)} custom-call(f32[14,128,128]{2,1,0:T(8,128)} %fusion.91), custom_call_target="Cholesky" | custom-call | tf_op jit(solution)/shard_map/jit(cholesky)/cholesky | solution.py:152
  2085.0 139.0 %custom-call.15 = f32[14,1,128,128]{2,3,1,0:T(8,128)} custom-call(f32[14,1,128,128]{3,2,1,0:T(8,128)} %get-tuple-element.689), custom_call_target="InvertDiagBlocksLowerTriangular" | custom-call | tf_op jit(solution)/shard_map/jit(_solve_triangular)/vmap()/triangular_solve | solution.py:153
  2229.9 139.1 %custom-call.13 = f32[14,1,128,128]{2,3,1,0:T(8,128)} custom-call(f32[14,1,128,128]{3,2,1,0:T(8,128)} %get-tuple-element.690), custom_call_target="InvertDiagBlocksLowerTriangular" | custom-call | tf_op jit(solution)/shard_map/jit(_solve_triangular)/vmap()/triangular_solve | solution.py:153
  (645 shorter events, 582.2 us)
Async XLA Ops:
  7.2 1899.2 %copy-start = (f32[14,128,128]{2,1,0:T(8,128)S(1)}, f32[14,128,128]{2,1,0:T(8,128)}, u32[]{:S(2)}) copy-start(f32[14,128,128]{2,1,0:T(8,128)} %param.33) | copy-start | bytes 2752516
  7.2 109.4 %all-gather.4.cloned.1.call-start = ((), (), s32[]{:S(2)}) async-start(), calls=%async_computation.3 | async-start | bytes 15138816 | tf_op jit(solution)/shard_map/all_gather | solution.py:255
  9.4 268.4 %all-gather.6.cloned.1.call-start = ((), (), s32[]{:S(2)}) async-start(), calls=%async_computation.4 | async-start | bytes 5419008 | tf_op jit(solution)/shard_map/all_gather | solution.py:287
  10.9 185.8 %copy-start.79 = (f32[768]{0:T(1024)}, f32[768]{0:T(1024)S(1)}, u32[]{:S(2)}) copy-start(f32[768]{0:T(1024)S(1)} %get-tuple-element.688) | copy-start | bytes 9220
  10.9 185.8 %copy-start.106 = (f32[768]{0:T(1024)}, f32[768]{0:T(1024)S(1)}, u32[]{:S(2)}) copy-start(f32[768]{0:T(1024)S(1)} %get-tuple-element.687) | copy-start | bytes 9220
  10.9 513.3 %copy-start.108 = (f32[768]{0:T(1024)}, f32[768]{0:T(1024)S(1)}, u32[]{:S(2)}) copy-start(f32[768]{0:T(1024)S(1)} %get-tuple-element.683) | copy-start | bytes 9220
  10.9 513.3 %copy-start.116 = (f32[768]{0:T(1024)}, f32[768]{0:T(1024)S(1)}, u32[]{:S(2)}) copy-start(f32[768]{0:T(1024)S(1)} %get-tuple-element.682) | copy-start | bytes 9220
  12.2 184.5 %copy-start.87 = (f32[392]{0:T(512)}, f32[392]{0:T(512)S(1)}, u32[]{:S(2)}) copy-start(f32[392]{0:T(512)S(1)} %broadcast_multiply_fusion.2) | copy-start | bytes 4708
  12.5 113.0 %copy-start.96 = (f32[392]{0:T(512)}, f32[392]{0:T(512)S(1)}, u32[]{:S(2)}) copy-start(f32[392]{0:T(512)S(1)} %fusion.73) | copy-start | bytes 4708
  12.6 184.2 %copy-start.91 = (f32[392]{0:T(512)}, f32[392]{0:T(512)S(1)}, u32[]{:S(2)}) copy-start(f32[392]{0:T(512)S(1)} %fusion.508) | copy-start | bytes 4708
  12.6 112.9 %copy-start.98 = (s32[448]{0:T(512)}, s32[448]{0:T(512)S(1)}, u32[]{:S(2)}) copy-start(s32[448]{0:T(512)S(1)} %compare_select_fusion) | copy-start | bytes 5380
  198.8 7.3 copy-start.131
  198.8 7.3 copy-start.132
  200.0 159.9 %all-gather.8.cloned.1.call-start = ((), (), s32[]{:S(2)}) async-start(), calls=%async_computation.5 | async-start | bytes 5419008 | tf_op jit(solution)/shard_map/all_gather | solution.py:288
  200.7 871.8 %reduce-scatter.10.cloned.1.call-start = ((), (), s32[]{:S(2)}) async-start(), calls=%async_computation.8 | async-start | bytes 5419008
  207.1 7.5 copy-start.44
  375.2 6.5 copy-start.1
  393.2 6.5 copy-start.1
  521.3 19.1 slice-start.3
  523.8 16.6 copy-start.24
  523.9 16.5 copy-start.93
  524.2 16.2 copy-start.100
  524.2 16.2 copy-start.113
  524.2 16.2 slice-start.4
  524.2 16.2 copy-start.118
  550.4 15.9 copy-start.66
  576.9 8.6 copy-start.58
  576.9 8.6 copy-start.25
  576.9 8.6 copy-start.94
  576.9 8.6 copy-start.109
  576.9 8.6 copy-start.114
  975.1 197.2 %reduce-scatter.12.cloned.1.call-start = ((), (), s32[]{:S(2)}) async-start(), calls=%async_computation.9 | async-start | bytes 5419008
  989.2 556.1 %reduce-scatter.8.cloned.1.call-start = ((), (), s32[]{:S(2)}) async-start(), calls=%async_computation.6 | async-start | bytes 30277632 | tf_op jit(solution)/shard_map/reduce_scatter | solution.py:503
  1003.8 6.8 copy-start.59
  1020.8 10.0 copy-start.3
  1031.0 142.7 %copy-start.12 = (bf16[1,392,768]{2,1,0:T(8,128)(2,1)S(1)}, bf16[1,392,768]{2,1,0:T(8,128)(2,1)}, u32[]{:S(2)}) copy-start(bf16[1,392,768]{2,1,0:T(8,128)(2,1)} %param.22) | copy-start | bytes 1806340
  1031.0 142.7 %copy-start.80 = (f32[768]{0:T(1024)S(1)}, f32[768]{0:T(1024)}, u32[]{:S(2)}) copy-start(f32[768]{0:T(1024)} %copy-done.79) | copy-start | bytes 9220
  1031.0 142.7 %copy-start.88 = (f32[392]{0:T(512)S(1)}, f32[392]{0:T(512)}, u32[]{:S(2)}) copy-start(f32[392]{0:T(512)} %copy-done.87) | copy-start | bytes 4708
  1190.7 6.5 slice-start
  1190.7 6.5 slice-start.1
  1235.9 444.3 %all-reduce.37.cloned.1.call-start = ((), (), s32[]{:S(2)}) async-start(), calls=%async_computation.7 | async-start | bytes 548864 | tf_op jit(solution)/shard_map/psum | solution.py:506
  1245.5 6.7 copy-start.104
  1245.5 6.7 copy-start.105
  1249.8 474.7 %copy-start.52 = (f32[14,128,128]{2,1,0:T(8,128)S(1)}, f32[14,128,128]{2,1,0:T(8,128)}, u32[]{:S(2)}) copy-start(f32[14,128,128]{2,1,0:T(8,128)} %param.30) | copy-start | bytes 2752516
  1252.1 475.9 %copy-start.16 = (f32[14,128,128]{2,1,0:T(8,128)S(1)}, f32[14,128,128]{2,1,0:T(8,128)}, u32[]{:S(2)}) copy-start(f32[14,128,128]{2,1,0:T(8,128)} %param.32) | copy-start | bytes 2752516
  1731.7 171.0 %copy-start.4 = (f32[14,128,128]{2,1,0:T(8,128)S(1)}, f32[14,128,128]{2,1,0:T(8,128)}, u32[]{:S(2)}) copy-start(f32[14,128,128]{2,1,0:T(8,128)} %reduce-scatter.8.cloned.1.call-done) | copy-start | bytes 2752516
  1910.9 170.5 %copy-start.77 = (pred[128,128]{1,0:T(8,128)(4,1)S(1)}, pred[128,128]{1,0:T(8,128)(4,1)}, u32[]{:S(2)}) copy-start(pred[128,128]{1,0:T(8,128)(4,1)} %iota_compare_fusion.1) | copy-start | bytes 49156
  1913.4 170.0 %copy-start.76 = (pred[128,128]{1,0:T(8,128)(4,1)S(1)}, pred[128,128]{1,0:T(8,128)(4,1)}, u32[]{:S(2)}) copy-start(pred[128,128]{1,0:T(8,128)(4,1)} %iota_compare_fusion) | copy-start | bytes 49156
  (113 other events, 324.2 us)
Sparse Core Ops, SparseCore 0:
  11.5 105.0 all-gather.3
  200.1 77.7 all-gather.5
  280.6 79.2 all-gather.7
  975.2 97.2 reduce-scatter.9
  1076.0 96.2 reduce-scatter.11
  1236.0 309.2 reduce-scatter.7
  1551.2 128.9 all-reduce.36
where the time goes:
time: 2420 us; the launch traced here: 2400 us
  waiting for transfers between devices  767 us (32%)
  other arithmetic  755 us (31%)
  local copies, waits for them, and re-layouts  497 us (21%)
  matrix products  318 us (13%)
  blocking collectives  41.3 us (2%)
    another operation x5, other arithmetic, cholesky_basis(): lower_factor = jnp.linalg.cholesky(gram_matrix)  334 us
    another operation x4, other arithmetic, cholesky_basis(): jax.scipy.linalg.solve_triangular(lower_factor, jnp.swapaxes(product, 1,...  280 us
    reduce_scatter x1, waiting for transfers between devices, on_device(): lax.psum_scatter(grad_blocks[block_owner], ('frame', 'batch'), scatter_di...  274 us
    unnamed x9, waiting for transfers between devices  140 us
    psum x1, waiting for transfers between devices, on_device(): lax.psum((small_local, jnp.sum(owned_grads * owned_grads)), ('frame', 'ba...  133 us
    all_gather x1, waiting for transfers between devices, on_device(): lax.all_gather(master.astype(jnp.bfloat16), ('frame', 'batch'), axis=0, t...  104 us
    unnamed x298, local copies, waits for them, and re-layouts  76.6 us
    all_gather x1, waiting for transfers between devices, on_device(): value_piece = lax.all_gather(value_rows, 'frame', axis=0, tiled=True)  74.7 us
  transfers between devices with their start and end apart: 7, of which 7 were waited for; matrix products, arithmetic and copies ran while one was open for 6% of the time, Pallas kernels for 0%

commit v1 on v0

v1 whole, which is shorter than its diff:
```python
import math

import jax
import jax.numpy as jnp
from jax import lax
from jax.experimental import pallas as pl
from jax.experimental.pallas import tpu as pltpu
from jax.sharding import Mesh
from jax.sharding import PartitionSpec as P

D = 768
HEADS = 12
HD = 64
FF = 3072
GRID = 14
NT = 8
BLOCK_SIDE = 128
STEP = 10
MATRIX_BLOCKS = 432


FULL_PRECISION = lax.Precision.HIGHEST
NORM_EPSILON = 1e-06
BETA_ONE = 0.9
BETA_TWO = 0.95
STAT_DECAY = 0.95
LEARN_RATE = 0.1
WEIGHT_DECAY = 0.01
ADAM_EPSILON = 1e-08
CLIP_NORM = 1.0
MASK_FLOOR = -1e30


def layout():
    return [
        ("gain_one", (D,)),
        ("shift_one", (D,)),
        ("gain_two", (D,)),
        ("shift_two", (D,)),
        ("gain_three", (D,)),
        ("shift_three", (D,)),
        ("bias_query", (D,)),
        ("bias_value", (D,)),
        ("bias_out", (D,)),
        ("bias_up", (FF,)),
        ("bias_down", (D,)),
        ("conv_first", (D, 9, NT)),
        ("conv_second", (9, NT, NT)),
        ("conv_third", (9, NT, NT)),
        ("conv_fourth", (9, NT, NT)),
        ("conv_bias", (4, NT)),
    ]


def unpack(vector):
    params_split = {}
    offset = 0
    for part_name, part_shape in layout():
        entries = math.prod(part_shape)
        params_split[part_name] = vector[offset : offset + entries].reshape(part_shape)
        offset = offset + entries
    return params_split


def matrix_shapes():
    return [(D, 3 * D), (D, D), (D, FF), (FF, D)]


def to_blocks(matrix):
    row_count, col_count = matrix.shape
    tiled = matrix.reshape(row_count // BLOCK_SIDE, BLOCK_SIDE, col_count // BLOCK_SIDE, BLOCK_SIDE)
    return tiled.transpose(0, 2, 1, 3).reshape(-1, BLOCK_SIDE, BLOCK_SIDE)


def from_blocks(blocks):
    matrices = []
    offset = 0
    for row_count, col_count in matrix_shapes():
        tiles = row_count // BLOCK_SIDE * (col_count // BLOCK_SIDE)
        piece_tiles = blocks[offset : offset + tiles].reshape(
            row_count // BLOCK_SIDE, col_count // BLOCK_SIDE, BLOCK_SIDE, BLOCK_SIDE
        )
        matrices.append(piece_tiles.transpose(0, 2, 1, 3).reshape(row_count, col_count))
        offset = offset + tiles
    return matrices


def layer_norm(values, gain_vec, shift_vec):
    centre = jnp.mean(values, -1, keepdims=True)
    centered = values - centre
    spread = jnp.mean(centered * centered, -1, keepdims=True)
    return centered * lax.rsqrt(spread + NORM_EPSILON) * gain_vec + shift_vec


def gelu_exact(values):
    return jax.nn.gelu(values, approximate=False)


def taps_sum(taps):
    padded = jnp.pad(taps, ((0, 0), (1, 1), (1, 1), (0, 0), (0, 0)))
    summed = jnp.zeros(taps.shape[:3] + taps.shape[4:], taps.dtype)
    for tap_index in range(9):
        row_off = tap_index // 3 - 1
        col_off = tap_index % 3 - 1
        summed = (
            summed
            + padded[
                :, 1 + row_off : 1 + row_off + GRID, 1 + col_off : 1 + col_off + GRID, tap_index
            ]
        )
    return summed


def taps_back(grads):
    padded = jnp.pad(grads, ((0, 0), (1, 1), (1, 1), (0, 0)))
    shifted = []
    for tap_index in range(9):
        row_off = tap_index // 3 - 1
        col_off = tap_index % 3 - 1
        shifted.append(
            padded[:, 1 - row_off : 1 - row_off + GRID, 1 - col_off : 1 - col_off + GRID]
        )
    return jnp.stack(shifted, axis=3)


def conv_small(values, weight):
    taps = jnp.einsum("fyxc,tco->fyxto", values, weight, precision=FULL_PRECISION)
    return taps_sum(taps)


def learner_tail(first_pre, values, second_w, third_w, fourth_w, tail_bias):
    frames = first_pre.shape[0]
    act_one = gelu_exact(first_pre)
    act_two = gelu_exact(conv_small(act_one, second_w) + tail_bias[0])
    act_three = gelu_exact(conv_small(act_two, third_w) + tail_bias[1])
    maps = jax.nn.sigmoid(conv_small(act_three, fourth_w) + tail_bias[2])
    grid_values = values.reshape(frames, GRID, GRID, values.shape[-1])
    pooled = jnp.einsum("fyxk,fyxd->fkd", maps, grid_values, precision=FULL_PRECISION)
    return pooled.reshape(frames * NT, values.shape[-1])


def clip_segments(lengths, order_row, group_frames, frames_dev, frame_count):
    clip_ids = jnp.arange(lengths.shape[0], dtype=jnp.int32)
    ordered_len = jnp.sum(
        jnp.where(order_row[:, None] == clip_ids[None, :], lengths[None, :], 0), 1
    )
    ends = jnp.cumsum(ordered_len)
    slots = jnp.arange(group_frames, dtype=jnp.int32)
    places = slots % frames_dev * frame_count + slots // frames_dev
    return jnp.sum((ends[None, :] <= places[:, None]).astype(jnp.int32), 1)


F32=jnp.float32; BF=jnp.bfloat16
NN=(((1,),(0,)),((),()))
NT_=(((1,),(1,)),((),()))
TN=(((0,),(0,)),((),()))

def halves(a):
    high = a.astype(BF)
    return high, (a - high.astype(F32)).astype(BF)

def dot_low(a, b, dims):
    return lax.dot_general(a, b, dims, preferred_element_type=F32)

def dot_parts(a, b, dims):
    ah, al = a
    bh, bl = b
    return dot_low(ah, bh, dims) + (dot_low(ah, bl, dims) + dot_low(al, bh, dims))

def dot_wide(a, b, dims):
    return dot_parts(halves(a), halves(b), dims)

def stat_kernel(sl, sr, bl, br, ol, orr):
    ol[0] = STAT_DECAY * dot_wide(bl[0], sl[0], TN)
    orr[0] = STAT_DECAY * dot_wide(br[0], sr[0], TN)

def slot_spec():
    return pl.BlockSpec((1, BLOCK_SIDE, BLOCK_SIDE), lambda i: (i, 0, 0))

def stat_products(sl, sr, bl, br):
    n = sl.shape[0]
    shape = jax.ShapeDtypeStruct(sl.shape, F32)
    return pl.pallas_call(stat_kernel, grid=(n,), in_specs=[slot_spec()]*4, out_specs=[slot_spec()]*2, out_shape=[shape]*2)(sl, sr, bl, br)

def raw_kernel(g, bl, br, rot, gl, gr, ql, qr):
    gp = halves(g[0]); blp = halves(bl[0]); brp = halves(br[0])
    u = halves(dot_parts(blp, gp, TN))
    v = halves(dot_parts(gp, brp, NN))
    rot[0] = dot_parts(u, brp, NN)
    gl[0] = dot_parts(gp, gp, NT_)
    gr[0] = dot_parts(gp, gp, TN)
    ql[0] = dot_parts(u, gp, NT_)
    qr[0] = dot_parts(v, gp, TN)

def raw_products(g, bl, br):
    n = g.shape[0]
    shape = jax.ShapeDtypeStruct(g.shape, F32)
    return pl.pallas_call(raw_kernel, grid=(n,), in_specs=[slot_spec()]*3, out_specs=[slot_spec()]*5, out_shape=[shape]*5)(g, bl, br)

NB=32
def finish_kernel(factor, rot, gl, gr, ql, qr, pl_, pr_, sl, sr, bl, br, master, m1, m2,
                  o_master, o_m1, o_m2, o_left, o_right, o_bl, o_br, work, elim, mom):
    n = rot.shape[0]
    f = factor[0]
    f2 = (1.0 - STAT_DECAY) * f * f
    for s in range(n):
        r = f * rot[s]
        m = BETA_ONE * m1[s] + (1.0 - BETA_ONE) * r
        v = BETA_TWO * m2[s] + (1.0 - BETA_TWO) * r * r
        mom[s] = m
        o_m2[s] = v
        o_left[s] = STAT_DECAY * sl[s] + f2 * gl[s]
        o_right[s] = STAT_DECAY * sr[s] + f2 * gr[s]
        for side, (p_, q_) in enumerate(((pl_, ql), (pr_, qr))):
            at = p_[s] + f2 * q_[s]
            work[2*s+side, :, 128:] = at
            atp = halves(at)
            work[2*s+side, :, :128] = dot_parts(atp, atp, NT_)
    rows = lax.broadcasted_iota(jnp.int32, (1, 8, 2*NB), 1)
    lanes = lax.broadcasted_iota(jnp.int32, (1, 8, 2*NB), 2)
    count = 2*n

    def panel(p, carry):
        for q in range(128 // NB):
            @pl.when(p == q)
            def _(q=q):
                for t in range(NB // 8):
                    block = work[:, NB*q+8*t:NB*q+8*t+8, NB*q:NB*q+NB]
                    eye = jnp.where(lanes - NB == rows + 8*t, 1.0, 0.0).astype(F32)
                    eye = jnp.broadcast_to(eye, (count, 8, 2*NB))
                    elim[:, 8*t:8*t+8, :] = jnp.concatenate([block, eye[:, :, NB:]], axis=2)
        tiles = [elim[:, 8*t:8*t+8, :] for t in range(NB // 8)]
        for k in range(NB):
            t0, j = divmod(k, 8)
            pivot = tiles[t0][:, j:j+1, k:k+1]
            scale = lax.rsqrt(pivot)
            row = tiles[t0][:, j:j+1, :] * scale
            for t in range(t0, NB // 8):
                col = tiles[t][:, :, k:k+1] * scale
                new = tiles[t] - col * row
                if t == t0:
                    new = jnp.where(rows > j, new, jnp.where(rows == j, row, tiles[t]))
                tiles[t] = new
        for t in range(NB // 8):
            elim[:, 8*t:8*t+8, :] = tiles[t]
        for q in range(128 // NB):
            @pl.when(p == q)
            def _(q=q):
                lo, hi = NB*q, NB*q+NB
                for m in range(count):
                    inv = halves(elim[m, :, NB:])
                    y = dot_parts(inv, halves(work[m, lo:hi, :]), NN)
                    if m % 2 == 0:
                        o_bl[m // 2, lo:hi, :] = y[:, 128:]
                    else:
                        o_br[m // 2, lo:hi, :] = y[:, 128:]
                    if hi < 128:
                        yp = halves(y)
                        up = (yp[0][:, hi:128], yp[1][:, hi:128])
                        work[m, hi:, :] = work[m, hi:, :] - dot_parts(up, yp, TN)
        return carry
    lax.fori_loop(0, 128 // NB, panel, 0)

    for s in range(n):
        m = mom[s]
        v = o_m2[s]
        direction = m / (1.0 - BETA_ONE**STEP) / (jnp.sqrt(v / (1.0 - BETA_TWO**STEP)) + ADAM_EPSILON)
        blp, brp = halves(bl[s]), halves(br[s])
        back = halves(dot_parts(blp, halves(direction), NN))
        returned = dot_parts(back, brp, NT_)
        o_master[s] = master[s] - LEARN_RATE * (returned + WEIGHT_DECAY * master[s])
        qlt, qrt = o_bl[s], o_br[s]
        qltp, qrtp = halves(qlt), halves(qrt)
        turn_l = halves(dot_parts(qltp, blp, NN))
        turn_r = halves(dot_parts(qrtp, brp, NN))
        half = halves(dot_parts(turn_l, halves(m), NN))
        o_m1[s] = dot_parts(half, turn_r, NT_)
        o_bl[s] = qlt.T
        o_br[s] = qrt.T

def finish(factor, rot, gl, gr, ql, qr, pl_, pr_, sl, sr, bl, br, master, m1, m2):
    n = rot.shape[0]
    shape = jax.ShapeDtypeStruct(rot.shape, F32)
    vm = pl.BlockSpec(memory_space=pltpu.VMEM)
    return pl.pallas_call(finish_kernel,
        in_specs=[pl.BlockSpec(memory_space=pltpu.SMEM)] + [vm]*14, out_specs=[vm]*7, out_shape=[shape]*7,
        scratch_shapes=[pltpu.VMEM((2*n,128,256),F32), pltpu.VMEM((2*n,NB,2*NB),F32), pltpu.VMEM((n,128,128),F32)],
        compiler_params=pltpu.CompilerParams(vmem_limit_bytes=56*1024*1024),
    )(factor, rot, gl, gr, ql, qr, pl_, pr_, sl, sr, bl, br, master, m1, m2)

def soap(g, factor, master, m1, m2, sl, sr, bl, br):
    p_l, p_r = stat_products(sl, sr, bl, br)
    rot, gl, gr, ql, qr = raw_products(g, bl, br)
    return finish(factor.reshape(1), rot, gl, gr, ql, qr, p_l, p_r, sl, sr, bl, br, master, m1, m2)


def adam_update(clipped, params_old, first_old, second_old):
    first_new = BETA_ONE * first_old + (1.0 - BETA_ONE) * clipped
    second_new = BETA_TWO * second_old + (1.0 - BETA_TWO) * clipped * clipped
    stepped = (
        first_new
        / (1.0 - BETA_ONE**STEP)
        / (jnp.sqrt(second_new / (1.0 - BETA_TWO**STEP)) + ADAM_EPSILON)
    )
    return (first_new, second_new, params_old - LEARN_RATE * stepped)


FRAME_ROWS = GRID * GRID
PAD_ROWS = 208
PAIRS = HEADS // 2
PAIR = 2 * HD
ALL_AXES = ("fz", "fx", "by", "core")
FRAME_AXES = ("fz", "fx")


def matrix_places():
    places = []
    first = 0
    for row_count, col_count in matrix_shapes():
        cols = col_count // BLOCK_SIDE
        count = row_count // BLOCK_SIDE * cols
        places.append((first, count, cols))
        first = first + count
    return places


def tile_at(ref, tile, cols):
    row = pl.multiple_of(lax.div(tile, cols) * BLOCK_SIDE, BLOCK_SIDE)
    col = pl.multiple_of(lax.rem(tile, cols) * BLOCK_SIDE, BLOCK_SIDE)
    return ref.at[pl.ds(row, BLOCK_SIDE), pl.ds(col, BLOCK_SIDE)]


def place_kernel(owner, gathered, w_qkv, w_out, w_up, w_down, sems):
    outs = (w_qkv, w_out, w_up, w_down)

    def one_slot(slot, carry):
        block = owner[slot]
        for which, (first, count, cols) in enumerate(matrix_places()):
            @pl.when((block >= first) & (block < first + count))
            def _():
                pltpu.make_async_copy(
                    gathered.at[slot], tile_at(outs[which], block - first, cols), sems.at[which]
                ).start()
        return carry

    lax.fori_loop(0, gathered.shape[0], one_slot, 0)
    for which in range(4):
        pltpu.make_async_copy(outs[which], outs[which], sems.at[which]).wait()


def place_blocks(owner, gathered):
    anywhere = pl.BlockSpec(memory_space=pl.ANY)
    return pl.pallas_call(
        place_kernel,
        grid_spec=pltpu.PrefetchScalarGridSpec(
            num_scalar_prefetch=1,
            grid=(1,),
            in_specs=[anywhere],
            out_specs=[pl.BlockSpec(memory_space=pltpu.VMEM)] * 4,
            scratch_shapes=[pltpu.SemaphoreType.DMA((4,))],
        ),
        out_shape=[jax.ShapeDtypeStruct(shape, BF) for shape in matrix_shapes()],
        compiler_params=pltpu.CompilerParams(vmem_limit_bytes=48 * 1024 * 1024),
    )(owner, gathered)


def spread_kernel(sizes, slots_dev, owner, coords, g_qkv, g_out, g_up, g_down, blank, part_a, part_b, sems):
    grads = (g_qkv, g_out, g_up, g_down)
    parts = (part_a, part_b)
    nz, nx, ny, nc = sizes
    half = slots_dev // 2

    def one_slot(slot, carry):
        block = owner[slot]
        device = lax.div(slot, slots_dev)
        inner = lax.rem(slot, slots_dev)
        offs = []
        for axis, size in ((3, nc), (2, ny), (1, nx), (0, nz)):
            offs.append(lax.rem(lax.rem(device, size) - coords[axis] + size, size))
            device = lax.div(device, size)
        rc, ry, rx, rz = offs
        place_a = (((rc * nx + rx) * ny + ry) * nz + rz) * half + inner
        place_b = (((rc * ny + ry) * nx + rx) * nz + rz) * half + inner - half
        for part in range(2):
            chosen = (inner < half) if part == 0 else (inner >= half)
            place = place_a if part == 0 else place_b
            for which, (first, count, cols) in enumerate(matrix_places()):
                @pl.when(chosen & (block >= first) & (block < first + count))
                def _():
                    pltpu.make_async_copy(
                        tile_at(grads[which], block - first, cols), parts[part].at[place], sems.at[part]
                    ).start()

            @pl.when(chosen & (block >= MATRIX_BLOCKS))
            def _():
                pltpu.make_async_copy(blank, parts[part].at[place], sems.at[part]).start()
        return carry

    lax.fori_loop(0, nz * nx * ny * nc * slots_dev, one_slot, 0)
    for part in range(2):
        pltpu.make_async_copy(parts[part], parts[part], sems.at[part]).wait()


def spread_blocks(sizes, slots_dev, owner, coords, grads):
    anywhere = pl.BlockSpec(memory_space=pl.ANY)
    nz, nx, ny, nc = sizes
    half = slots_dev // 2
    shape = jax.ShapeDtypeStruct((nz * nx * ny * nc * half, BLOCK_SIDE, BLOCK_SIDE), BF)

    def kernel(*refs):
        spread_kernel(sizes, slots_dev, *refs)

    part_a, part_b = pl.pallas_call(
        kernel,
        grid_spec=pltpu.PrefetchScalarGridSpec(
            num_scalar_prefetch=2,
            grid=(1,),
            in_specs=[pl.BlockSpec(memory_space=pltpu.VMEM)] * 5,
            out_specs=[anywhere] * 2,
            scratch_shapes=[pltpu.SemaphoreType.DMA((2,))],
        ),
        out_shape=[shape, shape],
        compiler_params=pltpu.CompilerParams(vmem_limit_bytes=48 * 1024 * 1024),
    )(owner, coords, *grads, jnp.zeros((BLOCK_SIDE, BLOCK_SIDE), BF))
    tail = (half, BLOCK_SIDE, BLOCK_SIDE)
    return part_a.reshape((nc, nx, ny, nz) + tail), part_b.reshape((nc, ny, nx, nz) + tail)


def moved(value, axis, size, step):
    return lax.ppermute(value, axis, [(i, (i + step) % size) for i in range(size)])


def reduce_axis(buf, axis, size):
    total = buf[0].astype(F32)
    for step in range(1, size):
        total = total + moved(buf[step], axis, size, step).astype(F32)
    return total


def gather_axis(value, axis, size):
    return jnp.stack([value] + [moved(value, axis, size, -step) for step in range(1, size)])


def rolled(value, axis, size, step):
    return lax.dynamic_slice_in_dim(jnp.concatenate([value, value], axis), step, size, axis)


def attend_kernel(long_rows, q, k, v, bias, out):
    lanes = lax.broadcasted_iota(jnp.int32, (1, PAIR), 1)
    first = lanes < HD
    total = k.shape[0]
    for frame, (lo, hi) in enumerate(((0, long_rows), (long_rows, total))):
        rows = slice(frame * PAD_ROWS, (frame + 1) * PAD_ROWS)
        query = q[rows, :]
        keys, values = k[lo:hi, :], v[lo:hi, :]
        results = []
        for side in range(2):
            chosen = jnp.where(first if side == 0 else ~first, query, jnp.zeros_like(query))
            scores = dot_low(chosen, keys, NT_) + bias[:, lo:hi]
            weights = jnp.exp(scores - jnp.max(scores, axis=1, keepdims=True))
            norm = jnp.sum(weights, axis=1, keepdims=True)
            results.append(dot_low(weights.astype(BF), values, NN) / norm)
        out[rows, :] = jnp.where(first, results[0], results[1]).astype(BF)


def attend_back_kernel(long_rows, q, k, v, bias, grad, dq, dk, dv):
    lanes = lax.broadcasted_iota(jnp.int32, (1, PAIR), 1)
    first = lanes < HD
    total = k.shape[0]
    for frame, (lo, hi) in enumerate(((0, long_rows), (long_rows, total))):
        rows = slice(frame * PAD_ROWS, (frame + 1) * PAD_ROWS)
        query, arriving = q[rows, :], grad[rows, :]
        keys, values = k[lo:hi, :], v[lo:hi, :]
        query_parts, key_total, value_total = [], 0.0, 0.0
        for side in range(2):
            mask = first if side == 0 else ~first
            chosen = jnp.where(mask, query, jnp.zeros_like(query))
            incoming = jnp.where(mask, arriving, jnp.zeros_like(arriving))
            scores = dot_low(keys, chosen, NT_) + bias[lo:hi, :]
            weights = jnp.exp(scores - jnp.max(scores, axis=0, keepdims=True))
            soft = weights * (1.0 / jnp.sum(weights, axis=0, keepdims=True))
            grad_soft = dot_low(values, incoming, NT_)
            delta = jnp.sum(soft * grad_soft, axis=0, keepdims=True)
            grad_scores = (soft * (grad_soft - delta)).astype(BF)
            key_total = key_total + dot_low(grad_scores, chosen, NN)
            value_total = value_total + dot_low(soft.astype(BF), incoming, NN)
            query_parts.append(dot_low(grad_scores, keys, TN))
        dq[rows, :] = (jnp.where(first, query_parts[0], query_parts[1]) * (1.0 / math.sqrt(HD))).astype(BF)
        dk[lo:hi, :] = key_total.astype(BF)
        dv[lo:hi, :] = value_total.astype(BF)


def pair_spec(rows, offset=0):
    return pl.BlockSpec((rows, PAIR), lambda i: (0, i + offset))


def attend(q, kv, bias):
    keys_total = kv.shape[0]
    long_rows = keys_total - 2 * PAD_ROWS

    def kernel(*refs):
        attend_kernel(long_rows, *refs)

    return pl.pallas_call(
        kernel,
        grid=(PAIRS,),
        in_specs=[
            pair_spec(2 * PAD_ROWS),
            pair_spec(keys_total),
            pair_spec(keys_total, PAIRS),
            pl.BlockSpec((1, keys_total), lambda i: (0, 0)),
        ],
        out_specs=pair_spec(2 * PAD_ROWS),
        out_shape=jax.ShapeDtypeStruct((2 * PAD_ROWS, D), BF),
        compiler_params=pltpu.CompilerParams(vmem_limit_bytes=48 * 1024 * 1024),
    )(q, kv, kv, bias.reshape(1, -1))


def attend_back(q, kv, bias, grad):
    keys_total = kv.shape[0]
    long_rows = keys_total - 2 * PAD_ROWS

    def kernel(*refs):
        attend_back_kernel(long_rows, *refs)

    return pl.pallas_call(
        kernel,
        grid=(PAIRS,),
        in_specs=[
            pair_spec(2 * PAD_ROWS),
            pair_spec(keys_total),
            pair_spec(keys_total, PAIRS),
            pl.BlockSpec((keys_total, 1), lambda i: (0, 0)),
            pair_spec(2 * PAD_ROWS),
        ],
        out_specs=[pair_spec(2 * PAD_ROWS), pair_spec(keys_total), pair_spec(keys_total)],
        out_shape=[
            jax.ShapeDtypeStruct((2 * PAD_ROWS, D), BF),
            jax.ShapeDtypeStruct((keys_total, D), BF),
            jax.ShapeDtypeStruct((keys_total, D), BF),
        ],
        compiler_params=pltpu.CompilerParams(vmem_limit_bytes=48 * 1024 * 1024),
    )(q, kv, kv, bias.reshape(-1, 1), grad)


def pad_frames(values):
    frames = values.reshape(2, FRAME_ROWS, values.shape[-1])
    return jnp.pad(frames, ((0, 0), (0, PAD_ROWS - FRAME_ROWS), (0, 0)))


def unpad_frames(values):
    frames = values.reshape(2, PAD_ROWS, values.shape[-1])[:, :FRAME_ROWS]
    return frames.reshape(2 * FRAME_ROWS, values.shape[-1])


def normalized(values):
    centered = values - jnp.mean(values, -1, keepdims=True)
    spread = lax.rsqrt(jnp.mean(centered * centered, -1, keepdims=True) + NORM_EPSILON)
    return centered * spread, spread


def on_device(
    tokens,
    cotangent,
    clip_lengths,
    clip_order,
    block_owner,
    master,
    moment1,
    moment2,
    stat_left,
    stat_right,
    basis_left,
    basis_right,
    small_params,
    small_moment1,
    small_moment2,
):
    sizes = tuple(lax.axis_size(name) for name in ALL_AXES)
    coords = [lax.axis_index(name) for name in ALL_AXES]
    nz, nx, ny, nc = sizes
    device_count = nz * nx * ny * nc
    frame_count = nz * nx
    frame_index = coords[0] * nx + coords[1]
    slots_dev = master.shape[0]
    params_split = unpack(small_params)

    segment_slots = clip_segments(
        clip_lengths[0], clip_order[0], 2 * frame_count, 2, frame_count
    ).reshape(frame_count, 2)
    ordered_len = clip_lengths[0][clip_order[0]]
    longest = jnp.argmax(ordered_len).astype(jnp.int32)
    second_long = segment_slots[:, 1] == longest
    short_segment = jnp.where(second_long, segment_slots[:, 0], segment_slots[:, 1])
    swap = second_long[frame_index]
    padded_segment = jnp.pad(short_segment, (1, 1), constant_values=-1)
    near = lax.dynamic_slice_in_dim(padded_segment, frame_index, 3)
    with_previous = near[0] == near[1]
    with_next = near[2] == near[1]

    own_frames = pad_frames(tokens[0])
    own_frames = jnp.where(swap, own_frames[::-1], own_frames)
    long_frame, short_frame = own_frames[0], own_frames[1]
    frame_perm = [(i, (i + 1) % frame_count) for i in range(frame_count)]
    back_perm = [(j, i) for i, j in frame_perm]
    from_previous = lax.ppermute(short_frame, FRAME_AXES, frame_perm)
    from_next = lax.ppermute(short_frame, FRAME_AXES, back_perm)
    partner = jnp.where(with_next, from_next, from_previous)
    long_frames = gather_axis(gather_axis(long_frame, "fx", nx), "fz", nz)
    frames_seen = frame_count + 2
    seen = jnp.concatenate(
        [long_frames.reshape(frame_count, PAD_ROWS, D), short_frame[None], partner[None]]
    ).reshape(frames_seen * PAD_ROWS, D)
    row_ids = jnp.arange(frames_seen * PAD_ROWS, dtype=jnp.int32)
    hidden_key = (row_ids % PAD_ROWS >= FRAME_ROWS) | (
        (row_ids >= (frames_seen - 1) * PAD_ROWS) & ~(with_previous | with_next)
    )
    key_bias = jnp.where(hidden_key, MASK_FLOOR, 0.0).astype(F32)

    gathered = lax.all_gather(master.astype(BF), ALL_AXES, axis=0, tiled=True)
    w_qkv, w_out, w_up, w_down = place_blocks(block_owner, gathered)

    seen_hat, seen_rstd = normalized(seen.astype(F32))
    seen_low = (seen_hat * params_split["gain_one"] + params_split["shift_one"]).astype(BF)

    def own_rows(rows):
        return jnp.concatenate(
            [rows[:PAD_ROWS], rows[frame_count * PAD_ROWS : (frame_count + 1) * PAD_ROWS]]
        )

    own_low = own_rows(seen_low)
    query = (
        jnp.dot(own_low, w_qkv[:, :D], preferred_element_type=F32) + params_split["bias_query"]
    ).astype(BF) * jnp.asarray(1.0 / math.sqrt(HD), BF)
    kv_bias = jnp.concatenate(
        [jnp.zeros_like(params_split["bias_value"]), params_split["bias_value"]]
    )
    key_value = (jnp.dot(seen_low, w_qkv[:, D:], preferred_element_type=F32) + kv_bias).astype(BF)
    attended_low = unpad_frames(attend(query, key_value, key_bias))
    own_inputs = unpad_frames(own_frames.astype(F32))

    mixed_sum = (
        own_inputs
        + jnp.dot(attended_low, w_out, preferred_element_type=F32)
        + params_split["bias_out"]
    )
    normed_two, norm_two_back = jax.vjp(
        layer_norm, mixed_sum, params_split["gain_two"], params_split["shift_two"]
    )
    normed_two_low = normed_two.astype(BF)
    hidden = jnp.dot(normed_two_low, w_up, preferred_element_type=F32) + params_split["bias_up"]
    activated, gelu_back = jax.vjp(gelu_exact, hidden)
    activated_low = activated.astype(BF)
    output_two = (
        mixed_sum
        + jnp.dot(activated_low, w_down, preferred_element_type=F32)
        + params_split["bias_down"]
    )
    normed_three, norm_three_back = jax.vjp(
        layer_norm, output_two, params_split["gain_three"], params_split["shift_three"]
    )
    normed_three_low = normed_three.astype(BF)
    conv_low = params_split["conv_first"].astype(BF).reshape(D, 9 * NT)
    taps = jnp.dot(normed_three_low, conv_low, preferred_element_type=F32).reshape(
        2, GRID, GRID, 9, NT
    )
    first_pre = taps_sum(taps) + params_split["conv_bias"][0]
    learned, tail_back = jax.vjp(
        learner_tail,
        first_pre,
        output_two,
        params_split["conv_second"],
        params_split["conv_third"],
        params_split["conv_fourth"],
        params_split["conv_bias"][1:],
    )
    arriving = cotangent[0].astype(F32).reshape(2, NT, D)
    arriving = jnp.where(swap, arriving[::-1], arriving).reshape(2 * NT, D)
    grad_first, grad_values, grad_second_w, grad_third_w, grad_fourth_w, grad_tail_bias = tail_back(
        arriving
    )
    learned = learned.reshape(2, NT, D)
    learned = jnp.where(swap, learned[::-1], learned).reshape(2 * NT, D)
    grad_first_low = grad_first.astype(BF)
    grad_bias_first = jnp.sum(grad_first_low, axis=(0, 1, 2), dtype=F32)
    grad_taps = taps_back(grad_first_low).reshape(2 * FRAME_ROWS, 9 * NT)
    grad_conv_first = jnp.einsum("nd,nt->dt", normed_three_low, grad_taps, preferred_element_type=F32)
    grad_normed_three = jnp.einsum("nt,dt->nd", grad_taps, conv_low, preferred_element_type=F32)
    grad_output_norm, grad_gain_three, grad_shift_three = norm_three_back(grad_normed_three)
    grad_output_two = grad_values + grad_output_norm
    grad_down_out = grad_output_two.astype(BF)
    grad_bias_down = jnp.sum(grad_down_out, 0, dtype=F32)
    grad_w_down = jnp.einsum(
        "nf,nd->fd", activated_low, grad_down_out, preferred_element_type=F32
    ).astype(BF)
    grad_activated = jnp.einsum("nd,fd->nf", grad_down_out, w_down, preferred_element_type=F32)
    (grad_hidden,) = gelu_back(grad_activated)
    grad_hidden_low = grad_hidden.astype(BF)
    grad_bias_up = jnp.sum(grad_hidden_low, 0, dtype=F32)
    grad_w_up = jnp.einsum(
        "nd,nf->df", normed_two_low, grad_hidden_low, preferred_element_type=F32
    ).astype(BF)
    grad_normed_two = jnp.einsum("nf,df->nd", grad_hidden_low, w_up, preferred_element_type=F32)
    grad_mixed_norm, grad_gain_two, grad_shift_two = norm_two_back(grad_normed_two)
    grad_mixed = grad_output_two + grad_mixed_norm
    grad_branch = grad_mixed.astype(BF)
    grad_bias_out = jnp.sum(grad_branch, 0, dtype=F32)
    grad_w_out = jnp.einsum(
        "nc,nd->cd", attended_low, grad_branch, preferred_element_type=F32
    ).astype(BF)
    grad_attended = jnp.einsum("nd,cd->nc", grad_branch, w_out, preferred_element_type=F32).astype(BF)
    grad_heads = pad_frames(grad_attended).reshape(2 * PAD_ROWS, D)

    grad_query, grad_key, grad_value = attend_back(query, key_value, key_bias, grad_heads)
    grad_bias_query = jnp.sum(grad_query, 0, dtype=F32)
    grad_bias_value = jnp.sum(grad_value, 0, dtype=F32)
    grad_kv = jnp.concatenate([grad_key, grad_value], 1)
    grad_w_qkv = jnp.concatenate(
        [
            jnp.einsum("nd,ne->de", own_low, grad_query, preferred_element_type=F32),
            jnp.einsum("nd,ne->de", seen_low, grad_kv, preferred_element_type=F32),
        ],
        1,
    ).astype(BF)
    grad_seen = jnp.einsum("ne,de->nd", grad_kv, w_qkv[:, D:], preferred_element_type=F32)
    grad_own = jnp.einsum("ne,de->nd", grad_query, w_qkv[:, :D], preferred_element_type=F32)
    own_hat = own_rows(seen_hat)
    grad_gain_one = jnp.sum(grad_seen * seen_hat, 0) + jnp.sum(grad_own * own_hat, 0)
    grad_shift_one = jnp.sum(grad_seen, 0) + jnp.sum(grad_own, 0)

    conv_bias_grad = jnp.concatenate([grad_bias_first[None, :], grad_tail_bias], 0)
    small_local = jnp.concatenate(
        [
            grad_gain_one,
            grad_shift_one,
            grad_gain_two,
            grad_shift_two,
            grad_gain_three,
            grad_shift_three,
            grad_bias_query,
            grad_bias_value,
            grad_bias_out,
            grad_bias_up,
            grad_bias_down,
            grad_conv_first.reshape(-1),
            grad_second_w.reshape(-1),
            grad_third_w.reshape(-1),
            grad_fourth_w.reshape(-1),
            conv_bias_grad.reshape(-1),
        ]
    )

    part_a, part_b = spread_blocks(
        sizes, slots_dev, block_owner, jnp.stack(coords).astype(jnp.int32),
        (grad_w_qkv, grad_w_out, grad_w_up, grad_w_down),
    )
    part_a = reduce_axis(part_a, "core", nc).astype(BF)
    part_b = reduce_axis(part_b, "core", nc).astype(BF)
    part_a = reduce_axis(part_a, "fx", nx).astype(BF)
    part_b = reduce_axis(part_b, "by", ny).astype(BF)
    part_a = reduce_axis(part_a, "by", ny).astype(BF)
    part_b = reduce_axis(part_b, "fx", nx).astype(BF)
    part_a = reduce_axis(part_a, "fz", nz)
    part_b = reduce_axis(part_b, "fz", nz)
    owned_grads = jnp.concatenate([part_a, part_b])

    small_total = small_local.shape[0]
    share = -(-small_total // (device_count * 128)) * 128
    padded_small = jnp.pad(small_local, (0, device_count * share - small_total))
    small_sum = padded_small.reshape(sizes + (share,))
    for axis, size in enumerate(sizes):
        small_sum = rolled(small_sum, axis, size, coords[axis])
    for axis in range(4):
        small_sum = reduce_axis(small_sum, ALL_AXES[axis], sizes[axis])
    squares = jnp.sum(owned_grads * owned_grads) + jnp.sum(small_sum * small_sum)
    carried = jnp.concatenate([small_sum, jnp.full((128,), squares, F32)])
    for axis in reversed(range(4)):
        carried = gather_axis(carried, ALL_AXES[axis], sizes[axis])
    for axis, size in enumerate(sizes):
        carried = rolled(carried, axis, size, size - coords[axis])
    carried = carried.reshape(device_count, share + 128)
    small_grad = carried[:, :share].reshape(-1)[:small_total]
    grad_norm = jnp.sqrt(jnp.sum(carried[:, share]))
    factor = 1.0 / jnp.maximum(grad_norm, CLIP_NORM)

    soap_out = soap(
        owned_grads, factor, master, moment1, moment2, stat_left, stat_right, basis_left, basis_right
    )
    small_first, small_second, small_new = adam_update(
        small_grad * factor, small_params, small_moment1, small_moment2
    )

    seen_frames = grad_seen.astype(BF).reshape(frames_seen, PAD_ROWS, D)
    long_terms = seen_frames[:frame_count].reshape(nz, nx, PAD_ROWS, D)
    long_terms = reduce_axis(long_terms.transpose(1, 0, 2, 3), "fx", nx).astype(BF)
    long_total = reduce_axis(long_terms, "fz", nz)
    partner_term = seen_frames[frame_count + 1]
    nothing = jnp.zeros_like(partner_term)
    to_previous = jnp.where(with_previous, partner_term, nothing)
    to_next = jnp.where(with_next, partner_term, nothing)
    short_total = (
        seen_frames[frame_count].astype(F32)
        + lax.ppermute(to_previous, FRAME_AXES, back_perm).astype(F32)
        + lax.ppermute(to_next, FRAME_AXES, frame_perm).astype(F32)
    )
    grad_normed_one = unpad_frames(jnp.concatenate([long_total, short_total]) + grad_own)
    hat, rstd = unpad_frames(own_hat), unpad_frames(own_rows(jnp.broadcast_to(seen_rstd, seen_hat.shape)))
    scaled = grad_normed_one * params_split["gain_one"]
    grad_inputs = grad_mixed + rstd * (
        scaled
        - jnp.mean(scaled, -1, keepdims=True)
        - hat * jnp.mean(scaled * hat, -1, keepdims=True)
    )
    grad_inputs = grad_inputs.reshape(2, FRAME_ROWS, D)
    grad_inputs = jnp.where(swap, grad_inputs[::-1], grad_inputs).reshape(2 * FRAME_ROWS, D)
    return (
        learned[None],
        grad_inputs[None],
        soap_out[0],
        soap_out[1],
        soap_out[2],
        soap_out[3],
        soap_out[4],
        soap_out[5],
        soap_out[6],
        small_first,
        small_second,
        small_new,
        grad_norm,
    )


def solution(mesh):
    frames, batches = mesh.shape["frame"], mesh.shape["batch"]
    split = Mesh(mesh.devices.reshape(frames // 2, 2, batches // 2, 2), ALL_AXES)
    batch = ("by", "core")
    slots = P(ALL_AXES, None, None)
    rows = P(batch, FRAME_AXES, None)
    return jax.shard_map(
        on_device,
        mesh=split,
        in_specs=(rows, rows, P(batch, None), P(batch, None), P()) + (slots,) * 7 + (P(),) * 3,
        out_specs=(rows, rows) + (slots,) * 7 + (P(),) * 4,
        check_vma=False,
    )
```

time: 2420 us -> 690 us (0.29)
  other arithmetic: 755 us -> 63.6 us
  waiting for transfers between devices: 767 us -> 205 us
  local copies, waits for them, and re-layouts: 497 us -> 73.2 us
  matrix products: 318 us -> 100 us
  Pallas kernels: 0 us -> 175 us
  blocking collectives: 41.3 us -> 0 us
  starting transfers between devices: 0.75 us -> 40 us
    another operation x12 -> x9, other arithmetic: 616 us -> 6.28 us  [the longest x5 4.08 us: gather_axis(): jnp.stack([value] + [moved(value, axis, size, -step) for step in range(1,...]
    reduce_scatter x1 -> x0, waiting for transfers between devices: 274 us -> none  [on_device(): lax.psum_scatter(grad_blocks[block_owner], ('frame', 'batch'), scatter_di...]
    all_gather x3 -> x1, waiting for transfers between devices: 220 us -> 7.64 us  [on_device(): gathered = lax.all_gather(master.astype(BF), ALL_AXES, axis=0, tiled=True)]
    dot_general x81 -> x14, matrix products: 279 us -> 68.1 us  [the longest x1 15.6 us: on_device(): jnp.dot(normed_two_low, w_up, preferred_element_type=F32)]
    ppermute x0 -> x36, waiting for transfers between devices: none -> 197 us  [the longest x32 197 us: moved(): lax.ppermute(value, axis, [(i, (i + step) % size) for i in range(size)])]
    pallas_call x0 -> x7, Pallas kernels: none -> 175 us  [the longest x1 43.1 us: finish(): pl.pallas_call(finish_kernel, in_specs=[pl.BlockSpec(memory_space=pltpu.S...]
    dynamic_update_slice x16 -> x0, local copies, waits for them, and re-layouts: 147 us -> none  [the longest x8 73.5 us: backward_one_block(): lax.dynamic_update_slice_in_dim(value_total, lax.dynamic_slice_in_dim(val...]
    unnamed x9 -> x1, waiting for transfers between devices: 140 us -> 0.02 us
  transfers between devices with their start and end apart: 7 -> 37, of which waited for: 7 -> 20; matrix products, arithmetic and copies ran while one was open for 6% -> 14% of each run, Pallas kernels for 0% -> 9%
where the time goes in v1:
time: 690 us; the launch traced here: 679 us
  waiting for transfers between devices  205 us (30%)
  Pallas kernels  175 us (25%)
  matrix products  100 us (14%)
  local copies, waits for them, and re-layouts  73.2 us (11%)
  other arithmetic  63.6 us (9%)
  starting transfers between devices  40 us (6%)
  between operations  22.4 us (3%)
    ppermute x32, waiting for transfers between devices, moved(): lax.ppermute(value, axis, [(i, (i + step) % size) for i in range(size)])  197 us
    pallas_call x1, Pallas kernels, finish(): pl.pallas_call(finish_kernel, in_specs=[pl.BlockSpec(memory_space=pltpu.S...  43.1 us
    pallas_call x1, Pallas kernels, spread_blocks(): pl.pallas_call(kernel, grid_spec=pltpu.PrefetchScalarGridSpec(num_scalar_...  39.8 us
    pallas_call x1, Pallas kernels, attend_back(): pl.pallas_call(kernel, grid=(PAIRS,), in_specs=[pair_spec(2 * PAD_ROWS),...  36.3 us
    ppermute x32, starting transfers between devices, moved(): lax.ppermute(value, axis, [(i, (i + step) % size) for i in range(size)])  35.9 us
    pallas_call x1, Pallas kernels, place_blocks(): pl.pallas_call(place_kernel, grid_spec=pltpu.PrefetchScalarGridSpec(num_s...  20.1 us
    unnamed x252, local copies, waits for them, and re-layouts  17.4 us
    dot_general x1, matrix products, on_device(): jnp.dot(normed_two_low, w_up, preferred_element_type=F32)  15.6 us
  transfers between devices with their start and end apart: 37, of which 20 were waited for; matrix products, arithmetic and copies ran while one was open for 14% of the time, Pallas kernels for 9%

profile of v1, /device:TPU:15, one launch (start us, length us, event | category | flops | bytes accessed | tf_op | source)
XLA Modules:
  0.0 679.1 jit_solution(1818921857926409879)
XLA Ops:
  25.1 16.8 %collective-permute-done = bf16[208,768]{1,0:T(8,128)(2,1)} collective-permute-done((bf16[208,768]{1,0:T(8,128)(2,1)}, bf16[208,768]{1,0:T(8,128)(2,1)}, u32[]{:S(2)}, u32[]{:S(2)}) %collective-permute-start) | collective-permute-done | bytes 319520 | tf_op jit(solution)/shard_map/ppermute | solution.py:430
  55.1 10.2 %shard_map.251 = (f32[14,128,128]{2,1,0:T(8,128)}, f32[14,128,128]{2,1,0:T(8,128)}) custom-call(f32[14,128,128]{2,1,0:T(8,128)} %sl.3, f32[14,128,128]{2,1,0:T(8,128)} %sr.3, f32[14,128,128]{2,1,0:T(8,128)} %bl.5, f32[14,128,128]{2,1,0:T(8,128)} %br.5), custom_call_target="tpu_custom_call" | custom-call | tf_op jit(solution)/shard_map/pallas_call | solution.py:183
  66.4 11.4 %collective-permute-done.3 = bf16[2,208,768]{2,1,0:T(8,128)(2,1)} collective-permute-done((bf16[2,208,768]{2,1,0:T(8,128)(2,1)}, bf16[2,208,768]{2,1,0:T(8,128)(2,1)}, u32[]{:S(2)}, u32[]{:S(2)}) %collective-permute-start.3) | collective-permute-done | bytes 639008 | tf_op jit(solution)/shard_map/ppermute | solution.py:430
  77.8 52.9 %collective-permute-done.2 = bf16[2,208,768]{2,1,0:T(8,128)(2,1)} collective-permute-done((bf16[2,208,768]{2,1,0:T(8,128)(2,1)}, bf16[2,208,768]{2,1,0:T(8,128)(2,1)}, u32[]{:S(2)}, u32[]{:S(2)}) %collective-permute-start.2) | collective-permute-done | bytes 639008 | tf_op jit(solution)/shard_map/ppermute | solution.py:430
  130.7 5.7 collective-permute-done.1
  140.3 3.7 multiply_reduce_fusion.1
  153.4 7.6 %all-gather.2.cloned.1.call-done.gathered = bf16[448,128,128]{2,1,0:T(8,128)(2,1)} async-done(((bf16[14,128,128]{2,1,0:T(8,128)(2,1)}), bf16[448,128,128]{2,1,0:T(8,128)(2,1)}) %all-gather.2.cloned.1.call-update) | async-done | bytes 14680080 | tf_op jit(solution)/shard_map/all_gather | solution.py:620
  161.1 20.1 %shard_map.246 = (bf16[768,2304]{1,0:T(8,128)(2,1)S(1)}, bf16[768,768]{1,0:T(8,128)(2,1)S(1)}, bf16[768,3072]{1,0:T(8,128)(2,1)}, bf16[3072,768]{1,0:T(8,128)(2,1)}) custom-call(s32[448]{0:T(512)S(1)} %copy-done.2, bf16[448,128,128]{2,1,0:T(8,128)(2,1)} %all-gather.2.cloned.1.call-done.gathered), custom_call_target="tpu_custom_call" | custom-call | tf_op jit(solution)/shard_map/pallas_call | solution.py:353
  181.2 7.1 %fusion.refs_1_.refs_2_ = bf16[2080,1536]{1,0:T(8,128)(2,1)} fusion(bf16[2080,768]{1,0:T(8,128)(2,1)S(1)} %copy-done.24, f32[1536]{0:T(1024)S(1)} %concatenate.64, bf16[768,2304]{1,0:T(8,128)(2,1)S(1)} %get-tuple-element.38), kind=kOutput, calls=%fused_computation.2 | convolution fusion | flops 4913725440 | bytes 11952128 | tf_op jit(solution)/shard_map/dot_general | solution.py:638
  189.0 13.5 %shard_map.247 = bf16[416,768]{1,0:T(8,128)(2,1)S(1)} custom-call(bf16[416,768]{1,0:T(8,128)(2,1)S(1)} %fusion.21.refs_0_, bf16[2080,1536]{1,0:T(8,128)(2,1)} %fusion.refs_1_.refs_2_, bf16[2080,1536]{1,0:T(8,128)(2,1)} %fusion.refs_1_.refs_2_, f32[1,2080]{1,0:T(1,128)S(1)} %or_select_fusion.refs_3_), custom_call_target="tpu_custom_call" | custom-call | tf_op jit(solution)/shard_map/pallas_call | solution.py:504
  203.5 2.4 fusion.545
  206.3 15.6 %multiply_convert_fusion = (bf16[392,3072]{1,0:T(8,128)(2,1)S(1)}, f32[392,3072]{1,0:T(8,128)}, f32[392,3072]{1,0:T(8,128)}) fusion(f32[3072]{0:T(1024)S(1)} %copy-done.86, bf16[768,3072]{1,0:T(8,128)(2,1)} %get-tuple-element.40, f32[392,768]{1,0:T(8,128)S(1)} %get-tuple-element.164, f32[768]{0:T(1024)S(1)} %copy-done.90, f32[768]{0:T(1024)S(1)} %copy-done.84, ...), kind=kOutput, calls=%fused_computation.19 | convolution fusion | flops 1930672128 | bytes 17986624 | tf_op jit(solution)/shard_map/dot_general | solution.py:651
  221.9 3.1 fusion.546
  225.1 2.9 reshape.544
  240.9 2.4 fusion.548
  243.3 2.6 reshape.545
  245.9 6.4 fusion.547
  261.5 2.4 reshape.546
  263.9 2.8 multiply_reduce_fusion.4
  268.8 8.9 %convert_reduce_fusion.1 = (f32[3072]{0:T(1024)}, bf16[392,3072]{1,0:T(8,128)(2,1)S(1)}) fusion(f32[392,3072]{1,0:T(8,128)} %get-tuple-element.99, f32[392,3072]{1,0:T(8,128)} %get-tuple-element.165, f32[3072]{0:T(1024)S(1)} %copy-done.86, bf16[392,768]{1,0:T(8,128)(2,1)S(1)} %get-tuple-element.89, bf16[3072,768]{1,0:T(8,128)(2,1)} %get-tuple-element.41), kind=kOutput, calls=%fused_computation.17 | convolution fusion | flops 1870156800 | bytes 17387520 | tf_op jit(solution)/shard_map/nd,fd->nf/dot_general | solution.py:696
  277.8 2.9 multiply_reduce_fusion.5
  285.9 36.3 %shard_map.248 = (bf16[416,768]{1,0:T(8,128)(2,1)S(1)}, bf16[2080,768]{1,0:T(8,128)(2,1)S(1)}, bf16[2080,768]{1,0:T(8,128)(2,1)}) custom-call(bf16[416,768]{1,0:T(8,128)(2,1)S(1)} %fusion.21.refs_0_, bf16[2080,1536]{1,0:T(8,128)(2,1)} %fusion.refs_1_.refs_2_, bf16[2080,1536]{1,0:T(8,128)(2,1)} %fusion.refs_1_.refs_2_, f32[2080,1]{1,0:T(8,128)S(1)} %fusion.27.refs_3_, ...), custom_call_target="tpu_custom_call" | custom-call | tf_op jit(solution)/shard_map/pallas_call | solution.py:526
  326.1 10.6 %fusion.525 = (f32[768]{0:T(1024)}, f32[768]{0:T(1024)}, bf16[2080,768]{1,0:T(8,128)(2,1)S(1)}) fusion(f32[2080,768]{1,0:T(8,128)} %copy-done.15, bf16[2080,1536]{1,0:T(8,128)(2,1)S(1)} %constant_dynamic-update-slice_fusion, bf16[768,2304]{1,0:T(8,128)(2,1)S(1)} %copy-done.1), kind=kOutput, calls=%fused_computation.822 | convolution fusion | flops 4913723392 | bytes 18339840 | tf_op jit(solution)/shard_map/ne,de->nd/dot_general | solution.py:725
  343.1 6.1 convolution_convert_fusion.2
  352.3 4.5 convolution_convert_fusion.1.refs_4_
  356.8 4.4 convolution_convert_fusion.refs_5_
  363.2 4.6 collective-permute-start.6
  368.1 39.8 %shard_map.249 = (bf16[224,128,128]{2,1,0:T(8,128)(2,1)}, bf16[224,128,128]{2,1,0:T(8,128)(2,1)}) custom-call(s32[448]{0:T(512)S(1)} %copy-done.2, s32[4]{0:T(128)S(1)} %pad_add_fusion.22.refs_1_, bf16[768,2304]{1,0:T(8,128)(2,1)S(1)} %pad_maximum_fusion.refs_2_, bf16[768,768]{1,0:T(8,128)(2,1)S(1)} %convolution_convert_fusion.3.refs_3_, ...), custom_call_target="tpu_custom_call" | custom-call | tf_op jit(solution)/shard_map/pallas_call | solution.py:413
  410.3 10.8 %fusion.535 = (bf16[112,128,128]{2,1,0:T(8,128)(2,1)}, bf16[112,128,128]{2,1,0:T(8,128)(2,1)}, bf16[112,128,128]{2,1,0:T(8,128)(2,1)}, bf16[112,128,128]{2,1,0:T(8,128)(2,1)}) fusion(bf16[224,128,128]{2,1,0:T(8,128)(2,1)} %get-tuple-element.45, bf16[224,128,128]{2,1,0:T(8,128)(2,1)} %get-tuple-element.46), kind=kLoop, calls=%fused_computation.828 | loop fusion | bytes 29360128 | tf_op jit(solution)/shard_map/slice | solution.py:436
  423.4 2.6 collective-permute-start.9
  433.4 13.6 %collective-permute-done.8 = bf16[208,768]{1,0:T(8,128)(2,1)} collective-permute-done((bf16[208,768]{1,0:T(8,128)(2,1)}, bf16[208,768]{1,0:T(8,128)(2,1)}, u32[]{:S(2)}, u32[]{:S(2)}) %collective-permute-start.8) | collective-permute-done | bytes 319520 | tf_op jit(solution)/shard_map/ppermute | solution.py:430
  447.1 6.8 %collective-permute-done.7 = bf16[208,768]{1,0:T(8,128)(2,1)} collective-permute-done((bf16[208,768]{1,0:T(8,128)(2,1)}, bf16[208,768]{1,0:T(8,128)(2,1)}, u32[]{:S(2)}, u32[]{:S(2)}) %collective-permute-start.7) | collective-permute-done | bytes 319520 | tf_op jit(solution)/shard_map/ppermute | solution.py:430
  455.5 3.6 fusion.526
  462.7 3.4 collective-permute-start.13
  467.7 2.4 reshape.548
  473.6 5.4 fusion.1
  481.0 4.3 fusion.2
  487.5 31.6 %collective-permute-done.16 = f32[2,2176]{1,0:T(2,128)S(1)} collective-permute-done((f32[2,2176]{1,0:T(2,128)S(1)}, f32[2,2176]{1,0:T(2,128)S(1)}, u32[]{:S(2)}, u32[]{:S(2)}) %collective-permute-start.16) | collective-permute-done | bytes 17440 | tf_op jit(solution)/shard_map/ppermute | solution.py:430
  519.1 3.1 collective-permute-start.17
  528.2 17.5 %collective-permute-done.26 = bf16[4,7,128,128]{3,2,1,0:T(8,128)(2,1)S(1)} collective-permute-done((bf16[4,7,128,128]{3,2,1,0:T(8,128)(2,1)S(1)}, bf16[4,7,128,128]{3,2,1,0:T(8,128)(2,1)S(1)}, u32[]{:S(2)}, u32[]{:S(2)}) %collective-permute-start.26) | collective-permute-done | bytes 917536 | tf_op jit(solution)/shard_map/ppermute | solution.py:430
  554.7 11.2 %collective-permute-done.28 = bf16[7,128,128]{2,1,0:T(8,128)(2,1)S(1)} collective-permute-done((bf16[7,128,128]{2,1,0:T(8,128)(2,1)S(1)}, bf16[7,128,128]{2,1,0:T(8,128)(2,1)S(1)}, u32[]{:S(2)}, u32[]{:S(2)}) %collective-permute-start.28) | collective-permute-done | bytes 229408 | tf_op jit(solution)/shard_map/ppermute | solution.py:430
  565.9 12.9 %collective-permute-done.27 = bf16[7,128,128]{2,1,0:T(8,128)(2,1)S(1)} collective-permute-done((bf16[7,128,128]{2,1,0:T(8,128)(2,1)S(1)}, bf16[7,128,128]{2,1,0:T(8,128)(2,1)S(1)}, u32[]{:S(2)}, u32[]{:S(2)}) %collective-permute-start.27) | collective-permute-done | bytes 229408 | tf_op jit(solution)/shard_map/ppermute | solution.py:430
  578.9 3.0 collective-permute-done.23
  583.7 4.9 collective-permute-done.21
  592.3 2.4 reshape.555
  596.5 3.4 multiply_add_fusion
  603.6 11.9 %shard_map.250 = (f32[14,128,128]{2,1,0:T(8,128)}, f32[14,128,128]{2,1,0:T(8,128)}, f32[14,128,128]{2,1,0:T(8,128)}, f32[14,128,128]{2,1,0:T(8,128)}, f32[14,128,128]{2,1,0:T(8,128)}) custom-call(f32[14,128,128]{2,1,0:T(8,128)} %get-tuple-element.120.g, f32[14,128,128]{2,1,0:T(8,128)} %bl.5, f32[14,128,128]{2,1,0:T(8,128)} %br.5), custom_call_target="tpu_custom_call" | custom-call | tf_op jit(solution)/shard_map/pallas_call | solution.py:198
  627.5 43.1 %shard_map.252 = (f32[14,128,128]{2,1,0:T(8,128)}, f32[14,128,128]{2,1,0:T(8,128)}, f32[14,128,128]{2,1,0:T(8,128)}, f32[14,128,128]{2,1,0:T(8,128)}, f32[14,128...) custom-call(f32[1]{0:T(128)} %bitcast.136.factor, f32[14,128,128]{2,1,0:T(8,128)} %get-tuple-element.47.rot, ...), custom_call_target="tpu_custom_call" | custom-call | tf_op jit(solution)/shard_map/pallas_call | solution.py:285
  (498 shorter events, 150.9 us)
Async XLA Ops:
  7.2 153.9 %all-gather.2.cloned.1.call-start = ((), (), s32[]{:S(2)}) async-start(), calls=%async_computation | async-start | bytes 15138816 | tf_op jit(solution)/shard_map/all_gather | solution.py:620
  15.6 49.7 %collective-permute-start.4 = (bf16[208,768]{1,0:T(8,128)(2,1)}, bf16[208,768]{1,0:T(8,128)(2,1)}, u32[]{:S(2)}, u32[]{:S(2)}) collective-permute-start(bf16[208,768]{1,0:T(8,128)(2,1)} %get-tuple-element.132), channel_id=1, source_target_pairs={{4,0},{8,4},{12,8},{16,12},{20,16},{24,20},{28,24},{0,28},{5,1},{9... | collective-permute-start | bytes 958472 | tf_op jit(solution)/shard_map/ppermute | solution.py:607
  15.9 49.5 %collective-permute-start.5 = (bf16[208,768]{1,0:T(8,128)(2,1)}, bf16[208,768]{1,0:T(8,128)(2,1)}, u32[]{:S(2)}, u32[]{:S(2)}) collective-permute-start(bf16[208,768]{1,0:T(8,128)(2,1)} %get-tuple-element.132), channel_id=1, source_target_pairs={{0,4},{4,8},{8,12},{12,16},{16,20},{20,24},{24,28},{28,0},{1,5},{5... | collective-permute-start | bytes 958472 | tf_op jit(solution)/shard_map/ppermute | solution.py:606
  18.0 23.9 %collective-permute-start = (bf16[208,768]{1,0:T(8,128)(2,1)}, bf16[208,768]{1,0:T(8,128)(2,1)}, u32[]{:S(2)}, u32[]{:S(2)}) collective-permute-start(bf16[208,768]{1,0:T(8,128)(2,1)} %get-tuple-element.131), channel_id=1, source_target_pairs={{0,4},{4,0},{1,5},{5,1},{2,6},{6,2},{3,7},{7,3},{8,12},{12,8},{9,1... | collective-permute-start | bytes 958472 | tf_op jit(solution)/shard_map/ppermute | solution.py:430
  22.6 124.4 %copy-start.67 = (f32[768]{0:T(1024)}, f32[768]{0:T(1024)S(1)}, u32[]{:S(2)}) copy-start(f32[768]{0:T(1024)S(1)} %get-tuple-element.153) | copy-start | bytes 9220
  44.1 33.7 %collective-permute-start.3 = (bf16[2,208,768]{2,1,0:T(8,128)(2,1)}, bf16[2,208,768]{2,1,0:T(8,128)(2,1)}, u32[]{:S(2)}, u32[]{:S(2)}) collective-permute-start(bf16[2,208,768]{2,1,0:T(8,128)(2,1)} %get-tuple-element.129), channel_id=1, source_target_pairs={{0,8},{8,16},{16,24},{24,0},{1,9},{9,17},{17,25},{25,1},{2,10},{10... | collective-permute-start | bytes 1916936 | tf_op jit(solution)/shard_map/ppermute | solution.py:430
  45.4 85.3 %collective-permute-start.2 = (bf16[2,208,768]{2,1,0:T(8,128)(2,1)}, bf16[2,208,768]{2,1,0:T(8,128)(2,1)}, u32[]{:S(2)}, u32[]{:S(2)}) collective-permute-start(bf16[2,208,768]{2,1,0:T(8,128)(2,1)} %get-tuple-element.129), channel_id=1, source_target_pairs={{0,16},{8,24},{16,0},{24,8},{1,17},{9,25},{17,1},{25,9},{2,18},{10... | collective-permute-start | bytes 1916936 | tf_op jit(solution)/shard_map/ppermute | solution.py:430
  47.7 88.7 %collective-permute-start.1 = (bf16[2,208,768]{2,1,0:T(8,128)(2,1)}, bf16[2,208,768]{2,1,0:T(8,128)(2,1)}, u32[]{:S(2)}, u32[]{:S(2)}) collective-permute-start(bf16[2,208,768]{2,1,0:T(8,128)(2,1)} %get-tuple-element.129), channel_id=1, source_target_pairs={{0,24},{8,0},{16,8},{24,16},{1,25},{9,1},{17,9},{25,17},{2,26},{10... | collective-permute-start | bytes 1916936 | tf_op jit(solution)/shard_map/ppermute | solution.py:430
  55.1 81.3 %copy-start.29 = (bf16[1,2,208,768]{3,2,1,0:T(8,128)(2,1)S(1)}, bf16[1,2,208,768]{3,2,1,0:T(8,128)(2,1)}, u32[]{:S(2)}) copy-start(bf16[1,2,208,768]{3,2,1,0:T(8,128)(2,1)} %get-tuple-element.128) | copy-start | bytes 1916932
  150.2 38.0 %copy-start.57 = (bf16[208,768]{1,0:T(8,128)(2,1)}, bf16[208,768]{1,0:T(8,128)(2,1)S(1)}, u32[]{:S(2)}) copy-start(bf16[208,768]{1,0:T(8,128)(2,1)S(1)} %get-tuple-element.111) | copy-start | bytes 958468
  150.2 38.0 %copy-start.59 = (bf16[208,768]{1,0:T(8,128)(2,1)}, bf16[208,768]{1,0:T(8,128)(2,1)S(1)}, u32[]{:S(2)}) copy-start(bf16[208,768]{1,0:T(8,128)(2,1)S(1)} %get-tuple-element.112) | copy-start | bytes 958468
  361.2 69.2 %collective-permute-start.11 = (bf16[208,768]{1,0:T(8,128)(2,1)}, bf16[208,768]{1,0:T(8,128)(2,1)}, u32[]{:S(2)}, u32[]{:S(2)}) collective-permute-start(bf16[208,768]{1,0:T(8,128)(2,1)} %get-tuple-element.110), channel_id=1, source_target_pairs={{0,4},{4,8},{8,12},{12,16},{16,20},{20,24},{24,28},{28,0},{1,5},{5... | collective-permute-start | bytes 958472 | tf_op jit(solution)/shard_map/ppermute | solution.py:804
  362.9 69.2 %collective-permute-start.10 = (bf16[208,768]{1,0:T(8,128)(2,1)}, bf16[208,768]{1,0:T(8,128)(2,1)}, u32[]{:S(2)}, u32[]{:S(2)}) collective-permute-start(bf16[208,768]{1,0:T(8,128)(2,1)} %get-tuple-element.109), channel_id=1, source_target_pairs={{4,0},{8,4},{12,8},{16,12},{20,16},{24,20},{28,24},{0,28},{5,1},{9... | collective-permute-start | bytes 958472 | tf_op jit(solution)/shard_map/ppermute | solution.py:803
  363.2 57.9 %collective-permute-start.6 = (bf16[4,208,768]{2,1,0:T(8,128)(2,1)S(1)}, bf16[4,208,768]{2,1,0:T(8,128)(2,1)S(1)}, u32[]{:S(2)}, u32[]{:S(2)}) collective-permute-start(bf16[4,208,768]{2,1,0:T(8,128)(2,1)S(1)} %slice_bitcast_fusion.4), channel_id=1, source_target_pairs={{0,4},{4,0},{1,5},{5,1},{2,6},{6,2},{3,7},{7,3},{8,12},{12,8},{9,1... | collective-permute-start | bytes 3833864 | tf_op jit(solution)/shard_map/ppermute | solution.py:430
  368.1 39.8 %copy-start.44 = (bf16[392,72]{0,1:T(8,128)(2,1)S(1)}, bf16[392,72]{0,1:T(8,128)(2,1)}, u32[]{:S(2)}) copy-start(bf16[392,72]{0,1:T(8,128)(2,1)} %reshape.546) | copy-start | bytes 169348
  368.1 40.2 %copy-start.36 = (f32[2,16,16,9,8]{2,4,1,0,3:T(8,128)S(1)}, f32[2,16,16,9,8]{2,4,1,0,3:T(8,128)}, u32[]{:S(2)}) copy-start(f32[2,16,16,9,8]{2,4,1,0,3:T(8,128)} %copy-done.35) | copy-start | bytes 442372
  368.1 40.2 %copy-start.48 = (f32[2,14,14,8]{2,3,1,0:T(8,128)S(1)}, f32[2,14,14,8]{2,3,1,0:T(8,128)}, u32[]{:S(2)}) copy-start(f32[2,14,14,8]{2,3,1,0:T(8,128)} %copy-done.47) | copy-start | bytes 37636
  368.1 40.2 %copy-start.64 = (f32[2,14,14,1,8]{2,4,1,0,3:T(8,128)S(1)}, f32[2,14,14,1,8]{2,4,1,0,3:T(8,128)}, u32[]{:S(2)}) copy-start(f32[2,14,14,1,8]{2,4,1,0,3:T(8,128)} %copy-done.63) | copy-start | bytes 37636
  368.1 40.2 %copy-start.102 = (f32[8]{0:T(128)S(1)}, f32[8]{0:T(128)}, u32[]{:S(2)}) copy-start(f32[8]{0:T(128)} %get-tuple-element.138) | copy-start | bytes 100
  423.4 31.9 %copy-start.27 = (f32[208,768]{1,0:T(8,128)S(1)}, f32[208,768]{1,0:T(8,128)}, u32[]{:S(2)}) copy-start(f32[208,768]{1,0:T(8,128)} %get-tuple-element.107) | copy-start | bytes 1916932
  423.4 31.9 %copy-start.28 = (f32[208,768]{1,0:T(8,128)S(1)}, f32[208,768]{1,0:T(8,128)}, u32[]{:S(2)}) copy-start(f32[208,768]{1,0:T(8,128)} %get-tuple-element.108) | copy-start | bytes 1916932
  423.4 10.0 %collective-permute-start.9 = (bf16[208,768]{1,0:T(8,128)(2,1)}, bf16[208,768]{1,0:T(8,128)(2,1)}, u32[]{:S(2)}, u32[]{:S(2)}) collective-permute-start(bf16[208,768]{1,0:T(8,128)(2,1)} %get-tuple-element.118), channel_id=1, source_target_pairs={{0,24},{8,0},{16,8},{24,16},{1,25},{9,1},{17,9},{25,17},{2,26},{10... | collective-permute-start | bytes 958472 | tf_op jit(solution)/shard_map/ppermute | solution.py:430
  426.0 21.0 %collective-permute-start.8 = (bf16[208,768]{1,0:T(8,128)(2,1)}, bf16[208,768]{1,0:T(8,128)(2,1)}, u32[]{:S(2)}, u32[]{:S(2)}) collective-permute-start(bf16[208,768]{1,0:T(8,128)(2,1)} %get-tuple-element.119), channel_id=1, source_target_pairs={{0,16},{8,24},{16,0},{24,8},{1,17},{9,25},{17,1},{25,9},{2,18},{10... | collective-permute-start | bytes 958472 | tf_op jit(solution)/shard_map/ppermute | solution.py:430
  426.0 27.9 %collective-permute-start.7 = (bf16[208,768]{1,0:T(8,128)(2,1)}, bf16[208,768]{1,0:T(8,128)(2,1)}, u32[]{:S(2)}, u32[]{:S(2)}) collective-permute-start(bf16[208,768]{1,0:T(8,128)(2,1)} %get-tuple-element.117), channel_id=1, source_target_pairs={{0,8},{8,16},{16,24},{24,0},{1,9},{9,17},{17,25},{25,1},{2,10},{10... | collective-permute-start | bytes 958472 | tf_op jit(solution)/shard_map/ppermute | solution.py:430
  430.4 43.2 %collective-permute-start.24 = (bf16[2,2,4,7,128,128]{5,4,3,2,1,0:T(8,128)(2,1)}, bf16[2,2,4,7,128,128]{5,4,3,2,1,0:T(8,128)(2,1)}, u32[]{:S(2)}, u32[]{:S(2)}) collective-permute-start(bf16[2,2,4,7,128,128]{5,4,3,2,1,0:T(8,128)(2,1)} %bitcast.399), channel_id=1, source_target_pairs={{0,1},{1,0},{2,3},{3,2},{4,5},{5,4},{6,7},{7,6},{8,9},{9,8},{10,11... | collective-permute-start | bytes 11010056 | tf_op jit(solution)/shard_map/ppermute | solution.py:430
  432.1 47.5 %collective-permute-start.18 = (bf16[2,2,4,7,128,128]{5,4,3,2,1,0:T(8,128)(2,1)}, bf16[2,2,4,7,128,128]{5,4,3,2,1,0:T(8,128)(2,1)}, u32[]{:S(2)}, u32[]{:S(2)}) collective-permute-start(bf16[2,2,4,7,128,128]{5,4,3,2,1,0:T(8,128)(2,1)} %bitcast.398), channel_id=1, source_target_pairs={{0,1},{1,0},{2,3},{3,2},{4,5},{5,4},{6,7},{7,6},{8,9},{9,8},{10,11... | collective-permute-start | bytes 11010056 | tf_op jit(solution)/shard_map/ppermute | solution.py:430
  462.6 7.5 %collective-permute-start.14 = (f32[2,2,2,2176]{3,2,1,0:T(2,128)S(1)}, f32[2,2,2,2176]{3,2,1,0:T(2,128)S(1)}, u32[]{:S(2)}, u32[]{:S(2)}) collective-permute-start(f32[2,2,2,2176]{3,2,1,0:T(2,128)S(1)} %get-tuple-element.136), channel_id=1, source_target_pairs={{0,24},{8,0},{16,8},{24,16},{1,25},{9,1},{17,9},{25,17},{2,26},{10... | collective-permute-start | bytes 208904 | tf_op jit(solution)/shard_map/ppermute | solution.py:430
  462.7 7.5 %collective-permute-start.13 = (f32[2,2,2,2176]{3,2,1,0:T(2,128)S(1)}, f32[2,2,2,2176]{3,2,1,0:T(2,128)S(1)}, u32[]{:S(2)}, u32[]{:S(2)}) collective-permute-start(f32[2,2,2,2176]{3,2,1,0:T(2,128)S(1)} %get-tuple-element.135), channel_id=1, source_target_pairs={{0,16},{8,24},{16,0},{24,8},{1,17},{9,25},{17,1},{25,9},{2,18},{10... | collective-permute-start | bytes 208904 | tf_op jit(solution)/shard_map/ppermute | solution.py:430
  466.0 4.6 collective-permute-start.12
  470.7 2.9 collective-permute-start.15
  479.2 43.0 %collective-permute-start.25 = (bf16[2,4,7,128,128]{4,3,2,1,0:T(8,128)(2,1)S(1)}, bf16[2,4,7,128,128]{4,3,2,1,0:T(8,128)(2,1)S(1)}, u32[]{:S(2)}, u32[]{:S(2)}) collective-permute-start(bf16[2,4,7,128,128]{4,3,2,1,0:T(8,128)(2,1)S(1)} %slice_bitcast_fusion), channel_id=1, source_target_pairs={{0,2},{2,0},{1,3},{3,1},{4,6},{6,4},{5,7},{7,5},{8,10},{10,8},{9,1... | collective-permute-start | bytes 5505032 | tf_op jit(solution)/shard_map/ppermute | solution.py:430
  485.6 39.4 %collective-permute-start.19 = (bf16[2,4,7,128,128]{4,3,2,1,0:T(8,128)(2,1)S(1)}, bf16[2,4,7,128,128]{4,3,2,1,0:T(8,128)(2,1)S(1)}, u32[]{:S(2)}, u32[]{:S(2)}) collective-permute-start(bf16[2,4,7,128,128]{4,3,2,1,0:T(8,128)(2,1)S(1)} %slice_bitcast_fusion.2), channel_id=1, source_target_pairs={{0,4},{4,0},{1,5},{5,1},{2,6},{6,2},{3,7},{7,3},{8,12},{12,8},{9,1... | collective-permute-start | bytes 5505032 | tf_op jit(solution)/shard_map/ppermute | solution.py:430
  486.0 33.0 %collective-permute-start.16 = (f32[2,2176]{1,0:T(2,128)S(1)}, f32[2,2176]{1,0:T(2,128)S(1)}, u32[]{:S(2)}, u32[]{:S(2)}) collective-permute-start(f32[2,2176]{1,0:T(2,128)S(1)} %slice_bitcast_fusion.28), channel_id=1, source_target_pairs={{0,2},{2,0},{1,3},{3,1},{4,6},{6,4},{5,7},{7,5},{8,10},{10,8},{9,1... | collective-permute-start | bytes 52232 | tf_op jit(solution)/shard_map/ppermute | solution.py:430
  519.1 8.5 %collective-permute-start.17 = (f32[2176]{0:T(1024)S(1)}, f32[2176]{0:T(1024)S(1)}, u32[]{:S(2)}, u32[]{:S(2)}) collective-permute-start(f32[2176]{0:T(1024)S(1)} %get-tuple-element.73), channel_id=1, source_target_pairs={{0,1},{1,0},{2,3},{3,2},{4,5},{5,4},{6,7},{7,6},{8,9},{9,8},{10,11... | collective-permute-start | bytes 26120 | tf_op jit(solution)/shard_map/ppermute | solution.py:430
  523.3 22.5 %collective-permute-start.26 = (bf16[4,7,128,128]{3,2,1,0:T(8,128)(2,1)S(1)}, bf16[4,7,128,128]{3,2,1,0:T(8,128)(2,1)S(1)}, u32[]{:S(2)}, u32[]{:S(2)}) collective-permute-start(bf16[4,7,128,128]{3,2,1,0:T(8,128)(2,1)S(1)} %slice_bitcast_fusion.6), channel_id=1, source_target_pairs={{0,4},{4,0},{1,5},{5,1},{2,6},{6,2},{3,7},{7,3},{8,12},{12,8},{9,1... | collective-permute-start | bytes 2752520 | tf_op jit(solution)/shard_map/ppermute | solution.py:430
  526.0 24.3 %collective-permute-start.20 = (bf16[4,7,128,128]{3,2,1,0:T(8,128)(2,1)S(1)}, bf16[4,7,128,128]{3,2,1,0:T(8,128)(2,1)S(1)}, u32[]{:S(2)}, u32[]{:S(2)}) collective-permute-start(bf16[4,7,128,128]{3,2,1,0:T(8,128)(2,1)S(1)} %slice_bitcast_fusion.8), channel_id=1, source_target_pairs={{0,2},{2,0},{1,3},{3,1},{4,6},{6,4},{5,7},{7,5},{8,10},{10,8},{9,1... | collective-permute-start | bytes 2752520 | tf_op jit(solution)/shard_map/ppermute | solution.py:430
  546.2 6.2 collective-permute-start.29
  548.0 17.9 %collective-permute-start.28 = (bf16[7,128,128]{2,1,0:T(8,128)(2,1)S(1)}, bf16[7,128,128]{2,1,0:T(8,128)(2,1)S(1)}, u32[]{:S(2)}, u32[]{:S(2)}) collective-permute-start(bf16[7,128,128]{2,1,0:T(8,128)(2,1)S(1)} %get-tuple-element.127), channel_id=1, source_target_pairs={{0,16},{8,24},{16,0},{24,8},{1,17},{9,25},{17,1},{25,9},{2,18},{10... | collective-permute-start | bytes 688136 | tf_op jit(solution)/shard_map/ppermute | solution.py:430
  549.7 29.1 %collective-permute-start.27 = (bf16[7,128,128]{2,1,0:T(8,128)(2,1)S(1)}, bf16[7,128,128]{2,1,0:T(8,128)(2,1)S(1)}, u32[]{:S(2)}, u32[]{:S(2)}) collective-permute-start(bf16[7,128,128]{2,1,0:T(8,128)(2,1)S(1)} %get-tuple-element.125), channel_id=1, source_target_pairs={{0,8},{8,16},{16,24},{24,0},{1,9},{9,17},{17,25},{25,1},{2,10},{10... | collective-permute-start | bytes 688136 | tf_op jit(solution)/shard_map/ppermute | solution.py:430
  550.8 31.2 %collective-permute-start.23 = (bf16[7,128,128]{2,1,0:T(8,128)(2,1)S(1)}, bf16[7,128,128]{2,1,0:T(8,128)(2,1)S(1)}, u32[]{:S(2)}, u32[]{:S(2)}) collective-permute-start(bf16[7,128,128]{2,1,0:T(8,128)(2,1)S(1)} %get-tuple-element.123), channel_id=1, source_target_pairs={{0,24},{8,0},{16,8},{24,16},{1,25},{9,1},{17,9},{25,17},{2,26},{10... | collective-permute-start | bytes 688136 | tf_op jit(solution)/shard_map/ppermute | solution.py:430
  551.7 32.1 %collective-permute-start.22 = (bf16[7,128,128]{2,1,0:T(8,128)(2,1)S(1)}, bf16[7,128,128]{2,1,0:T(8,128)(2,1)S(1)}, u32[]{:S(2)}, u32[]{:S(2)}) collective-permute-start(bf16[7,128,128]{2,1,0:T(8,128)(2,1)S(1)} %get-tuple-element.124), channel_id=1, source_target_pairs={{0,16},{8,24},{16,0},{24,8},{1,17},{9,25},{17,1},{25,9},{2,18},{10... | collective-permute-start | bytes 688136 | tf_op jit(solution)/shard_map/ppermute | solution.py:430
  552.5 36.2 %collective-permute-start.21 = (bf16[7,128,128]{2,1,0:T(8,128)(2,1)S(1)}, bf16[7,128,128]{2,1,0:T(8,128)(2,1)S(1)}, u32[]{:S(2)}, u32[]{:S(2)}) collective-permute-start(bf16[7,128,128]{2,1,0:T(8,128)(2,1)S(1)} %get-tuple-element.122), channel_id=1, source_target_pairs={{0,8},{8,16},{16,24},{24,0},{1,9},{9,17},{17,25},{25,1},{2,10},{10... | collective-permute-start | bytes 688136 | tf_op jit(solution)/shard_map/ppermute | solution.py:430
  591.8 4.3 collective-permute-start.30
  596.2 5.1 collective-permute-start.31
  601.3 14.2 %collective-permute-start.32 = (f32[2,2,2304]{2,1,0:T(2,128)S(1)}, f32[2,2,2304]{2,1,0:T(2,128)S(1)}, u32[]{:S(2)}, u32[]{:S(2)}) collective-permute-start(f32[2,2,2304]{2,1,0:T(2,128)S(1)} %get-tuple-element.155), channel_id=1, source_target_pairs={{0,4},{4,0},{1,5},{5,1},{2,6},{6,2},{3,7},{7,3},{8,12},{12,8},{9,1... | collective-permute-start | bytes 110600 | tf_op jit(solution)/shard_map/ppermute | solution.py:430
  615.5 4.4 collective-permute-start.33
  617.1 5.1 collective-permute-start.34
  619.0 4.7 collective-permute-start.35
  (108 other events, 462.9 us)
Sparse Core Ops, SparseCore 0:
  11.4 149.5 all-gather.1

commit v2 on v1

--- a/solution.py
+++ b/solution.py
@@ -2,6 +2,7 @@
 
 import jax
 import jax.numpy as jnp
+import numpy as np
 from jax import lax
 from jax.experimental import pallas as pl
 from jax.experimental.pallas import tpu as pltpu
@@ -192,10 +193,23 @@
     ql[0] = dot_parts(u, gp, NT_)
     qr[0] = dot_parts(v, gp, TN)
 
-def raw_products(g, bl, br):
+def raw_products(ranks, g, bl, br):
     n = g.shape[0]
     shape = jax.ShapeDtypeStruct(g.shape, F32)
-    return pl.pallas_call(raw_kernel, grid=(n,), in_specs=[slot_spec()]*3, out_specs=[slot_spec()]*5, out_shape=[shape]*5)(g, bl, br)
+    here = pl.BlockSpec((1, BLOCK_SIDE, BLOCK_SIDE), lambda i, ranks: (i, 0, 0))
+    ranked = pl.BlockSpec((1, BLOCK_SIDE, BLOCK_SIDE), lambda i, ranks: (ranks[i], 0, 0))
+
+    def kernel(ranks, *refs):
+        raw_kernel(*refs)
+
+    return pl.pallas_call(
+        kernel,
+        grid_spec=pltpu.PrefetchScalarGridSpec(
+            num_scalar_prefetch=1, grid=(n,), in_specs=[ranked, here, here], out_specs=[here] * 5
+        ),
+        out_shape=[shape] * 5,
+    )(ranks, g, bl, br)
+
 
 NB=32
 def finish_kernel(factor, rot, gl, gr, ql, qr, pl_, pr_, sl, sr, bl, br, master, m1, m2,
@@ -288,10 +302,9 @@
         compiler_params=pltpu.CompilerParams(vmem_limit_bytes=56*1024*1024),
     )(factor, rot, gl, gr, ql, qr, pl_, pr_, sl, sr, bl, br, master, m1, m2)
 
-def soap(g, factor, master, m1, m2, sl, sr, bl, br):
-    p_l, p_r = stat_products(sl, sr, bl, br)
-    rot, gl, gr, ql, qr = raw_products(g, bl, br)
-    return finish(factor.reshape(1), rot, gl, gr, ql, qr, p_l, p_r, sl, sr, bl, br, master, m1, m2)
+def soap(ranks, g, factor, stat_parts, master, m1, m2, sl, sr, bl, br):
+    rot, gl, gr, ql, qr = raw_products(ranks, g, bl, br)
+    return finish(factor.reshape(1), rot, gl, gr, ql, qr, *stat_parts, sl, sr, bl, br, master, m1, m2)
 
 
 def adam_update(clipped, params_old, first_old, second_old):
@@ -307,10 +320,24 @@
 
 FRAME_ROWS = GRID * GRID
 PAD_ROWS = 208
+OWN_ROWS = 2 * PAD_ROWS
+LANES = 512
 PAIRS = HEADS // 2
 PAIR = 2 * HD
+QKV_BLOCKS = 108
+CODE_BASE = 1 << 16
+VMEM_MOST = 58 * 1024 * 1024
 ALL_AXES = ("fz", "fx", "by", "core")
 FRAME_AXES = ("fz", "fx")
+TAP_OFFSETS = [(tap // 3 - 1) * GRID + tap % 3 - 1 for tap in range(9)]
+
+
+def in_vmem():
+    return pl.BlockSpec(memory_space=pltpu.VMEM)
+
+
+def anywhere():
+    return pl.BlockSpec(memory_space=pl.ANY)
 
 
 def matrix_places():
@@ -324,125 +351,118 @@
     return places
 
 
-def tile_at(ref, tile, cols):
-    row = pl.multiple_of(lax.div(tile, cols) * BLOCK_SIDE, BLOCK_SIDE)
-    col = pl.multiple_of(lax.rem(tile, cols) * BLOCK_SIDE, BLOCK_SIDE)
+def tile_at(ref, row, col):
+    row = pl.multiple_of(row * BLOCK_SIDE, BLOCK_SIDE)
+    col = pl.multiple_of(col * BLOCK_SIDE, BLOCK_SIDE)
     return ref.at[pl.ds(row, BLOCK_SIDE), pl.ds(col, BLOCK_SIDE)]
 
 
-def place_kernel(owner, gathered, w_qkv, w_out, w_up, w_down, sems):
-    outs = (w_qkv, w_out, w_up, w_down)
-
-    def one_slot(slot, carry):
-        block = owner[slot]
-        for which, (first, count, cols) in enumerate(matrix_places()):
-            @pl.when((block >= first) & (block < first + count))
+def load_matrix(which, codes, buffers, matrix, sem):
+    first, count, cols = matrix_places()[which]
+
+    def one_block(tile, carry):
+        code = codes[first + tile]
+        row, col = lax.div(tile, cols), lax.rem(tile, cols)
+        for index, buffer in enumerate(buffers):
+            @pl.when(lax.div(code, CODE_BASE) == index)
             def _():
                 pltpu.make_async_copy(
-                    gathered.at[slot], tile_at(outs[which], block - first, cols), sems.at[which]
+                    buffer.at[lax.rem(code, CODE_BASE)], tile_at(matrix, row, col), sem
                 ).start()
         return carry
 
-    lax.fori_loop(0, gathered.shape[0], one_slot, 0)
-    for which in range(4):
-        pltpu.make_async_copy(outs[which], outs[which], sems.at[which]).wait()
-
-
-def place_blocks(owner, gathered):
-    anywhere = pl.BlockSpec(memory_space=pl.ANY)
+    lax.fori_loop(0, count, one_block, 0)
+
+
+def wait_whole(ref, sem):
+    pltpu.make_async_copy(ref, ref, sem).wait()
+
+
+def send_tile(code, buffers, tile, sem, first=0):
+    for index, buffer in enumerate(buffers):
+        @pl.when(lax.div(code, CODE_BASE) == first + index)
+        def _():
+            pltpu.make_async_copy(tile, buffer.at[lax.rem(code, CODE_BASE)], sem).start()
+
+
+def normalized(values):
+    centered = values - jnp.mean(values, -1, keepdims=True)
+    spread = lax.rsqrt(jnp.mean(centered * centered, -1, keepdims=True) + NORM_EPSILON)
+    return centered * spread, spread
+
+
+def norm_back(grad, hat, spread, gain):
+    scaled = grad * gain
+    return spread * (
+        scaled
+        - jnp.mean(scaled, -1, keepdims=True)
+        - hat * jnp.mean(scaled * hat, -1, keepdims=True)
+    )
+
+
+def project(codes, buffers, seen, rows14):
+    rows = seen.shape[0]
+    steps = rows // OWN_ROWS
+    count = len(buffers)
+
+    def kernel(codes, *refs):
+        sources = refs[:count]
+        seen, rows14, q, kv, low, own_low, w_qkv, sem = refs[count:]
+        step = pl.program_id(0)
+
+        @pl.when(step == 0)
+        def _():
+            load_matrix(0, codes, sources, w_qkv, sem)
+
+        hat, _ = normalized(seen[...].astype(F32))
+        normed = (hat * rows14[0:1] + rows14[1:2]).astype(BF)
+        low[...] = normed
+
+        @pl.when(step == 0)
+        def _():
+            wait_whole(w_qkv, sem)
+
+        kv[:, :D] = dot_low(normed, w_qkv[:, D : 2 * D], NN).astype(BF)
+        kv[:, D:] = (dot_low(normed, w_qkv[:, 2 * D :], NN) + rows14[7:8]).astype(BF)
+
+        def own(place):
+            part = normed[:PAD_ROWS]
+            query = (dot_low(part, w_qkv[:, :D], NN) + rows14[6:7]).astype(BF)
+            q[place : place + PAD_ROWS] = query * jnp.asarray(1.0 / math.sqrt(HD), BF)
+            own_low[place : place + PAD_ROWS] = part
+
+        @pl.when(step == 0)
+        def _():
+            own(0)
+
+        @pl.when(step == steps - 1)
+        def _():
+            own(PAD_ROWS)
+
+    def whole(shape):
+        return pl.BlockSpec(shape, lambda i, codes: (0, 0))
+
+    def moving(width):
+        return pl.BlockSpec((OWN_ROWS, width), lambda i, codes: (i, 0))
+
     return pl.pallas_call(
-        place_kernel,
+        kernel,
         grid_spec=pltpu.PrefetchScalarGridSpec(
             num_scalar_prefetch=1,
-            grid=(1,),
-            in_specs=[anywhere],
-            out_specs=[pl.BlockSpec(memory_space=pltpu.VMEM)] * 4,
-            scratch_shapes=[pltpu.SemaphoreType.DMA((4,))],
+            grid=(steps,),
+            in_specs=[anywhere()] * count + [moving(D), whole((14, D))],
+            out_specs=[whole((OWN_ROWS, D)), moving(2 * D), moving(D), whole((OWN_ROWS, D)), whole((D, 3 * D))],
+            scratch_shapes=[pltpu.SemaphoreType.DMA],
         ),
-        out_shape=[jax.ShapeDtypeStruct(shape, BF) for shape in matrix_shapes()],
-        compiler_params=pltpu.CompilerParams(vmem_limit_bytes=48 * 1024 * 1024),
-    )(owner, gathered)
-
-
-def spread_kernel(sizes, slots_dev, owner, coords, g_qkv, g_out, g_up, g_down, blank, part_a, part_b, sems):
-    grads = (g_qkv, g_out, g_up, g_down)
-    parts = (part_a, part_b)
-    nz, nx, ny, nc = sizes
-    half = slots_dev // 2
-
-    def one_slot(slot, carry):
-        block = owner[slot]
-        device = lax.div(slot, slots_dev)
-        inner = lax.rem(slot, slots_dev)
-        offs = []
-        for axis, size in ((3, nc), (2, ny), (1, nx), (0, nz)):
-            offs.append(lax.rem(lax.rem(device, size) - coords[axis] + size, size))
-            device = lax.div(device, size)
-        rc, ry, rx, rz = offs
-        place_a = (((rc * nx + rx) * ny + ry) * nz + rz) * half + inner
-        place_b = (((rc * ny + ry) * nx + rx) * nz + rz) * half + inner - half
-        for part in range(2):
-            chosen = (inner < half) if part == 0 else (inner >= half)
-            place = place_a if part == 0 else place_b
-            for which, (first, count, cols) in enumerate(matrix_places()):
-                @pl.when(chosen & (block >= first) & (block < first + count))
-                def _():
-                    pltpu.make_async_copy(
-                        tile_at(grads[which], block - first, cols), parts[part].at[place], sems.at[part]
-                    ).start()
-
-            @pl.when(chosen & (block >= MATRIX_BLOCKS))
-            def _():
-                pltpu.make_async_copy(blank, parts[part].at[place], sems.at[part]).start()
-        return carry
-
-    lax.fori_loop(0, nz * nx * ny * nc * slots_dev, one_slot, 0)
-    for part in range(2):
-        pltpu.make_async_copy(parts[part], parts[part], sems.at[part]).wait()
-
-
-def spread_blocks(sizes, slots_dev, owner, coords, grads):
-    anywhere = pl.BlockSpec(memory_space=pl.ANY)
-    nz, nx, ny, nc = sizes
-    half = slots_dev // 2
-    shape = jax.ShapeDtypeStruct((nz * nx * ny * nc * half, BLOCK_SIDE, BLOCK_SIDE), BF)
-
-    def kernel(*refs):
-        spread_kernel(sizes, slots_dev, *refs)
-
-    part_a, part_b = pl.pallas_call(
-        kernel,
-        grid_spec=pltpu.PrefetchScalarGridSpec(
-            num_scalar_prefetch=2,
-            grid=(1,),
-            in_specs=[pl.BlockSpec(memory_space=pltpu.VMEM)] * 5,
-            out_specs=[anywhere] * 2,
-            scratch_shapes=[pltpu.SemaphoreType.DMA((2,))],
-        ),
-        out_shape=[shape, shape],
-        compiler_params=pltpu.CompilerParams(vmem_limit_bytes=48 * 1024 * 1024),
-    )(owner, coords, *grads, jnp.zeros((BLOCK_SIDE, BLOCK_SIDE), BF))
-    tail = (half, BLOCK_SIDE, BLOCK_SIDE)
-    return part_a.reshape((nc, nx, ny, nz) + tail), part_b.reshape((nc, ny, nx, nz) + tail)
-
-
-def moved(value, axis, size, step):
-    return lax.ppermute(value, axis, [(i, (i + step) % size) for i in range(size)])
-
-
-def reduce_axis(buf, axis, size):
-    total = buf[0].astype(F32)
-    for step in range(1, size):
-        total = total + moved(buf[step], axis, size, step).astype(F32)
-    return total
-
-
-def gather_axis(value, axis, size):
-    return jnp.stack([value] + [moved(value, axis, size, -step) for step in range(1, size)])
-
-
-def rolled(value, axis, size, step):
-    return lax.dynamic_slice_in_dim(jnp.concatenate([value, value], axis), step, size, axis)
+        out_shape=[
+            jax.ShapeDtypeStruct((OWN_ROWS, D), BF),
+            jax.ShapeDtypeStruct((rows, 2 * D), BF),
+            jax.ShapeDtypeStruct((rows, D), BF),
+            jax.ShapeDtypeStruct((OWN_ROWS, D), BF),
+            jax.ShapeDtypeStruct((D, 3 * D), BF),
+        ],
+        compiler_params=pltpu.CompilerParams(vmem_limit_bytes=VMEM_MOST),
+    )(codes, *buffers, seen, rows14)
 
 
 def attend_kernel(long_rows, q, k, v, bias, out):
@@ -496,7 +516,7 @@
 
 def attend(q, kv, bias):
     keys_total = kv.shape[0]
-    long_rows = keys_total - 2 * PAD_ROWS
+    long_rows = keys_total - OWN_ROWS
 
     def kernel(*refs):
         attend_kernel(long_rows, *refs)
@@ -505,20 +525,20 @@
         kernel,
         grid=(PAIRS,),
         in_specs=[
-            pair_spec(2 * PAD_ROWS),
+            pair_spec(OWN_ROWS),
             pair_spec(keys_total),
             pair_spec(keys_total, PAIRS),
             pl.BlockSpec((1, keys_total), lambda i: (0, 0)),
         ],
-        out_specs=pair_spec(2 * PAD_ROWS),
-        out_shape=jax.ShapeDtypeStruct((2 * PAD_ROWS, D), BF),
+        out_specs=pair_spec(OWN_ROWS),
+        out_shape=jax.ShapeDtypeStruct((OWN_ROWS, D), BF),
         compiler_params=pltpu.CompilerParams(vmem_limit_bytes=48 * 1024 * 1024),
     )(q, kv, kv, bias.reshape(1, -1))
 
 
 def attend_back(q, kv, bias, grad):
     keys_total = kv.shape[0]
-    long_rows = keys_total - 2 * PAD_ROWS
+    long_rows = keys_total - OWN_ROWS
 
     def kernel(*refs):
         attend_back_kernel(long_rows, *refs)
@@ -527,15 +547,15 @@
         kernel,
         grid=(PAIRS,),
         in_specs=[
-            pair_spec(2 * PAD_ROWS),
+            pair_spec(OWN_ROWS),
             pair_spec(keys_total),
             pair_spec(keys_total, PAIRS),
             pl.BlockSpec((keys_total, 1), lambda i: (0, 0)),
-            pair_spec(2 * PAD_ROWS),
+            pair_spec(OWN_ROWS),
         ],
-        out_specs=[pair_spec(2 * PAD_ROWS), pair_spec(keys_total), pair_spec(keys_total)],
+        out_specs=[pair_spec(OWN_ROWS), pair_spec(keys_total), pair_spec(keys_total)],
         out_shape=[
-            jax.ShapeDtypeStruct((2 * PAD_ROWS, D), BF),
+            jax.ShapeDtypeStruct((OWN_ROWS, D), BF),
             jax.ShapeDtypeStruct((keys_total, D), BF),
             jax.ShapeDtypeStruct((keys_total, D), BF),
         ],
@@ -543,20 +563,461 @@
     )(q, kv, kv, bias.reshape(-1, 1), grad)
 
 
+def lane_masks():
+    lane = np.arange(LANES)
+    inner = lane % PAD_ROWS
+    token = (lane < OWN_ROWS) & (inner < FRAME_ROWS)
+    row, col = inner // GRID, inner % GRID
+    masks = []
+    for tap in range(9):
+        far_row, far_col = row + tap // 3 - 1, col + tap % 3 - 1
+        masks.append(token & (far_row >= 0) & (far_row < GRID) & (far_col >= 0) & (far_col < GRID))
+    masks.append(token & (lane < PAD_ROWS))
+    masks.append(token & (lane >= PAD_ROWS))
+    masks = masks + [np.zeros(LANES, bool)] * (16 - len(masks))
+    return np.stack(masks).astype(np.float32)
+
+
+def ahead(values, offset):
+    return values if offset == 0 else pltpu.roll(values, (-offset) % LANES, axis=1)
+
+
+def cumulative(values):
+    return 0.5 + 0.5 * lax.erf(values * math.sqrt(0.5))
+
+
+def gelu_slope(values, portion):
+    return portion + values * jnp.exp(-0.5 * values * values) * (1.0 / math.sqrt(2.0 * math.pi))
+
+
+def column_sum(values):
+    return jnp.sum(values, axis=0, keepdims=True)
+
+
+def widened(values):
+    return jnp.concatenate([values, jnp.zeros((values.shape[0], LANES - OWN_ROWS), values.dtype)], axis=1)
+
+
+def middle_kernel(weight_count, codes, targets, *refs):
+    sources = refs[:weight_count]
+    (
+        att, own, cot, rows14, conv_t, taps_forward, taps_backward, tail_bias, masks, blank,
+        learned, grad_mixed, grad_att, vectors, grad_up_bias, grad_conv, grad_tail, grad_tail_bias,
+    ) = refs[weight_count : weight_count + 18]
+    buffers = refs[weight_count + 18 : -14]
+    (
+        w_out, w_up, w_down, d_out, d_up, d_down, activated, slopes, normed, hat_two, mixed, gathered_sum,
+        load_sems, send_sems,
+    ) = refs[-14:]
+    chunks = FF // D
+    load_matrix(1, codes, sources, w_out, load_sems.at[0])
+    load_matrix(2, codes, sources, w_up, load_sems.at[1])
+    load_matrix(3, codes, sources, w_down, load_sems.at[2])
+
+    def one_blank(block, total):
+        code = targets[block]
+        early = lax.div(code, CODE_BASE) < 4
+        filled = (block >= MATRIX_BLOCKS) | ((block < QKV_BLOCKS) & early)
+
+        @pl.when(filled)
+        def _():
+            send_tile(code, buffers, blank, send_sems.at[3])
+
+        return total + filled.astype(jnp.int32)
+
+    blanks = lax.fori_loop(0, QKV_BLOCKS, one_blank, jnp.int32(0))
+    blanks = lax.fori_loop(MATRIX_BLOCKS, targets.shape[0], one_blank, blanks)
+
+    wait_whole(w_out, load_sems.at[0])
+    start = own[...].astype(F32) + dot_low(att[...], w_out[...], NN) + rows14[8:9]
+    mixed[...] = start
+    hat, spread_two = normalized(start)
+    hat_two[...] = hat
+    normed[...] = (hat * rows14[2:3] + rows14[3:4]).astype(BF)
+    gathered_sum[...] = start + rows14[13:14]
+    wait_whole(w_up, load_sems.at[1])
+    wait_whole(w_down, load_sems.at[2])
+
+    for chunk in range(chunks):
+        at = slice(chunk * D, (chunk + 1) * D)
+        hidden = dot_low(normed[...], w_up[:, at], NN) + rows14[9 + chunk : 10 + chunk]
+        portion = cumulative(hidden)
+        active = (hidden * portion).astype(BF)
+        activated[chunk] = active
+        slopes[chunk] = gelu_slope(hidden, portion)
+        gathered_sum[...] += dot_low(active, w_down[at, :], NN)
+
+    out_two = gathered_sum[...]
+    hat, spread_three = normalized(out_two)
+    low_three = (hat * rows14[4:5] + rows14[5:6]).astype(BF)
+
+    taps = widened(dot_low(conv_t[...], low_three, NT_))
+    first = tail_bias[:, 0:1]
+    for tap in range(9):
+        first = first + ahead(taps[NT * tap : NT * (tap + 1)], TAP_OFFSETS[tap]) * masks[tap : tap + 1]
+
+    def around(values, sign):
+        order = range(9) if sign > 0 else range(8, -1, -1)
+        return jnp.concatenate(
+            [
+                ahead(values, sign * TAP_OFFSETS[tap]) * masks[seen : seen + 1]
+                for tap, seen in zip(range(9), order)
+            ],
+            axis=0,
+        )
+
+    before, stacks, portions = [first], [], []
+    for layer in range(3):
+        portions.append(cumulative(before[-1]))
+        stacks.append(around(before[-1] * portions[-1], 1))
+        before.append(dot_wide(taps_forward[layer], stacks[-1], NN) + tail_bias[:, layer + 1 : layer + 2])
+    maps = 1.0 / (1.0 + jnp.exp(-before[3]))
+    both = jnp.concatenate([maps * masks[9:10], maps * masks[10:11]], axis=0)[:, :OWN_ROWS]
+    both = halves(both)
+    out_parts = halves(out_two)
+    arriving = cot[...]
+    learned[...] = dot_parts(both, out_parts, NN)
+    seen_maps = widened(dot_low(arriving, out_parts[0], NT_) + dot_low(arriving, out_parts[1], NT_))
+    grad = (seen_maps[:NT] * masks[9:10] + seen_maps[NT:] * masks[10:11]) * maps * (1.0 - maps)
+    sums = [None] * 4
+    for layer in (2, 1, 0):
+        sums[layer + 1] = jnp.sum(grad, axis=1, keepdims=True)
+        grad_tail[layer] = dot_wide(stacks[layer], grad, NT_)
+        grad = dot_wide(taps_backward[layer], around(grad, -1), NN)
+        grad = grad * gelu_slope(before[layer], portions[layer])
+    grad = grad.astype(BF).astype(F32)
+    sums[0] = jnp.sum(grad, axis=1, keepdims=True)
+    grad_tail_bias[...] = jnp.concatenate(sums, axis=1)
+    grad_taps = around(grad, -1)[:, :OWN_ROWS].astype(BF)
+    grad_conv[...] = dot_low(grad_taps, low_three, NN)
+    grad_norm_three = dot_low(grad_taps, conv_t[...], TN)
+    vectors[2:3] = column_sum(grad_norm_three * hat)
+    vectors[3:4] = column_sum(grad_norm_three)
+    grad_out = (
+        norm_back(grad_norm_three, hat, spread_three, rows14[4:5])
+        + dot_low(both[0], arriving, TN)
+        + dot_low(both[1], arriving, TN)
+    )
+    grad_down = grad_out.astype(BF)
+    vectors[5:6] = column_sum(grad_down.astype(F32))
+
+    for chunk in range(chunks):
+        at = slice(chunk * D, (chunk + 1) * D)
+        grad_active = dot_low(grad_down, w_down[at, :], NT_)
+        grad_hidden = (grad_active * slopes[chunk]).astype(BF)
+        grad_up_bias[chunk : chunk + 1] = column_sum(grad_hidden.astype(F32))
+        part = dot_low(grad_hidden, w_up[:, at], NT_)
+        if chunk == 0:
+            gathered_sum[...] = part
+        else:
+            gathered_sum[...] += part
+        d_down[at, :] = dot_low(activated[chunk], grad_down, TN).astype(BF)
+        d_up[:, at] = dot_low(normed[...], grad_hidden, TN).astype(BF)
+        side = D // BLOCK_SIDE
+
+        def one_tile(tile, carry, chunk=chunk):
+            row, col = lax.div(tile, side), lax.rem(tile, side)
+            first_up, first_down = matrix_places()[2][0], matrix_places()[3][0]
+            up_block = first_up + row * (FF // BLOCK_SIDE) + chunk * side + col
+            send_tile(targets[up_block], buffers, tile_at(d_up, row, chunk * side + col), send_sems.at[1])
+            down_block = first_down + (chunk * side + row) * side + col
+            send_tile(targets[down_block], buffers, tile_at(d_down, chunk * side + row, col), send_sems.at[2])
+            return carry
+
+        lax.fori_loop(0, side * side, one_tile, 0)
+
+    grad_norm_two = gathered_sum[...]
+    vectors[0:1] = column_sum(grad_norm_two * hat_two[...])
+    vectors[1:2] = column_sum(grad_norm_two)
+    total = grad_out + norm_back(grad_norm_two, hat_two[...], spread_two, rows14[2:3])
+    grad_mixed[...] = total
+    branch = total.astype(BF)
+    vectors[4:5] = column_sum(branch.astype(F32))
+    d_out[...] = dot_low(att[...], branch, TN).astype(BF)
+
+    def one_out(tile, carry):
+        side = D // BLOCK_SIDE
+        code = targets[matrix_places()[1][0] + tile]
+        send_tile(code, buffers, tile_at(d_out, lax.div(tile, side), lax.rem(tile, side)), send_sems.at[0])
+        return carry
+
+    lax.fori_loop(0, matrix_places()[1][1], one_out, 0)
+    grad_att[...] = dot_low(branch, w_out[...], NT_).astype(BF)
+    wait_whole(d_out, send_sems.at[0])
+    wait_whole(d_up, send_sems.at[1])
+    wait_whole(d_down, send_sems.at[2])
+
+    def one_wait(index, carry):
+        wait_whole(blank, send_sems.at[3])
+        return carry
+
+    lax.fori_loop(0, blanks, one_wait, 0)
+
+
+def middle(codes, targets, weights, buffer_shapes, att, own, cot, rows14, conv_t, taps_forward, taps_backward, tail_bias):
+    count = len(weights)
+
+    def kernel(*refs):
+        middle_kernel(count, *refs)
+
+    def f32(*shape):
+        return jax.ShapeDtypeStruct(shape, F32)
+
+    outs = [
+        f32(2 * NT, D), f32(OWN_ROWS, D), jax.ShapeDtypeStruct((OWN_ROWS, D), BF), f32(8, D),
+        f32(FF // D, D), f32(9 * NT, D), f32(3, 9 * NT, NT), f32(NT, 4),
+    ]
+    results = pl.pallas_call(
+        kernel,
+        grid_spec=pltpu.PrefetchScalarGridSpec(
+            num_scalar_prefetch=2,
+            grid=(1,),
+            in_specs=[anywhere()] * count + [in_vmem()] * 10,
+            out_specs=[in_vmem()] * len(outs) + [anywhere()] * len(buffer_shapes),
+            scratch_shapes=[
+                pltpu.VMEM((D, D), BF),
+                pltpu.VMEM((D, FF), BF),
+                pltpu.VMEM((FF, D), BF),
+                pltpu.VMEM((D, D), BF),
+                pltpu.VMEM((D, FF), BF),
+                pltpu.VMEM((FF, D), BF),
+                pltpu.VMEM((FF // D, OWN_ROWS, D), BF),
+                pltpu.VMEM((FF // D, OWN_ROWS, D), F32),
+                pltpu.VMEM((OWN_ROWS, D), BF),
+                pltpu.VMEM((OWN_ROWS, D), F32),
+                pltpu.VMEM((OWN_ROWS, D), F32),
+                pltpu.VMEM((OWN_ROWS, D), F32),
+                pltpu.SemaphoreType.DMA((3,)),
+                pltpu.SemaphoreType.DMA((4,)),
+            ],
+        ),
+        out_shape=outs + buffer_shapes,
+        compiler_params=pltpu.CompilerParams(vmem_limit_bytes=VMEM_MOST),
+    )(
+        codes, targets, *weights, att, own, cot, rows14, conv_t, taps_forward, taps_backward, tail_bias,
+        jnp.asarray(lane_masks()), jnp.zeros((BLOCK_SIDE, BLOCK_SIDE), BF),
+    )
+    return results[: len(outs)], results[len(outs) :]
+
+
+def qkv_grads(targets, low, own_low, dq, dk, dv, buffers, late):
+    steps = low.shape[0] // OWN_ROWS
+    count = len(buffers)
+
+    def kernel(targets, low, own_low, dq, dk, dv, *refs):
+        filled = refs[count : 2 * count]
+        matrix = refs[2 * count]
+        totals, sem = refs[2 * count + 1 :]
+        step = pl.program_id(0)
+
+        @pl.when(step == 0)
+        def _():
+            totals[...] = jnp.zeros_like(totals)
+            matrix[:, :D] = dot_low(own_low[...], dq[...], TN).astype(BF)
+
+        totals[:, :D] += dot_low(low[...], dk[...], TN)
+        totals[:, D:] += dot_low(low[...], dv[...], TN)
+
+        @pl.when(step == steps - 1)
+        def _():
+            matrix[:, D:] = totals[...].astype(BF)
+            cols = 3 * D // BLOCK_SIDE
+
+            def one_tile(tile, sent):
+                code = targets[tile]
+                send_tile(code, filled, tile_at(matrix, lax.div(tile, cols), lax.rem(tile, cols)), sem, late)
+                return sent + (lax.div(code, CODE_BASE) >= late).astype(jnp.int32)
+
+            sent = lax.fori_loop(0, QKV_BLOCKS, one_tile, jnp.int32(0))
+
+            def one_wait(index, carry):
+                wait_whole(tile_at(matrix, 0, 0), sem)
+                return carry
+
+            lax.fori_loop(0, sent, one_wait, 0)
+
+    def whole(shape):
+        return pl.BlockSpec(shape, lambda i, targets: (0, 0))
+
+    def moving(width):
+        return pl.BlockSpec((OWN_ROWS, width), lambda i, targets: (i, 0))
+
+    results = pl.pallas_call(
+        kernel,
+        grid_spec=pltpu.PrefetchScalarGridSpec(
+            num_scalar_prefetch=1,
+            grid=(steps,),
+            in_specs=[moving(D), whole((OWN_ROWS, D)), whole((OWN_ROWS, D)), moving(D), moving(D)]
+            + [anywhere()] * count,
+            out_specs=[anywhere()] * count + [whole((D, 3 * D))],
+            scratch_shapes=[pltpu.VMEM((D, 2 * D), F32), pltpu.SemaphoreType.DMA],
+        ),
+        out_shape=[jax.ShapeDtypeStruct(b.shape, b.dtype) for b in buffers]
+        + [jax.ShapeDtypeStruct((D, 3 * D), BF)],
+        input_output_aliases={6 + i: i for i in range(count)},
+        compiler_params=pltpu.CompilerParams(vmem_limit_bytes=VMEM_MOST),
+    )(targets, low, own_low, dq, dk, dv, *buffers)
+    return results[:count], results[count]
+
+
+def input_grads(seen, own, dq, dk, dv, w_qkv):
+    rows = seen.shape[0]
+    steps = rows // OWN_ROWS
+
+    def kernel(seen, own, dq, dk, dv, w_qkv, grad_seen, grad_own, sums):
+        step = pl.program_id(0)
+
+        @pl.when(step == 0)
+        def _():
+            grad = dot_low(dq[...], w_qkv[:, :D], NT_)
+            grad_own[...] = grad
+            hat, _ = normalized(own[...].astype(F32))
+            sums[...] = jnp.zeros_like(sums)
+            sums[0:1] = column_sum(grad * hat)
+            sums[1:2] = column_sum(grad)
+            sums[2:3] = column_sum(dq[...].astype(F32))
+
+        grad = dot_low(dk[...], w_qkv[:, D : 2 * D], NT_) + dot_low(dv[...], w_qkv[:, 2 * D :], NT_)
+        grad_seen[...] = grad.astype(BF)
+        hat, _ = normalized(seen[...].astype(F32))
+        sums[0:1] += column_sum(grad * hat)
+        sums[1:2] += column_sum(grad)
+        sums[3:4] += column_sum(dv[...].astype(F32))
+
+    def whole(shape):
+        return pl.BlockSpec(shape, lambda i: (0, 0))
+
+    moving = pl.BlockSpec((OWN_ROWS, D), lambda i: (i, 0))
+    return pl.pallas_call(
+        kernel,
+        grid=(steps,),
+        in_specs=[moving, whole((OWN_ROWS, D)), whole((OWN_ROWS, D)), moving, moving, whole((D, 3 * D))],
+        out_specs=[moving, whole((OWN_ROWS, D)), whole((8, D))],
+        out_shape=[
+            jax.ShapeDtypeStruct((rows, D), BF),
+            jax.ShapeDtypeStruct((OWN_ROWS, D), F32),
+            jax.ShapeDtypeStruct((8, D), F32),
+        ],
+        compiler_params=pltpu.CompilerParams(vmem_limit_bytes=VMEM_MOST),
+    )(seen, own, dq, dk, dv, w_qkv)
+
+
+def moved(value, axis, size, step):
+    return lax.ppermute(value, axis, [(i, (i + step) % size) for i in range(size)])
+
+
+def reduce_axis(terms, axis, size):
+    total = terms[0].astype(F32)
+    for step in range(1, size):
+        total = total + moved(terms[step], axis, size, step).astype(F32)
+    return total
+
+
+def gather_axis(value, axis, size):
+    return jnp.stack([value] + [moved(value, axis, size, -step) for step in range(1, size)])
+
+
+def rolled(value, axis, size, step):
+    return lax.dynamic_slice_in_dim(jnp.concatenate([value, value], axis), step, size, axis)
+
+
+def slot_chunks(slots_dev):
+    early = slots_dev * 3 // 14
+    late = slots_dev - 2 * early
+    chunks = []
+    first = 0
+    for index, count in enumerate((early, early, late - late // 2, late // 2)):
+        chunks.append((first, count, ("fx", "by", "fz") if index % 2 == 0 else ("by", "fx", "fz")))
+        first = first + count
+    return chunks
+
+
+def send_table(block_owner, sizes, coords, slots_dev):
+    nz, nx, ny, nc = sizes
+    slots = jnp.arange(block_owner.shape[0], dtype=jnp.int32)
+    device = slots // slots_dev
+    place = {}
+    for axis in range(3, -1, -1):
+        place[ALL_AXES[axis]] = (device % sizes[axis] - coords[axis] + sizes[axis]) % sizes[axis]
+        device = device // sizes[axis]
+    is_late = (block_owner < QKV_BLOCKS).astype(jnp.int32).reshape(-1, slots_dev)
+    late_before = jnp.cumsum(is_late, 1) - is_late
+    early_before = jnp.arange(slots_dev, dtype=jnp.int32)[None] - late_before
+    late_count = jnp.sum(is_late, 1, keepdims=True)
+    ranks = jnp.where(is_late == 1, slots_dev - late_count + late_before, early_before)
+    rank = ranks.reshape(-1)
+    size_of = dict(zip(ALL_AXES, sizes))
+    code = jnp.zeros_like(slots)
+    for index, (first, count, axes) in enumerate(slot_chunks(slots_dev)):
+        at = jnp.zeros_like(slots)
+        for name in axes:
+            at = at * size_of[name] + place[name]
+        at = at * count + rank - first
+        inside = (rank >= first) & (rank < first + count)
+        code = jnp.where(inside, (2 * index + place["core"]) * CODE_BASE + at, code)
+    owned = block_owner[:, None] == slots[None, :]
+    table = jnp.sum(jnp.where(owned, code[:, None], 0), 0)
+    return table, ranks, jnp.max(late_count)
+
+
+def reduce_chunk(kept, sent, count, axes, sizes):
+    size_of = dict(zip(ALL_AXES, sizes))
+    total = kept.astype(F32) + moved(sent, "core", 2, 1).astype(F32)
+    total = total.astype(BF).reshape([size_of[name] for name in axes] + [count, BLOCK_SIDE, BLOCK_SIDE])
+    for name in axes:
+        total = reduce_axis(total, name, size_of[name])
+        if name != axes[-1]:
+            total = total.astype(BF)
+    return total
+
+
+def spread_early(targets, matrix, buffer_shapes):
+    count = len(buffer_shapes)
+
+    def kernel(targets, matrix, blank, *refs):
+        buffers, sem = refs[:count], refs[count]
+
+        def one_block(block, sent):
+            code = targets[block]
+            cols = 3 * D // BLOCK_SIDE
+            early = lax.div(code, CODE_BASE) < count
+
+            @pl.when(early & (block < QKV_BLOCKS))
+            def _():
+                tile = tile_at(matrix, lax.div(block, cols), lax.rem(block, cols))
+                send_tile(code, buffers, tile, sem)
+
+            @pl.when(early & (block >= QKV_BLOCKS))
+            def _():
+                send_tile(code, buffers, blank, sem)
+
+            return sent + early.astype(jnp.int32)
+
+        sent = lax.fori_loop(0, targets.shape[0], one_block, jnp.int32(0))
+
+        def one_wait(index, carry):
+            wait_whole(blank, sem)
+            return carry
+
+        lax.fori_loop(0, sent, one_wait, 0)
+
+    return pl.pallas_call(
+        kernel,
+        grid_spec=pltpu.PrefetchScalarGridSpec(
+            num_scalar_prefetch=1,
+            grid=(1,),
+            in_specs=[in_vmem()] * 2,
+            out_specs=[anywhere()] * count,
+            scratch_shapes=[pltpu.SemaphoreType.DMA],
+        ),
+        out_shape=buffer_shapes,
+        compiler_params=pltpu.CompilerParams(vmem_limit_bytes=VMEM_MOST),
+    )(targets, matrix, jnp.zeros((BLOCK_SIDE, BLOCK_SIDE), BF))
+
+
 def pad_frames(values):
     frames = values.reshape(2, FRAME_ROWS, values.shape[-1])
     return jnp.pad(frames, ((0, 0), (0, PAD_ROWS - FRAME_ROWS), (0, 0)))
-
-
-def unpad_frames(values):
-    frames = values.reshape(2, PAD_ROWS, values.shape[-1])[:, :FRAME_ROWS]
-    return frames.reshape(2 * FRAME_ROWS, values.shape[-1])
-
-
-def normalized(values):
-    centered = values - jnp.mean(values, -1, keepdims=True)
-    spread = lax.rsqrt(jnp.mean(centered * centered, -1, keepdims=True) + NORM_EPSILON)
-    return centered * spread, spread
 
 
 def on_device(
@@ -583,7 +1044,6 @@
     frame_count = nz * nx
     frame_index = coords[0] * nx + coords[1]
     slots_dev = master.shape[0]
-    params_split = unpack(small_params)
 
     segment_slots = clip_segments(
         clip_lengths[0], clip_order[0], 2 * frame_count, 2, frame_count
@@ -606,164 +1066,92 @@
     from_previous = lax.ppermute(short_frame, FRAME_AXES, frame_perm)
     from_next = lax.ppermute(short_frame, FRAME_AXES, back_perm)
     partner = jnp.where(with_next, from_next, from_previous)
-    long_frames = gather_axis(gather_axis(long_frame, "fx", nx), "fz", nz)
+    long_frames = gather_axis(gather_axis(long_frame, "fz", nz), "fx", nx)
     frames_seen = frame_count + 2
     seen = jnp.concatenate(
         [long_frames.reshape(frame_count, PAD_ROWS, D), short_frame[None], partner[None]]
     ).reshape(frames_seen * PAD_ROWS, D)
+    own = own_frames.reshape(OWN_ROWS, D)
     row_ids = jnp.arange(frames_seen * PAD_ROWS, dtype=jnp.int32)
     hidden_key = (row_ids % PAD_ROWS >= FRAME_ROWS) | (
         (row_ids >= (frames_seen - 1) * PAD_ROWS) & ~(with_previous | with_next)
     )
     key_bias = jnp.where(hidden_key, MASK_FLOOR, 0.0).astype(F32)
 
+    slot_ids = jnp.arange(block_owner.shape[0], dtype=jnp.int32)
+    weight_codes = jnp.sum(jnp.where(block_owner[:, None] == slot_ids[None, :], slot_ids[:, None], 0), 0)
+    targets, ranks, late_most = send_table(block_owner, sizes, coords, slots_dev)
+    device_index = ((coords[0] * nx + coords[1]) * ny + coords[2]) * nc + coords[3]
+    own_ranks = lax.dynamic_index_in_dim(ranks, device_index, 0, keepdims=False)
+    chunks = slot_chunks(slots_dev)
+
+    split = unpack(small_params)
+    rows14 = small_params[: 14 * D].reshape(14, D)
+    conv_t = split["conv_first"].astype(BF).reshape(D, 9 * NT).T
+    tail = jnp.stack([split["conv_second"], split["conv_third"], split["conv_fourth"]])
+    taps_forward = tail.transpose(0, 3, 1, 2).reshape(3, NT, 9 * NT)
+    taps_backward = tail.transpose(0, 2, 1, 3).reshape(3, NT, 9 * NT)
+    tail_bias = split["conv_bias"].T
+    arriving = cotangent[0].reshape(2, NT, D)
+    arriving = jnp.where(swap, arriving[::-1], arriving).reshape(2 * NT, D)
+
     gathered = lax.all_gather(master.astype(BF), ALL_AXES, axis=0, tiled=True)
-    w_qkv, w_out, w_up, w_down = place_blocks(block_owner, gathered)
-
-    seen_hat, seen_rstd = normalized(seen.astype(F32))
-    seen_low = (seen_hat * params_split["gain_one"] + params_split["shift_one"]).astype(BF)
-
-    def own_rows(rows):
-        return jnp.concatenate(
-            [rows[:PAD_ROWS], rows[frame_count * PAD_ROWS : (frame_count + 1) * PAD_ROWS]]
-        )
-
-    own_low = own_rows(seen_low)
-    query = (
-        jnp.dot(own_low, w_qkv[:, :D], preferred_element_type=F32) + params_split["bias_query"]
-    ).astype(BF) * jnp.asarray(1.0 / math.sqrt(HD), BF)
-    kv_bias = jnp.concatenate(
-        [jnp.zeros_like(params_split["bias_value"]), params_split["bias_value"]]
-    )
-    key_value = (jnp.dot(seen_low, w_qkv[:, D:], preferred_element_type=F32) + kv_bias).astype(BF)
-    attended_low = unpad_frames(attend(query, key_value, key_bias))
-    own_inputs = unpad_frames(own_frames.astype(F32))
-
-    mixed_sum = (
-        own_inputs
-        + jnp.dot(attended_low, w_out, preferred_element_type=F32)
-        + params_split["bias_out"]
-    )
-    normed_two, norm_two_back = jax.vjp(
-        layer_norm, mixed_sum, params_split["gain_two"], params_split["shift_two"]
-    )
-    normed_two_low = normed_two.astype(BF)
-    hidden = jnp.dot(normed_two_low, w_up, preferred_element_type=F32) + params_split["bias_up"]
-    activated, gelu_back = jax.vjp(gelu_exact, hidden)
-    activated_low = activated.astype(BF)
-    output_two = (
-        mixed_sum
-        + jnp.dot(activated_low, w_down, preferred_element_type=F32)
-        + params_split["bias_down"]
-    )
-    normed_three, norm_three_back = jax.vjp(
-        layer_norm, output_two, params_split["gain_three"], params_split["shift_three"]
-    )
-    normed_three_low = normed_three.astype(BF)
-    conv_low = params_split["conv_first"].astype(BF).reshape(D, 9 * NT)
-    taps = jnp.dot(normed_three_low, conv_low, preferred_element_type=F32).reshape(
-        2, GRID, GRID, 9, NT
-    )
-    first_pre = taps_sum(taps) + params_split["conv_bias"][0]
-    learned, tail_back = jax.vjp(
-        learner_tail,
-        first_pre,
-        output_two,
-        params_split["conv_second"],
-        params_split["conv_third"],
-        params_split["conv_fourth"],
-        params_split["conv_bias"][1:],
-    )
-    arriving = cotangent[0].astype(F32).reshape(2, NT, D)
-    arriving = jnp.where(swap, arriving[::-1], arriving).reshape(2 * NT, D)
-    grad_first, grad_values, grad_second_w, grad_third_w, grad_fourth_w, grad_tail_bias = tail_back(
-        arriving
+    stat_parts = stat_products(stat_left, stat_right, basis_left, basis_right)
+
+    query, key_value, low, own_low, w_qkv = project(weight_codes, [gathered], seen, rows14)
+    attended = attend(query, key_value, key_bias)
+    buffer_shapes = []
+    for first, count, axes in chunks:
+        shape = jax.ShapeDtypeStruct((device_count // nc * max(count, 1), BLOCK_SIDE, BLOCK_SIDE), BF)
+        buffer_shapes = buffer_shapes + [shape, shape]
+    (learned, grad_mixed, grad_att, vectors, grad_up_bias, grad_conv, grad_tail, grad_tail_bias), buffers = middle(
+        weight_codes, targets, [gathered], buffer_shapes, attended, own, arriving, rows14, conv_t,
+        taps_forward, taps_backward, tail_bias,
     )
     learned = learned.reshape(2, NT, D)
     learned = jnp.where(swap, learned[::-1], learned).reshape(2 * NT, D)
-    grad_first_low = grad_first.astype(BF)
-    grad_bias_first = jnp.sum(grad_first_low, axis=(0, 1, 2), dtype=F32)
-    grad_taps = taps_back(grad_first_low).reshape(2 * FRAME_ROWS, 9 * NT)
-    grad_conv_first = jnp.einsum("nd,nt->dt", normed_three_low, grad_taps, preferred_element_type=F32)
-    grad_normed_three = jnp.einsum("nt,dt->nd", grad_taps, conv_low, preferred_element_type=F32)
-    grad_output_norm, grad_gain_three, grad_shift_three = norm_three_back(grad_normed_three)
-    grad_output_two = grad_values + grad_output_norm
-    grad_down_out = grad_output_two.astype(BF)
-    grad_bias_down = jnp.sum(grad_down_out, 0, dtype=F32)
-    grad_w_down = jnp.einsum(
-        "nf,nd->fd", activated_low, grad_down_out, preferred_element_type=F32
-    ).astype(BF)
-    grad_activated = jnp.einsum("nd,fd->nf", grad_down_out, w_down, preferred_element_type=F32)
-    (grad_hidden,) = gelu_back(grad_activated)
-    grad_hidden_low = grad_hidden.astype(BF)
-    grad_bias_up = jnp.sum(grad_hidden_low, 0, dtype=F32)
-    grad_w_up = jnp.einsum(
-        "nd,nf->df", normed_two_low, grad_hidden_low, preferred_element_type=F32
-    ).astype(BF)
-    grad_normed_two = jnp.einsum("nf,df->nd", grad_hidden_low, w_up, preferred_element_type=F32)
-    grad_mixed_norm, grad_gain_two, grad_shift_two = norm_two_back(grad_normed_two)
-    grad_mixed = grad_output_two + grad_mixed_norm
-    grad_branch = grad_mixed.astype(BF)
-    grad_bias_out = jnp.sum(grad_branch, 0, dtype=F32)
-    grad_w_out = jnp.einsum(
-        "nc,nd->cd", attended_low, grad_branch, preferred_element_type=F32
-    ).astype(BF)
-    grad_attended = jnp.einsum("nd,cd->nc", grad_branch, w_out, preferred_element_type=F32).astype(BF)
-    grad_heads = pad_frames(grad_attended).reshape(2 * PAD_ROWS, D)
-
-    grad_query, grad_key, grad_value = attend_back(query, key_value, key_bias, grad_heads)
-    grad_bias_query = jnp.sum(grad_query, 0, dtype=F32)
-    grad_bias_value = jnp.sum(grad_value, 0, dtype=F32)
-    grad_kv = jnp.concatenate([grad_key, grad_value], 1)
-    grad_w_qkv = jnp.concatenate(
-        [
-            jnp.einsum("nd,ne->de", own_low, grad_query, preferred_element_type=F32),
-            jnp.einsum("nd,ne->de", seen_low, grad_kv, preferred_element_type=F32),
-        ],
-        1,
-    ).astype(BF)
-    grad_seen = jnp.einsum("ne,de->nd", grad_kv, w_qkv[:, D:], preferred_element_type=F32)
-    grad_own = jnp.einsum("ne,de->nd", grad_query, w_qkv[:, :D], preferred_element_type=F32)
-    own_hat = own_rows(seen_hat)
-    grad_gain_one = jnp.sum(grad_seen * seen_hat, 0) + jnp.sum(grad_own * own_hat, 0)
-    grad_shift_one = jnp.sum(grad_seen, 0) + jnp.sum(grad_own, 0)
-
-    conv_bias_grad = jnp.concatenate([grad_bias_first[None, :], grad_tail_bias], 0)
+
+    reduced = []
+    for index in range(2):
+        first, count, axes = chunks[index]
+        if count:
+            reduced.append(reduce_chunk(buffers[2 * index], buffers[2 * index + 1], count, axes, sizes))
+
+    grad_query, grad_key, grad_value = attend_back(query, key_value, key_bias, grad_att)
+    late_buffers, grad_w_qkv = qkv_grads(
+        targets, low, own_low, grad_query, grad_key, grad_value, list(buffers[4:]), 4
+    )
+    grad_seen, grad_own, sums = input_grads(seen, own, grad_query, grad_key, grad_value, w_qkv)
+
+    if reduced:
+        def whole_early(early):
+            shapes = buffer_shapes[:4]
+            extra = spread_early(targets, grad_w_qkv, shapes)
+            return [
+                part + reduce_chunk(extra[2 * i], extra[2 * i + 1], chunks[i][1], chunks[i][2], sizes)
+                for i, part in enumerate(early)
+            ]
+
+        late_room = chunks[2][1] + chunks[3][1]
+        reduced = lax.cond(late_most <= late_room, lambda early: early, whole_early, reduced)
+    for index in (2, 3):
+        first, count, axes = chunks[index]
+        reduced.append(reduce_chunk(late_buffers[2 * index - 4], late_buffers[2 * index - 3], count, axes, sizes))
+    owned_grads = jnp.concatenate(reduced)
+
     small_local = jnp.concatenate(
         [
-            grad_gain_one,
-            grad_shift_one,
-            grad_gain_two,
-            grad_shift_two,
-            grad_gain_three,
-            grad_shift_three,
-            grad_bias_query,
-            grad_bias_value,
-            grad_bias_out,
-            grad_bias_up,
-            grad_bias_down,
-            grad_conv_first.reshape(-1),
-            grad_second_w.reshape(-1),
-            grad_third_w.reshape(-1),
-            grad_fourth_w.reshape(-1),
-            conv_bias_grad.reshape(-1),
+            sums[:2].reshape(-1),
+            vectors[:4].reshape(-1),
+            sums[2:4].reshape(-1),
+            vectors[4],
+            grad_up_bias.reshape(-1),
+            vectors[5],
+            grad_conv.T.reshape(-1),
+            grad_tail.reshape(-1),
+            grad_tail_bias.T.reshape(-1),
         ]
     )
-
-    part_a, part_b = spread_blocks(
-        sizes, slots_dev, block_owner, jnp.stack(coords).astype(jnp.int32),
-        (grad_w_qkv, grad_w_out, grad_w_up, grad_w_down),
-    )
-    part_a = reduce_axis(part_a, "core", nc).astype(BF)
-    part_b = reduce_axis(part_b, "core", nc).astype(BF)
-    part_a = reduce_axis(part_a, "fx", nx).astype(BF)
-    part_b = reduce_axis(part_b, "by", ny).astype(BF)
-    part_a = reduce_axis(part_a, "by", ny).astype(BF)
-    part_b = reduce_axis(part_b, "fx", nx).astype(BF)
-    part_a = reduce_axis(part_a, "fz", nz)
-    part_b = reduce_axis(part_b, "fz", nz)
-    owned_grads = jnp.concatenate([part_a, part_b])
-
     small_total = small_local.shape[0]
     share = -(-small_total // (device_count * 128)) * 128
     padded_small = jnp.pad(small_local, (0, device_count * share - small_total))
@@ -784,15 +1172,17 @@
     factor = 1.0 / jnp.maximum(grad_norm, CLIP_NORM)
 
     soap_out = soap(
-        owned_grads, factor, master, moment1, moment2, stat_left, stat_right, basis_left, basis_right
+        own_ranks, owned_grads, factor, stat_parts, master, moment1, moment2, stat_left, stat_right,
+        basis_left, basis_right,
     )
     small_first, small_second, small_new = adam_update(
         small_grad * factor, small_params, small_moment1, small_moment2
     )
 
-    seen_frames = grad_seen.astype(BF).reshape(frames_seen, PAD_ROWS, D)
-    long_terms = seen_frames[:frame_count].reshape(nz, nx, PAD_ROWS, D)
-    long_terms = reduce_axis(long_terms.transpose(1, 0, 2, 3), "fx", nx).astype(BF)
+    grad_seen, _ = lax.optimization_barrier((grad_seen, owned_grads))
+    seen_frames = grad_seen.reshape(frames_seen, PAD_ROWS, D)
+    long_terms = seen_frames[:frame_count].reshape(nx, nz, PAD_ROWS, D)
+    long_terms = reduce_axis(long_terms, "fx", nx).astype(BF)
     long_total = reduce_axis(long_terms, "fz", nz)
     partner_term = seen_frames[frame_count + 1]
     nothing = jnp.zeros_like(partner_term)
@@ -803,15 +1193,10 @@
         + lax.ppermute(to_previous, FRAME_AXES, back_perm).astype(F32)
         + lax.ppermute(to_next, FRAME_AXES, frame_perm).astype(F32)
     )
-    grad_normed_one = unpad_frames(jnp.concatenate([long_total, short_total]) + grad_own)
-    hat, rstd = unpad_frames(own_hat), unpad_frames(own_rows(jnp.broadcast_to(seen_rstd, seen_hat.shape)))
-    scaled = grad_normed_one * params_split["gain_one"]
-    grad_inputs = grad_mixed + rstd * (
-        scaled
-        - jnp.mean(scaled, -1, keepdims=True)
-        - hat * jnp.mean(scaled * hat, -1, keepdims=True)
-    )
-    grad_inputs = grad_inputs.reshape(2, FRAME_ROWS, D)
+    grad_normed_one = jnp.concatenate([long_total, short_total]) + grad_own
+    hat, spread = normalized(own.astype(F32))
+    grad_inputs = grad_mixed + norm_back(grad_normed_one, hat, spread, rows14[0:1])
+    grad_inputs = grad_inputs.reshape(2, PAD_ROWS, D)[:, :FRAME_ROWS]
     grad_inputs = jnp.where(swap, grad_inputs[::-1], grad_inputs).reshape(2 * FRAME_ROWS, D)
     return (
         learned[None],

time: 690 us -> 568 us (0.82)
  matrix products: 100 us -> 0 us
  local copies, waits for them, and re-layouts: 73.2 us -> 28.2 us
  Pallas kernels: 175 us -> 210 us
  starting transfers between devices: 40 us -> 66.6 us
  other arithmetic: 63.6 us -> 39.7 us
  waiting for transfers between devices: 205 us -> 192 us
    dot_general x30 -> x0, matrix products: 100 us -> none  [the longest x1 15.6 us: on_device(): jnp.dot(normed_two_low, w_up, preferred_element_type=F32)]
    ppermute x32 -> x44, waiting for transfers between devices: 197 us -> 142 us  [moved(): lax.ppermute(value, axis, [(i, (i + step) % size) for i in range(size)])]
    all_gather x1, waiting for transfers between devices: 7.64 us -> 49.5 us  [on_device(): gathered = lax.all_gather(master.astype(BF), ALL_AXES, axis=0, tiled=True)]
    pallas_call x5 -> x7, Pallas kernels: 122 us -> 157 us  [the longest x1 52.3 us: middle(): pl.pallas_call(kernel, grid_spec=pltpu.PrefetchScalarGridSpec(num_scalar_...]
    ppermute x32 -> x44, starting transfers between devices: 35.9 us -> 61.9 us  [moved(): lax.ppermute(value, axis, [(i, (i + step) % size) for i in range(size)])]
    reshape x16 -> x11, local copies, waits for them, and re-layouts: 20.1 us -> 2.64 us  [the longest x1 0.7 us: on_device(): taps_backward = tail.transpose(0, 2, 1, 3).reshape(3, NT, 9 * NT)]
    unnamed x252 -> x85, local copies, waits for them, and re-layouts: 17.4 us -> 7.61 us
    slice x9 -> x14, local copies, waits for them, and re-layouts: 14.7 us -> 5.23 us  [the longest x6 4.29 us: reduce_axis(): total = total + moved(terms[step], axis, size, step).astype(F32)]
  transfers between devices with their start and end apart: 37 -> 49, of which waited for: 20 -> 22; matrix products, arithmetic and copies ran while one was open for 14% -> 9% of each run, Pallas kernels for 9% -> 23%
where the time goes in v2:
time: 568 us; the launch traced here: 558 us
  Pallas kernels  210 us (37%)
  waiting for transfers between devices  192 us (34%)
  starting transfers between devices  66.6 us (12%)
  other arithmetic  39.7 us (7%)
  local copies, waits for them, and re-layouts  28.2 us (5%)
  between operations  21.9 us (4%)
    ppermute x44, waiting for transfers between devices, moved(): lax.ppermute(value, axis, [(i, (i + step) % size) for i in range(size)])  142 us
    ppermute x44, starting transfers between devices, moved(): lax.ppermute(value, axis, [(i, (i + step) % size) for i in range(size)])  61.9 us
    pallas_call x1, Pallas kernels, middle(): pl.pallas_call(kernel, grid_spec=pltpu.PrefetchScalarGridSpec(num_scalar_...  52.3 us
    all_gather x1, waiting for transfers between devices, on_device(): gathered = lax.all_gather(master.astype(BF), ALL_AXES, axis=0, tiled=True)  49.5 us
    pallas_call x1, Pallas kernels, finish(): pl.pallas_call(finish_kernel, in_specs=[pl.BlockSpec(memory_space=pltpu.S...  43 us
    pallas_call x1, Pallas kernels, attend_back(): pl.pallas_call(kernel, grid=(PAIRS,), in_specs=[pair_spec(OWN_ROWS), pair...  36.2 us
    pallas_call x1, Pallas kernels, project(): pl.pallas_call(kernel, grid_spec=pltpu.PrefetchScalarGridSpec(num_scalar_...  15.7 us
    pallas_call x1, Pallas kernels, qkv_grads(): pl.pallas_call(kernel, grid_spec=pltpu.PrefetchScalarGridSpec(num_scalar_...  14.2 us
  transfers between devices with their start and end apart: 49, of which 22 were waited for; matrix products, arithmetic and copies ran while one was open for 9% of the time, Pallas kernels for 23%

profile of v2, /device:TPU:15, one launch (start us, length us, event | category | flops | bytes accessed | tf_op | source)
XLA Modules:
  0.0 558.0 jit_solution(18078692308043705833)
XLA Ops:
  7.3 2.1 convert_element_type.354
  14.1 2.3 collective-permute-start.13
  16.4 2.2 collective-permute-start.14
  18.8 2.1 collective-permute-start.17
  32.4 11.9 %collective-permute-done.13 = bf16[208,768]{1,0:T(8,128)(2,1)} collective-permute-done((bf16[208,768]{1,0:T(8,128)(2,1)S(1)}, bf16[208,768]{1,0:T(8,128)(2,1)}, u32[]{:S(2)}, u32[]{:S(2)}) %collective-permute-start.13) | collective-permute-done | bytes 319520 | tf_op jit(solution)/shard_map/ppermute | solution.py:906
  44.4 8.3 %collective-permute-done.14 = bf16[208,768]{1,0:T(8,128)(2,1)} collective-permute-done((bf16[208,768]{1,0:T(8,128)(2,1)S(1)}, bf16[208,768]{1,0:T(8,128)(2,1)}, u32[]{:S(2)}, u32[]{:S(2)}) %collective-permute-start.14) | collective-permute-done | bytes 319520 | tf_op jit(solution)/shard_map/ppermute | solution.py:906
  54.0 7.7 %collective-permute-start.15 = (bf16[4,208,768]{2,1,0:T(8,128)(2,1)S(1)}, bf16[4,208,768]{2,1,0:T(8,128)(2,1)S(1)}, u32[]{:S(2)}, u32[]{:S(2)}) collective-permute-start(bf16[4,208,768]{2,1,0:T(8,128)(2,1)S(1)} %get-tuple-element.177), channel_id=1, source_target_pairs={{0,4},{4,0},{1,5},{5,1},{2,6},{6,2},{3,7},{7,3},{8,12},{12,8},{9,1... | collective-permute-start | bytes 3833864 | tf_op jit(solution)/shard_map/ppermute | solution.py:906
  64.3 37.7 %collective-permute-done.15 = bf16[4,208,768]{2,1,0:T(8,128)(2,1)S(1)} collective-permute-done((bf16[4,208,768]{2,1,0:T(8,128)(2,1)S(1)}, bf16[4,208,768]{2,1,0:T(8,128)(2,1)S(1)}, u32[]{:S(2)}, u32[]{:S(2)}) %collective-permute-start.15) | collective-permute-done | bytes 1277984 | tf_op jit(solution)/shard_map/ppermute | solution.py:906
  102.2 2.1 pad_maximum_fusion
  104.3 49.5 %all-gather.2.cloned.1.call-done.refs_0_.refs_2_ = bf16[448,128,128]{2,1,0:T(8,128)(2,1)} async-done(((bf16[14,128,128]{2,1,0:T(8,128)(2,1)}), bf16[448,128,128]{2,1,0:T(8,128)(2,1)}) %all-gather.2.cloned.1.call-update) | async-done | bytes 14680080 | tf_op jit(solution)/shard_map/all_gather | solution.py:1098
  153.8 15.7 %shard_map.255 = (bf16[416,768]{1,0:T(8,128)(2,1)}, bf16[2080,1536]{1,0:T(8,128)(2,1)}, bf16[2080,768]{1,0:T(8,128)(2,1)}, bf16[416,768]{1,0:T(8,128)(2,1)}, bf16[768,2304]{1,0:T(8,128)(2,1)}) custom-call(s32[448]{0:T(512)} %get-tuple-element.142.codes.refs_0_, bf16[448,128,128]{2,1,0:T(8,128)(2,1)} %all-gather.2.cloned.1.call-done.refs_0_.refs_2_, ...), custom_call_target="tpu_custom_call" | custom-call | tf_op jit(solution)/shard_map/pallas_call | solution.py:448
  170.6 13.5 %shard_map.256.refs_3_ = bf16[416,768]{1,0:T(8,128)(2,1)S(1)} custom-call(bf16[416,768]{1,0:T(8,128)(2,1)S(1)} %copy-done.2, bf16[2080,1536]{1,0:T(8,128)(2,1)} %get-tuple-element.85.refs_1_.refs_2_, bf16[2080,1536]{1,0:T(8,128)(2,1)} %get-tuple-element.85.refs_1_.refs_2_, f32[1,2080]{1,0:T(1,128)S(1)} %or_select_fusion.refs_3_), custom_call_target="tpu_custom_call" | custom-call | tf_op jit(solution)/shard_map/pallas_call | solution.py:524
  185.5 52.3 %shard_map.257 = (f32[16,768]{1,0:T(8,128)}, f32[416,768]{1,0:T(8,128)}, bf16[416,768]{1,0:T(8,128)(2,1)}, f32[8,768]{1,0:T(8,128)}, f32[4,768]{1,0:T(4,128)}, /...) custom-call(s32[448]{0:T(512)} %get-tuple-element.142.codes.refs_0_,, ...), custom_call_target="tpu_custom_call" | custom-call | tf_op jit(solution)/shard_map/pallas_call | solution.py:770
  239.2 36.2 %shard_map.258 = (bf16[416,768]{1,0:T(8,128)(2,1)S(1)}, bf16[2080,768]{1,0:T(8,128)(2,1)S(1)}, bf16[2080,768]{1,0:T(8,128)(2,1)}) custom-call(bf16[416,768]{1,0:T(8,128)(2,1)S(1)} %copy-done.3, bf16[2080,1536]{1,0:T(8,128)(2,1)} %get-tuple-element.85.refs_1_.refs_2_, bf16[2080,1536]{1,0:T(8,128)(2,1)} %get-tuple-element.85.refs_1_.refs_2_, ...), custom_call_target="tpu_custom_call" | custom-call | tf_op jit(solution)/shard_map/pallas_call | solution.py:546
  275.4 1.8 copy-done
  278.0 12.2 %shard_map.259 = (bf16[2080,768]{1,0:T(8,128)(2,1)}, f32[416,768]{1,0:T(8,128)}, f32[8,768]{1,0:T(8,128)}) custom-call(bf16[2080,768]{1,0:T(8,128)(2,1)} %bitcast.235, bf16[416,768]{1,0:T(8,128)(2,1)} %bitcast.232, bf16[416,768]{1,0:T(8,128)(2,1)} %copy-done.1, bf16[2080,768]{1,0:T(8,128)(2,1)} %copy-done, bf16[2080,768]{1,0:T(8,128)(2,1)} %get-tuple-element.91.dv, ...), custom_call_target="tpu_custom_call" | custom-call | tf_op jit(solution)/shard_map/pallas_call | solution.py:891
  291.8 1.7 concatenate.43
  302.7 14.2 %shard_map.260 = (bf16[64,128,128]{2,1,0:T(8,128)(2,1)}, bf16[64,128,128]{2,1,0:T(8,128)(2,1)}, bf16[64,128,128]{2,1,0:T(8,128)(2,1)}, bf16[64,128,128]{2,1,0:T(8,128)(2,1)}, bf16[768,2304]{1,0:T(8,128)(2,1)S(1)}) custom-call(s32[448]{0:T(512)S(1)} %copy-done.28, ...), custom_call_target="tpu_custom_call", output_to_operand_aliasing={{0}: (6, {}), {1}: (7, {}), {2}: (8, {}), {3}: (9, {})} | custom-call | tf_op jit(solution)/shard_map/pallas_call | solution.py:845
  322.8 5.9 %collective-permute-done.26 = bf16[4,3,128,128]{3,2,1,0:T(8,128)(2,1)S(1)} collective-permute-done((bf16[4,3,128,128]{3,2,1,0:T(8,128)(2,1)S(1)}, bf16[4,3,128,128]{3,2,1,0:T(8,128)(2,1)S(1)}, u32[]{:S(2)}, u32[]{:S(2)}) %collective-permute-start.26) | collective-permute-done | bytes 393248 | tf_op jit(solution)/shard_map/ppermute | solution.py:906
  330.0 2.0 collective-permute-start.28
  333.7 2.1 collective-permute-start.22
  336.3 6.8 %collective-permute-done.29 = bf16[3,128,128]{2,1,0:T(8,128)(2,1)S(1)} collective-permute-done((bf16[3,128,128]{2,1,0:T(8,128)(2,1)S(1)}, bf16[3,128,128]{2,1,0:T(8,128)(2,1)S(1)}, u32[]{:S(2)}, u32[]{:S(2)}) %collective-permute-start.29) | collective-permute-done | bytes 98336 | tf_op jit(solution)/shard_map/ppermute | solution.py:906
  343.8 2.2 collective-permute-done.22
  346.1 2.8 collective-permute-done.23
  351.9 2.9 collective-permute-start.30
  354.8 3.2 collective-permute-done.50
  358.8 1.8 fusion.78.ranks
  360.8 10.2 %shard_map.262 = (f32[14,128,128]{2,1,0:T(8,128)}, f32[14,128,128]{2,1,0:T(8,128)}) custom-call(f32[14,128,128]{2,1,0:T(8,128)} %sl.3, f32[14,128,128]{2,1,0:T(8,128)} %sr.3, f32[14,128,128]{2,1,0:T(8,128)} %bl.3, f32[14,128,128]{2,1,0:T(8,128)} %br.3), custom_call_target="tpu_custom_call" | custom-call | tf_op jit(solution)/shard_map/pallas_call | solution.py:184
  371.5 2.4 add_convert_fusion.3
  375.5 2.4 add_convert_fusion.2
  379.4 2.4 collective-permute-start.53
  381.9 15.1 %collective-permute-done.31 = bf16[2,4,4,128,128]{4,3,2,1,0:T(8,128)(2,1)S(1)} collective-permute-done((bf16[2,4,4,128,128]{4,3,2,1,0:T(8,128)(2,1)S(1)}, bf16[2,4,4,128,128]{4,3,2,1,0:T(8,128)(2,1)S(1)}, u32[]{:S(2)}, u32[]{:S(2)}) %collective-permute-start.31) | collective-permute-done | bytes 1048608 | tf_op jit(solution)/shard_map/ppermute | solution.py:906
  398.5 2.2 collective-permute-done.37
  403.1 8.8 %collective-permute-done.32 = bf16[4,4,128,128]{3,2,1,0:T(8,128)(2,1)S(1)} collective-permute-done((bf16[4,4,128,128]{3,2,1,0:T(8,128)(2,1)S(1)}, bf16[4,4,128,128]{3,2,1,0:T(8,128)(2,1)S(1)}, u32[]{:S(2)}, u32[]{:S(2)}) %collective-permute-start.32) | collective-permute-done | bytes 524320 | tf_op jit(solution)/shard_map/ppermute | solution.py:906
  415.2 3.0 collective-permute-start.40
  418.3 8.9 %collective-permute-done.35 = bf16[4,128,128]{2,1,0:T(8,128)(2,1)S(1)} collective-permute-done((bf16[4,128,128]{2,1,0:T(8,128)(2,1)S(1)}, bf16[4,128,128]{2,1,0:T(8,128)(2,1)S(1)}, u32[]{:S(2)}, u32[]{:S(2)}) %collective-permute-start.35) | collective-permute-done | bytes 131104 | tf_op jit(solution)/shard_map/ppermute | solution.py:906
  427.2 5.2 collective-permute-done.40
  432.4 2.5 collective-permute-done.41
  435.0 1.7 multiply_reduce_fusion.1
  438.0 2.4 collective-permute-start.54
  443.0 1.9 fusion.90
  446.0 1.9 broadcast_select_fusion
  447.9 12.6 %shard_map.261 = (f32[14,128,128]{2,1,0:T(8,128)}, f32[14,128,128]{2,1,0:T(8,128)}, f32[14,128,128]{2,1,0:T(8,128)}, f32[14,128,128]{2,1,0:T(8,128)}, f32[14,128,128]{2,1,0:T(8,128)}) custom-call(s32[14]{0:T(128)} %fusion.78.ranks, f32[14,128,128]{2,1,0:T(8,128)} %get-tuple-element.179.refs_0_, f32[14,128,128]{2,1,0:T(8,128)} %bl.3, f32[14,128,128]{2,1,0:T(8,128)} %br.3), custom_call_target="tpu_custom_call" | custom-call | tf_op jit(solution)/shard_map/pallas_call | solution.py:205
  463.4 3.2 collective-permute-start.58
  467.0 7.7 %collective-permute-start.59 = (f32[2,2,2,2304]{3,2,1,0:T(2,128)S(1)}, f32[2,2,2,2304]{3,2,1,0:T(2,128)S(1)}, u32[]{:S(2)}, u32[]{:S(2)}) collective-permute-start(f32[2,2,2,2304]{3,2,1,0:T(2,128)S(1)} %pad_maximum_fusion.4), channel_id=1, source_target_pairs={{0,8},{8,16},{16,24},{24,0},{1,9},{9,17},{17,25},{25,1},{2,10},{10... | collective-permute-start | bytes 221192 | tf_op jit(solution)/shard_map/ppermute | solution.py:906
  479.1 16.7 %collective-permute-done.42 = bf16[4,208,768]{2,1,0:T(8,128)(2,1)} collective-permute-done((bf16[4,208,768]{2,1,0:T(8,128)(2,1)S(1)}, bf16[4,208,768]{2,1,0:T(8,128)(2,1)}, u32[]{:S(2)}, u32[]{:S(2)}) %collective-permute-start.42) | collective-permute-done | bytes 1277984 | tf_op jit(solution)/shard_map/ppermute | solution.py:906
  497.6 1.8 collective-permute-start.44
  501.3 43.0 %shard_map.263 = (f32[14,128,128]{2,1,0:T(8,128)}, f32[14,128,128]{2,1,0:T(8,128)}, f32[14,128,128]{2,1,0:T(8,128)}, f32[14,128,128]{2,1,0:T(8,128)}, f32[14,128...) custom-call(f32[1]{0:T(128)} %bitcast.108.factor, f32[14,128,128]{2,1,0:T(8,128)} %get-tuple-element.119.rot, ...), custom_call_target="tpu_custom_call" | custom-call | tf_op jit(solution)/shard_map/pallas_call | solution.py:299
  (299 shorter events, 76.9 us)
Async XLA Ops:
  7.2 146.6 %all-gather.2.cloned.1.call-start = ((), (), s32[]{:S(2)}) async-start(), calls=%async_computation | async-start | bytes 15138816 | tf_op jit(solution)/shard_map/all_gather | solution.py:1098
  13.8 18.6 %collective-permute-start.12 = (bf16[208,768]{1,0:T(8,128)(2,1)S(1)}, bf16[208,768]{1,0:T(8,128)(2,1)S(1)}, u32[]{:S(2)}, u32[]{:S(2)}) collective-permute-start(bf16[208,768]{1,0:T(8,128)(2,1)S(1)} %get-tuple-element.182), channel_id=1, source_target_pairs={{0,24},{8,0},{16,8},{24,16},{1,25},{9,1},{17,9},{25,17},{2,26},{10... | collective-permute-start | bytes 958472 | tf_op jit(solution)/shard_map/ppermute | solution.py:906
  14.1 30.3 %collective-permute-start.13 = (bf16[208,768]{1,0:T(8,128)(2,1)S(1)}, bf16[208,768]{1,0:T(8,128)(2,1)}, u32[]{:S(2)}, u32[]{:S(2)}) collective-permute-start(bf16[208,768]{1,0:T(8,128)(2,1)S(1)} %get-tuple-element.182), channel_id=1, source_target_pairs={{0,16},{8,24},{16,0},{24,8},{1,17},{9,25},{17,1},{25,9},{2,18},{10... | collective-permute-start | bytes 958472 | tf_op jit(solution)/shard_map/ppermute | solution.py:906
  16.4 36.3 %collective-permute-start.14 = (bf16[208,768]{1,0:T(8,128)(2,1)S(1)}, bf16[208,768]{1,0:T(8,128)(2,1)}, u32[]{:S(2)}, u32[]{:S(2)}) collective-permute-start(bf16[208,768]{1,0:T(8,128)(2,1)S(1)} %get-tuple-element.182), channel_id=1, source_target_pairs={{0,8},{8,16},{16,24},{24,0},{1,9},{9,17},{17,25},{25,1},{2,10},{10... | collective-permute-start | bytes 958472 | tf_op jit(solution)/shard_map/ppermute | solution.py:906
  18.6 45.7 %collective-permute-start.16 = (bf16[208,768]{1,0:T(8,128)(2,1)S(1)}, bf16[208,768]{1,0:T(8,128)(2,1)S(1)}, u32[]{:S(2)}, u32[]{:S(2)}) collective-permute-start(bf16[208,768]{1,0:T(8,128)(2,1)S(1)} %get-tuple-element.181), channel_id=1, source_target_pairs={{4,0},{8,4},{12,8},{16,12},{20,16},{24,20},{28,24},{0,28},{5,1},{9... | collective-permute-start | bytes 958472 | tf_op jit(solution)/shard_map/ppermute | solution.py:1067
  18.8 45.4 %collective-permute-start.17 = (bf16[208,768]{1,0:T(8,128)(2,1)S(1)}, bf16[208,768]{1,0:T(8,128)(2,1)S(1)}, u32[]{:S(2)}, u32[]{:S(2)}) collective-permute-start(bf16[208,768]{1,0:T(8,128)(2,1)S(1)} %get-tuple-element.181), channel_id=1, source_target_pairs={{0,4},{4,8},{8,12},{12,16},{16,20},{20,24},{24,28},{28,0},{1,5},{5... | collective-permute-start | bytes 958472 | tf_op jit(solution)/shard_map/ppermute | solution.py:1066
  54.0 48.0 %collective-permute-start.15 = (bf16[4,208,768]{2,1,0:T(8,128)(2,1)S(1)}, bf16[4,208,768]{2,1,0:T(8,128)(2,1)S(1)}, u32[]{:S(2)}, u32[]{:S(2)}) collective-permute-start(bf16[4,208,768]{2,1,0:T(8,128)(2,1)S(1)} %get-tuple-element.177), channel_id=1, source_target_pairs={{0,4},{4,0},{1,5},{5,1},{2,6},{6,2},{3,7},{7,3},{8,12},{12,8},{9,1... | collective-permute-start | bytes 3833864 | tf_op jit(solution)/shard_map/ppermute | solution.py:906
  237.8 59.0 %collective-permute-start.24 = (bf16[48,128,128]{2,1,0:T(8,128)(2,1)}, bf16[48,128,128]{2,1,0:T(8,128)(2,1)S(1)}, u32[]{:S(2)}, u32[]{:S(2)}) collective-permute-start(bf16[48,128,128]{2,1,0:T(8,128)(2,1)} %get-tuple-element.104), channel_id=1, source_target_pairs={{0,1},{1,0},{2,3},{3,2},{4,5},{5,4},{6,7},{7,6},{8,9},{9,8},{10,11... | collective-permute-start | bytes 4718600 | tf_op jit(solution)/shard_map/ppermute | solution.py:906
  295.4 4.1 collective-permute-start.18
  298.4 19.2 %collective-permute-start.25 = (bf16[2,4,3,128,128]{4,3,2,1,0:T(8,128)(2,1)}, bf16[2,4,3,128,128]{4,3,2,1,0:T(8,128)(2,1)}, u32[]{:S(2)}, u32[]{:S(2)}) collective-permute-start(bf16[2,4,3,128,128]{4,3,2,1,0:T(8,128)(2,1)} %bitcast.60), channel_id=1, source_target_pairs={{0,2},{2,0},{1,3},{3,1},{4,6},{6,4},{5,7},{7,5},{8,10},{10,8},{9,1... | collective-permute-start | bytes 2359304 | tf_op jit(solution)/shard_map/ppermute | solution.py:906
  301.3 19.0 %collective-permute-start.19 = (bf16[2,4,3,128,128]{4,3,2,1,0:T(8,128)(2,1)}, bf16[2,4,3,128,128]{4,3,2,1,0:T(8,128)(2,1)}, u32[]{:S(2)}, u32[]{:S(2)}) collective-permute-start(bf16[2,4,3,128,128]{4,3,2,1,0:T(8,128)(2,1)} %bitcast.52), channel_id=1, source_target_pairs={{0,4},{4,0},{1,5},{5,1},{2,6},{6,2},{3,7},{7,3},{8,12},{12,8},{9,1... | collective-permute-start | bytes 2359304 | tf_op jit(solution)/shard_map/ppermute | solution.py:906
  319.0 9.6 %collective-permute-start.26 = (bf16[4,3,128,128]{3,2,1,0:T(8,128)(2,1)S(1)}, bf16[4,3,128,128]{3,2,1,0:T(8,128)(2,1)S(1)}, u32[]{:S(2)}, u32[]{:S(2)}) collective-permute-start(bf16[4,3,128,128]{3,2,1,0:T(8,128)(2,1)S(1)} %slice_bitcast_fusion.16), channel_id=1, source_target_pairs={{0,4},{4,0},{1,5},{5,1},{2,6},{6,2},{3,7},{7,3},{8,12},{12,8},{9,1... | collective-permute-start | bytes 1179656 | tf_op jit(solution)/shard_map/ppermute | solution.py:906
  321.7 10.3 %collective-permute-start.20 = (bf16[4,3,128,128]{3,2,1,0:T(8,128)(2,1)S(1)}, bf16[4,3,128,128]{3,2,1,0:T(8,128)(2,1)S(1)}, u32[]{:S(2)}, u32[]{:S(2)}) collective-permute-start(bf16[4,3,128,128]{3,2,1,0:T(8,128)(2,1)S(1)} %slice_bitcast_fusion.18), channel_id=1, source_target_pairs={{0,2},{2,0},{1,3},{3,1},{4,6},{6,4},{5,7},{7,5},{8,10},{10,8},{9,1... | collective-permute-start | bytes 1179656 | tf_op jit(solution)/shard_map/ppermute | solution.py:906
  328.8 7.0 %collective-permute-start.27 = (bf16[3,128,128]{2,1,0:T(8,128)(2,1)S(1)}, bf16[3,128,128]{2,1,0:T(8,128)(2,1)S(1)}, u32[]{:S(2)}, u32[]{:S(2)}) collective-permute-start(bf16[3,128,128]{2,1,0:T(8,128)(2,1)S(1)} %get-tuple-element.190), channel_id=1, source_target_pairs={{0,8},{8,16},{16,24},{24,0},{1,9},{9,17},{17,25},{25,1},{2,10},{10... | collective-permute-start | bytes 294920 | tf_op jit(solution)/shard_map/ppermute | solution.py:906
  330.0 6.2 %collective-permute-start.28 = (bf16[3,128,128]{2,1,0:T(8,128)(2,1)S(1)}, bf16[3,128,128]{2,1,0:T(8,128)(2,1)S(1)}, u32[]{:S(2)}, u32[]{:S(2)}) collective-permute-start(bf16[3,128,128]{2,1,0:T(8,128)(2,1)S(1)} %get-tuple-element.192), channel_id=1, source_target_pairs={{0,16},{8,24},{16,0},{24,8},{1,17},{9,25},{17,1},{25,9},{2,18},{10... | collective-permute-start | bytes 294920 | tf_op jit(solution)/shard_map/ppermute | solution.py:906
  332.1 11.0 %collective-permute-start.29 = (bf16[3,128,128]{2,1,0:T(8,128)(2,1)S(1)}, bf16[3,128,128]{2,1,0:T(8,128)(2,1)S(1)}, u32[]{:S(2)}, u32[]{:S(2)}) collective-permute-start(bf16[3,128,128]{2,1,0:T(8,128)(2,1)S(1)} %get-tuple-element.191), channel_id=1, source_target_pairs={{0,24},{8,0},{16,8},{24,16},{1,25},{9,1},{17,9},{25,17},{2,26},{10... | collective-permute-start | bytes 294920 | tf_op jit(solution)/shard_map/ppermute | solution.py:906
  332.2 11.6 %collective-permute-start.21 = (bf16[3,128,128]{2,1,0:T(8,128)(2,1)S(1)}, bf16[3,128,128]{2,1,0:T(8,128)(2,1)S(1)}, u32[]{:S(2)}, u32[]{:S(2)}) collective-permute-start(bf16[3,128,128]{2,1,0:T(8,128)(2,1)S(1)} %get-tuple-element.193), channel_id=1, source_target_pairs={{0,8},{8,16},{16,24},{24,0},{1,9},{9,17},{17,25},{25,1},{2,10},{10... | collective-permute-start | bytes 294920 | tf_op jit(solution)/shard_map/ppermute | solution.py:906
  333.7 12.4 %collective-permute-start.22 = (bf16[3,128,128]{2,1,0:T(8,128)(2,1)S(1)}, bf16[3,128,128]{2,1,0:T(8,128)(2,1)S(1)}, u32[]{:S(2)}, u32[]{:S(2)}) collective-permute-start(bf16[3,128,128]{2,1,0:T(8,128)(2,1)S(1)} %get-tuple-element.195), channel_id=1, source_target_pairs={{0,16},{8,24},{16,0},{24,8},{1,17},{9,25},{17,1},{25,9},{2,18},{10... | collective-permute-start | bytes 294920 | tf_op jit(solution)/shard_map/ppermute | solution.py:906
  335.9 13.0 %collective-permute-start.23 = (bf16[3,128,128]{2,1,0:T(8,128)(2,1)S(1)}, bf16[3,128,128]{2,1,0:T(8,128)(2,1)S(1)}, u32[]{:S(2)}, u32[]{:S(2)}) collective-permute-start(bf16[3,128,128]{2,1,0:T(8,128)(2,1)S(1)} %get-tuple-element.194), channel_id=1, source_target_pairs={{0,24},{8,0},{16,8},{24,16},{1,25},{9,1},{17,9},{25,17},{2,26},{10... | collective-permute-start | bytes 294920 | tf_op jit(solution)/shard_map/ppermute | solution.py:906
  349.8 5.0 collective-permute-start.48
  349.9 4.9 collective-permute-start.49
  351.0 7.0 %collective-permute-start.50 = (f32[2,2,2,2176]{3,2,1,0:T(2,128)S(1)}, f32[2,2,2,2176]{3,2,1,0:T(2,128)S(1)}, u32[]{:S(2)}, u32[]{:S(2)}) collective-permute-start(f32[2,2,2,2176]{3,2,1,0:T(2,128)S(1)} %get-tuple-element.198), channel_id=1, source_target_pairs={{0,24},{8,0},{16,8},{24,16},{1,25},{9,1},{17,9},{25,17},{2,26},{10... | collective-permute-start | bytes 208904 | tf_op jit(solution)/shard_map/ppermute | solution.py:906
  351.9 19.6 %collective-permute-start.30 = (bf16[64,128,128]{2,1,0:T(8,128)(2,1)}, bf16[64,128,128]{2,1,0:T(8,128)(2,1)}, u32[]{:S(2)}, u32[]{:S(2)}) collective-permute-start(bf16[64,128,128]{2,1,0:T(8,128)(2,1)} %get-tuple-element.108), channel_id=1, source_target_pairs={{0,1},{1,0},{2,3},{3,2},{4,5},{5,4},{6,7},{7,6},{8,9},{9,8},{10,11... | collective-permute-start | bytes 6291464 | tf_op jit(solution)/shard_map/ppermute | solution.py:906
  354.8 20.6 %collective-permute-start.36 = (bf16[64,128,128]{2,1,0:T(8,128)(2,1)}, bf16[64,128,128]{2,1,0:T(8,128)(2,1)}, u32[]{:S(2)}, u32[]{:S(2)}) collective-permute-start(bf16[64,128,128]{2,1,0:T(8,128)(2,1)} %get-tuple-element.110), channel_id=1, source_target_pairs={{0,1},{1,0},{2,3},{3,2},{4,5},{5,4},{6,7},{7,6},{8,9},{9,8},{10,11... | collective-permute-start | bytes 6291464 | tf_op jit(solution)/shard_map/ppermute | solution.py:906
  358.0 13.0 %collective-permute-start.51 = (f32[2,2,2176]{2,1,0:T(2,128)S(1)}, f32[2,2,2176]{2,1,0:T(2,128)S(1)}, u32[]{:S(2)}, u32[]{:S(2)}) collective-permute-start(f32[2,2,2176]{2,1,0:T(2,128)S(1)} %slice_bitcast_fusion.44), channel_id=1, source_target_pairs={{0,4},{4,0},{1,5},{5,1},{2,6},{6,2},{3,7},{7,3},{8,12},{12,8},{9,1... | collective-permute-start | bytes 104456 | tf_op jit(solution)/shard_map/ppermute | solution.py:906
  371.1 8.2 %collective-permute-start.52 = (f32[2,2176]{1,0:T(2,128)S(1)}, f32[2,2176]{1,0:T(2,128)S(1)}, u32[]{:S(2)}, u32[]{:S(2)}) collective-permute-start(f32[2,2176]{1,0:T(2,128)S(1)} %slice_bitcast_fusion.46), channel_id=1, source_target_pairs={{0,2},{2,0},{1,3},{3,1},{4,6},{6,4},{5,7},{7,5},{8,10},{10,8},{9,1... | collective-permute-start | bytes 52232 | tf_op jit(solution)/shard_map/ppermute | solution.py:906
  374.2 22.7 %collective-permute-start.31 = (bf16[2,4,4,128,128]{4,3,2,1,0:T(8,128)(2,1)S(1)}, bf16[2,4,4,128,128]{4,3,2,1,0:T(8,128)(2,1)S(1)}, u32[]{:S(2)}, u32[]{:S(2)}) collective-permute-start(bf16[2,4,4,128,128]{4,3,2,1,0:T(8,128)(2,1)S(1)} %bitcast.247), channel_id=1, source_target_pairs={{0,4},{4,0},{1,5},{5,1},{2,6},{6,2},{3,7},{7,3},{8,12},{12,8},{9,1... | collective-permute-start | bytes 3145736 | tf_op jit(solution)/shard_map/ppermute | solution.py:906
  378.2 22.5 %collective-permute-start.37 = (bf16[2,4,4,128,128]{4,3,2,1,0:T(8,128)(2,1)S(1)}, bf16[2,4,4,128,128]{4,3,2,1,0:T(8,128)(2,1)S(1)}, u32[]{:S(2)}, u32[]{:S(2)}) collective-permute-start(bf16[2,4,4,128,128]{4,3,2,1,0:T(8,128)(2,1)S(1)} %bitcast.248), channel_id=1, source_target_pairs={{0,2},{2,0},{1,3},{3,1},{4,6},{6,4},{5,7},{7,5},{8,10},{10,8},{9,1... | collective-permute-start | bytes 3145736 | tf_op jit(solution)/shard_map/ppermute | solution.py:906
  379.4 23.1 %collective-permute-start.53 = (f32[2176]{0:T(1024)S(1)}, f32[2176]{0:T(1024)S(1)}, u32[]{:S(2)}, u32[]{:S(2)}) collective-permute-start(f32[2176]{0:T(1024)S(1)} %get-tuple-element.137), channel_id=1, source_target_pairs={{0,1},{1,0},{2,3},{3,2},{4,5},{5,4},{6,7},{7,6},{8,9},{9,8},{10,11... | collective-permute-start | bytes 26120 | tf_op jit(solution)/shard_map/ppermute | solution.py:906
  397.3 14.6 %collective-permute-start.32 = (bf16[4,4,128,128]{3,2,1,0:T(8,128)(2,1)S(1)}, bf16[4,4,128,128]{3,2,1,0:T(8,128)(2,1)S(1)}, u32[]{:S(2)}, u32[]{:S(2)}) collective-permute-start(bf16[4,4,128,128]{3,2,1,0:T(8,128)(2,1)S(1)} %slice_bitcast_fusion.14), channel_id=1, source_target_pairs={{0,2},{2,0},{1,3},{3,1},{4,6},{6,4},{5,7},{7,5},{8,10},{10,8},{9,1... | collective-permute-start | bytes 1572872 | tf_op jit(solution)/shard_map/ppermute | solution.py:906
  401.1 12.7 %collective-permute-start.38 = (bf16[4,4,128,128]{3,2,1,0:T(8,128)(2,1)S(1)}, bf16[4,4,128,128]{3,2,1,0:T(8,128)(2,1)S(1)}, u32[]{:S(2)}, u32[]{:S(2)}) collective-permute-start(bf16[4,4,128,128]{3,2,1,0:T(8,128)(2,1)S(1)} %slice_bitcast_fusion.12), channel_id=1, source_target_pairs={{0,4},{4,0},{1,5},{5,1},{2,6},{6,2},{3,7},{7,3},{8,12},{12,8},{9,1... | collective-permute-start | bytes 1572872 | tf_op jit(solution)/shard_map/ppermute | solution.py:906
  412.1 6.2 %collective-permute-start.33 = (bf16[4,128,128]{2,1,0:T(8,128)(2,1)S(1)}, bf16[4,128,128]{2,1,0:T(8,128)(2,1)S(1)}, u32[]{:S(2)}, u32[]{:S(2)}) collective-permute-start(bf16[4,128,128]{2,1,0:T(8,128)(2,1)S(1)} %get-tuple-element.184), channel_id=1, source_target_pairs={{0,8},{8,16},{16,24},{24,0},{1,9},{9,17},{17,25},{25,1},{2,10},{10... | collective-permute-start | bytes 393224 | tf_op jit(solution)/shard_map/ppermute | solution.py:906
  412.2 6.1 %collective-permute-start.34 = (bf16[4,128,128]{2,1,0:T(8,128)(2,1)S(1)}, bf16[4,128,128]{2,1,0:T(8,128)(2,1)S(1)}, u32[]{:S(2)}, u32[]{:S(2)}) collective-permute-start(bf16[4,128,128]{2,1,0:T(8,128)(2,1)S(1)} %get-tuple-element.186), channel_id=1, source_target_pairs={{0,16},{8,24},{16,0},{24,8},{1,17},{9,25},{17,1},{25,9},{2,18},{10... | collective-permute-start | bytes 393224 | tf_op jit(solution)/shard_map/ppermute | solution.py:906
  412.3 14.9 %collective-permute-start.35 = (bf16[4,128,128]{2,1,0:T(8,128)(2,1)S(1)}, bf16[4,128,128]{2,1,0:T(8,128)(2,1)S(1)}, u32[]{:S(2)}, u32[]{:S(2)}) collective-permute-start(bf16[4,128,128]{2,1,0:T(8,128)(2,1)S(1)} %get-tuple-element.185), channel_id=1, source_target_pairs={{0,24},{8,0},{16,8},{24,16},{1,25},{9,1},{17,9},{25,17},{2,26},{10... | collective-permute-start | bytes 393224 | tf_op jit(solution)/shard_map/ppermute | solution.py:906
  414.0 13.3 %collective-permute-start.39 = (bf16[4,128,128]{2,1,0:T(8,128)(2,1)S(1)}, bf16[4,128,128]{2,1,0:T(8,128)(2,1)S(1)}, u32[]{:S(2)}, u32[]{:S(2)}) collective-permute-start(bf16[4,128,128]{2,1,0:T(8,128)(2,1)S(1)} %get-tuple-element.187), channel_id=1, source_target_pairs={{0,8},{8,16},{16,24},{24,0},{1,9},{9,17},{17,25},{25,1},{2,10},{10... | collective-permute-start | bytes 393224 | tf_op jit(solution)/shard_map/ppermute | solution.py:906
  415.2 17.2 %collective-permute-start.40 = (bf16[4,128,128]{2,1,0:T(8,128)(2,1)S(1)}, bf16[4,128,128]{2,1,0:T(8,128)(2,1)S(1)}, u32[]{:S(2)}, u32[]{:S(2)}) collective-permute-start(bf16[4,128,128]{2,1,0:T(8,128)(2,1)S(1)} %get-tuple-element.189), channel_id=1, source_target_pairs={{0,16},{8,24},{16,0},{24,8},{1,17},{9,25},{17,1},{25,9},{2,18},{10... | collective-permute-start | bytes 393224 | tf_op jit(solution)/shard_map/ppermute | solution.py:906
  418.3 16.7 %collective-permute-start.41 = (bf16[4,128,128]{2,1,0:T(8,128)(2,1)S(1)}, bf16[4,128,128]{2,1,0:T(8,128)(2,1)S(1)}, u32[]{:S(2)}, u32[]{:S(2)}) collective-permute-start(bf16[4,128,128]{2,1,0:T(8,128)(2,1)S(1)} %get-tuple-element.188), channel_id=1, source_target_pairs={{0,24},{8,0},{16,8},{24,16},{1,25},{9,1},{17,9},{25,17},{2,26},{10... | collective-permute-start | bytes 393224 | tf_op jit(solution)/shard_map/ppermute | solution.py:906
  438.0 3.6 collective-permute-start.54
  444.9 18.4 %collective-permute-start.56 = (f32[2,2,2304]{2,1,0:T(2,128)S(1)}, f32[2,2,2304]{2,1,0:T(2,128)S(1)}, u32[]{:S(2)}, u32[]{:S(2)}) collective-permute-start(f32[2,2,2304]{2,1,0:T(2,128)S(1)} %get-tuple-element.203), channel_id=1, source_target_pairs={{0,4},{4,0},{1,5},{5,1},{2,6},{6,2},{3,7},{7,3},{8,12},{12,8},{9,1... | collective-permute-start | bytes 110600 | tf_op jit(solution)/shard_map/ppermute | solution.py:906
  460.4 35.3 %collective-permute-start.42 = (bf16[4,208,768]{2,1,0:T(8,128)(2,1)S(1)}, bf16[4,208,768]{2,1,0:T(8,128)(2,1)}, u32[]{:S(2)}, u32[]{:S(2)}) collective-permute-start(bf16[4,208,768]{2,1,0:T(8,128)(2,1)S(1)} %bitcast.245), channel_id=1, source_target_pairs={{0,4},{4,0},{1,5},{5,1},{2,6},{6,2},{3,7},{7,3},{8,12},{12,8},{9,1... | collective-permute-start | bytes 3833864 | tf_op jit(solution)/shard_map/ppermute | solution.py:906
  460.9 83.5 %collective-permute-start.46 = (bf16[208,768]{1,0:T(8,128)(2,1)}, bf16[208,768]{1,0:T(8,128)(2,1)}, u32[]{:S(2)}, u32[]{:S(2)}) collective-permute-start(bf16[208,768]{1,0:T(8,128)(2,1)} %get-tuple-element.163), channel_id=1, source_target_pairs={{4,0},{8,4},{12,8},{16,12},{20,16},{24,20},{28,24},{0,28},{5,1},{9... | collective-permute-start | bytes 958472 | tf_op jit(solution)/shard_map/ppermute | solution.py:1193
  461.9 82.5 %collective-permute-start.47 = (bf16[208,768]{1,0:T(8,128)(2,1)}, bf16[208,768]{1,0:T(8,128)(2,1)}, u32[]{:S(2)}, u32[]{:S(2)}) collective-permute-start(bf16[208,768]{1,0:T(8,128)(2,1)} %get-tuple-element.164), channel_id=1, source_target_pairs={{0,4},{4,8},{8,12},{12,16},{16,20},{20,24},{24,28},{28,0},{1,5},{5... | collective-permute-start | bytes 958472 | tf_op jit(solution)/shard_map/ppermute | solution.py:1194
  463.3 3.7 collective-permute-start.57
  463.4 12.1 %collective-permute-start.58 = (f32[2,2,2,2304]{3,2,1,0:T(2,128)S(1)}, f32[2,2,2,2304]{3,2,1,0:T(2,128)S(1)}, u32[]{:S(2)}, u32[]{:S(2)}) collective-permute-start(f32[2,2,2,2304]{3,2,1,0:T(2,128)S(1)} %pad_maximum_fusion.4), channel_id=1, source_target_pairs={{0,16},{8,24},{16,0},{24,8},{1,17},{9,25},{17,1},{25,9},{2,18},{10... | collective-permute-start | bytes 221192 | tf_op jit(solution)/shard_map/ppermute | solution.py:906
  467.0 9.4 %collective-permute-start.59 = (f32[2,2,2,2304]{3,2,1,0:T(2,128)S(1)}, f32[2,2,2,2304]{3,2,1,0:T(2,128)S(1)}, u32[]{:S(2)}, u32[]{:S(2)}) collective-permute-start(f32[2,2,2,2304]{3,2,1,0:T(2,128)S(1)} %pad_maximum_fusion.4), channel_id=1, source_target_pairs={{0,8},{8,16},{16,24},{24,0},{1,9},{9,17},{17,25},{25,1},{2,10},{10... | collective-permute-start | bytes 221192 | tf_op jit(solution)/shard_map/ppermute | solution.py:906
  497.5 48.3 %collective-permute-start.43 = (bf16[208,768]{1,0:T(8,128)(2,1)S(1)}, bf16[208,768]{1,0:T(8,128)(2,1)S(1)}, u32[]{:S(2)}, u32[]{:S(2)}) collective-permute-start(bf16[208,768]{1,0:T(8,128)(2,1)S(1)} %get-tuple-element.173), channel_id=1, source_target_pairs={{0,8},{8,16},{16,24},{24,0},{1,9},{9,17},{17,25},{25,1},{2,10},{10... | collective-permute-start | bytes 958472 | tf_op jit(solution)/shard_map/ppermute | solution.py:906
  497.6 48.3 %collective-permute-start.44 = (bf16[208,768]{1,0:T(8,128)(2,1)S(1)}, bf16[208,768]{1,0:T(8,128)(2,1)S(1)}, u32[]{:S(2)}, u32[]{:S(2)}) collective-permute-start(bf16[208,768]{1,0:T(8,128)(2,1)S(1)} %get-tuple-element.175), channel_id=1, source_target_pairs={{0,16},{8,24},{16,0},{24,8},{1,17},{9,25},{17,1},{25,9},{2,18},{10... | collective-permute-start | bytes 958472 | tf_op jit(solution)/shard_map/ppermute | solution.py:906
  499.4 46.5 %collective-permute-start.45 = (bf16[208,768]{1,0:T(8,128)(2,1)S(1)}, bf16[208,768]{1,0:T(8,128)(2,1)S(1)}, u32[]{:S(2)}, u32[]{:S(2)}) collective-permute-start(bf16[208,768]{1,0:T(8,128)(2,1)S(1)} %get-tuple-element.174), channel_id=1, source_target_pairs={{0,24},{8,0},{16,8},{24,16},{1,25},{9,1},{17,9},{25,17},{2,26},{10... | collective-permute-start | bytes 958472 | tf_op jit(solution)/shard_map/ppermute | solution.py:906
  (42 other events, 417.0 us)
Sparse Core Ops, SparseCore 0:
  11.4 142.3 all-gather.1

commit v3 on v2

--- a/solution.py
+++ b/solution.py
@@ -171,136 +171,217 @@
 def dot_wide(a, b, dims):
     return dot_parts(halves(a), halves(b), dims)
 
-def stat_kernel(sl, sr, bl, br, ol, orr):
-    ol[0] = STAT_DECAY * dot_wide(bl[0], sl[0], TN)
-    orr[0] = STAT_DECAY * dot_wide(br[0], sr[0], TN)
-
-def slot_spec():
-    return pl.BlockSpec((1, BLOCK_SIDE, BLOCK_SIDE), lambda i: (i, 0, 0))
+def slots_step(n):
+    return 7 if n % 7 == 0 else 2 if n % 2 == 0 else 1
+
 
 def stat_products(sl, sr, bl, br):
     n = sl.shape[0]
-    shape = jax.ShapeDtypeStruct(sl.shape, F32)
-    return pl.pallas_call(stat_kernel, grid=(n,), in_specs=[slot_spec()]*4, out_specs=[slot_spec()]*2, out_shape=[shape]*2)(sl, sr, bl, br)
-
-def raw_kernel(g, bl, br, rot, gl, gr, ql, qr):
-    gp = halves(g[0]); blp = halves(bl[0]); brp = halves(br[0])
-    u = halves(dot_parts(blp, gp, TN))
-    v = halves(dot_parts(gp, brp, NN))
-    rot[0] = dot_parts(u, brp, NN)
-    gl[0] = dot_parts(gp, gp, NT_)
-    gr[0] = dot_parts(gp, gp, TN)
-    ql[0] = dot_parts(u, gp, NT_)
-    qr[0] = dot_parts(v, gp, TN)
+    many = slots_step(n)
+    spec = pl.BlockSpec((many, BLOCK_SIDE, BLOCK_SIDE), lambda i: (i, 0, 0))
+
+    def kernel(sl, sr, bl, br, out_left, out_right):
+        for s in range(many):
+            out_left[s] = STAT_DECAY * dot_wide(bl[s], sl[s], TN)
+            out_right[s] = STAT_DECAY * dot_wide(br[s], sr[s], TN)
+
+    return pl.pallas_call(
+        kernel,
+        grid=(n // many,),
+        in_specs=[spec] * 4,
+        out_specs=[spec] * 2,
+        out_shape=[jax.ShapeDtypeStruct(sl.shape, F32)] * 2,
+        cost_estimate=about(7),
+    )(sl, sr, bl, br)
+
 
 def raw_products(ranks, g, bl, br):
     n = g.shape[0]
-    shape = jax.ShapeDtypeStruct(g.shape, F32)
-    here = pl.BlockSpec((1, BLOCK_SIDE, BLOCK_SIDE), lambda i, ranks: (i, 0, 0))
-    ranked = pl.BlockSpec((1, BLOCK_SIDE, BLOCK_SIDE), lambda i, ranks: (ranks[i], 0, 0))
+    many = slots_step(n)
+    here = pl.BlockSpec((many, BLOCK_SIDE, BLOCK_SIDE), lambda i, ranks: (i, 0, 0))
+
+    def ranked(s):
+        return pl.BlockSpec((1, BLOCK_SIDE, BLOCK_SIDE), lambda i, ranks: (ranks[i * many + s], 0, 0))
 
     def kernel(ranks, *refs):
-        raw_kernel(*refs)
+        grads, (bl, br, rot, gl, gr, ql, qr) = refs[:many], refs[many:]
+        each = range(many)
+        gp = [halves(grads[s][0]) for s in each]
+        blp, brp = [halves(bl[s]) for s in each], [halves(br[s]) for s in each]
+        u = [halves(dot_parts(blp[s], gp[s], TN)) for s in each]
+        v = [halves(dot_parts(gp[s], brp[s], NN)) for s in each]
+        for s in each:
+            gl[s] = dot_parts(gp[s], gp[s], NT_)
+        for s in each:
+            gr[s] = dot_parts(gp[s], gp[s], TN)
+        for s in each:
+            rot[s] = dot_parts(u[s], brp[s], NN)
+        for s in each:
+            ql[s] = dot_parts(u[s], gp[s], NT_)
+        for s in each:
+            qr[s] = dot_parts(v[s], gp[s], TN)
 
     return pl.pallas_call(
         kernel,
         grid_spec=pltpu.PrefetchScalarGridSpec(
-            num_scalar_prefetch=1, grid=(n,), in_specs=[ranked, here, here], out_specs=[here] * 5
+            num_scalar_prefetch=1,
+            grid=(n // many,),
+            in_specs=[ranked(s) for s in range(many)] + [here, here],
+            out_specs=[here] * 5,
         ),
-        out_shape=[shape] * 5,
-    )(ranks, g, bl, br)
+        out_shape=[jax.ShapeDtypeStruct(g.shape, F32)] * 5,
+        cost_estimate=about(8),
+    )(ranks, *([g] * many), bl, br)
 
 
 NB=32
-def finish_kernel(factor, rot, gl, gr, ql, qr, pl_, pr_, sl, sr, bl, br, master, m1, m2,
-                  o_master, o_m1, o_m2, o_left, o_right, o_bl, o_br, work, elim, mom):
+def tall(parts, order):
+    return jnp.concatenate([parts[which] for which in order], axis=0)
+
+
+def wide(parts, order):
+    return jnp.concatenate([parts[which] for which in order], axis=1)
+
+
+def finish_kernel(factor, *refs):
+    inputs, refs = refs[:14], refs[14:]
+    results, refs = refs[:7], refs[7:]
+    held, made = refs[:14], refs[14:21]
+    work, elim, load_sems, store_sems = refs[21:]
+    p_l, p_r, ql, qr, rot, gl, gr, sl, sr, bl, br, master, m1, m2 = held
+    o_master, o_m1, o_m2, o_left, o_right, o_bl, o_br = made
+    for index in range(14):
+        pltpu.make_async_copy(inputs[index], held[index], load_sems.at[index]).start()
+
+    def ready(*indices):
+        for index in indices:
+            pltpu.make_async_copy(inputs[index], held[index], load_sems.at[index]).wait()
+
+    def store(*indices):
+        for index in indices:
+            pltpu.make_async_copy(made[index], results[index], store_sems.at[index]).start()
+
     n = rot.shape[0]
+    count = 2 * n
     f = factor[0]
     f2 = (1.0 - STAT_DECAY) * f * f
-    for s in range(n):
-        r = f * rot[s]
-        m = BETA_ONE * m1[s] + (1.0 - BETA_ONE) * r
-        v = BETA_TWO * m2[s] + (1.0 - BETA_TWO) * r * r
-        mom[s] = m
-        o_m2[s] = v
-        o_left[s] = STAT_DECAY * sl[s] + f2 * gl[s]
-        o_right[s] = STAT_DECAY * sr[s] + f2 * gr[s]
-        for side, (p_, q_) in enumerate(((pl_, ql), (pr_, qr))):
-            at = p_[s] + f2 * q_[s]
-            work[2*s+side, :, 128:] = at
-            atp = halves(at)
-            work[2*s+side, :, :128] = dot_parts(atp, atp, NT_)
-    rows = lax.broadcasted_iota(jnp.int32, (1, 8, 2*NB), 1)
-    lanes = lax.broadcasted_iota(jnp.int32, (1, 8, 2*NB), 2)
-    count = 2*n
+    ready(0, 1, 2, 3)
+    group = 7 if n % 7 == 0 else n
+    for start in range(0, n, group):
+        members = range(start, start + group)
+        sums = [p_[s] + f2 * q_[s] for s in members for p_, q_ in ((p_l, ql), (p_r, qr))]
+        parts = [halves(at) for at in sums]
+        grams = [dot_parts(atp, atp, NT_) for atp in parts]
+        for i in range(2 * group):
+            work[2 * start + i, :, BLOCK_SIDE:] = sums[i]
+            work[2 * start + i, :, :BLOCK_SIDE] = grams[i]
+
+    rows = lax.broadcasted_iota(jnp.int32, (1, 8, 2 * NB), 1)
+    lanes = lax.broadcasted_iota(jnp.int32, (1, 8, 2 * NB), 2)
+    panels = BLOCK_SIDE // NB
+    tile_count = NB // 8
 
     def panel(p, carry):
-        for q in range(128 // NB):
+        for q in range(panels):
             @pl.when(p == q)
             def _(q=q):
-                for t in range(NB // 8):
-                    block = work[:, NB*q+8*t:NB*q+8*t+8, NB*q:NB*q+NB]
-                    eye = jnp.where(lanes - NB == rows + 8*t, 1.0, 0.0).astype(F32)
-                    eye = jnp.broadcast_to(eye, (count, 8, 2*NB))
-                    elim[:, 8*t:8*t+8, :] = jnp.concatenate([block, eye[:, :, NB:]], axis=2)
-        tiles = [elim[:, 8*t:8*t+8, :] for t in range(NB // 8)]
+                for t in range(tile_count):
+                    block = work[:, NB * q + 8 * t : NB * q + 8 * t + 8, NB * q : NB * q + NB]
+                    eye = jnp.where(lanes - NB == rows + 8 * t, 1.0, 0.0).astype(F32)
+                    eye = jnp.broadcast_to(eye, (count, 8, 2 * NB))
+                    elim[:, 8 * t : 8 * t + 8, :] = jnp.concatenate([block, eye[:, :, NB:]], axis=2)
+        tiles = [elim[:, 8 * t : 8 * t + 8, :] for t in range(tile_count)]
         for k in range(NB):
             t0, j = divmod(k, 8)
-            pivot = tiles[t0][:, j:j+1, k:k+1]
-            scale = lax.rsqrt(pivot)
-            row = tiles[t0][:, j:j+1, :] * scale
-            for t in range(t0, NB // 8):
-                col = tiles[t][:, :, k:k+1] * scale
-                new = tiles[t] - col * row
+            columns = [jnp.broadcast_to(tiles[t][:, :, k : k + 1], tiles[t].shape) for t in range(t0, tile_count)]
+            row = tiles[t0][:, j : j + 1, :] * (1.0 / columns[0][:, j : j + 1, :])
+            for t in range(t0, tile_count):
+                new = tiles[t] - columns[t - t0] * row
                 if t == t0:
-                    new = jnp.where(rows > j, new, jnp.where(rows == j, row, tiles[t]))
+                    new = jnp.where(rows > j, new, tiles[t])
                 tiles[t] = new
-        for t in range(NB // 8):
-            elim[:, 8*t:8*t+8, :] = tiles[t]
-        for q in range(128 // NB):
+        for t in range(tile_count):
+            pivots = jnp.sum(jnp.where(lanes == rows + 8 * t, tiles[t], 0.0), axis=2, keepdims=True)
+            elim[:, 8 * t : 8 * t + 8, :] = tiles[t] * lax.rsqrt(pivots)
+        for q in range(panels):
             @pl.when(p == q)
             def _(q=q):
-                lo, hi = NB*q, NB*q+NB
-                for m in range(count):
-                    inv = halves(elim[m, :, NB:])
-                    y = dot_parts(inv, halves(work[m, lo:hi, :]), NN)
-                    if m % 2 == 0:
-                        o_bl[m // 2, lo:hi, :] = y[:, 128:]
-                    else:
-                        o_br[m // 2, lo:hi, :] = y[:, 128:]
-                    if hi < 128:
-                        yp = halves(y)
-                        up = (yp[0][:, hi:128], yp[1][:, hi:128])
-                        work[m, hi:, :] = work[m, hi:, :] - dot_parts(up, yp, TN)
+                lo, hi = NB * q, NB * q + NB
+                for start in range(0, count, group):
+                    members = range(start, start + group)
+                    inverses = [wide(halves(elim[m, :, NB:]), (0, 0, 1)) for m in members]
+                    sources = [tall(halves(work[m, lo:hi, :]), (0, 1, 0)) for m in members]
+                    solved = [dot_low(inverses[i], sources[i], NN) for i in range(group)]
+                    for i, m in enumerate(members):
+                        (o_bl if m % 2 == 0 else o_br)[m // 2, lo:hi, :] = solved[i][:, BLOCK_SIDE:]
+                    if hi < BLOCK_SIDE:
+                        parts = [halves(y) for y in solved]
+                        updates = [
+                            dot_low(tall(yp, (0, 0, 1))[:, :BLOCK_SIDE], tall(yp, (0, 1, 0)), TN) for yp in parts
+                        ]
+                        for i, m in enumerate(members):
+                            work[m, hi:, :] = work[m, hi:, :] - updates[i][hi:]
         return carry
-    lax.fori_loop(0, 128 // NB, panel, 0)
-
-    for s in range(n):
-        m = mom[s]
-        v = o_m2[s]
-        direction = m / (1.0 - BETA_ONE**STEP) / (jnp.sqrt(v / (1.0 - BETA_TWO**STEP)) + ADAM_EPSILON)
-        blp, brp = halves(bl[s]), halves(br[s])
-        back = halves(dot_parts(blp, halves(direction), NN))
-        returned = dot_parts(back, brp, NT_)
-        o_master[s] = master[s] - LEARN_RATE * (returned + WEIGHT_DECAY * master[s])
-        qlt, qrt = o_bl[s], o_br[s]
-        qltp, qrtp = halves(qlt), halves(qrt)
-        turn_l = halves(dot_parts(qltp, blp, NN))
-        turn_r = halves(dot_parts(qrtp, brp, NN))
-        half = halves(dot_parts(turn_l, halves(m), NN))
-        o_m1[s] = dot_parts(half, turn_r, NT_)
-        o_bl[s] = qlt.T
-        o_br[s] = qrt.T
-
-def finish(factor, rot, gl, gr, ql, qr, pl_, pr_, sl, sr, bl, br, master, m1, m2):
+
+    lax.fori_loop(0, panels, panel, 0)
+
+    ready(4, 5, 6, 7, 8, 9, 10, 11, 12, 13)
+    for start in range(0, n, group):
+        members = range(start, start + group)
+        firsts, directions = [], []
+        for s in members:
+            r = f * rot[s]
+            m = BETA_ONE * m1[s] + (1.0 - BETA_ONE) * r
+            v = BETA_TWO * m2[s] + (1.0 - BETA_TWO) * r * r
+            o_m2[s] = v
+            o_left[s] = STAT_DECAY * sl[s] + f2 * gl[s]
+            o_right[s] = STAT_DECAY * sr[s] + f2 * gr[s]
+            firsts.append(halves(m))
+            directions.append(
+                halves(m / (1.0 - BETA_ONE**STEP) / (jnp.sqrt(v / (1.0 - BETA_TWO**STEP)) + ADAM_EPSILON))
+            )
+        old_left = [halves(bl[s]) for s in members]
+        old_right = [halves(br[s]) for s in members]
+        new_left = [o_bl[s] for s in members]
+        new_right = [o_br[s] for s in members]
+        each = range(group)
+        backs = [halves(dot_parts(old_left[i], directions[i], NN)) for i in each]
+        turns_left = [halves(dot_parts(halves(new_left[i]), old_left[i], NN)) for i in each]
+        turns_right = [halves(dot_parts(halves(new_right[i]), old_right[i], NN)) for i in each]
+        returned = [dot_parts(backs[i], old_right[i], NT_) for i in each]
+        parts = [halves(dot_parts(turns_left[i], firsts[i], NN)) for i in each]
+        moved_firsts = [dot_parts(parts[i], turns_right[i], NT_) for i in each]
+        for i, s in enumerate(members):
+            o_master[s] = master[s] - LEARN_RATE * (returned[i] + WEIGHT_DECAY * master[s])
+            o_m1[s] = moved_firsts[i]
+            o_bl[s] = new_left[i].T
+            o_br[s] = new_right[i].T
+    store(0, 1, 2, 3, 4, 5, 6)
+    for index in range(7):
+        pltpu.make_async_copy(made[index], results[index], store_sems.at[index]).wait()
+
+
+def finish(factor, rot, gl, gr, ql, qr, p_l, p_r, sl, sr, bl, br, master, m1, m2):
     n = rot.shape[0]
     shape = jax.ShapeDtypeStruct(rot.shape, F32)
-    vm = pl.BlockSpec(memory_space=pltpu.VMEM)
-    return pl.pallas_call(finish_kernel,
-        in_specs=[pl.BlockSpec(memory_space=pltpu.SMEM)] + [vm]*14, out_specs=[vm]*7, out_shape=[shape]*7,
-        scratch_shapes=[pltpu.VMEM((2*n,128,256),F32), pltpu.VMEM((2*n,NB,2*NB),F32), pltpu.VMEM((n,128,128),F32)],
-        compiler_params=pltpu.CompilerParams(vmem_limit_bytes=56*1024*1024),
-    )(factor, rot, gl, gr, ql, qr, pl_, pr_, sl, sr, bl, br, master, m1, m2)
+    hbm = pl.BlockSpec(memory_space=pl.ANY)
+    block = pltpu.VMEM((n, BLOCK_SIDE, BLOCK_SIDE), F32)
+    return pl.pallas_call(
+        finish_kernel,
+        in_specs=[pl.BlockSpec(memory_space=pltpu.SMEM)] + [hbm] * 14,
+        out_specs=[hbm] * 7,
+        out_shape=[shape] * 7,
+        scratch_shapes=[block] * 21
+        + [
+            pltpu.VMEM((2 * n, BLOCK_SIDE, 2 * BLOCK_SIDE), F32),
+            pltpu.VMEM((2 * n, NB, 2 * NB), F32),
+            pltpu.SemaphoreType.DMA((14,)),
+            pltpu.SemaphoreType.DMA((7,)),
+        ],
+        compiler_params=pltpu.CompilerParams(vmem_limit_bytes=56 * 1024 * 1024),
+        cost_estimate=about(30),
+    )(factor, p_l, p_r, ql, qr, rot, gl, gr, sl, sr, bl, br, master, m1, m2)
+
 
 def soap(ranks, g, factor, stat_parts, master, m1, m2, sl, sr, bl, br):
     rot, gl, gr, ql, qr = raw_products(ranks, g, bl, br)
@@ -332,6 +413,10 @@
 TAP_OFFSETS = [(tap // 3 - 1) * GRID + tap % 3 - 1 for tap in range(9)]
 
 
+def about(microseconds):
+    return pl.CostEstimate(flops=0, bytes_accessed=int(microseconds * 3e6), transcendentals=0)
+
+
 def in_vmem():
     return pl.BlockSpec(memory_space=pltpu.VMEM)
 
@@ -357,14 +442,14 @@
     return ref.at[pl.ds(row, BLOCK_SIDE), pl.ds(col, BLOCK_SIDE)]
 
 
-def load_matrix(which, codes, buffers, matrix, sem):
+def load_matrix(which, codes, buffers, matrix, sem, first_buffer=0):
     first, count, cols = matrix_places()[which]
 
     def one_block(tile, carry):
         code = codes[first + tile]
         row, col = lax.div(tile, cols), lax.rem(tile, cols)
         for index, buffer in enumerate(buffers):
-            @pl.when(lax.div(code, CODE_BASE) == index)
+            @pl.when(lax.div(code, CODE_BASE) == first_buffer + index)
             def _():
                 pltpu.make_async_copy(
                     buffer.at[lax.rem(code, CODE_BASE)], tile_at(matrix, row, col), sem
@@ -400,7 +485,7 @@
     )
 
 
-def project(codes, buffers, seen, rows14):
+def project(codes, buffers, first_buffer, seen, rows14):
     rows = seen.shape[0]
     steps = rows // OWN_ROWS
     count = len(buffers)
@@ -412,7 +497,7 @@
 
         @pl.when(step == 0)
         def _():
-            load_matrix(0, codes, sources, w_qkv, sem)
+            load_matrix(0, codes, sources, w_qkv, sem, first_buffer)
 
         hat, _ = normalized(seen[...].astype(F32))
         normed = (hat * rows14[0:1] + rows14[1:2]).astype(BF)
@@ -462,52 +547,63 @@
             jax.ShapeDtypeStruct((D, 3 * D), BF),
         ],
         compiler_params=pltpu.CompilerParams(vmem_limit_bytes=VMEM_MOST),
+        cost_estimate=about(15),
     )(codes, *buffers, seen, rows14)
 
 
-def attend_kernel(long_rows, q, k, v, bias, out):
-    lanes = lax.broadcasted_iota(jnp.int32, (1, PAIR), 1)
-    first = lanes < HD
+ROW_STEP = 16
+
+
+def stacked(values):
+    first = lax.broadcasted_iota(jnp.int32, (1, PAIR), 1) < HD
+    nothing = jnp.zeros_like(values)
+    return jnp.concatenate([jnp.where(first, values, nothing), jnp.where(first, nothing, values)], axis=0)
+
+
+def unstacked(values):
+    first = lax.broadcasted_iota(jnp.int32, (1, PAIR), 1) < HD
+    return jnp.where(first, values[:PAD_ROWS], values[PAD_ROWS:])
+
+
+def attend_kernel(long_rows, q, k, v, bias, out, logs, scores, soft):
     total = k.shape[0]
     for frame, (lo, hi) in enumerate(((0, long_rows), (long_rows, total))):
         rows = slice(frame * PAD_ROWS, (frame + 1) * PAD_ROWS)
-        query = q[rows, :]
-        keys, values = k[lo:hi, :], v[lo:hi, :]
-        results = []
-        for side in range(2):
-            chosen = jnp.where(first if side == 0 else ~first, query, jnp.zeros_like(query))
-            scores = dot_low(chosen, keys, NT_) + bias[:, lo:hi]
-            weights = jnp.exp(scores - jnp.max(scores, axis=1, keepdims=True))
-            norm = jnp.sum(weights, axis=1, keepdims=True)
-            results.append(dot_low(weights.astype(BF), values, NN) / norm)
-        out[rows, :] = jnp.where(first, results[0], results[1]).astype(BF)
-
-
-def attend_back_kernel(long_rows, q, k, v, bias, grad, dq, dk, dv):
-    lanes = lax.broadcasted_iota(jnp.int32, (1, PAIR), 1)
-    first = lanes < HD
+        width = hi - lo
+        scores[:, :width] = dot_low(stacked(q[rows, :]), k[lo:hi, :], NT_)
+        norms, peaks = [], []
+        for row in range(0, OWN_ROWS, ROW_STEP):
+            block = scores[row : row + ROW_STEP, :width] + bias[:, lo:hi]
+            peak = jnp.max(block, axis=1, keepdims=True)
+            weights = jnp.exp(block - peak)
+            norms.append(jnp.sum(weights, axis=1, keepdims=True))
+            peaks.append(peak)
+            soft[row : row + ROW_STEP, :width] = weights.astype(BF)
+        norm = jnp.concatenate(norms, axis=0)
+        out[rows, :] = unstacked(dot_low(soft[:, :width], v[lo:hi, :], NN) / norm).astype(BF)
+        logs[rows, :] = unstacked(jnp.broadcast_to(jnp.concatenate(peaks, axis=0) + jnp.log(norm), (OWN_ROWS, PAIR)))
+
+
+def attend_back_kernel(long_rows, q, k, v, bias, out, logs, grad, dq, dk, dv, scores, soft_grads, soft, changes):
     total = k.shape[0]
     for frame, (lo, hi) in enumerate(((0, long_rows), (long_rows, total))):
         rows = slice(frame * PAD_ROWS, (frame + 1) * PAD_ROWS)
-        query, arriving = q[rows, :], grad[rows, :]
-        keys, values = k[lo:hi, :], v[lo:hi, :]
-        query_parts, key_total, value_total = [], 0.0, 0.0
-        for side in range(2):
-            mask = first if side == 0 else ~first
-            chosen = jnp.where(mask, query, jnp.zeros_like(query))
-            incoming = jnp.where(mask, arriving, jnp.zeros_like(arriving))
-            scores = dot_low(keys, chosen, NT_) + bias[lo:hi, :]
-            weights = jnp.exp(scores - jnp.max(scores, axis=0, keepdims=True))
-            soft = weights * (1.0 / jnp.sum(weights, axis=0, keepdims=True))
-            grad_soft = dot_low(values, incoming, NT_)
-            delta = jnp.sum(soft * grad_soft, axis=0, keepdims=True)
-            grad_scores = (soft * (grad_soft - delta)).astype(BF)
-            key_total = key_total + dot_low(grad_scores, chosen, NN)
-            value_total = value_total + dot_low(soft.astype(BF), incoming, NN)
-            query_parts.append(dot_low(grad_scores, keys, TN))
-        dq[rows, :] = (jnp.where(first, query_parts[0], query_parts[1]) * (1.0 / math.sqrt(HD))).astype(BF)
-        dk[lo:hi, :] = key_total.astype(BF)
-        dv[lo:hi, :] = value_total.astype(BF)
+        width = hi - lo
+        query, arriving = stacked(q[rows, :]), stacked(grad[rows, :])
+        products = stacked(grad[rows, :].astype(F32) * out[rows, :].astype(F32))
+        delta = jnp.sum(products, axis=1, keepdims=True)
+        log = jnp.concatenate([logs[rows, 0:1], logs[rows, HD : HD + 1]], axis=0)
+        scores[:, :width] = dot_low(query, k[lo:hi, :], NT_)
+        soft_grads[:, :width] = dot_low(arriving, v[lo:hi, :], NT_)
+        for row in range(0, OWN_ROWS, ROW_STEP):
+            here = slice(row, row + ROW_STEP)
+            weights = jnp.exp(scores[here, :width] + bias[:, lo:hi] - log[here])
+            soft[here, :width] = weights.astype(BF)
+            changes[here, :width] = (weights * (soft_grads[here, :width] - delta[here])).astype(BF)
+        part = unstacked(dot_low(changes[:, :width], k[lo:hi, :], NN))
+        dq[rows, :] = (part * (1.0 / math.sqrt(HD))).astype(BF)
+        dk[lo:hi, :] = dot_low(query, changes[:, :width], TN).T.astype(BF)
+        dv[lo:hi, :] = dot_low(arriving, soft[:, :width], TN).T.astype(BF)
 
 
 def pair_spec(rows, offset=0):
@@ -530,13 +626,15 @@
             pair_spec(keys_total, PAIRS),
             pl.BlockSpec((1, keys_total), lambda i: (0, 0)),
         ],
-        out_specs=pair_spec(OWN_ROWS),
-        out_shape=jax.ShapeDtypeStruct((OWN_ROWS, D), BF),
-        compiler_params=pltpu.CompilerParams(vmem_limit_bytes=48 * 1024 * 1024),
+        out_specs=[pair_spec(OWN_ROWS)] * 2,
+        out_shape=[jax.ShapeDtypeStruct((OWN_ROWS, D), BF), jax.ShapeDtypeStruct((OWN_ROWS, D), F32)],
+        scratch_shapes=[pltpu.VMEM((OWN_ROWS, long_rows), F32), pltpu.VMEM((OWN_ROWS, long_rows), BF)],
+        compiler_params=pltpu.CompilerParams(vmem_limit_bytes=VMEM_MOST),
+        cost_estimate=about(12),
     )(q, kv, kv, bias.reshape(1, -1))
 
 
-def attend_back(q, kv, bias, grad):
+def attend_back(q, kv, bias, out, logs, grad):
     keys_total = kv.shape[0]
     long_rows = keys_total - OWN_ROWS
 
@@ -550,7 +648,9 @@
             pair_spec(OWN_ROWS),
             pair_spec(keys_total),
             pair_spec(keys_total, PAIRS),
-            pl.BlockSpec((keys_total, 1), lambda i: (0, 0)),
+            pl.BlockSpec((1, keys_total), lambda i: (0, 0)),
+            pair_spec(OWN_ROWS),
+            pair_spec(OWN_ROWS),
             pair_spec(OWN_ROWS),
         ],
         out_specs=[pair_spec(OWN_ROWS), pair_spec(keys_total), pair_spec(keys_total)],
@@ -559,8 +659,10 @@
             jax.ShapeDtypeStruct((keys_total, D), BF),
             jax.ShapeDtypeStruct((keys_total, D), BF),
         ],
-        compiler_params=pltpu.CompilerParams(vmem_limit_bytes=48 * 1024 * 1024),
-    )(q, kv, kv, bias.reshape(-1, 1), grad)
+        scratch_shapes=[pltpu.VMEM((OWN_ROWS, long_rows), F32)] * 2 + [pltpu.VMEM((OWN_ROWS, long_rows), BF)] * 2,
+        compiler_params=pltpu.CompilerParams(vmem_limit_bytes=VMEM_MOST),
+        cost_estimate=about(24),
+    )(q, kv, kv, bias.reshape(1, -1), out, logs, grad)
 
 
 def lane_masks():
@@ -598,7 +700,7 @@
     return jnp.concatenate([values, jnp.zeros((values.shape[0], LANES - OWN_ROWS), values.dtype)], axis=1)
 
 
-def middle_kernel(weight_count, codes, targets, *refs):
+def middle_kernel(weight_count, first_buffer, codes, targets, *refs):
     sources = refs[:weight_count]
     (
         att, own, cot, rows14, conv_t, taps_forward, taps_backward, tail_bias, masks, blank,
@@ -610,9 +712,9 @@
         load_sems, send_sems,
     ) = refs[-14:]
     chunks = FF // D
-    load_matrix(1, codes, sources, w_out, load_sems.at[0])
-    load_matrix(2, codes, sources, w_up, load_sems.at[1])
-    load_matrix(3, codes, sources, w_down, load_sems.at[2])
+    load_matrix(1, codes, sources, w_out, load_sems.at[0], first_buffer)
+    load_matrix(2, codes, sources, w_up, load_sems.at[1], first_buffer)
+    load_matrix(3, codes, sources, w_down, load_sems.at[2], first_buffer)
 
     def one_blank(block, total):
         code = targets[block]
@@ -754,11 +856,11 @@
     lax.fori_loop(0, blanks, one_wait, 0)
 
 
-def middle(codes, targets, weights, buffer_shapes, att, own, cot, rows14, conv_t, taps_forward, taps_backward, tail_bias):
+def middle(codes, targets, weights, first_buffer, buffer_shapes, att, own, cot, rows14, conv_t, taps_forward, taps_backward, tail_bias):
     count = len(weights)
 
     def kernel(*refs):
-        middle_kernel(count, *refs)
+        middle_kernel(count, first_buffer, *refs)
 
     def f32(*shape):
         return jax.ShapeDtypeStruct(shape, F32)
@@ -793,6 +895,7 @@
         ),
         out_shape=outs + buffer_shapes,
         compiler_params=pltpu.CompilerParams(vmem_limit_bytes=VMEM_MOST),
+        cost_estimate=about(40),
     )(
         codes, targets, *weights, att, own, cot, rows14, conv_t, taps_forward, taps_backward, tail_bias,
         jnp.asarray(lane_masks()), jnp.zeros((BLOCK_SIDE, BLOCK_SIDE), BF),
@@ -856,6 +959,7 @@
         + [jax.ShapeDtypeStruct((D, 3 * D), BF)],
         input_output_aliases={6 + i: i for i in range(count)},
         compiler_params=pltpu.CompilerParams(vmem_limit_bytes=VMEM_MOST),
+        cost_estimate=about(14),
     )(targets, low, own_low, dq, dk, dv, *buffers)
     return results[:count], results[count]
 
@@ -899,6 +1003,7 @@
             jax.ShapeDtypeStruct((8, D), F32),
         ],
         compiler_params=pltpu.CompilerParams(vmem_limit_bytes=VMEM_MOST),
+        cost_estimate=about(12),
     )(seen, own, dq, dk, dv, w_qkv)
 
 
@@ -906,11 +1011,16 @@
     return lax.ppermute(value, axis, [(i, (i + step) % size) for i in range(size)])
 
 
-def reduce_axis(terms, axis, size):
-    total = terms[0].astype(F32)
+def reduce_axis(terms, axis, size, dim=0):
+    total = lax.index_in_dim(terms, 0, dim, keepdims=False).astype(F32)
     for step in range(1, size):
-        total = total + moved(terms[step], axis, size, step).astype(F32)
+        term = lax.index_in_dim(terms, step, dim, keepdims=False)
+        total = total + moved(term, axis, size, step).astype(F32)
     return total
+
+
+def after(value, *others):
+    return lax.optimization_barrier((value, others))[0]
 
 
 def gather_axis(value, axis, size):
@@ -921,12 +1031,16 @@
     return lax.dynamic_slice_in_dim(jnp.concatenate([value, value], axis), step, size, axis)
 
 
+def early_slots(slots_dev):
+    return slots_dev * 6 // 14
+
+
 def slot_chunks(slots_dev):
-    early = slots_dev * 3 // 14
-    late = slots_dev - 2 * early
+    early = early_slots(slots_dev)
+    late = slots_dev - early
     chunks = []
     first = 0
-    for index, count in enumerate((early, early, late - late // 2, late // 2)):
+    for index, count in enumerate((early - early // 2, early // 2, late - late // 2, late // 2)):
         chunks.append((first, count, ("fx", "by", "fz") if index % 2 == 0 else ("by", "fx", "fz")))
         first = first + count
     return chunks
@@ -957,18 +1071,86 @@
         code = jnp.where(inside, (2 * index + place["core"]) * CODE_BASE + at, code)
     owned = block_owner[:, None] == slots[None, :]
     table = jnp.sum(jnp.where(owned, code[:, None], 0), 0)
-    return table, ranks, jnp.max(late_count)
+    early = early_slots(slots_dev)
+    gathered = jnp.where(rank < early, slots // slots_dev * early + rank, code - 3 * CODE_BASE)
+    weight_table = jnp.sum(jnp.where(owned, gathered[:, None], 0), 0)
+    return table, weight_table, ranks, jnp.max(late_count)
+
+
+def reduce_core(kept, sent, count, axes, sizes):
+    size_of = dict(zip(ALL_AXES, sizes))
+    total = (kept.astype(F32) + moved(sent, "core", 2, 1).astype(F32)).astype(BF)
+    return total.reshape([size_of[name] for name in axes] + [count, BLOCK_SIDE, BLOCK_SIDE])
+
+
+def reduce_stage(total, axes, stage, sizes):
+    name = axes[stage]
+    total = reduce_axis(total, name, sizes[ALL_AXES.index(name)])
+    return total if stage == len(axes) - 1 else total.astype(BF)
+
+
+def reduce_rest(total, axes, sizes):
+    for stage in range(len(axes)):
+        total = reduce_stage(total, axes, stage, sizes)
+    return total
 
 
 def reduce_chunk(kept, sent, count, axes, sizes):
-    size_of = dict(zip(ALL_AXES, sizes))
-    total = kept.astype(F32) + moved(sent, "core", 2, 1).astype(F32)
-    total = total.astype(BF).reshape([size_of[name] for name in axes] + [count, BLOCK_SIDE, BLOCK_SIDE])
-    for name in axes:
-        total = reduce_axis(total, name, size_of[name])
-        if name != axes[-1]:
-            total = total.astype(BF)
-    return total
+    return reduce_rest(reduce_core(kept, sent, count, axes, sizes), axes, sizes)
+
+
+def gather_stage(shard, axes, stage, sizes):
+    name = axes[len(axes) - 1 - stage]
+    return gather_axis(shard, name, sizes[ALL_AXES.index(name)])
+
+
+def gather_core(shard):
+    shard = shard.reshape(-1, BLOCK_SIDE, BLOCK_SIDE)
+    return [shard, moved(shard, "core", 2, 1)]
+
+
+def gather_chunk(shard, axes, sizes):
+    for stage in range(len(axes)):
+        shard = gather_stage(shard, axes, stage, sizes)
+    return gather_core(shard)
+
+
+def sorted_shards(device_index, block_owner, master):
+    slots_dev = master.shape[0]
+    chunks = [(0, early_slots(slots_dev), ())] + slot_chunks(slots_dev)[2:]
+
+    def kernel(where, owner, blocks, *outs):
+        base = where[0] * slots_dev
+        late_count = jnp.int32(0)
+        for slot in range(slots_dev):
+            late_count = late_count + (owner[base + slot] < QKV_BLOCKS).astype(jnp.int32)
+        early_at, late_at = jnp.int32(0), slots_dev - late_count
+        for slot in range(slots_dev):
+            late = owner[base + slot] < QKV_BLOCKS
+            rank = jnp.where(late, late_at, early_at)
+            late_at = late_at + late.astype(jnp.int32)
+            early_at = early_at + 1 - late.astype(jnp.int32)
+            for index, (first, count, axes) in enumerate(chunks):
+                if count == 0:
+                    continue
+
+                @pl.when((rank >= first) & (rank < first + count))
+                def _(index=index, first=first):
+                    outs[index][rank - first] = blocks[slot].astype(BF)
+
+    return pl.pallas_call(
+        kernel,
+        grid_spec=pltpu.PrefetchScalarGridSpec(
+            num_scalar_prefetch=2,
+            grid=(1,),
+            in_specs=[in_vmem()],
+            out_specs=[in_vmem()] * len(chunks),
+        ),
+        out_shape=[
+            jax.ShapeDtypeStruct((max(count, 1), BLOCK_SIDE, BLOCK_SIDE), BF) for first, count, axes in chunks
+        ],
+        cost_estimate=about(3),
+    )(device_index.reshape(1), block_owner, master)
 
 
 def spread_early(targets, matrix, buffer_shapes):
@@ -980,7 +1162,7 @@
         def one_block(block, sent):
             code = targets[block]
             cols = 3 * D // BLOCK_SIDE
-            early = lax.div(code, CODE_BASE) < count
+            early = lax.div(code, CODE_BASE) < 4
 
             @pl.when(early & (block < QKV_BLOCKS))
             def _():
@@ -1058,15 +1240,37 @@
     with_previous = near[0] == near[1]
     with_next = near[2] == near[1]
 
+    device_index = ((coords[0] * nx + coords[1]) * ny + coords[2]) * nc + coords[3]
+    early = early_slots(slots_dev)
+    chunks = slot_chunks(slots_dev)
+    shards = sorted_shards(device_index, block_owner, master)
+    orders = [axes for first, count, axes in chunks]
+    late_shards = [gather_stage(shards[1 + i], orders[2 + i], 0, sizes) for i in range(2)]
+
     own_frames = pad_frames(tokens[0])
     own_frames = jnp.where(swap, own_frames[::-1], own_frames)
     long_frame, short_frame = own_frames[0], own_frames[1]
     frame_perm = [(i, (i + 1) % frame_count) for i in range(frame_count)]
     back_perm = [(j, i) for i, j in frame_perm]
+    def gather_early(shard):
+        return lax.all_gather(shard, ALL_AXES, axis=0, tiled=True)
+
+    weights = [gather_early(shards[0])] if early else []
+    long_pair = gather_axis(long_frame, "fx", nx)
+    long_pair, late_shards = lax.optimization_barrier((long_pair, late_shards))
+    late_shards = [gather_stage(part, orders[2 + i], 1, sizes) for i, part in enumerate(late_shards)]
+    long_frames = [long_pair] + [moved(long_pair, "fz", nz, -step) for step in range(1, nz)]
+    late_shards, long_frames[1] = lax.optimization_barrier((late_shards, long_frames[1]))
+    late_shards = [gather_stage(part, orders[2 + i], 2, sizes) for i, part in enumerate(late_shards)]
     from_previous = lax.ppermute(short_frame, FRAME_AXES, frame_perm)
     from_next = lax.ppermute(short_frame, FRAME_AXES, back_perm)
+    late_shards, long_frames, from_previous, from_next = lax.optimization_barrier(
+        (late_shards, long_frames, from_previous, from_next)
+    )
+    weights = weights + gather_core(late_shards[0]) + gather_core(late_shards[1])
+    long_frames = jnp.stack(long_frames)
     partner = jnp.where(with_next, from_next, from_previous)
-    long_frames = gather_axis(gather_axis(long_frame, "fz", nz), "fx", nx)
+
     frames_seen = frame_count + 2
     seen = jnp.concatenate(
         [long_frames.reshape(frame_count, PAD_ROWS, D), short_frame[None], partner[None]]
@@ -1078,12 +1282,9 @@
     )
     key_bias = jnp.where(hidden_key, MASK_FLOOR, 0.0).astype(F32)
 
-    slot_ids = jnp.arange(block_owner.shape[0], dtype=jnp.int32)
-    weight_codes = jnp.sum(jnp.where(block_owner[:, None] == slot_ids[None, :], slot_ids[:, None], 0), 0)
-    targets, ranks, late_most = send_table(block_owner, sizes, coords, slots_dev)
-    device_index = ((coords[0] * nx + coords[1]) * ny + coords[2]) * nc + coords[3]
+    targets, weight_codes, ranks, late_most = send_table(block_owner, sizes, coords, slots_dev)
     own_ranks = lax.dynamic_index_in_dim(ranks, device_index, 0, keepdims=False)
-    chunks = slot_chunks(slots_dev)
+    late_fits = late_most <= slots_dev - early
 
     split = unpack(small_params)
     rows14 = small_params[: 14 * D].reshape(14, D)
@@ -1095,49 +1296,62 @@
     arriving = cotangent[0].reshape(2, NT, D)
     arriving = jnp.where(swap, arriving[::-1], arriving).reshape(2 * NT, D)
 
-    gathered = lax.all_gather(master.astype(BF), ALL_AXES, axis=0, tiled=True)
+    first_buffer = 0 if early else 1
     stat_parts = stat_products(stat_left, stat_right, basis_left, basis_right)
-
-    query, key_value, low, own_low, w_qkv = project(weight_codes, [gathered], seen, rows14)
-    attended = attend(query, key_value, key_bias)
+    weights, stat_parts = lax.optimization_barrier((weights, stat_parts))
+    query, key_value, low, own_low, w_qkv = project(weight_codes, weights, first_buffer, seen, rows14)
+    attended, logs = attend(query, key_value, key_bias)
     buffer_shapes = []
     for first, count, axes in chunks:
         shape = jax.ShapeDtypeStruct((device_count // nc * max(count, 1), BLOCK_SIDE, BLOCK_SIDE), BF)
         buffer_shapes = buffer_shapes + [shape, shape]
     (learned, grad_mixed, grad_att, vectors, grad_up_bias, grad_conv, grad_tail, grad_tail_bias), buffers = middle(
-        weight_codes, targets, [gathered], buffer_shapes, attended, own, arriving, rows14, conv_t,
+        weight_codes, targets, weights, first_buffer, buffer_shapes, attended, own, arriving, rows14, conv_t,
         taps_forward, taps_backward, tail_bias,
     )
     learned = learned.reshape(2, NT, D)
     learned = jnp.where(swap, learned[::-1], learned).reshape(2 * NT, D)
 
-    reduced = []
-    for index in range(2):
-        first, count, axes = chunks[index]
-        if count:
-            reduced.append(reduce_chunk(buffers[2 * index], buffers[2 * index + 1], count, axes, sizes))
-
-    grad_query, grad_key, grad_value = attend_back(query, key_value, key_bias, grad_att)
+    used = [index for index in range(2) if chunks[index][1]]
+    halfway = [
+        reduce_core(buffers[2 * i], buffers[2 * i + 1], chunks[i][1], orders[i], sizes) for i in used
+    ]
+    grad_query, grad_key, grad_value = attend_back(query, key_value, key_bias, attended, logs, grad_att)
+    grad_query, halfway = lax.optimization_barrier((grad_query, halfway))
+    halfway = [reduce_stage(part, orders[i], 0, sizes) for i, part in zip(used, halfway)]
     late_buffers, grad_w_qkv = qkv_grads(
         targets, low, own_low, grad_query, grad_key, grad_value, list(buffers[4:]), 4
     )
+    late_buffers, halfway = lax.optimization_barrier((late_buffers, halfway))
+    halfway = [reduce_stage(part, orders[i], 1, sizes) for i, part in zip(used, halfway)]
+    late_parts = []
+    for index in range(2):
+        kept, sent = late_buffers[2 * index : 2 * index + 2]
+        late_parts.append(reduce_core(kept, sent, chunks[2 + index][1], orders[2 + index], sizes))
+    grad_query, late_buffers = lax.optimization_barrier((grad_query, late_buffers))
     grad_seen, grad_own, sums = input_grads(seen, own, grad_query, grad_key, grad_value, w_qkv)
-
-    if reduced:
+    late_parts, halfway, grad_seen, sums = lax.optimization_barrier((late_parts, halfway, grad_seen, sums))
+
+    seen_frames = grad_seen.reshape(frames_seen, PAD_ROWS, D)
+    long_terms = seen_frames[:frame_count].reshape(nz, nx, PAD_ROWS, D)
+    late_parts = [reduce_stage(part, orders[2 + i], 0, sizes) for i, part in enumerate(late_parts)]
+    reduced = [reduce_stage(part, orders[i], 2, sizes) for i, part in zip(used, halfway)]
+    late_parts, reduced, long_terms = lax.optimization_barrier((late_parts, reduced, long_terms))
+    late_parts = [reduce_stage(part, orders[2 + i], 1, sizes) for i, part in enumerate(late_parts)]
+    late_parts, long_terms = lax.optimization_barrier((late_parts, long_terms))
+    late_parts = [reduce_stage(part, orders[2 + i], 2, sizes) for i, part in enumerate(late_parts)]
+    long_terms = reduce_axis(long_terms, "fx", nx, 1).astype(BF)
+    late_parts, long_terms = lax.optimization_barrier((late_parts, long_terms))
+    if used:
         def whole_early(early):
-            shapes = buffer_shapes[:4]
-            extra = spread_early(targets, grad_w_qkv, shapes)
+            extra = spread_early(targets, grad_w_qkv, buffer_shapes[:4])
             return [
-                part + reduce_chunk(extra[2 * i], extra[2 * i + 1], chunks[i][1], chunks[i][2], sizes)
-                for i, part in enumerate(early)
+                part + reduce_chunk(extra[2 * i], extra[2 * i + 1], chunks[i][1], orders[i], sizes)
+                for i, part in zip(used, early)
             ]
 
-        late_room = chunks[2][1] + chunks[3][1]
-        reduced = lax.cond(late_most <= late_room, lambda early: early, whole_early, reduced)
-    for index in (2, 3):
-        first, count, axes = chunks[index]
-        reduced.append(reduce_chunk(late_buffers[2 * index - 4], late_buffers[2 * index - 3], count, axes, sizes))
-    owned_grads = jnp.concatenate(reduced)
+        reduced = lax.cond(late_fits, lambda early: early, whole_early, reduced)
+    owned_grads = jnp.concatenate(list(reduced) + late_parts)
 
     small_local = jnp.concatenate(
         [
@@ -1171,20 +1385,18 @@
     grad_norm = jnp.sqrt(jnp.sum(carried[:, share]))
     factor = 1.0 / jnp.maximum(grad_norm, CLIP_NORM)
 
+    small_first, small_second, small_new = adam_update(
+        small_grad * factor, small_params, small_moment1, small_moment2
+    )
+
+    long_terms, partner_term, factor = lax.optimization_barrier(
+        (long_terms, seen_frames[frame_count + 1], factor)
+    )
+    long_total = reduce_axis(long_terms, "fz", nz)
     soap_out = soap(
         own_ranks, owned_grads, factor, stat_parts, master, moment1, moment2, stat_left, stat_right,
         basis_left, basis_right,
     )
-    small_first, small_second, small_new = adam_update(
-        small_grad * factor, small_params, small_moment1, small_moment2
-    )
-
-    grad_seen, _ = lax.optimization_barrier((grad_seen, owned_grads))
-    seen_frames = grad_seen.reshape(frames_seen, PAD_ROWS, D)
-    long_terms = seen_frames[:frame_count].reshape(nx, nz, PAD_ROWS, D)
-    long_terms = reduce_axis(long_terms, "fx", nx).astype(BF)
-    long_total = reduce_axis(long_terms, "fz", nz)
-    partner_term = seen_frames[frame_count + 1]
     nothing = jnp.zeros_like(partner_term)
     to_previous = jnp.where(with_previous, partner_term, nothing)
     to_next = jnp.where(with_next, partner_term, nothing)

time: 568 us -> 503 us (0.89)
  waiting for transfers between devices: 192 us -> 132 us
  Pallas kernels: 210 us -> 174 us
  starting transfers between devices: 66.6 us -> 81 us
  other arithmetic: 39.7 us -> 52.7 us
    all_gather x1, waiting for transfers between devices: 49.5 us -> 0.01 us  [gather_early(): return lax.all_gather(shard, ALL_AXES, axis=0, tiled=True)]
    ppermute x44 -> x56, waiting for transfers between devices: 142 us -> 110 us  [moved(): lax.ppermute(value, axis, [(i, (i + step) % size) for i in range(size)])]
    ppermute x1, waiting for transfers between devices: 0.01 us -> 21.7 us  [on_device(): from_previous = lax.ppermute(short_frame, FRAME_AXES, frame_perm)]
    ppermute x44 -> x56, starting transfers between devices: 61.9 us -> 77.4 us  [moved(): lax.ppermute(value, axis, [(i, (i + step) % size) for i in range(size)])]
    pallas_call x1, Pallas kernels: 36.2 us -> 20.8 us  [attend_back(): pl.pallas_call(kernel, grid=(PAIRS,), in_specs=[pair_spec(OWN_ROWS), pair...]
    pallas_call x1, Pallas kernels: 43 us -> 28.3 us  [finish(): pl.pallas_call(finish_kernel, in_specs=[pl.BlockSpec(memory_space=pltpu.S...]
    another operation x5 -> x10, other arithmetic: 1.6 us -> 7.48 us  [gather_axis(): jnp.stack([value] + [moved(value, axis, size, -step) for step in range(1,...]
    convert_element_type x14 -> x13, other arithmetic: 13.9 us -> 18.4 us  [the longest x4 9.97 us: reduce_core(): (kept.astype(F32) + moved(sent, 'core', 2, 1).astype(F32)).astype(BF)]
  transfers between devices with their start and end apart: 49 -> 61, of which waited for: 22 -> 24; matrix products, arithmetic and copies ran while one was open for 9% -> 11% of each run, Pallas kernels for 23% -> 18%
where the time goes in v3:
time: 503 us; the launch traced here: 495 us
  Pallas kernels  174 us (35%)
  waiting for transfers between devices  132 us (26%)
  starting transfers between devices  81 us (16%)
  other arithmetic  52.7 us (10%)
  local copies, waits for them, and re-layouts  33.1 us (7%)
  between operations  22 us (4%)
    ppermute x56, waiting for transfers between devices, moved(): lax.ppermute(value, axis, [(i, (i + step) % size) for i in range(size)])  110 us
    ppermute x56, starting transfers between devices, moved(): lax.ppermute(value, axis, [(i, (i + step) % size) for i in range(size)])  77.4 us
    pallas_call x1, Pallas kernels, middle(): pl.pallas_call(kernel, grid_spec=pltpu.PrefetchScalarGridSpec(num_scalar_...  53.1 us
    pallas_call x1, Pallas kernels, finish(): pl.pallas_call(finish_kernel, in_specs=[pl.BlockSpec(memory_space=pltpu.S...  28.3 us
    ppermute x1, waiting for transfers between devices, on_device(): from_previous = lax.ppermute(short_frame, FRAME_AXES, frame_perm)  21.7 us
    pallas_call x1, Pallas kernels, attend_back(): pl.pallas_call(kernel, grid=(PAIRS,), in_specs=[pair_spec(OWN_ROWS), pair...  20.8 us
    pallas_call x1, Pallas kernels, project(): pl.pallas_call(kernel, grid_spec=pltpu.PrefetchScalarGridSpec(num_scalar_...  16 us
    pallas_call x1, Pallas kernels, qkv_grads(): pl.pallas_call(kernel, grid_spec=pltpu.PrefetchScalarGridSpec(num_scalar_...  15.6 us
  transfers between devices with their start and end apart: 61, of which 24 were waited for; matrix products, arithmetic and copies ran while one was open for 11% of the time, Pallas kernels for 18%

profile of v3, /device:TPU:15, one launch (start us, length us, event | category | flops | bytes accessed | tf_op | source)
XLA Modules:
  0.0 494.9 jit_solution(16326501648440023272)
XLA Ops:
  7.2 3.1 shard_map.255
  22.4 3.1 collective-permute-start.17
  26.8 2.6 collective-permute-done.18
  29.4 8.5 %collective-permute-done.17 = bf16[4,128,128]{2,1,0:T(8,128)(2,1)S(1)} collective-permute-done((bf16[4,128,128]{2,1,0:T(8,128)(2,1)S(1)}, bf16[4,128,128]{2,1,0:T(8,128)(2,1)S(1)}, u32[]{:S(2)}, u32[]{:S(2)}) %collective-permute-start.17) | collective-permute-done | bytes 131104 | tf_op jit(solution)/shard_map/ppermute | solution.py:1011
  37.9 2.8 collective-permute-done.16
  42.3 15.8 %collective-permute-done.19 = bf16[4,4,128,128]{3,2,1,0:T(8,128)(2,1)S(1)} collective-permute-done((bf16[4,4,128,128]{3,2,1,0:T(8,128)(2,1)S(1)}, bf16[4,4,128,128]{3,2,1,0:T(8,128)(2,1)S(1)}, u32[]{:S(2)}, u32[]{:S(2)}) %collective-permute-start.19) | collective-permute-done | bytes 524320 | tf_op jit(solution)/shard_map/ppermute | solution.py:1011
  58.3 2.9 collective-permute-done.20
  62.2 4.4 collective-permute-done.21
  71.6 2.6 collective-permute-start.24
  80.1 28.1 %collective-permute-done.22 = bf16[2,4,4,128,128]{4,3,2,1,0:T(8,128)(2,1)S(1)} collective-permute-done((bf16[2,4,4,128,128]{4,3,2,1,0:T(8,128)(2,1)S(1)}, bf16[2,4,4,128,128]{4,3,2,1,0:T(8,128)(2,1)S(1)}, u32[]{:S(2)}, u32[]{:S(2)}) %collective-permute-start.22) | collective-permute-done | bytes 1048608 | tf_op jit(solution)/shard_map/ppermute | solution.py:1011
  110.7 3.8 pad_maximum_fusion.3
  114.5 21.7 %collective-permute-done.26 = bf16[208,768]{1,0:T(8,128)(2,1)S(1)} collective-permute-done((bf16[208,768]{1,0:T(8,128)(2,1)}, bf16[208,768]{1,0:T(8,128)(2,1)S(1)}, u32[]{:S(2)}, u32[]{:S(2)}) %collective-permute-start.26) | collective-permute-done | bytes 319520 | tf_op jit(solution)/shard_map/ppermute | solution.py:1265
  141.3 3.7 shard_map.256
  147.8 1.8 pad_maximum_fusion.1
  149.7 2.1 pad_maximum_fusion
  151.8 16.0 %shard_map.257 = (bf16[416,768]{1,0:T(8,128)(2,1)}, bf16[2080,1536]{1,0:T(8,128)(2,1)}, bf16[2080,768]{1,0:T(8,128)(2,1)}, bf16[416,768]{1,0:T(8,128)(2,1)}, bf16[768,2304]{1,0:T(8,128)(2,1)}) custom-call(s32[448]{0:T(512)} %get-tuple-element.252.codes.refs_0_, bf16[192,128,128]{2,1,0:T(8,128)(2,1)} %all-gather.2.cloned.1.call-done.refs_0_.refs_2_, ...), custom_call_target="tpu_custom_call" | custom-call | bytes 45000000 | tf_op jit(solution)/shard_map/pallas_call | solution.py:533
  167.8 14.4 %shard_map.258 = (bf16[416,768]{1,0:T(8,128)(2,1)}, f32[416,768]{1,0:T(8,128)}) custom-call(bf16[416,768]{1,0:T(8,128)(2,1)} %get-tuple-element.163.refs_0_, bf16[2080,1536]{1,0:T(8,128)(2,1)} %get-tuple-element.164.refs_1_.refs_2_, bf16[2080,1536]{1,0:T(8,128)(2,1)} %get-tuple-element.164.refs_1_.refs_2_, f32[1,2080]{1,0:T(1,128)} %or_select_fusion.refs_3_), custom_call_target="tpu_custom_call" | custom-call | bytes 36000000 | tf_op jit(solution)/shard_map/pallas_call | solution.py:620
  182.8 53.1 %shard_map.259 = (f32[16,768]{1,0:T(8,128)}, f32[416,768]{1,0:T(8,128)}, bf16[416,768]{1,0:T(8,128)(2,1)}, f32[8,768]{1,0:T(8,128)}, f32[4,768]{1,0:T(4,128)}, /...) custom-call(s32[448]{0:T(512)} %get-tuple-element.252.codes.refs_0_,, ...), custom_call_target="tpu_custom_call" | custom-call | bytes 120000000 | tf_op jit(solution)/shard_map/pallas_call | solution.py:872
  236.6 20.8 %shard_map.260 = (bf16[416,768]{1,0:T(8,128)(2,1)}, bf16[2080,768]{1,0:T(8,128)(2,1)}, bf16[2080,768]{1,0:T(8,128)(2,1)}) custom-call(bf16[416,768]{1,0:T(8,128)(2,1)} %get-tuple-element.163.refs_0_, bf16[2080,1536]{1,0:T(8,128)(2,1)} %get-tuple-element.164.refs_1_.refs_2_, bf16[2080,1536]{1,0:T(8,128)(2,1)} %get-tuple-element.164.refs_1_.refs_2_, ...), custom_call_target="tpu_custom_call" | custom-call | bytes 72000000 | tf_op jit(solution)/shard_map/pallas_call | solution.py:644
  258.5 2.3 add_convert_fusion.5
  263.2 15.6 %shard_map.261 = (bf16[64,128,128]{2,1,0:T(8,128)(2,1)}, bf16[64,128,128]{2,1,0:T(8,128)(2,1)}, bf16[64,128,128]{2,1,0:T(8,128)(2,1)}, bf16[64,128,128]{2,1,0:T(8,128)(2,1)}, bf16[768,2304]{1,0:T(8,128)(2,1)}) custom-call(s32[448]{0:T(512)S(1)} %get-tuple-element.251.refs_1_.targets, ...), custom_call_target="tpu_custom_call", output_to_operand_aliasing={{0}: (6, {}), {1}: (7, {}), {2}: (8, {}), {3}: (9, {})} | custom-call | bytes 42000000 | tf_op jit(solution)/shard_map/pallas_call | solution.py:948
  278.9 1.7 collective-permute-done.33
  287.7 12.5 %shard_map.262 = (bf16[2080,768]{1,0:T(8,128)(2,1)}, f32[416,768]{1,0:T(8,128)}, f32[8,768]{1,0:T(8,128)}) custom-call(bf16[2080,768]{1,0:T(8,128)(2,1)} %bitcast.252, bf16[416,768]{1,0:T(8,128)(2,1)} %bitcast.249, bf16[416,768]{1,0:T(8,128)(2,1)} %get-tuple-element.196.dq, bf16[2080,768]{1,0:T(8,128)(2,1)} %get-tuple-element.178.dk, ...), custom_call_target="tpu_custom_call" | custom-call | bytes 36000000 | tf_op jit(solution)/shard_map/pallas_call | solution.py:995
  302.7 2.6 add_convert_fusion.3
  305.3 4.5 add_convert_fusion.2
  309.9 6.6 %concatenate.41 = f32[67808]{0:T(1024)} concatenate(f32[1536]{0:T(1024)S(1)} %reshape.382, f32[3072]{0:T(1024)S(1)} %reshape.383, f32[1536]{0:T(1024)S(1)} %reshape.384, f32[768]{0:T(1024)S(1)} %get-tuple-element.246, f32[3072]{0:T(1024)S(1)} %reshape.385, f32[768]{0:T(1024)S(1)} %get-tuple-element.245, f32[55296]{0:T(1024)S(1)} %reshape.386, f32[1728]{0:T(1024)S(1)} %reshape.387, ...), dimensions={0} | concatenate | bytes 542464 | tf_op jit(solution)/shard_map/concatenate | solution.py:1356
  320.5 2.3 collective-permute-start.55
  322.8 3.2 collective-permute-start.56
  329.6 1.9 collective-permute-start.41
  331.5 2.4 collective-permute-start.43
  333.9 1.7 collective-permute-start.44
  335.7 3.5 collective-permute-done.42
  346.7 16.0 %collective-permute-done.58 = f32[2,2,2176]{2,1,0:T(2,128)S(1)} collective-permute-done((f32[2,2,2176]{2,1,0:T(2,128)S(1)}, f32[2,2,2176]{2,1,0:T(2,128)S(1)}, u32[]{:S(2)}, u32[]{:S(2)}) %collective-permute-start.58) | collective-permute-done | bytes 34848 | tf_op jit(solution)/shard_map/ppermute | solution.py:1011
  371.4 5.2 %collective-permute-start.60 = (f32[2176]{0:T(1024)S(1)}, f32[2176]{0:T(1024)S(1)}, u32[]{:S(2)}, u32[]{:S(2)}) collective-permute-start(f32[2176]{0:T(1024)S(1)} %get-tuple-element.247), channel_id=1, source_target_pairs={{0,1},{1,0},{2,3},{3,2},{4,5},{5,4},{6,7},{7,6},{8,9},{9,8},{10,11... | collective-permute-start | bytes 26120 | tf_op jit(solution)/shard_map/ppermute | solution.py:1011
  380.2 3.1 collective-permute-start.48
  383.3 6.3 %collective-permute-start.50 = (bf16[4,128,128]{2,1,0:T(8,128)(2,1)S(1)}, bf16[4,128,128]{2,1,0:T(8,128)(2,1)S(1)}, u32[]{:S(2)}, u32[]{:S(2)}) collective-permute-start(bf16[4,128,128]{2,1,0:T(8,128)(2,1)S(1)} %get-tuple-element.284), channel_id=1, source_target_pairs={{0,24},{8,0},{16,8},{24,16},{1,25},{9,1},{17,9},{25,17},{2,26},{10... | collective-permute-start | bytes 393224 | tf_op jit(solution)/shard_map/ppermute | solution.py:1011
  389.6 2.8 collective-permute-start.49
  395.5 2.2 collective-permute-start.52
  397.7 7.4 %collective-permute-done.51 = bf16[4,128,128]{2,1,0:T(8,128)(2,1)S(1)} collective-permute-done((bf16[4,128,128]{2,1,0:T(8,128)(2,1)S(1)}, bf16[4,128,128]{2,1,0:T(8,128)(2,1)S(1)}, u32[]{:S(2)}, u32[]{:S(2)}) %collective-permute-start.51) | collective-permute-done | bytes 131104 | tf_op jit(solution)/shard_map/ppermute | solution.py:1011
  405.1 3.7 collective-permute-done.53
  408.7 2.0 collective-permute-done.52
  414.4 3.3 collective-permute-start.61
  424.6 7.1 %shard_map.263 = (f32[14,128,128]{2,1,0:T(8,128)}, f32[14,128,128]{2,1,0:T(8,128)}, f32[14,128,128]{2,1,0:T(8,128)}, f32[14,128,128]{2,1,0:T(8,128)}, f32[14,128,128]{2,1,0:T(8,128)}) custom-call(s32[14]{0:T(128)} %fusion.71.ranks, f32[14,128,128]{2,1,0:T(8,128)} %copy-done, f32[14,128,128]{2,1,0:T(8,128)} %copy-done, f32[14,128,128]{2,1,0:T(8,128)} %copy-done, ...), custom_call_target="tpu_custom_call" | custom-call | bytes 24000000 | tf_op jit(solution)/shard_map/pallas_call | solution.py:224
  431.8 5.7 %collective-permute-start.65 = (f32[2,2,2,2304]{3,2,1,0:T(2,128)S(1)}, f32[2,2,2,2304]{3,2,1,0:T(2,128)S(1)}, u32[]{:S(2)}, u32[]{:S(2)}) collective-permute-start(f32[2,2,2,2304]{3,2,1,0:T(2,128)S(1)} %pad_maximum_fusion.9), channel_id=1, source_target_pairs={{0,16},{8,24},{16,0},{24,8},{1,17},{9,25},{17,1},{25,9},{2,18},{10... | collective-permute-start | bytes 221192 | tf_op jit(solution)/shard_map/ppermute | solution.py:1011
  439.0 2.9 collective-permute-done.64
  446.4 2.1 collective-permute-start.71
  450.3 1.8 collective-permute-start.68
  453.1 28.3 %shard_map.264 = (f32[14,128,128]{2,1,0:T(8,128)}, f32[14,128,128]{2,1,0:T(8,128)}, f32[14,128,128]{2,1,0:T(8,128)}, f32[14,128,128]{2,1,0:T(8,128)}, f32[14,128...) custom-call(f32[1]{0:T(128)} %bitcast.132.factor, f32[14,128,128]{2,1,0:T(8,128)} %get-tuple-element.229.refs_0_, ...), custom_call_target="tpu_custom_call" | custom-call | bytes 90000000 | tf_op jit(solution)/shard_map/pallas_call | solution.py:369
  (364 shorter events, 101.1 us)
Async XLA Ops:
  7.2 144.6 %all-gather.2.cloned.1.call-start = ((), (), s32[]{:S(2)}) async-start(), calls=%async_computation | async-start | bytes 6488064 | tf_op jit(solution)/shard_map/all_gather | solution.py:1256
  10.3 12.1 %collective-permute-start.15 = (bf16[4,128,128]{2,1,0:T(8,128)(2,1)}, bf16[4,128,128]{2,1,0:T(8,128)(2,1)S(1)}, u32[]{:S(2)}, u32[]{:S(2)}) collective-permute-start(bf16[4,128,128]{2,1,0:T(8,128)(2,1)} %get-tuple-element.140), channel_id=1, source_target_pairs={{0,8},{8,16},{16,24},{24,0},{1,9},{9,17},{17,25},{25,1},{2,10},{10... | collective-permute-start | bytes 393224 | tf_op jit(solution)/shard_map/ppermute | solution.py:1011
  11.7 13.8 %collective-permute-start.14 = (bf16[4,128,128]{2,1,0:T(8,128)(2,1)}, bf16[4,128,128]{2,1,0:T(8,128)(2,1)S(1)}, u32[]{:S(2)}, u32[]{:S(2)}) collective-permute-start(bf16[4,128,128]{2,1,0:T(8,128)(2,1)} %get-tuple-element.140), channel_id=1, source_target_pairs={{0,16},{8,24},{16,0},{24,8},{1,17},{9,25},{17,1},{25,9},{2,18},{10... | collective-permute-start | bytes 393224 | tf_op jit(solution)/shard_map/ppermute | solution.py:1011
  12.8 14.0 %collective-permute-start.13 = (bf16[4,128,128]{2,1,0:T(8,128)(2,1)}, bf16[4,128,128]{2,1,0:T(8,128)(2,1)S(1)}, u32[]{:S(2)}, u32[]{:S(2)}) collective-permute-start(bf16[4,128,128]{2,1,0:T(8,128)(2,1)} %get-tuple-element.140), channel_id=1, source_target_pairs={{0,24},{8,0},{16,8},{24,16},{1,25},{9,1},{17,9},{25,17},{2,26},{10... | collective-permute-start | bytes 393224 | tf_op jit(solution)/shard_map/ppermute | solution.py:1011
  22.1 18.7 %collective-permute-start.12 = (bf16[208,768]{1,0:T(8,128)(2,1)S(1)}, bf16[208,768]{1,0:T(8,128)(2,1)S(1)}, u32[]{:S(2)}, u32[]{:S(2)}) collective-permute-start(bf16[208,768]{1,0:T(8,128)(2,1)S(1)} %get-tuple-element.278), channel_id=1, source_target_pairs={{0,4},{4,0},{1,5},{5,1},{2,6},{6,2},{3,7},{7,3},{8,12},{12,8},{9,1... | collective-permute-start | bytes 958472 | tf_op jit(solution)/shard_map/ppermute | solution.py:1011
  22.4 15.5 %collective-permute-start.17 = (bf16[4,128,128]{2,1,0:T(8,128)(2,1)S(1)}, bf16[4,128,128]{2,1,0:T(8,128)(2,1)S(1)}, u32[]{:S(2)}, u32[]{:S(2)}) collective-permute-start(bf16[4,128,128]{2,1,0:T(8,128)(2,1)S(1)} %copy-done.38), channel_id=1, source_target_pairs={{0,16},{8,24},{16,0},{24,8},{1,17},{9,25},{17,1},{25,9},{2,18},{10... | collective-permute-start | bytes 393224 | tf_op jit(solution)/shard_map/ppermute | solution.py:1011
  25.5 15.2 %collective-permute-start.16 = (bf16[4,128,128]{2,1,0:T(8,128)(2,1)S(1)}, bf16[4,128,128]{2,1,0:T(8,128)(2,1)S(1)}, u32[]{:S(2)}, u32[]{:S(2)}) collective-permute-start(bf16[4,128,128]{2,1,0:T(8,128)(2,1)S(1)} %copy-done.38), channel_id=1, source_target_pairs={{0,24},{8,0},{16,8},{24,16},{1,25},{9,1},{17,9},{25,17},{2,26},{10... | collective-permute-start | bytes 393224 | tf_op jit(solution)/shard_map/ppermute | solution.py:1011
  41.7 16.4 %collective-permute-start.19 = (bf16[4,4,128,128]{3,2,1,0:T(8,128)(2,1)S(1)}, bf16[4,4,128,128]{3,2,1,0:T(8,128)(2,1)S(1)}, u32[]{:S(2)}, u32[]{:S(2)}) collective-permute-start(bf16[4,4,128,128]{3,2,1,0:T(8,128)(2,1)S(1)} %pad_maximum_fusion.7), channel_id=1, source_target_pairs={{0,2},{2,0},{1,3},{3,1},{4,6},{6,4},{5,7},{7,5},{8,10},{10,8},{9,1... | collective-permute-start | bytes 1572872 | tf_op jit(solution)/shard_map/ppermute | solution.py:1011
  41.9 19.2 %collective-permute-start.20 = (bf16[4,4,128,128]{3,2,1,0:T(8,128)(2,1)S(1)}, bf16[4,4,128,128]{3,2,1,0:T(8,128)(2,1)S(1)}, u32[]{:S(2)}, u32[]{:S(2)}) collective-permute-start(bf16[4,4,128,128]{3,2,1,0:T(8,128)(2,1)S(1)} %pad_maximum_fusion.8), channel_id=1, source_target_pairs={{0,4},{4,0},{1,5},{5,1},{2,6},{6,2},{3,7},{7,3},{8,12},{12,8},{9,1... | collective-permute-start | bytes 1572872 | tf_op jit(solution)/shard_map/ppermute | solution.py:1011
  42.3 24.3 %collective-permute-start.21 = (bf16[2,208,768]{2,1,0:T(8,128)(2,1)}, bf16[2,208,768]{2,1,0:T(8,128)(2,1)S(1)}, u32[]{:S(2)}, u32[]{:S(2)}) collective-permute-start(bf16[2,208,768]{2,1,0:T(8,128)(2,1)} %pad_maximum_fusion.6), channel_id=1, source_target_pairs={{0,24},{8,0},{16,8},{24,16},{1,25},{9,1},{17,9},{25,17},{2,26},{10... | collective-permute-start | bytes 1916936 | tf_op jit(solution)/shard_map/ppermute | solution.py:1011
  66.6 41.7 %collective-permute-start.22 = (bf16[2,4,4,128,128]{4,3,2,1,0:T(8,128)(2,1)S(1)}, bf16[2,4,4,128,128]{4,3,2,1,0:T(8,128)(2,1)S(1)}, u32[]{:S(2)}, u32[]{:S(2)}) collective-permute-start(bf16[2,4,4,128,128]{4,3,2,1,0:T(8,128)(2,1)S(1)} %pad_maximum_fusion.4), channel_id=1, source_target_pairs={{0,4},{4,0},{1,5},{5,1},{2,6},{6,2},{3,7},{7,3},{8,12},{12,8},{9,1... | collective-permute-start | bytes 3145736 | tf_op jit(solution)/shard_map/ppermute | solution.py:1011
  67.7 46.8 %collective-permute-start.27 = (bf16[208,768]{1,0:T(8,128)(2,1)}, bf16[208,768]{1,0:T(8,128)(2,1)}, u32[]{:S(2)}, u32[]{:S(2)}) collective-permute-start(bf16[208,768]{1,0:T(8,128)(2,1)} %get-tuple-element.277), channel_id=1, source_target_pairs={{4,0},{8,4},{12,8},{16,12},{20,16},{24,20},{28,24},{0,28},{5,1},{9... | collective-permute-start | bytes 958472 | tf_op jit(solution)/shard_map/ppermute | solution.py:1266
  68.0 42.6 %collective-permute-start.23 = (bf16[2,4,4,128,128]{4,3,2,1,0:T(8,128)(2,1)}, bf16[2,4,4,128,128]{4,3,2,1,0:T(8,128)(2,1)}, u32[]{:S(2)}, u32[]{:S(2)}) collective-permute-start(bf16[2,4,4,128,128]{4,3,2,1,0:T(8,128)(2,1)} %pad_maximum_fusion.5), channel_id=1, source_target_pairs={{0,2},{2,0},{1,3},{3,1},{4,6},{6,4},{5,7},{7,5},{8,10},{10,8},{9,1... | collective-permute-start | bytes 3145736 | tf_op jit(solution)/shard_map/ppermute | solution.py:1011
  71.5 64.7 %collective-permute-start.25 = (bf16[2,208,768]{2,1,0:T(8,128)(2,1)}, bf16[2,208,768]{2,1,0:T(8,128)(2,1)}, u32[]{:S(2)}, u32[]{:S(2)}) collective-permute-start(bf16[2,208,768]{2,1,0:T(8,128)(2,1)} %pad_maximum_fusion.6), channel_id=1, source_target_pairs={{0,8},{8,16},{16,24},{24,0},{1,9},{9,17},{17,25},{25,1},{2,10},{10... | collective-permute-start | bytes 1916936 | tf_op jit(solution)/shard_map/ppermute | solution.py:1011
  71.6 64.7 %collective-permute-start.24 = (bf16[2,208,768]{2,1,0:T(8,128)(2,1)}, bf16[2,208,768]{2,1,0:T(8,128)(2,1)}, u32[]{:S(2)}, u32[]{:S(2)}) collective-permute-start(bf16[2,208,768]{2,1,0:T(8,128)(2,1)} %pad_maximum_fusion.6), channel_id=1, source_target_pairs={{0,16},{8,24},{16,0},{24,8},{1,17},{9,25},{17,1},{25,9},{2,18},{10... | collective-permute-start | bytes 1916936 | tf_op jit(solution)/shard_map/ppermute | solution.py:1011
  108.2 28.0 %collective-permute-start.26 = (bf16[208,768]{1,0:T(8,128)(2,1)}, bf16[208,768]{1,0:T(8,128)(2,1)S(1)}, u32[]{:S(2)}, u32[]{:S(2)}) collective-permute-start(bf16[208,768]{1,0:T(8,128)(2,1)} %get-tuple-element.277), channel_id=1, source_target_pairs={{0,4},{4,8},{8,12},{12,16},{16,20},{20,24},{24,28},{28,0},{1,5},{5... | collective-permute-start | bytes 958472 | tf_op jit(solution)/shard_map/ppermute | solution.py:1265
  136.2 15.5 %collective-permute-start.29 = (bf16[64,128,128]{2,1,0:T(8,128)(2,1)}, bf16[64,128,128]{2,1,0:T(8,128)(2,1)}, u32[]{:S(2)}, u32[]{:S(2)}) collective-permute-start(bf16[64,128,128]{2,1,0:T(8,128)(2,1)} %bitcast.50.refs_3_.refs_5_), channel_id=1, source_target_pairs={{0,1},{1,0},{2,3},{3,2},{4,5},{5,4},{6,7},{7,6},{8,9},{9,8},{10,11... | collective-permute-start | bytes 6291464 | tf_op jit(solution)/shard_map/ppermute | solution.py:1011
  137.6 14.1 %collective-permute-start.28 = (bf16[64,128,128]{2,1,0:T(8,128)(2,1)S(1)}, bf16[64,128,128]{2,1,0:T(8,128)(2,1)}, u32[]{:S(2)}, u32[]{:S(2)}) collective-permute-start(bf16[64,128,128]{2,1,0:T(8,128)(2,1)S(1)} %bitcast.253), channel_id=1, source_target_pairs={{0,1},{1,0},{2,3},{3,2},{4,5},{5,4},{6,7},{7,6},{8,9},{9,8},{10,11... | collective-permute-start | bytes 6291464 | tf_op jit(solution)/shard_map/ppermute | solution.py:1011
  235.9 21.4 %collective-permute-start.30 = (bf16[48,128,128]{2,1,0:T(8,128)(2,1)}, bf16[48,128,128]{2,1,0:T(8,128)(2,1)S(1)}, u32[]{:S(2)}, u32[]{:S(2)}) collective-permute-start(bf16[48,128,128]{2,1,0:T(8,128)(2,1)} %get-tuple-element.174), channel_id=1, source_target_pairs={{0,1},{1,0},{2,3},{3,2},{4,5},{5,4},{6,7},{7,6},{8,9},{9,8},{10,11... | collective-permute-start | bytes 4718600 | tf_op jit(solution)/shard_map/ppermute | solution.py:1011
  236.5 24.3 %collective-permute-start.31 = (bf16[48,128,128]{2,1,0:T(8,128)(2,1)}, bf16[48,128,128]{2,1,0:T(8,128)(2,1)S(1)}, u32[]{:S(2)}, u32[]{:S(2)}) collective-permute-start(bf16[48,128,128]{2,1,0:T(8,128)(2,1)} %get-tuple-element.176), channel_id=1, source_target_pairs={{0,1},{1,0},{2,3},{3,2},{4,5},{5,4},{6,7},{7,6},{8,9},{9,8},{10,11... | collective-permute-start | bytes 4718600 | tf_op jit(solution)/shard_map/ppermute | solution.py:1011
  261.5 19.1 %collective-permute-start.33 = (bf16[2,4,3,128,128]{4,3,2,1,0:T(8,128)(2,1)S(1)}, bf16[2,4,3,128,128]{4,3,2,1,0:T(8,128)(2,1)}, u32[]{:S(2)}, u32[]{:S(2)}) collective-permute-start(bf16[2,4,3,128,128]{4,3,2,1,0:T(8,128)(2,1)S(1)} %slice_bitcast_fusion.16), channel_id=1, source_target_pairs={{0,2},{2,0},{1,3},{3,1},{4,6},{6,4},{5,7},{7,5},{8,10},{10,8},{9,1... | collective-permute-start | bytes 2359304 | tf_op jit(solution)/shard_map/ppermute | solution.py:1011
  263.2 18.8 %collective-permute-start.32 = (bf16[2,4,3,128,128]{4,3,2,1,0:T(8,128)(2,1)S(1)}, bf16[2,4,3,128,128]{4,3,2,1,0:T(8,128)(2,1)S(1)}, u32[]{:S(2)}, u32[]{:S(2)}) collective-permute-start(bf16[2,4,3,128,128]{4,3,2,1,0:T(8,128)(2,1)S(1)} %slice_bitcast_fusion.17), channel_id=1, source_target_pairs={{0,4},{4,0},{1,5},{5,1},{2,6},{6,2},{3,7},{7,3},{8,12},{12,8},{9,1... | collective-permute-start | bytes 2359304 | tf_op jit(solution)/shard_map/ppermute | solution.py:1011
  282.4 20.3 %collective-permute-start.34 = (bf16[64,128,128]{2,1,0:T(8,128)(2,1)}, bf16[64,128,128]{2,1,0:T(8,128)(2,1)}, u32[]{:S(2)}, u32[]{:S(2)}) collective-permute-start(bf16[64,128,128]{2,1,0:T(8,128)(2,1)} %get-tuple-element.191), channel_id=1, source_target_pairs={{0,1},{1,0},{2,3},{3,2},{4,5},{5,4},{6,7},{7,6},{8,9},{9,8},{10,11... | collective-permute-start | bytes 6291464 | tf_op jit(solution)/shard_map/ppermute | solution.py:1011
  283.6 21.7 %collective-permute-start.35 = (bf16[64,128,128]{2,1,0:T(8,128)(2,1)}, bf16[64,128,128]{2,1,0:T(8,128)(2,1)}, u32[]{:S(2)}, u32[]{:S(2)}) collective-permute-start(bf16[64,128,128]{2,1,0:T(8,128)(2,1)} %get-tuple-element.193), channel_id=1, source_target_pairs={{0,1},{1,0},{2,3},{3,2},{4,5},{5,4},{6,7},{7,6},{8,9},{9,8},{10,11... | collective-permute-start | bytes 6291464 | tf_op jit(solution)/shard_map/ppermute | solution.py:1011
  283.7 16.5 %collective-permute-start.37 = (bf16[4,3,128,128]{3,2,1,0:T(8,128)(2,1)S(1)}, bf16[4,3,128,128]{3,2,1,0:T(8,128)(2,1)}, u32[]{:S(2)}, u32[]{:S(2)}) collective-permute-start(bf16[4,3,128,128]{3,2,1,0:T(8,128)(2,1)S(1)} %slice_bitcast_fusion.20), channel_id=1, source_target_pairs={{0,4},{4,0},{1,5},{5,1},{2,6},{6,2},{3,7},{7,3},{8,12},{12,8},{9,1... | collective-permute-start | bytes 1179656 | tf_op jit(solution)/shard_map/ppermute | solution.py:1011
  283.8 17.7 %collective-permute-start.36 = (bf16[4,3,128,128]{3,2,1,0:T(8,128)(2,1)S(1)}, bf16[4,3,128,128]{3,2,1,0:T(8,128)(2,1)}, u32[]{:S(2)}, u32[]{:S(2)}) collective-permute-start(bf16[4,3,128,128]{3,2,1,0:T(8,128)(2,1)S(1)} %slice_bitcast_fusion.21), channel_id=1, source_target_pairs={{0,2},{2,0},{1,3},{3,1},{4,6},{6,4},{5,7},{7,5},{8,10},{10,8},{9,1... | collective-permute-start | bytes 1179656 | tf_op jit(solution)/shard_map/ppermute | solution.py:1011
  320.5 9.1 %collective-permute-start.55 = (f32[2,2,2,2176]{3,2,1,0:T(2,128)S(1)}, f32[2,2,2,2176]{3,2,1,0:T(2,128)S(1)}, u32[]{:S(2)}, u32[]{:S(2)}) collective-permute-start(f32[2,2,2,2176]{3,2,1,0:T(2,128)S(1)} %get-tuple-element.294), channel_id=1, source_target_pairs={{0,8},{8,16},{16,24},{24,0},{1,9},{9,17},{17,25},{25,1},{2,10},{10... | collective-permute-start | bytes 208904 | tf_op jit(solution)/shard_map/ppermute | solution.py:1011
  327.5 11.7 %collective-permute-start.42 = (bf16[3,128,128]{2,1,0:T(8,128)(2,1)S(1)}, bf16[3,128,128]{2,1,0:T(8,128)(2,1)S(1)}, u32[]{:S(2)}, u32[]{:S(2)}) collective-permute-start(bf16[3,128,128]{2,1,0:T(8,128)(2,1)S(1)} %get-tuple-element.290), channel_id=1, source_target_pairs={{0,24},{8,0},{16,8},{24,16},{1,25},{9,1},{17,9},{25,17},{2,26},{10... | collective-permute-start | bytes 294920 | tf_op jit(solution)/shard_map/ppermute | solution.py:1011
  329.6 11.1 %collective-permute-start.41 = (bf16[3,128,128]{2,1,0:T(8,128)(2,1)S(1)}, bf16[3,128,128]{2,1,0:T(8,128)(2,1)S(1)}, u32[]{:S(2)}, u32[]{:S(2)}) collective-permute-start(bf16[3,128,128]{2,1,0:T(8,128)(2,1)S(1)} %get-tuple-element.291), channel_id=1, source_target_pairs={{0,16},{8,24},{16,0},{24,8},{1,17},{9,25},{17,1},{25,9},{2,18},{10... | collective-permute-start | bytes 294920 | tf_op jit(solution)/shard_map/ppermute | solution.py:1011
  331.5 13.1 %collective-permute-start.43 = (bf16[3,128,128]{2,1,0:T(8,128)(2,1)S(1)}, bf16[3,128,128]{2,1,0:T(8,128)(2,1)S(1)}, u32[]{:S(2)}, u32[]{:S(2)}) collective-permute-start(bf16[3,128,128]{2,1,0:T(8,128)(2,1)S(1)} %get-tuple-element.286), channel_id=1, source_target_pairs={{0,8},{8,16},{16,24},{24,0},{1,9},{9,17},{17,25},{25,1},{2,10},{10... | collective-permute-start | bytes 294920 | tf_op jit(solution)/shard_map/ppermute | solution.py:1011
  333.8 12.7 %collective-permute-start.45 = (bf16[3,128,128]{2,1,0:T(8,128)(2,1)S(1)}, bf16[3,128,128]{2,1,0:T(8,128)(2,1)S(1)}, u32[]{:S(2)}, u32[]{:S(2)}) collective-permute-start(bf16[3,128,128]{2,1,0:T(8,128)(2,1)S(1)} %get-tuple-element.287), channel_id=1, source_target_pairs={{0,24},{8,0},{16,8},{24,16},{1,25},{9,1},{17,9},{25,17},{2,26},{10... | collective-permute-start | bytes 294920 | tf_op jit(solution)/shard_map/ppermute | solution.py:1011
  333.9 12.8 %collective-permute-start.44 = (bf16[3,128,128]{2,1,0:T(8,128)(2,1)S(1)}, bf16[3,128,128]{2,1,0:T(8,128)(2,1)S(1)}, u32[]{:S(2)}, u32[]{:S(2)}) collective-permute-start(bf16[3,128,128]{2,1,0:T(8,128)(2,1)S(1)} %get-tuple-element.288), channel_id=1, source_target_pairs={{0,16},{8,24},{16,0},{24,8},{1,17},{9,25},{17,1},{25,9},{2,18},{10... | collective-permute-start | bytes 294920 | tf_op jit(solution)/shard_map/ppermute | solution.py:1011
  339.2 23.6 %collective-permute-start.39 = (bf16[2,4,4,128,128]{4,3,2,1,0:T(8,128)(2,1)S(1)}, bf16[2,4,4,128,128]{4,3,2,1,0:T(8,128)(2,1)S(1)}, u32[]{:S(2)}, u32[]{:S(2)}) collective-permute-start(bf16[2,4,4,128,128]{4,3,2,1,0:T(8,128)(2,1)S(1)} %slice_bitcast_fusion.14), channel_id=1, source_target_pairs={{0,2},{2,0},{1,3},{3,1},{4,6},{6,4},{5,7},{7,5},{8,10},{10,8},{9,1... | collective-permute-start | bytes 3145736 | tf_op jit(solution)/shard_map/ppermute | solution.py:1011
  340.7 23.5 %collective-permute-start.38 = (bf16[2,4,4,128,128]{4,3,2,1,0:T(8,128)(2,1)S(1)}, bf16[2,4,4,128,128]{4,3,2,1,0:T(8,128)(2,1)S(1)}, u32[]{:S(2)}, u32[]{:S(2)}) collective-permute-start(bf16[2,4,4,128,128]{4,3,2,1,0:T(8,128)(2,1)S(1)} %slice_bitcast_fusion.15), channel_id=1, source_target_pairs={{0,4},{4,0},{1,5},{5,1},{2,6},{6,2},{3,7},{7,3},{8,12},{12,8},{9,1... | collective-permute-start | bytes 3145736 | tf_op jit(solution)/shard_map/ppermute | solution.py:1011
  344.6 18.2 %collective-permute-start.58 = (f32[2,2,2176]{2,1,0:T(2,128)S(1)}, f32[2,2,2176]{2,1,0:T(2,128)S(1)}, u32[]{:S(2)}, u32[]{:S(2)}) collective-permute-start(f32[2,2,2176]{2,1,0:T(2,128)S(1)} %slice_bitcast_fusion.41), channel_id=1, source_target_pairs={{0,4},{4,0},{1,5},{5,1},{2,6},{6,2},{3,7},{7,3},{8,12},{12,8},{9,1... | collective-permute-start | bytes 104456 | tf_op jit(solution)/shard_map/ppermute | solution.py:1011
  379.2 31.6 %collective-permute-start.54 = (bf16[4,208,768]{2,1,0:T(8,128)(2,1)S(1)}, bf16[4,208,768]{2,1,0:T(8,128)(2,1)S(1)}, u32[]{:S(2)}, u32[]{:S(2)}) collective-permute-start(bf16[4,208,768]{2,1,0:T(8,128)(2,1)S(1)} %slice_bitcast_fusion.12), channel_id=1, source_target_pairs={{0,4},{4,0},{1,5},{5,1},{2,6},{6,2},{3,7},{7,3},{8,12},{12,8},{9,1... | collective-permute-start | bytes 3833864 | tf_op jit(solution)/shard_map/ppermute | solution.py:1011
  380.2 13.9 %collective-permute-start.48 = (bf16[4,128,128]{2,1,0:T(8,128)(2,1)S(1)}, bf16[4,128,128]{2,1,0:T(8,128)(2,1)S(1)}, u32[]{:S(2)}, u32[]{:S(2)}) collective-permute-start(bf16[4,128,128]{2,1,0:T(8,128)(2,1)S(1)} %get-tuple-element.283), channel_id=1, source_target_pairs={{0,8},{8,16},{16,24},{24,0},{1,9},{9,17},{17,25},{25,1},{2,10},{10... | collective-permute-start | bytes 393224 | tf_op jit(solution)/shard_map/ppermute | solution.py:1011
  383.3 12.1 %collective-permute-start.50 = (bf16[4,128,128]{2,1,0:T(8,128)(2,1)S(1)}, bf16[4,128,128]{2,1,0:T(8,128)(2,1)S(1)}, u32[]{:S(2)}, u32[]{:S(2)}) collective-permute-start(bf16[4,128,128]{2,1,0:T(8,128)(2,1)S(1)} %get-tuple-element.284), channel_id=1, source_target_pairs={{0,24},{8,0},{16,8},{24,16},{1,25},{9,1},{17,9},{25,17},{2,26},{10... | collective-permute-start | bytes 393224 | tf_op jit(solution)/shard_map/ppermute | solution.py:1011
  392.4 12.6 %collective-permute-start.51 = (bf16[4,128,128]{2,1,0:T(8,128)(2,1)S(1)}, bf16[4,128,128]{2,1,0:T(8,128)(2,1)S(1)}, u32[]{:S(2)}, u32[]{:S(2)}) collective-permute-start(bf16[4,128,128]{2,1,0:T(8,128)(2,1)S(1)} %get-tuple-element.280), channel_id=1, source_target_pairs={{0,8},{8,16},{16,24},{24,0},{1,9},{9,17},{17,25},{25,1},{2,10},{10... | collective-permute-start | bytes 393224 | tf_op jit(solution)/shard_map/ppermute | solution.py:1011
  394.1 14.6 %collective-permute-start.53 = (bf16[4,128,128]{2,1,0:T(8,128)(2,1)S(1)}, bf16[4,128,128]{2,1,0:T(8,128)(2,1)S(1)}, u32[]{:S(2)}, u32[]{:S(2)}) collective-permute-start(bf16[4,128,128]{2,1,0:T(8,128)(2,1)S(1)} %get-tuple-element.281), channel_id=1, source_target_pairs={{0,24},{8,0},{16,8},{24,16},{1,25},{9,1},{17,9},{25,17},{2,26},{10... | collective-permute-start | bytes 393224 | tf_op jit(solution)/shard_map/ppermute | solution.py:1011
  395.5 15.3 %collective-permute-start.52 = (bf16[4,128,128]{2,1,0:T(8,128)(2,1)S(1)}, bf16[4,128,128]{2,1,0:T(8,128)(2,1)S(1)}, u32[]{:S(2)}, u32[]{:S(2)}) collective-permute-start(bf16[4,128,128]{2,1,0:T(8,128)(2,1)S(1)} %get-tuple-element.282), channel_id=1, source_target_pairs={{0,16},{8,24},{16,0},{24,8},{1,17},{9,25},{17,1},{25,9},{2,18},{10... | collective-permute-start | bytes 393224 | tf_op jit(solution)/shard_map/ppermute | solution.py:1011
  421.3 10.4 %collective-permute-start.63 = (f32[2,2,2304]{2,1,0:T(2,128)S(1)}, f32[2,2,2304]{2,1,0:T(2,128)S(1)}, u32[]{:S(2)}, u32[]{:S(2)}) collective-permute-start(f32[2,2,2304]{2,1,0:T(2,128)S(1)} %get-tuple-element.301), channel_id=1, source_target_pairs={{0,4},{4,0},{1,5},{5,1},{2,6},{6,2},{3,7},{7,3},{8,12},{12,8},{9,1... | collective-permute-start | bytes 110600 | tf_op jit(solution)/shard_map/ppermute | solution.py:1011
  431.8 10.1 %collective-permute-start.65 = (f32[2,2,2,2304]{3,2,1,0:T(2,128)S(1)}, f32[2,2,2,2304]{3,2,1,0:T(2,128)S(1)}, u32[]{:S(2)}, u32[]{:S(2)}) collective-permute-start(f32[2,2,2,2304]{3,2,1,0:T(2,128)S(1)} %pad_maximum_fusion.9), channel_id=1, source_target_pairs={{0,16},{8,24},{16,0},{24,8},{1,17},{9,25},{17,1},{25,9},{2,18},{10... | collective-permute-start | bytes 221192 | tf_op jit(solution)/shard_map/ppermute | solution.py:1011
  445.4 36.0 %collective-permute-start.70 = (bf16[208,768]{1,0:T(8,128)(2,1)S(1)}, bf16[208,768]{1,0:T(8,128)(2,1)S(1)}, u32[]{:S(2)}, u32[]{:S(2)}) collective-permute-start(bf16[208,768]{1,0:T(8,128)(2,1)S(1)} %get-tuple-element.292), channel_id=1, source_target_pairs={{4,0},{8,4},{12,8},{16,12},{20,16},{24,20},{28,24},{0,28},{5,1},{9... | collective-permute-start | bytes 958472 | tf_op jit(solution)/shard_map/ppermute | solution.py:1405
  446.4 35.0 %collective-permute-start.71 = (bf16[208,768]{1,0:T(8,128)(2,1)S(1)}, bf16[208,768]{1,0:T(8,128)(2,1)S(1)}, u32[]{:S(2)}, u32[]{:S(2)}) collective-permute-start(bf16[208,768]{1,0:T(8,128)(2,1)S(1)} %get-tuple-element.293), channel_id=1, source_target_pairs={{0,4},{4,8},{8,12},{12,16},{16,20},{20,24},{24,28},{28,0},{1,5},{5... | collective-permute-start | bytes 958472 | tf_op jit(solution)/shard_map/ppermute | solution.py:1406
  448.6 34.1 %collective-permute-start.67 = (bf16[208,768]{1,0:T(8,128)(2,1)S(1)}, bf16[208,768]{1,0:T(8,128)(2,1)S(1)}, u32[]{:S(2)}, u32[]{:S(2)}) collective-permute-start(bf16[208,768]{1,0:T(8,128)(2,1)S(1)} %get-tuple-element.273), channel_id=1, source_target_pairs={{0,8},{8,16},{16,24},{24,0},{1,9},{9,17},{17,25},{25,1},{2,10},{10... | collective-permute-start | bytes 958472 | tf_op jit(solution)/shard_map/ppermute | solution.py:1011
  450.3 32.4 %collective-permute-start.69 = (bf16[208,768]{1,0:T(8,128)(2,1)S(1)}, bf16[208,768]{1,0:T(8,128)(2,1)S(1)}, u32[]{:S(2)}, u32[]{:S(2)}) collective-permute-start(bf16[208,768]{1,0:T(8,128)(2,1)S(1)} %get-tuple-element.274), channel_id=1, source_target_pairs={{0,24},{8,0},{16,8},{24,16},{1,25},{9,1},{17,9},{25,17},{2,26},{10... | collective-permute-start | bytes 958472 | tf_op jit(solution)/shard_map/ppermute | solution.py:1011
  450.3 32.4 %collective-permute-start.68 = (bf16[208,768]{1,0:T(8,128)(2,1)S(1)}, bf16[208,768]{1,0:T(8,128)(2,1)S(1)}, u32[]{:S(2)}, u32[]{:S(2)}) collective-permute-start(bf16[208,768]{1,0:T(8,128)(2,1)S(1)} %get-tuple-element.275), channel_id=1, source_target_pairs={{0,16},{8,24},{16,0},{24,8},{1,17},{9,25},{17,1},{25,9},{2,18},{10... | collective-permute-start | bytes 958472 | tf_op jit(solution)/shard_map/ppermute | solution.py:1011
  (69 other events, 593.4 us)
Sparse Core Ops, SparseCore 0:
  11.5 123.2 all-gather.1

commit v4 on v3

--- a/solution.py
+++ b/solution.py
@@ -383,11 +383,6 @@
     )(factor, p_l, p_r, ql, qr, rot, gl, gr, sl, sr, bl, br, master, m1, m2)
 
 
-def soap(ranks, g, factor, stat_parts, master, m1, m2, sl, sr, bl, br):
-    rot, gl, gr, ql, qr = raw_products(ranks, g, bl, br)
-    return finish(factor.reshape(1), rot, gl, gr, ql, qr, *stat_parts, sl, sr, bl, br, master, m1, m2)
-
-
 def adam_update(clipped, params_old, first_old, second_old):
     first_new = BETA_ONE * first_old + (1.0 - BETA_ONE) * clipped
     second_new = BETA_TWO * second_old + (1.0 - BETA_TWO) * clipped * clipped
@@ -407,6 +402,9 @@
 PAIR = 2 * HD
 QKV_BLOCKS = 108
 CODE_BASE = 1 << 16
+UP_ROWS = (D + FF) // BLOCK_SIDE
+BLANK_ROW = (D + 2 * FF) // BLOCK_SIDE
+ALL_ROWS = BLANK_ROW * BLOCK_SIDE
 VMEM_MOST = 58 * 1024 * 1024
 ALL_AXES = ("fz", "fx", "by", "core")
 FRAME_AXES = ("fz", "fx")
@@ -442,21 +440,27 @@
     return ref.at[pl.ds(row, BLOCK_SIDE), pl.ds(col, BLOCK_SIDE)]
 
 
-def load_matrix(which, codes, buffers, matrix, sem, first_buffer=0):
-    first, count, cols = matrix_places()[which]
-
-    def one_block(tile, carry):
-        code = codes[first + tile]
-        row, col = lax.div(tile, cols), lax.rem(tile, cols)
-        for index, buffer in enumerate(buffers):
-            @pl.when(lax.div(code, CODE_BASE) == first_buffer + index)
+def tile_of(matrix, code):
+    return tile_at(matrix, lax.bitwise_and(lax.shift_right_logical(code, 5), 63), lax.bitwise_and(code, 31))
+
+
+def load_blocks(tiles, buffers, matrix, sems, matrices, base=0, count=None):
+    for buffer in buffers:
+        def one_load(place, carry, buffer=buffer, base=base):
+            code = tiles[base + place]
+            which = lax.shift_right_logical(code, 11)
+
+            @pl.when(which < matrices)
             def _():
-                pltpu.make_async_copy(
-                    buffer.at[lax.rem(code, CODE_BASE)], tile_at(matrix, row, col), sem
-                ).start()
-        return carry
-
-    lax.fori_loop(0, count, one_block, 0)
+                pltpu.make_async_copy(buffer.at[place], tile_of(matrix, code), sems.at[which]).start()
+
+            return carry
+
+        if count is None:
+            lax.fori_loop(0, buffer.shape[0], one_load, 0, unroll=4)
+        else:
+            lax.fori_loop(0, count, one_load, 0)
+        base = base + buffer.shape[0]
 
 
 def wait_whole(ref, sem):
@@ -485,19 +489,23 @@
     )
 
 
-def project(codes, buffers, first_buffer, seen, rows14):
+def project(tiles, early, buffers, early_buffers, seen, rows14):
     rows = seen.shape[0]
     steps = rows // OWN_ROWS
     count = len(buffers)
 
-    def kernel(codes, *refs):
+    def kernel(tiles, early, *refs):
         sources = refs[:count]
-        seen, rows14, q, kv, low, own_low, w_qkv, sem = refs[count:]
+        seen, rows14, q, kv, low, own_low, w_qkv, sems = refs[count:]
         step = pl.program_id(0)
 
         @pl.when(step == 0)
         def _():
-            load_matrix(0, codes, sources, w_qkv, sem, first_buffer)
+            base = 0
+            if early_buffers:
+                load_blocks(tiles, sources[:1], w_qkv, sems, 1, 0, early[0])
+                base = sources[0].shape[0]
+            load_blocks(tiles, sources[early_buffers:], w_qkv, sems, 1, base)
 
         hat, _ = normalized(seen[...].astype(F32))
         normed = (hat * rows14[0:1] + rows14[1:2]).astype(BF)
@@ -505,7 +513,7 @@
 
         @pl.when(step == 0)
         def _():
-            wait_whole(w_qkv, sem)
+            wait_whole(w_qkv, sems.at[0])
 
         kv[:, :D] = dot_low(normed, w_qkv[:, D : 2 * D], NN).astype(BF)
         kv[:, D:] = (dot_low(normed, w_qkv[:, 2 * D :], NN) + rows14[7:8]).astype(BF)
@@ -525,19 +533,19 @@
             own(PAD_ROWS)
 
     def whole(shape):
-        return pl.BlockSpec(shape, lambda i, codes: (0, 0))
+        return pl.BlockSpec(shape, lambda i, tiles, early: (0, 0))
 
     def moving(width):
-        return pl.BlockSpec((OWN_ROWS, width), lambda i, codes: (i, 0))
+        return pl.BlockSpec((OWN_ROWS, width), lambda i, tiles, early: (i, 0))
 
     return pl.pallas_call(
         kernel,
         grid_spec=pltpu.PrefetchScalarGridSpec(
-            num_scalar_prefetch=1,
+            num_scalar_prefetch=2,
             grid=(steps,),
             in_specs=[anywhere()] * count + [moving(D), whole((14, D))],
             out_specs=[whole((OWN_ROWS, D)), moving(2 * D), moving(D), whole((OWN_ROWS, D)), whole((D, 3 * D))],
-            scratch_shapes=[pltpu.SemaphoreType.DMA],
+            scratch_shapes=[pltpu.SemaphoreType.DMA((1,))],
         ),
         out_shape=[
             jax.ShapeDtypeStruct((OWN_ROWS, D), BF),
@@ -548,7 +556,7 @@
         ],
         compiler_params=pltpu.CompilerParams(vmem_limit_bytes=VMEM_MOST),
         cost_estimate=about(15),
-    )(codes, *buffers, seen, rows14)
+    )(tiles, early, *buffers, seen, rows14)
 
 
 ROW_STEP = 16
@@ -634,35 +642,41 @@
     )(q, kv, kv, bias.reshape(1, -1))
 
 
-def attend_back(q, kv, bias, out, logs, grad):
+def attend_back(pairs, before, q, kv, bias, out, logs, grad):
     keys_total = kv.shape[0]
     long_rows = keys_total - OWN_ROWS
+    start, count = pairs
 
     def kernel(*refs):
-        attend_back_kernel(long_rows, *refs)
+        attend_back_kernel(long_rows, *refs[:7], *refs[7 + len(before) :])
+
+    def spec(rows, offset=0):
+        return pair_spec(rows, offset + start)
 
     return pl.pallas_call(
         kernel,
-        grid=(PAIRS,),
+        grid=(count,),
         in_specs=[
-            pair_spec(OWN_ROWS),
-            pair_spec(keys_total),
-            pair_spec(keys_total, PAIRS),
+            spec(OWN_ROWS),
+            spec(keys_total),
+            spec(keys_total, PAIRS),
             pl.BlockSpec((1, keys_total), lambda i: (0, 0)),
-            pair_spec(OWN_ROWS),
-            pair_spec(OWN_ROWS),
-            pair_spec(OWN_ROWS),
-        ],
-        out_specs=[pair_spec(OWN_ROWS), pair_spec(keys_total), pair_spec(keys_total)],
+            spec(OWN_ROWS),
+            spec(OWN_ROWS),
+            spec(OWN_ROWS),
+        ]
+        + [anywhere()] * len(before),
+        out_specs=[spec(OWN_ROWS), spec(keys_total), spec(keys_total)],
         out_shape=[
             jax.ShapeDtypeStruct((OWN_ROWS, D), BF),
             jax.ShapeDtypeStruct((keys_total, D), BF),
             jax.ShapeDtypeStruct((keys_total, D), BF),
         ],
         scratch_shapes=[pltpu.VMEM((OWN_ROWS, long_rows), F32)] * 2 + [pltpu.VMEM((OWN_ROWS, long_rows), BF)] * 2,
+        input_output_aliases={7 + i: i for i in range(len(before))},
         compiler_params=pltpu.CompilerParams(vmem_limit_bytes=VMEM_MOST),
-        cost_estimate=about(24),
-    )(q, kv, kv, bias.reshape(1, -1), out, logs, grad)
+        cost_estimate=about(4 * count),
+    )(q, kv, kv, bias.reshape(1, -1), out, logs, grad, *before)
 
 
 def lane_masks():
@@ -700,36 +714,38 @@
     return jnp.concatenate([values, jnp.zeros((values.shape[0], LANES - OWN_ROWS), values.dtype)], axis=1)
 
 
-def middle_kernel(weight_count, first_buffer, codes, targets, *refs):
+def wait_tiles(matrix, count, sem):
+    side = D // BLOCK_SIDE
+    rest = count
+    while rest >= side:
+        rows = min(rest // side, BLANK_ROW)
+        wait_whole(matrix.at[: rows * BLOCK_SIDE], sem)
+        rest = rest - rows * side
+    for _ in range(rest):
+        wait_whole(tile_at(matrix, 0, 0), sem)
+
+
+def middle_kernel(weight_count, first_buffer, held_tiles, sent_tiles, targets, *refs):
     sources = refs[:weight_count]
     (
-        att, own, cot, rows14, conv_t, taps_forward, taps_backward, tail_bias, masks, blank,
+        att, own, cot, rows14, conv_t, taps_forward, taps_backward, tail_bias, masks,
         learned, grad_mixed, grad_att, vectors, grad_up_bias, grad_conv, grad_tail, grad_tail_bias,
-    ) = refs[weight_count : weight_count + 18]
-    buffers = refs[weight_count + 18 : -14]
+    ) = refs[weight_count : weight_count + 17]
+    buffers = refs[weight_count + 17 : -10]
     (
-        w_out, w_up, w_down, d_out, d_up, d_down, activated, slopes, normed, hat_two, mixed, gathered_sum,
-        load_sems, send_sems,
-    ) = refs[-14:]
+        w_all, d_all, activated, slopes, normed, hat_two, mixed, gathered_sum, load_sems, send_sems,
+    ) = refs[-10:]
     chunks = FF // D
-    load_matrix(1, codes, sources, w_out, load_sems.at[0], first_buffer)
-    load_matrix(2, codes, sources, w_up, load_sems.at[1], first_buffer)
-    load_matrix(3, codes, sources, w_down, load_sems.at[2], first_buffer)
-
-    def one_blank(block, total):
-        code = targets[block]
-        early = lax.div(code, CODE_BASE) < 4
-        filled = (block >= MATRIX_BLOCKS) | ((block < QKV_BLOCKS) & early)
-
-        @pl.when(filled)
-        def _():
-            send_tile(code, buffers, blank, send_sems.at[3])
-
-        return total + filled.astype(jnp.int32)
-
-    blanks = lax.fori_loop(0, QKV_BLOCKS, one_blank, jnp.int32(0))
-    blanks = lax.fori_loop(MATRIX_BLOCKS, targets.shape[0], one_blank, blanks)
-
+    side = D // BLOCK_SIDE
+    w_out = w_all.at[:D]
+    w_up = [w_all.at[(1 + chunk) * D : (2 + chunk) * D] for chunk in range(chunks)]
+    w_down = [w_all.at[(1 + chunks + chunk) * D : (2 + chunks + chunk) * D] for chunk in range(chunks)]
+    d_out = d_all.at[:D]
+    d_up = [d_all.at[(1 + chunk) * D : (2 + chunk) * D] for chunk in range(chunks)]
+    d_down = [d_all.at[(1 + chunks + chunk) * D : (2 + chunks + chunk) * D] for chunk in range(chunks)]
+
+    load_blocks(held_tiles, sources, w_all, load_sems, 3)
+    d_all[ALL_ROWS:, :BLOCK_SIDE] = jnp.zeros((BLOCK_SIDE, BLOCK_SIDE), BF)
     wait_whole(w_out, load_sems.at[0])
     start = own[...].astype(F32) + dot_low(att[...], w_out[...], NN) + rows14[8:9]
     mixed[...] = start
@@ -737,17 +753,16 @@
     hat_two[...] = hat
     normed[...] = (hat * rows14[2:3] + rows14[3:4]).astype(BF)
     gathered_sum[...] = start + rows14[13:14]
-    wait_whole(w_up, load_sems.at[1])
-    wait_whole(w_down, load_sems.at[2])
+    wait_whole(w_all.at[D : D + FF], load_sems.at[1])
+    wait_whole(w_all.at[D + FF : D + 2 * FF], load_sems.at[2])
 
     for chunk in range(chunks):
-        at = slice(chunk * D, (chunk + 1) * D)
-        hidden = dot_low(normed[...], w_up[:, at], NN) + rows14[9 + chunk : 10 + chunk]
+        hidden = dot_low(normed[...], w_up[chunk][...], NN) + rows14[9 + chunk : 10 + chunk]
         portion = cumulative(hidden)
         active = (hidden * portion).astype(BF)
         activated[chunk] = active
         slopes[chunk] = gelu_slope(hidden, portion)
-        gathered_sum[...] += dot_low(active, w_down[at, :], NN)
+        gathered_sum[...] += dot_low(active, w_down[chunk][...], NN)
 
     out_two = gathered_sum[...]
     hat, spread_three = normalized(out_two)
@@ -804,29 +819,30 @@
     vectors[5:6] = column_sum(grad_down.astype(F32))
 
     for chunk in range(chunks):
-        at = slice(chunk * D, (chunk + 1) * D)
-        grad_active = dot_low(grad_down, w_down[at, :], NT_)
+        grad_active = dot_low(grad_down, w_down[chunk][...], NT_)
         grad_hidden = (grad_active * slopes[chunk]).astype(BF)
         grad_up_bias[chunk : chunk + 1] = column_sum(grad_hidden.astype(F32))
-        part = dot_low(grad_hidden, w_up[:, at], NT_)
+        part = dot_low(grad_hidden, w_up[chunk][...], NT_)
         if chunk == 0:
             gathered_sum[...] = part
         else:
             gathered_sum[...] += part
-        d_down[at, :] = dot_low(activated[chunk], grad_down, TN).astype(BF)
-        d_up[:, at] = dot_low(normed[...], grad_hidden, TN).astype(BF)
-        side = D // BLOCK_SIDE
-
-        def one_tile(tile, carry, chunk=chunk):
-            row, col = lax.div(tile, side), lax.rem(tile, side)
-            first_up, first_down = matrix_places()[2][0], matrix_places()[3][0]
-            up_block = first_up + row * (FF // BLOCK_SIDE) + chunk * side + col
-            send_tile(targets[up_block], buffers, tile_at(d_up, row, chunk * side + col), send_sems.at[1])
-            down_block = first_down + (chunk * side + row) * side + col
-            send_tile(targets[down_block], buffers, tile_at(d_down, chunk * side + row, col), send_sems.at[2])
+        d_down[chunk][...] = dot_low(activated[chunk], grad_down, TN).astype(BF)
+        d_up[chunk][...] = dot_low(normed[...], grad_hidden, TN).astype(BF)
+
+    base = 0
+    for buffer in buffers:
+        def one_tile(place, carry, buffer=buffer, base=base):
+            code = sent_tiles[base + place]
+
+            @pl.when(code >= 2048)
+            def _():
+                pltpu.make_async_copy(tile_of(d_all, code), buffer.at[place], send_sems.at[1]).start()
+
             return carry
 
-        lax.fori_loop(0, side * side, one_tile, 0)
+        lax.fori_loop(0, buffer.shape[0], one_tile, 0, unroll=4)
+        base = base + buffer.shape[0]
 
     grad_norm_two = gathered_sum[...]
     vectors[0:1] = column_sum(grad_norm_two * hat_two[...])
@@ -838,25 +854,17 @@
     d_out[...] = dot_low(att[...], branch, TN).astype(BF)
 
     def one_out(tile, carry):
-        side = D // BLOCK_SIDE
         code = targets[matrix_places()[1][0] + tile]
-        send_tile(code, buffers, tile_at(d_out, lax.div(tile, side), lax.rem(tile, side)), send_sems.at[0])
+        send_tile(code, buffers, tile_at(d_out, lax.div(tile, side), lax.rem(tile, side)), send_sems.at[0], first_buffer)
         return carry
 
     lax.fori_loop(0, matrix_places()[1][1], one_out, 0)
     grad_att[...] = dot_low(branch, w_out[...], NT_).astype(BF)
-    wait_whole(d_out, send_sems.at[0])
-    wait_whole(d_up, send_sems.at[1])
-    wait_whole(d_down, send_sems.at[2])
-
-    def one_wait(index, carry):
-        wait_whole(blank, send_sems.at[3])
-        return carry
-
-    lax.fori_loop(0, blanks, one_wait, 0)
-
-
-def middle(codes, targets, weights, first_buffer, buffer_shapes, att, own, cot, rows14, conv_t, taps_forward, taps_backward, tail_bias):
+    wait_tiles(d_all, matrix_places()[1][1], send_sems.at[0])
+    wait_tiles(d_all, targets.shape[0] - matrix_places()[1][1], send_sems.at[1])
+
+
+def middle(held_tiles, sent_tiles, targets, weights, first_buffer, buffer_shapes, att, own, cot, rows14, conv_t, taps_forward, taps_backward, tail_bias):
     count = len(weights)
 
     def kernel(*refs):
@@ -872,17 +880,13 @@
     results = pl.pallas_call(
         kernel,
         grid_spec=pltpu.PrefetchScalarGridSpec(
-            num_scalar_prefetch=2,
+            num_scalar_prefetch=3,
             grid=(1,),
-            in_specs=[anywhere()] * count + [in_vmem()] * 10,
+            in_specs=[anywhere()] * count + [in_vmem()] * 9,
             out_specs=[in_vmem()] * len(outs) + [anywhere()] * len(buffer_shapes),
             scratch_shapes=[
-                pltpu.VMEM((D, D), BF),
-                pltpu.VMEM((D, FF), BF),
-                pltpu.VMEM((FF, D), BF),
-                pltpu.VMEM((D, D), BF),
-                pltpu.VMEM((D, FF), BF),
-                pltpu.VMEM((FF, D), BF),
+                pltpu.VMEM((ALL_ROWS + BLOCK_SIDE, D), BF),
+                pltpu.VMEM((ALL_ROWS + BLOCK_SIDE, D), BF),
                 pltpu.VMEM((FF // D, OWN_ROWS, D), BF),
                 pltpu.VMEM((FF // D, OWN_ROWS, D), F32),
                 pltpu.VMEM((OWN_ROWS, D), BF),
@@ -890,15 +894,15 @@
                 pltpu.VMEM((OWN_ROWS, D), F32),
                 pltpu.VMEM((OWN_ROWS, D), F32),
                 pltpu.SemaphoreType.DMA((3,)),
-                pltpu.SemaphoreType.DMA((4,)),
+                pltpu.SemaphoreType.DMA((2,)),
             ],
         ),
         out_shape=outs + buffer_shapes,
         compiler_params=pltpu.CompilerParams(vmem_limit_bytes=VMEM_MOST),
         cost_estimate=about(40),
     )(
-        codes, targets, *weights, att, own, cot, rows14, conv_t, taps_forward, taps_backward, tail_bias,
-        jnp.asarray(lane_masks()), jnp.zeros((BLOCK_SIDE, BLOCK_SIDE), BF),
+        held_tiles, sent_tiles, targets, *weights, att, own, cot, rows14, conv_t, taps_forward, taps_backward, tail_bias,
+        jnp.asarray(lane_masks()),
     )
     return results[: len(outs)], results[len(outs) :]
 
@@ -1031,6 +1035,19 @@
     return lax.dynamic_slice_in_dim(jnp.concatenate([value, value], axis), step, size, axis)
 
 
+def small_shares(vector, sizes, coords):
+    device_count = math.prod(sizes)
+    share = -(-vector.shape[0] // (device_count * 128)) * 128
+    shares = jnp.pad(vector, (0, device_count * share - vector.shape[0])).reshape(sizes + (share,))
+    for axis, size in enumerate(sizes):
+        shares = rolled(shares, axis, size, coords[axis])
+    return shares.transpose(3, 1, 2, 0, 4)
+
+
+def small_step(shares, axis, sizes):
+    return reduce_axis(shares, ALL_AXES[axis], sizes[axis])
+
+
 def early_slots(slots_dev):
     return slots_dev * 6 // 14
 
@@ -1062,41 +1079,74 @@
     rank = ranks.reshape(-1)
     size_of = dict(zip(ALL_AXES, sizes))
     code = jnp.zeros_like(slots)
-    for index, (first, count, axes) in enumerate(slot_chunks(slots_dev)):
+    chunks = slot_chunks(slots_dev)
+    device_count = nz * nx * ny * nc
+    for index, (first, count, axes) in enumerate(chunks):
         at = jnp.zeros_like(slots)
         for name in axes:
             at = at * size_of[name] + place[name]
         at = at * count + rank - first
+        if index % 2:
+            at = at + device_count // nc * chunks[index - 1][1]
         inside = (rank >= first) & (rank < first + count)
-        code = jnp.where(inside, (2 * index + place["core"]) * CODE_BASE + at, code)
+        code = jnp.where(inside, (index // 2 * 2 + place["core"]) * CODE_BASE + at, code)
     owned = block_owner[:, None] == slots[None, :]
     table = jnp.sum(jnp.where(owned, code[:, None], 0), 0)
     early = early_slots(slots_dev)
-    gathered = jnp.where(rank < early, slots // slots_dev * early + rank, code - 3 * CODE_BASE)
-    weight_table = jnp.sum(jnp.where(owned, gathered[:, None], 0), 0)
-    return table, weight_table, ranks, jnp.max(late_count)
-
-
-def reduce_core(kept, sent, count, axes, sizes):
+    late_size = device_count // nc * (slots_dev - early)
+    early_size = device_count // nc * early
+    buffer, at = code // CODE_BASE, code % CODE_BASE
+    sent_at = jnp.where(buffer < 2, buffer * early_size, 2 * early_size + (buffer - 2) * late_size) + at
+    held_at = jnp.where(buffer < 2, slots // slots_dev * early + rank, 2 * early_size + (buffer - 2) * late_size + at)
+    tile = tile_code(block_owner)
+    held_tiles = jnp.sum(jnp.where(held_at[:, None] == slots[None, :], tile[:, None], 0), 0)
+    sent_tiles = jnp.sum(jnp.where(sent_at[:, None] == slots[None, :], tile[:, None], 0), 0)
+    qkv_cols = 3 * D // BLOCK_SIDE
+    qkv_tile = jnp.where(block_owner < QKV_BLOCKS, block_owner // qkv_cols * 32 + block_owner % qkv_cols, 2048)
+    qkv_tiles = jnp.sum(jnp.where(held_at[:, None] == slots[None, :], qkv_tile[:, None], 0), 0)
+    return table, qkv_tiles, held_tiles, sent_tiles, ranks, jnp.max(late_count)
+
+
+def tile_code(block):
+    side = D // BLOCK_SIDE
+    out_tile = block - matrix_places()[1][0]
+    up_tile = block - matrix_places()[2][0]
+    down_tile = block - matrix_places()[3][0]
+    up_row, up_col = up_tile // (FF // BLOCK_SIDE), up_tile % (FF // BLOCK_SIDE)
+    row = jnp.where(
+        up_tile < 0,
+        out_tile // side,
+        jnp.where(down_tile < 0, side + up_col // side * side + up_row, UP_ROWS + down_tile // side),
+    )
+    col = jnp.where(up_tile < 0, out_tile % side, jnp.where(down_tile < 0, up_col % side, down_tile % side))
+    matrix = jnp.where(up_tile < 0, 0, jnp.where(down_tile < 0, 1, 2))
+    used = (out_tile >= 0) & (block < MATRIX_BLOCKS)
+    return jnp.where(used, matrix * 2048 + row * 32 + col, 3 * 2048 + BLANK_ROW * 32)
+
+
+def reduce_core(kept, sent, chunks, sizes):
     size_of = dict(zip(ALL_AXES, sizes))
     total = (kept.astype(F32) + moved(sent, "core", 2, 1).astype(F32)).astype(BF)
-    return total.reshape([size_of[name] for name in axes] + [count, BLOCK_SIDE, BLOCK_SIDE])
-
-
-def reduce_stage(total, axes, stage, sizes):
-    name = axes[stage]
-    total = reduce_axis(total, name, sizes[ALL_AXES.index(name)])
-    return total if stage == len(axes) - 1 else total.astype(BF)
-
-
-def reduce_rest(total, axes, sizes):
-    for stage in range(len(axes)):
-        total = reduce_stage(total, axes, stage, sizes)
-    return total
-
-
-def reduce_chunk(kept, sent, count, axes, sizes):
-    return reduce_rest(reduce_core(kept, sent, count, axes, sizes), axes, sizes)
+    parts = []
+    start = 0
+    for first, count, axes in chunks:
+        shape = [size_of[name] for name in axes] + [count, BLOCK_SIDE, BLOCK_SIDE]
+        stop = start + math.prod(shape[:-2])
+        parts.append(total[start:stop].reshape(shape))
+        start = stop
+    return parts
+
+
+def reduce_stage(parts, chunks, stage, sizes):
+    results = []
+    for part, (first, count, axes) in zip(parts, chunks):
+        name = axes[stage]
+        results.append(reduce_axis(part, name, sizes[ALL_AXES.index(name)]).astype(BF))
+    return results
+
+
+def reduce_last(parts, sizes):
+    return reduce_axis(jnp.concatenate(parts, axis=1), "fz", sizes[0])
 
 
 def gather_stage(shard, axes, stage, sizes):
@@ -1104,20 +1154,18 @@
     return gather_axis(shard, name, sizes[ALL_AXES.index(name)])
 
 
-def gather_core(shard):
-    shard = shard.reshape(-1, BLOCK_SIDE, BLOCK_SIDE)
-    return [shard, moved(shard, "core", 2, 1)]
-
-
-def gather_chunk(shard, axes, sizes):
-    for stage in range(len(axes)):
-        shard = gather_stage(shard, axes, stage, sizes)
-    return gather_core(shard)
+def gather_last(shards, orders, sizes):
+    pieces = []
+    for shard, axes in zip(shards, orders):
+        size = sizes[ALL_AXES.index(axes[0])]
+        pieces = pieces + [shard] + [moved(shard, axes[0], size, -step) for step in range(1, size)]
+    return [piece.reshape(-1, BLOCK_SIDE, BLOCK_SIDE) for piece in pieces]
 
 
 def sorted_shards(device_index, block_owner, master):
     slots_dev = master.shape[0]
-    chunks = [(0, early_slots(slots_dev), ())] + slot_chunks(slots_dev)[2:]
+    early = early_slots(slots_dev)
+    chunks = [(0, early, ()), (early, slots_dev - early, ())]
 
     def kernel(where, owner, blocks, *outs):
         base = where[0] * slots_dev
@@ -1162,7 +1210,7 @@
         def one_block(block, sent):
             code = targets[block]
             cols = 3 * D // BLOCK_SIDE
-            early = lax.div(code, CODE_BASE) < 4
+            early = lax.div(code, CODE_BASE) < 2
 
             @pl.when(early & (block < QKV_BLOCKS))
             def _():
@@ -1245,7 +1293,7 @@
     chunks = slot_chunks(slots_dev)
     shards = sorted_shards(device_index, block_owner, master)
     orders = [axes for first, count, axes in chunks]
-    late_shards = [gather_stage(shards[1 + i], orders[2 + i], 0, sizes) for i in range(2)]
+    late_shards = gather_axis(shards[1], "fz", nz)
 
     own_frames = pad_frames(tokens[0])
     own_frames = jnp.where(swap, own_frames[::-1], own_frames)
@@ -1257,24 +1305,19 @@
 
     weights = [gather_early(shards[0])] if early else []
     long_pair = gather_axis(long_frame, "fx", nx)
-    long_pair, late_shards = lax.optimization_barrier((long_pair, late_shards))
+    from_previous = lax.ppermute(short_frame, FRAME_AXES, frame_perm)
+    from_next = lax.ppermute(short_frame, FRAME_AXES, back_perm)
+    long_pair, late_shards, from_previous, from_next = lax.optimization_barrier(
+        (long_pair, late_shards, from_previous, from_next)
+    )
+    late_shards = [late_shards[:, : chunks[2][1]], late_shards[:, chunks[2][1] :]]
     late_shards = [gather_stage(part, orders[2 + i], 1, sizes) for i, part in enumerate(late_shards)]
     long_frames = [long_pair] + [moved(long_pair, "fz", nz, -step) for step in range(1, nz)]
-    late_shards, long_frames[1] = lax.optimization_barrier((late_shards, long_frames[1]))
-    late_shards = [gather_stage(part, orders[2 + i], 2, sizes) for i, part in enumerate(late_shards)]
-    from_previous = lax.ppermute(short_frame, FRAME_AXES, frame_perm)
-    from_next = lax.ppermute(short_frame, FRAME_AXES, back_perm)
-    late_shards, long_frames, from_previous, from_next = lax.optimization_barrier(
-        (late_shards, long_frames, from_previous, from_next)
-    )
-    weights = weights + gather_core(late_shards[0]) + gather_core(late_shards[1])
-    long_frames = jnp.stack(long_frames)
+    late_shards, long_frames[1:-1] = lax.optimization_barrier((late_shards, long_frames[1:-1]))
+    late_pieces = gather_last(late_shards, orders[2:], sizes)
     partner = jnp.where(with_next, from_next, from_previous)
 
     frames_seen = frame_count + 2
-    seen = jnp.concatenate(
-        [long_frames.reshape(frame_count, PAD_ROWS, D), short_frame[None], partner[None]]
-    ).reshape(frames_seen * PAD_ROWS, D)
     own = own_frames.reshape(OWN_ROWS, D)
     row_ids = jnp.arange(frames_seen * PAD_ROWS, dtype=jnp.int32)
     hidden_key = (row_ids % PAD_ROWS >= FRAME_ROWS) | (
@@ -1282,7 +1325,7 @@
     )
     key_bias = jnp.where(hidden_key, MASK_FLOOR, 0.0).astype(F32)
 
-    targets, weight_codes, ranks, late_most = send_table(block_owner, sizes, coords, slots_dev)
+    targets, qkv_tiles, held_tiles, sent_tiles, ranks, late_most = send_table(block_owner, sizes, coords, slots_dev)
     own_ranks = lax.dynamic_index_in_dim(ranks, device_index, 0, keepdims=False)
     late_fits = late_most <= slots_dev - early
 
@@ -1296,63 +1339,63 @@
     arriving = cotangent[0].reshape(2, NT, D)
     arriving = jnp.where(swap, arriving[::-1], arriving).reshape(2 * NT, D)
 
-    first_buffer = 0 if early else 1
     stat_parts = stat_products(stat_left, stat_right, basis_left, basis_right)
-    weights, stat_parts = lax.optimization_barrier((weights, stat_parts))
-    query, key_value, low, own_low, w_qkv = project(weight_codes, weights, first_buffer, seen, rows14)
+    early_looked = jnp.where(late_fits, 0, device_count * early).astype(jnp.int32).reshape(1)
+
+    (
+        late_pieces, long_frames, partner, stat_parts, key_bias, targets, qkv_tiles, held_tiles, sent_tiles, own_ranks,
+        early_looked, rows14, conv_t, taps_forward, taps_backward, tail_bias, arriving,
+    ) = lax.optimization_barrier(
+        (
+            late_pieces, long_frames, partner, stat_parts, key_bias, targets, qkv_tiles, held_tiles, sent_tiles, own_ranks,
+            early_looked, rows14, conv_t, taps_forward, taps_backward, tail_bias, arriving,
+        )
+    )
+    weights = weights + late_pieces + [moved(piece, "core", nc, 1) for piece in late_pieces]
+    seen = jnp.concatenate(
+        [frames.reshape(-1, D) for frames in long_frames] + [short_frame, partner]
+    )
+    query, key_value, low, own_low, w_qkv = project(
+        qkv_tiles, early_looked, weights, 1 if early else 0, seen, rows14
+    )
     attended, logs = attend(query, key_value, key_bias)
     buffer_shapes = []
-    for first, count, axes in chunks:
-        shape = jax.ShapeDtypeStruct((device_count // nc * max(count, 1), BLOCK_SIDE, BLOCK_SIDE), BF)
-        buffer_shapes = buffer_shapes + [shape, shape]
+    for slots in (early, slots_dev - early):
+        if slots:
+            shape = jax.ShapeDtypeStruct((device_count // nc * slots, BLOCK_SIDE, BLOCK_SIDE), BF)
+            buffer_shapes = buffer_shapes + [shape, shape]
     (learned, grad_mixed, grad_att, vectors, grad_up_bias, grad_conv, grad_tail, grad_tail_bias), buffers = middle(
-        weight_codes, targets, weights, first_buffer, buffer_shapes, attended, own, arriving, rows14, conv_t,
+        held_tiles, sent_tiles, targets, weights, 0 if early else 2, buffer_shapes, attended, own, arriving, rows14, conv_t,
         taps_forward, taps_backward, tail_bias,
     )
     learned = learned.reshape(2, NT, D)
     learned = jnp.where(swap, learned[::-1], learned).reshape(2 * NT, D)
 
-    used = [index for index in range(2) if chunks[index][1]]
-    halfway = [
-        reduce_core(buffers[2 * i], buffers[2 * i + 1], chunks[i][1], orders[i], sizes) for i in used
-    ]
-    grad_query, grad_key, grad_value = attend_back(query, key_value, key_bias, attended, logs, grad_att)
+    halfway = reduce_core(*buffers[:2], chunks[:2], sizes) if early else []
+    back = attend_back((0, PAIRS // 2), [], query, key_value, key_bias, attended, logs, grad_att)
+    back, halfway = lax.optimization_barrier((back, halfway))
+    halfway = reduce_stage(halfway, chunks, 0, sizes)
+    grad_query, grad_key, grad_value = attend_back(
+        (PAIRS // 2, PAIRS - PAIRS // 2), back, query, key_value, key_bias, attended, logs, grad_att
+    )
     grad_query, halfway = lax.optimization_barrier((grad_query, halfway))
-    halfway = [reduce_stage(part, orders[i], 0, sizes) for i, part in zip(used, halfway)]
+    halfway = reduce_stage(halfway, chunks, 1, sizes)
     late_buffers, grad_w_qkv = qkv_grads(
-        targets, low, own_low, grad_query, grad_key, grad_value, list(buffers[4:]), 4
-    )
-    late_buffers, halfway = lax.optimization_barrier((late_buffers, halfway))
-    halfway = [reduce_stage(part, orders[i], 1, sizes) for i, part in zip(used, halfway)]
-    late_parts = []
-    for index in range(2):
-        kept, sent = late_buffers[2 * index : 2 * index + 2]
-        late_parts.append(reduce_core(kept, sent, chunks[2 + index][1], orders[2 + index], sizes))
-    grad_query, late_buffers = lax.optimization_barrier((grad_query, late_buffers))
+        targets, low, own_low, grad_query, grad_key, grad_value, list(buffers[-2:]), 2
+    )
+    grad_query, late_buffers, halfway = lax.optimization_barrier((grad_query, late_buffers, halfway))
+    reduced = [reduce_last(halfway, sizes)] if early else []
+    late_parts = reduce_core(*late_buffers, chunks[2:], sizes)
     grad_seen, grad_own, sums = input_grads(seen, own, grad_query, grad_key, grad_value, w_qkv)
-    late_parts, halfway, grad_seen, sums = lax.optimization_barrier((late_parts, halfway, grad_seen, sums))
+    late_parts, reduced, grad_seen, sums = lax.optimization_barrier((late_parts, reduced, grad_seen, sums))
 
     seen_frames = grad_seen.reshape(frames_seen, PAD_ROWS, D)
     long_terms = seen_frames[:frame_count].reshape(nz, nx, PAD_ROWS, D)
-    late_parts = [reduce_stage(part, orders[2 + i], 0, sizes) for i, part in enumerate(late_parts)]
-    reduced = [reduce_stage(part, orders[i], 2, sizes) for i, part in zip(used, halfway)]
-    late_parts, reduced, long_terms = lax.optimization_barrier((late_parts, reduced, long_terms))
-    late_parts = [reduce_stage(part, orders[2 + i], 1, sizes) for i, part in enumerate(late_parts)]
-    late_parts, long_terms = lax.optimization_barrier((late_parts, long_terms))
-    late_parts = [reduce_stage(part, orders[2 + i], 2, sizes) for i, part in enumerate(late_parts)]
-    long_terms = reduce_axis(long_terms, "fx", nx, 1).astype(BF)
-    late_parts, long_terms = lax.optimization_barrier((late_parts, long_terms))
-    if used:
-        def whole_early(early):
-            extra = spread_early(targets, grad_w_qkv, buffer_shapes[:4])
-            return [
-                part + reduce_chunk(extra[2 * i], extra[2 * i + 1], chunks[i][1], orders[i], sizes)
-                for i, part in zip(used, early)
-            ]
-
-        reduced = lax.cond(late_fits, lambda early: early, whole_early, reduced)
-    owned_grads = jnp.concatenate(list(reduced) + late_parts)
-
+    partner_term = seen_frames[frame_count + 1]
+    nothing = jnp.zeros_like(partner_term)
+    to_previous = jnp.where(with_previous, partner_term, nothing)
+    to_next = jnp.where(with_next, partner_term, nothing)
+    late_parts = reduce_stage(late_parts, chunks[2:], 0, sizes)
     small_local = jnp.concatenate(
         [
             sums[:2].reshape(-1),
@@ -1367,44 +1410,53 @@
         ]
     )
     small_total = small_local.shape[0]
-    share = -(-small_total // (device_count * 128)) * 128
-    padded_small = jnp.pad(small_local, (0, device_count * share - small_total))
-    small_sum = padded_small.reshape(sizes + (share,))
+    small = small_step(small_shares(small_local, sizes, coords), 3, sizes)
+    late_parts, small = lax.optimization_barrier((late_parts, small))
+    late_parts = reduce_stage(late_parts, chunks[2:], 1, sizes)
+    small = small_step(small, 1, sizes)
+    late_parts, small, long_terms = lax.optimization_barrier((late_parts, small, long_terms))
+    late_total = reduce_last(late_parts, sizes)
+    small = small_step(small_step(small, 2, sizes), 0, sizes)
+    long_terms = reduce_axis(long_terms, "fx", nx, 1).astype(BF)
+    late_total, small, long_terms = lax.optimization_barrier((late_total, small, long_terms))
+    if early:
+        def whole_early(share):
+            extra = reduce_core(*spread_early(targets, grad_w_qkv, buffer_shapes[:2]), chunks[:2], sizes)
+            for stage in range(2):
+                extra = reduce_stage(extra, chunks, stage, sizes)
+            return share + reduce_last(extra, sizes)
+
+        reduced = [lax.cond(late_fits, lambda share: share, whole_early, reduced[0])]
+    owned_grads = jnp.concatenate(reduced + [late_total])
+
+    squares = jnp.sum(owned_grads * owned_grads) + jnp.sum(small * small)
+    carried = jnp.concatenate([small, jnp.full((128,), squares, F32)])
+    carried = gather_axis(carried, "fz", nz)
+    carried = gather_axis(carried, "fx", nx)
+    raw = raw_products(own_ranks, owned_grads, basis_left, basis_right)
+    carried = gather_axis(carried, "by", ny)
+    carried, raw = lax.optimization_barrier((carried, raw))
+    carried = gather_axis(carried, "core", nc)
+    share = small.shape[0]
+    grad_norm = jnp.sqrt(jnp.sum(carried[..., share]))
+    factor = 1.0 / jnp.maximum(grad_norm, CLIP_NORM)
+    long_terms, to_previous, to_next, factor = lax.optimization_barrier((long_terms, to_previous, to_next, factor))
+    long_total = reduce_axis(long_terms, "fz", nz)
+    from_next = lax.ppermute(to_previous, FRAME_AXES, back_perm)
+    from_previous = lax.ppermute(to_next, FRAME_AXES, frame_perm)
+    carried = carried[..., :share]
     for axis, size in enumerate(sizes):
-        small_sum = rolled(small_sum, axis, size, coords[axis])
-    for axis in range(4):
-        small_sum = reduce_axis(small_sum, ALL_AXES[axis], sizes[axis])
-    squares = jnp.sum(owned_grads * owned_grads) + jnp.sum(small_sum * small_sum)
-    carried = jnp.concatenate([small_sum, jnp.full((128,), squares, F32)])
-    for axis in reversed(range(4)):
-        carried = gather_axis(carried, ALL_AXES[axis], sizes[axis])
-    for axis, size in enumerate(sizes):
-        carried = rolled(carried, axis, size, size - coords[axis])
-    carried = carried.reshape(device_count, share + 128)
-    small_grad = carried[:, :share].reshape(-1)[:small_total]
-    grad_norm = jnp.sqrt(jnp.sum(carried[:, share]))
-    factor = 1.0 / jnp.maximum(grad_norm, CLIP_NORM)
+        carried = rolled(carried, 3 - axis, size, size - coords[axis])
+    small_grad = carried.transpose(3, 2, 1, 0, 4).reshape(-1)[:small_total]
 
     small_first, small_second, small_new = adam_update(
         small_grad * factor, small_params, small_moment1, small_moment2
     )
 
-    long_terms, partner_term, factor = lax.optimization_barrier(
-        (long_terms, seen_frames[frame_count + 1], factor)
-    )
-    long_total = reduce_axis(long_terms, "fz", nz)
-    soap_out = soap(
-        own_ranks, owned_grads, factor, stat_parts, master, moment1, moment2, stat_left, stat_right,
-        basis_left, basis_right,
-    )
-    nothing = jnp.zeros_like(partner_term)
-    to_previous = jnp.where(with_previous, partner_term, nothing)
-    to_next = jnp.where(with_next, partner_term, nothing)
-    short_total = (
-        seen_frames[frame_count].astype(F32)
-        + lax.ppermute(to_previous, FRAME_AXES, back_perm).astype(F32)
-        + lax.ppermute(to_next, FRAME_AXES, frame_perm).astype(F32)
-    )
+    soap_out = finish(
+        factor.reshape(1), *raw, *stat_parts, stat_left, stat_right, basis_left, basis_right, master, moment1, moment2
+    )
+    short_total = seen_frames[frame_count].astype(F32) + from_next.astype(F32) + from_previous.astype(F32)
     grad_normed_one = jnp.concatenate([long_total, short_total]) + grad_own
     hat, spread = normalized(own.astype(F32))
     grad_inputs = grad_mixed + norm_back(grad_normed_one, hat, spread, rows14[0:1])

time: 503 us -> 470 us (0.934)
  starting transfers between devices: 81 us -> 61.3 us
  Pallas kernels: 174 us -> 155 us
  local copies, waits for them, and re-layouts: 33.1 us -> 43.7 us
  other arithmetic: 52.7 us -> 42.4 us
    pallas_call x1, Pallas kernels: 53.1 us -> 32 us  [middle(): pl.pallas_call(kernel, grid_spec=pltpu.PrefetchScalarGridSpec(num_scalar_...]
    ppermute x56 -> x47, starting transfers between devices: 77.4 us -> 57.2 us  [moved(): lax.ppermute(value, axis, [(i, (i + step) % size) for i in range(size)])]
    ppermute x56 -> x47, waiting for transfers between devices: 110 us -> 127 us  [moved(): lax.ppermute(value, axis, [(i, (i + step) % size) for i in range(size)])]
    ppermute x1, waiting for transfers between devices: 21.7 us -> 5.89 us  [on_device(): from_previous = lax.ppermute(short_frame, FRAME_AXES, frame_perm)]
    unnamed x118 -> x97, local copies, waits for them, and re-layouts: 5.58 us -> 12.6 us
    pallas_call x1 -> x2, Pallas kernels: 20.8 us -> 23.6 us  [attend_back(): pl.pallas_call(kernel, grid=(count,), in_specs=[spec(OWN_ROWS), spec(keys...]
  transfers between devices with their start and end apart: 61 -> 52, of which waited for: 24 -> 19; matrix products, arithmetic and copies ran while one was open for 11% -> 12% of each run, Pallas kernels for 18% -> 20%
where the time goes in v4:
time: 470 us; the launch traced here: 461 us
  Pallas kernels  155 us (33%)
  waiting for transfers between devices  136 us (29%)
  starting transfers between devices  61.3 us (13%)
  local copies, waits for them, and re-layouts  43.7 us (9%)
  other arithmetic  42.4 us (9%)
  between operations  22.3 us (5%)
    ppermute x47, waiting for transfers between devices, moved(): lax.ppermute(value, axis, [(i, (i + step) % size) for i in range(size)])  127 us
    ppermute x47, starting transfers between devices, moved(): lax.ppermute(value, axis, [(i, (i + step) % size) for i in range(size)])  57.2 us
    pallas_call x1, Pallas kernels, middle(): pl.pallas_call(kernel, grid_spec=pltpu.PrefetchScalarGridSpec(num_scalar_...  32 us
    pallas_call x1, Pallas kernels, finish(): pl.pallas_call(finish_kernel, in_specs=[pl.BlockSpec(memory_space=pltpu.S...  28.4 us
    pallas_call x2, Pallas kernels, attend_back(): pl.pallas_call(kernel, grid=(count,), in_specs=[spec(OWN_ROWS), spec(keys...  23.6 us
    pallas_call x1, Pallas kernels, project(): pl.pallas_call(kernel, grid_spec=pltpu.PrefetchScalarGridSpec(num_scalar_...  15.7 us
    pallas_call x1, Pallas kernels, qkv_grads(): pl.pallas_call(kernel, grid_spec=pltpu.PrefetchScalarGridSpec(num_scalar_...  15.1 us
    pallas_call x1, Pallas kernels, attend(): pl.pallas_call(kernel, grid=(PAIRS,), in_specs=[pair_spec(OWN_ROWS), pair...  14.5 us
  transfers between devices with their start and end apart: 52, of which 19 were waited for; matrix products, arithmetic and copies ran while one was open for 12% of the time, Pallas kernels for 20%

profile of v4, /device:TPU:15, one launch (start us, length us, event | category | flops | bytes accessed | tf_op | source)
XLA Modules:
  0.0 460.7 jit_solution(15724974976397844947)
XLA Ops:
  7.2 3.0 shard_map.255
  10.5 2.3 collective-permute-start.10
  12.8 2.2 collective-permute-start.11
  30.2 1.9 collective-permute-done.10
  32.1 7.0 %collective-permute-done.11 = bf16[8,128,128]{2,1,0:T(8,128)(2,1)} collective-permute-done((bf16[8,128,128]{2,1,0:T(8,128)(2,1)}, bf16[8,128,128]{2,1,0:T(8,128)(2,1)}, u32[]{:S(2)}, u32[]{:S(2)}) %collective-permute-start.11) | collective-permute-done | bytes 262176 | tf_op jit(solution)/shard_map/ppermute | solution.py:1015
  40.3 5.9 %collective-permute-done.12 = bf16[208,768]{1,0:T(8,128)(2,1)S(1)} collective-permute-done((bf16[208,768]{1,0:T(8,128)(2,1)S(1)}, bf16[208,768]{1,0:T(8,128)(2,1)S(1)}, u32[]{:S(2)}, u32[]{:S(2)}) %collective-permute-start.12) | collective-permute-done | bytes 319520 | tf_op jit(solution)/shard_map/ppermute | solution.py:1308
  50.2 3.0 collective-permute-start.17
  55.4 10.9 %collective-permute-done.15 = bf16[4,4,128,128]{3,2,1,0:T(8,128)(2,1)S(1)} collective-permute-done((bf16[4,4,128,128]{3,2,1,0:T(8,128)(2,1)S(1)}, bf16[4,4,128,128]{3,2,1,0:T(8,128)(2,1)S(1)}, u32[]{:S(2)}, u32[]{:S(2)}) %collective-permute-start.15) | collective-permute-done | bytes 524320 | tf_op jit(solution)/shard_map/ppermute | solution.py:1015
  69.9 3.7 collective-permute-done.16
  73.6 28.9 %collective-permute-done.17 = bf16[2,208,768]{2,1,0:T(8,128)(2,1)} collective-permute-done((bf16[2,208,768]{2,1,0:T(8,128)(2,1)S(1)}, bf16[2,208,768]{2,1,0:T(8,128)(2,1)}, u32[]{:S(2)}, u32[]{:S(2)}) %collective-permute-start.17) | collective-permute-done | bytes 639008 | tf_op jit(solution)/shard_map/ppermute | solution.py:1015
  102.5 5.2 %collective-permute-start.18 = (bf16[2,4,4,128,128]{4,3,2,1,0:T(8,128)(2,1)S(1)}, bf16[2,4,4,128,128]{4,3,2,1,0:T(8,128)(2,1)}, u32[]{:S(2)}, u32[]{:S(2)}) collective-permute-start(bf16[2,4,4,128,128]{4,3,2,1,0:T(8,128)(2,1)S(1)} %pad_maximum_fusion.2), channel_id=1, source_target_pairs={{0,4},{4,0},{1,5},{5,1},{2,6},{6,2},{3,7},{7,3},{8,12},{12,8},{9,1... | collective-permute-start | bytes 3145736 | tf_op jit(solution)/shard_map/ppermute | solution.py:1015
  107.9 1.9 fusion.96.ranks
  111.3 1.6 reshape.343.refs_18_
  114.2 1.9 convert_element_type.279
  116.2 1.7 copy.68
  119.3 3.6 shard_map.256
  126.5 9.0 %collective-permute-done.20 = bf16[2,208,768]{2,1,0:T(8,128)(2,1)S(1)} collective-permute-done((bf16[2,208,768]{2,1,0:T(8,128)(2,1)S(1)}, bf16[2,208,768]{2,1,0:T(8,128)(2,1)S(1)}, u32[]{:S(2)}, u32[]{:S(2)}) %collective-permute-start.20) | collective-permute-done | bytes 639008 | tf_op jit(solution)/shard_map/ppermute | solution.py:1015
  135.5 4.5 collective-permute-start.21
  142.2 2.0 constant_dynamic-update-slice_fusion.7
  144.1 2.0 constant_dynamic-update-slice_fusion.6
  150.8 15.7 %shard_map.257 = (bf16[416,768]{1,0:T(8,128)(2,1)}, bf16[2080,1536]{1,0:T(8,128)(2,1)}, bf16[2080,768]{1,0:T(8,128)(2,1)}, bf16[416,768]{1,0:T(8,128)(2,1)}, bf16[768,2304]{1,0:T(8,128)(2,1)}) custom-call(s32[448]{0:T(512)} %get-tuple-element.166.tiles, s32[1]{0:T(128)} %bitcast.43.early, ...), custom_call_target="tpu_custom_call" | custom-call | bytes 45000000 | tf_op jit(solution)/shard_map/pallas_call | solution.py:541
  166.6 14.5 %shard_map.258 = (bf16[416,768]{1,0:T(8,128)(2,1)}, f32[416,768]{1,0:T(8,128)}) custom-call(bf16[416,768]{1,0:T(8,128)(2,1)} %get-tuple-element.174.refs_0_, bf16[2080,1536]{1,0:T(8,128)(2,1)} %get-tuple-element.175.refs_1_.refs_2_, bf16[2080,1536]{1,0:T(8,128)(2,1)} %get-tuple-element.175.refs_1_.refs_2_, f32[1,2080]{1,0:T(1,128)} %reshape.350.refs_3_), custom_call_target="tpu_custom_call" | custom-call | bytes 36000000 | tf_op jit(solution)/shard_map/pallas_call | solution.py:628
  181.0 32.0 %shard_map.259 = (f32[16,768]{1,0:T(8,128)}, f32[416,768]{1,0:T(8,128)}, bf16[416,768]{1,0:T(8,128)(2,1)}, f32[8,768]{1,0:T(8,128)}, f32[4,768]{1,0:T(4,128)}, /...) custom-call(s32[448]{0:T(512)} %get-tuple-element.158.refs_0_, ...), custom_call_target="tpu_custom_call" | custom-call | bytes 120000000 | tf_op jit(solution)/shard_map/pallas_call | solution.py:880
  213.4 11.7 %shard_map.260 = (bf16[416,768]{1,0:T(8,128)(2,1)}, bf16[2080,768]{1,0:T(8,128)(2,1)}, bf16[2080,768]{1,0:T(8,128)(2,1)}) custom-call(bf16[416,768]{1,0:T(8,128)(2,1)} %get-tuple-element.174.refs_0_, bf16[2080,1536]{1,0:T(8,128)(2,1)} %get-tuple-element.175.refs_1_.refs_2_, bf16[2080,1536]{1,0:T(8,128)(2,1)} %get-tuple-element.175.refs_1_.refs_2_, ...), custom_call_target="tpu_custom_call" | custom-call | bytes 36000000 | tf_op jit(solution)/shard_map/pallas_call | solution.py:656
  225.2 3.2 add_convert_fusion.2
  230.2 11.9 %shard_map.261 = (bf16[416,768]{1,0:T(8,128)(2,1)}, bf16[2080,768]{1,0:T(8,128)(2,1)}, bf16[2080,768]{1,0:T(8,128)(2,1)}) custom-call(bf16[416,768]{1,0:T(8,128)(2,1)} %get-tuple-element.174.refs_0_, bf16[2080,1536]{1,0:T(8,128)(2,1)} %get-tuple-element.175.refs_1_.refs_2_, ...), custom_call_target="tpu_custom_call", output_to_operand_aliasing={{0}: (7, {}), {1}: (8, {}), {2}: (9, {})} | custom-call | bytes 36000000 | tf_op jit(solution)/shard_map/pallas_call | solution.py:656
  242.1 5.7 %collective-permute-done.27 = bf16[2,4,3,128,128]{4,3,2,1,0:T(8,128)(2,1)} collective-permute-done((bf16[2,4,3,128,128]{4,3,2,1,0:T(8,128)(2,1)S(1)}, bf16[2,4,3,128,128]{4,3,2,1,0:T(8,128)(2,1)}, u32[]{:S(2)}, u32[]{:S(2)}) %collective-permute-start.27) | collective-permute-done | bytes 786464 | tf_op jit(solution)/shard_map/ppermute | solution.py:1015
  251.2 15.1 %shard_map.262 = (bf16[128,128,128]{2,1,0:T(8,128)(2,1)}, bf16[128,128,128]{2,1,0:T(8,128)(2,1)}, bf16[768,2304]{1,0:T(8,128)(2,1)}) custom-call(s32[448]{0:T(512)S(1)} %select_reduce_fusion.3.refs_2_.targets, bf16[2080,768]{1,0:T(8,128)(2,1)} %get-tuple-element.199.low, ...), custom_call_target="tpu_custom_call", output_to_operand_aliasing={{0}: (6, {}), {1}: (7, {})} | custom-call | bytes 42000000 | tf_op jit(solution)/shard_map/pallas_call | solution.py:952
  270.5 3.7 collective-permute-start.32
  276.1 12.4 %shard_map.263 = (bf16[2080,768]{1,0:T(8,128)(2,1)}, f32[416,768]{1,0:T(8,128)}, f32[8,768]{1,0:T(8,128)}) custom-call(bf16[2080,768]{1,0:T(8,128)(2,1)} %constant_dynamic-update-slice_fusion.3.refs_9_.seen, bf16[416,768]{1,0:T(8,128)(2,1)} %bitcast.208, bf16[416,768]{1,0:T(8,128)(2,1)} %get-tuple-element.213.dq, bf16[2080,768]{1,0:T(8,128)(2,1)} %get-tuple-element.201.dk, ...), custom_call_target="tpu_custom_call" | custom-call | bytes 36000000 | tf_op jit(solution)/shard_map/pallas_call | solution.py:999
  289.2 1.9 collective-permute-done.33
  292.3 4.0 add_convert_fusion.1
  296.3 1.7 fusion.106
  298.1 1.7 concatenate.50
  307.5 2.0 slice.324
  310.5 19.0 %collective-permute-done.35 = bf16[2,4,4,128,128]{4,3,2,1,0:T(8,128)(2,1)S(1)} collective-permute-done((bf16[2,4,4,128,128]{4,3,2,1,0:T(8,128)(2,1)}, bf16[2,4,4,128,128]{4,3,2,1,0:T(8,128)(2,1)S(1)}, u32[]{:S(2)}, u32[]{:S(2)}) %collective-permute-start.35) | collective-permute-done | bytes 1048608 | tf_op jit(solution)/shard_map/ppermute | solution.py:1015
  334.6 11.6 %collective-permute-done.38 = bf16[4,4,128,128]{3,2,1,0:T(8,128)(2,1)S(1)} collective-permute-done((bf16[4,4,128,128]{3,2,1,0:T(8,128)(2,1)S(1)}, bf16[4,4,128,128]{3,2,1,0:T(8,128)(2,1)S(1)}, u32[]{:S(2)}, u32[]{:S(2)}) %collective-permute-start.38) | collective-permute-done | bytes 524320 | tf_op jit(solution)/shard_map/ppermute | solution.py:1015
  351.2 1.6 collective-permute-start.40
  354.0 2.3 collective-permute-start.46
  356.6 21.4 %collective-permute-done.46 = f32[2176]{0:T(1024)S(1)} collective-permute-done((f32[2176]{0:T(1024)S(1)}, f32[2176]{0:T(1024)S(1)}, u32[]{:S(2)}, u32[]{:S(2)}) %collective-permute-start.46) | collective-permute-done | bytes 8736 | tf_op jit(solution)/shard_map/ppermute | solution.py:1015
  379.1 1.7 pad_maximum_fusion.4
  383.9 1.7 collective-permute-done.49
  391.7 7.0 %shard_map.264 = (f32[14,128,128]{2,1,0:T(8,128)}, f32[14,128,128]{2,1,0:T(8,128)}, f32[14,128,128]{2,1,0:T(8,128)}, f32[14,128,128]{2,1,0:T(8,128)}, f32[14,128,128]{2,1,0:T(8,128)}) custom-call(s32[14]{0:T(128)} %fusion.96.ranks, f32[14,128,128]{2,1,0:T(8,128)} %get-tuple-element.308.refs_0_.refs_1_.refs_2_.refs_3_.refs_4_.refs_5_.refs_6_, ...), custom_call_target="tpu_custom_call" | custom-call | bytes 24000000 | tf_op jit(solution)/shard_map/pallas_call | solution.py:224
  399.1 3.6 collective-permute-start.53
  407.1 1.8 collective-permute-start.54
  408.9 2.0 collective-permute-start.55
  415.6 28.4 %shard_map.265 = (f32[14,128,128]{2,1,0:T(8,128)}, f32[14,128,128]{2,1,0:T(8,128)}, f32[14,128,128]{2,1,0:T(8,128)}, f32[14,128,128]{2,1,0:T(8,128)}, f32[14,128...) custom-call(f32[1]{0:T(128)} %bitcast.104.factor, f32[14,128,128]{2,1,0:T(8,128)} %get-tuple-element.250.refs_0_, ...), custom_call_target="tpu_custom_call" | custom-call | bytes 90000000 | tf_op jit(solution)/shard_map/pallas_call | solution.py:369
  444.0 3.2 collective-permute-done.57
  (327 shorter events, 93.3 us)
Async XLA Ops:
  7.2 143.6 %all-gather.2.cloned.1.call-start = ((), (), s32[]{:S(2)}) async-start(), calls=%async_computation | async-start | bytes 6488064 | tf_op jit(solution)/shard_map/all_gather | solution.py:1304
  10.2 16.1 %collective-permute-start.9 = (bf16[8,128,128]{2,1,0:T(8,128)(2,1)}, bf16[8,128,128]{2,1,0:T(8,128)(2,1)S(1)}, u32[]{:S(2)}, u32[]{:S(2)}) collective-permute-start(bf16[8,128,128]{2,1,0:T(8,128)(2,1)} %get-tuple-element.147), channel_id=1, source_target_pairs={{0,24},{8,0},{16,8},{24,16},{1,25},{9,1},{17,9},{25,17},{2,26},{10... | collective-permute-start | bytes 786440 | tf_op jit(solution)/shard_map/ppermute | solution.py:1015
  10.5 21.6 %collective-permute-start.10 = (bf16[8,128,128]{2,1,0:T(8,128)(2,1)}, bf16[8,128,128]{2,1,0:T(8,128)(2,1)S(1)}, u32[]{:S(2)}, u32[]{:S(2)}) collective-permute-start(bf16[8,128,128]{2,1,0:T(8,128)(2,1)} %get-tuple-element.147), channel_id=1, source_target_pairs={{0,16},{8,24},{16,0},{24,8},{1,17},{9,25},{17,1},{25,9},{2,18},{10... | collective-permute-start | bytes 786440 | tf_op jit(solution)/shard_map/ppermute | solution.py:1015
  12.8 26.4 %collective-permute-start.11 = (bf16[8,128,128]{2,1,0:T(8,128)(2,1)}, bf16[8,128,128]{2,1,0:T(8,128)(2,1)}, u32[]{:S(2)}, u32[]{:S(2)}) collective-permute-start(bf16[8,128,128]{2,1,0:T(8,128)(2,1)} %get-tuple-element.147), channel_id=1, source_target_pairs={{0,8},{8,16},{16,24},{24,0},{1,9},{9,17},{17,25},{25,1},{2,10},{10... | collective-permute-start | bytes 786440 | tf_op jit(solution)/shard_map/ppermute | solution.py:1015
  22.1 18.1 %collective-permute-start.8 = (bf16[208,768]{1,0:T(8,128)(2,1)S(1)}, bf16[208,768]{1,0:T(8,128)(2,1)S(1)}, u32[]{:S(2)}, u32[]{:S(2)}) collective-permute-start(bf16[208,768]{1,0:T(8,128)(2,1)S(1)} %get-tuple-element.314), channel_id=1, source_target_pairs={{0,4},{4,0},{1,5},{5,1},{2,6},{6,2},{3,7},{7,3},{8,12},{12,8},{9,1... | collective-permute-start | bytes 958472 | tf_op jit(solution)/shard_map/ppermute | solution.py:1015
  22.5 23.8 %collective-permute-start.12 = (bf16[208,768]{1,0:T(8,128)(2,1)S(1)}, bf16[208,768]{1,0:T(8,128)(2,1)S(1)}, u32[]{:S(2)}, u32[]{:S(2)}) collective-permute-start(bf16[208,768]{1,0:T(8,128)(2,1)S(1)} %get-tuple-element.313), channel_id=1, source_target_pairs={{0,4},{4,8},{8,12},{12,16},{16,20},{20,24},{24,28},{28,0},{1,5},{5... | collective-permute-start | bytes 958472 | tf_op jit(solution)/shard_map/ppermute | solution.py:1308
  26.4 20.6 %collective-permute-start.13 = (bf16[208,768]{1,0:T(8,128)(2,1)S(1)}, bf16[208,768]{1,0:T(8,128)(2,1)}, u32[]{:S(2)}, u32[]{:S(2)}) collective-permute-start(bf16[208,768]{1,0:T(8,128)(2,1)S(1)} %get-tuple-element.313), channel_id=1, source_target_pairs={{4,0},{8,4},{12,8},{16,12},{20,16},{24,20},{28,24},{0,28},{5,1},{9... | collective-permute-start | bytes 958472 | tf_op jit(solution)/shard_map/ppermute | solution.py:1309
  48.3 18.1 %collective-permute-start.15 = (bf16[4,4,128,128]{3,2,1,0:T(8,128)(2,1)S(1)}, bf16[4,4,128,128]{3,2,1,0:T(8,128)(2,1)S(1)}, u32[]{:S(2)}, u32[]{:S(2)}) collective-permute-start(bf16[4,4,128,128]{3,2,1,0:T(8,128)(2,1)S(1)} %get-tuple-element.306), channel_id=1, source_target_pairs={{0,4},{4,0},{1,5},{5,1},{2,6},{6,2},{3,7},{7,3},{8,12},{12,8},{9,1... | collective-permute-start | bytes 1572872 | tf_op jit(solution)/shard_map/ppermute | solution.py:1015
  49.8 23.8 %collective-permute-start.16 = (bf16[2,208,768]{2,1,0:T(8,128)(2,1)S(1)}, bf16[2,208,768]{2,1,0:T(8,128)(2,1)}, u32[]{:S(2)}, u32[]{:S(2)}) collective-permute-start(bf16[2,208,768]{2,1,0:T(8,128)(2,1)S(1)} %pad_maximum_fusion.5), channel_id=1, source_target_pairs={{0,24},{8,0},{16,8},{24,16},{1,25},{9,1},{17,9},{25,17},{2,26},{10... | collective-permute-start | bytes 1916936 | tf_op jit(solution)/shard_map/ppermute | solution.py:1015
  50.2 52.3 %collective-permute-start.17 = (bf16[2,208,768]{2,1,0:T(8,128)(2,1)S(1)}, bf16[2,208,768]{2,1,0:T(8,128)(2,1)}, u32[]{:S(2)}, u32[]{:S(2)}) collective-permute-start(bf16[2,208,768]{2,1,0:T(8,128)(2,1)S(1)} %pad_maximum_fusion.5), channel_id=1, source_target_pairs={{0,16},{8,24},{16,0},{24,8},{1,17},{9,25},{17,1},{25,9},{2,18},{10... | collective-permute-start | bytes 1916936 | tf_op jit(solution)/shard_map/ppermute | solution.py:1015
  53.2 15.1 %collective-permute-start.14 = (bf16[4,4,128,128]{3,2,1,0:T(8,128)(2,1)S(1)}, bf16[4,4,128,128]{3,2,1,0:T(8,128)(2,1)}, u32[]{:S(2)}, u32[]{:S(2)}) collective-permute-start(bf16[4,4,128,128]{3,2,1,0:T(8,128)(2,1)S(1)} %get-tuple-element.307), channel_id=1, source_target_pairs={{0,2},{2,0},{1,3},{3,1},{4,6},{6,4},{5,7},{7,5},{8,10},{10,8},{9,1... | collective-permute-start | bytes 1572872 | tf_op jit(solution)/shard_map/ppermute | solution.py:1015
  102.5 33.0 %collective-permute-start.18 = (bf16[2,4,4,128,128]{4,3,2,1,0:T(8,128)(2,1)S(1)}, bf16[2,4,4,128,128]{4,3,2,1,0:T(8,128)(2,1)}, u32[]{:S(2)}, u32[]{:S(2)}) collective-permute-start(bf16[2,4,4,128,128]{4,3,2,1,0:T(8,128)(2,1)S(1)} %pad_maximum_fusion.2), channel_id=1, source_target_pairs={{0,4},{4,0},{1,5},{5,1},{2,6},{6,2},{3,7},{7,3},{8,12},{12,8},{9,1... | collective-permute-start | bytes 3145736 | tf_op jit(solution)/shard_map/ppermute | solution.py:1015
  107.7 27.8 %collective-permute-start.19 = (bf16[2,4,4,128,128]{4,3,2,1,0:T(8,128)(2,1)S(1)}, bf16[2,4,4,128,128]{4,3,2,1,0:T(8,128)(2,1)}, u32[]{:S(2)}, u32[]{:S(2)}) collective-permute-start(bf16[2,4,4,128,128]{4,3,2,1,0:T(8,128)(2,1)S(1)} %pad_maximum_fusion.3), channel_id=1, source_target_pairs={{0,2},{2,0},{1,3},{3,1},{4,6},{6,4},{5,7},{7,5},{8,10},{10,8},{9,1... | collective-permute-start | bytes 3145736 | tf_op jit(solution)/shard_map/ppermute | solution.py:1015
  123.1 12.4 %collective-permute-start.20 = (bf16[2,208,768]{2,1,0:T(8,128)(2,1)S(1)}, bf16[2,208,768]{2,1,0:T(8,128)(2,1)S(1)}, u32[]{:S(2)}, u32[]{:S(2)}) collective-permute-start(bf16[2,208,768]{2,1,0:T(8,128)(2,1)S(1)} %pad_maximum_fusion.5), channel_id=1, source_target_pairs={{0,8},{8,16},{16,24},{24,0},{1,9},{9,17},{17,25},{25,1},{2,10},{10... | collective-permute-start | bytes 1916936 | tf_op jit(solution)/shard_map/ppermute | solution.py:1015
  135.5 13.0 %collective-permute-start.21 = (bf16[32,128,128]{2,1,0:T(8,128)(2,1)S(1)}, bf16[32,128,128]{2,1,0:T(8,128)(2,1)S(1)}, u32[]{:S(2)}, u32[]{:S(2)}) collective-permute-start(bf16[32,128,128]{2,1,0:T(8,128)(2,1)S(1)} %bitcast.215), channel_id=1, source_target_pairs={{0,1},{1,0},{2,3},{3,2},{4,5},{5,4},{6,7},{7,6},{8,9},{9,8},{10,11... | collective-permute-start | bytes 3145736 | tf_op jit(solution)/shard_map/ppermute | solution.py:1015
  140.1 8.4 %collective-permute-start.22 = (bf16[32,128,128]{2,1,0:T(8,128)(2,1)}, bf16[32,128,128]{2,1,0:T(8,128)(2,1)S(1)}, u32[]{:S(2)}, u32[]{:S(2)}) collective-permute-start(bf16[32,128,128]{2,1,0:T(8,128)(2,1)} %bitcast.37.refs_2_.refs_5_), channel_id=1, source_target_pairs={{0,1},{1,0},{2,3},{3,2},{4,5},{5,4},{6,7},{7,6},{8,9},{9,8},{10,11... | collective-permute-start | bytes 3145736 | tf_op jit(solution)/shard_map/ppermute | solution.py:1015
  140.2 8.4 %collective-permute-start.23 = (bf16[32,128,128]{2,1,0:T(8,128)(2,1)S(1)}, bf16[32,128,128]{2,1,0:T(8,128)(2,1)S(1)}, u32[]{:S(2)}, u32[]{:S(2)}) collective-permute-start(bf16[32,128,128]{2,1,0:T(8,128)(2,1)S(1)} %bitcast.212), channel_id=1, source_target_pairs={{0,1},{1,0},{2,3},{3,2},{4,5},{5,4},{6,7},{7,6},{8,9},{9,8},{10,11... | collective-permute-start | bytes 3145736 | tf_op jit(solution)/shard_map/ppermute | solution.py:1015
  140.6 10.2 %collective-permute-start.24 = (bf16[32,128,128]{2,1,0:T(8,128)(2,1)}, bf16[32,128,128]{2,1,0:T(8,128)(2,1)}, u32[]{:S(2)}, u32[]{:S(2)}) collective-permute-start(bf16[32,128,128]{2,1,0:T(8,128)(2,1)} %bitcast.39.refs_4_.refs_7_), channel_id=1, source_target_pairs={{0,1},{1,0},{2,3},{3,2},{4,5},{5,4},{6,7},{7,6},{8,9},{9,8},{10,11... | collective-permute-start | bytes 3145736 | tf_op jit(solution)/shard_map/ppermute | solution.py:1015
  213.0 12.2 %collective-permute-start.25 = (bf16[96,128,128]{2,1,0:T(8,128)(2,1)}, bf16[96,128,128]{2,1,0:T(8,128)(2,1)}, u32[]{:S(2)}, u32[]{:S(2)}) collective-permute-start(bf16[96,128,128]{2,1,0:T(8,128)(2,1)} %get-tuple-element.191), channel_id=1, source_target_pairs={{0,1},{1,0},{2,3},{3,2},{4,5},{5,4},{6,7},{7,6},{8,9},{9,8},{10,11... | collective-permute-start | bytes 9437192 | tf_op jit(solution)/shard_map/ppermute | solution.py:1015
  228.7 19.2 %collective-permute-start.27 = (bf16[2,4,3,128,128]{4,3,2,1,0:T(8,128)(2,1)S(1)}, bf16[2,4,3,128,128]{4,3,2,1,0:T(8,128)(2,1)}, u32[]{:S(2)}, u32[]{:S(2)}) collective-permute-start(bf16[2,4,3,128,128]{4,3,2,1,0:T(8,128)(2,1)S(1)} %slice_bitcast_fusion.8), channel_id=1, source_target_pairs={{0,2},{2,0},{1,3},{3,1},{4,6},{6,4},{5,7},{7,5},{8,10},{10,8},{9,1... | collective-permute-start | bytes 2359304 | tf_op jit(solution)/shard_map/ppermute | solution.py:1015
  230.0 19.2 %collective-permute-start.26 = (bf16[2,4,3,128,128]{4,3,2,1,0:T(8,128)(2,1)S(1)}, bf16[2,4,3,128,128]{4,3,2,1,0:T(8,128)(2,1)S(1)}, u32[]{:S(2)}, u32[]{:S(2)}) collective-permute-start(bf16[2,4,3,128,128]{4,3,2,1,0:T(8,128)(2,1)S(1)} %slice_bitcast_fusion.9), channel_id=1, source_target_pairs={{0,4},{4,0},{1,5},{5,1},{2,6},{6,2},{3,7},{7,3},{8,12},{12,8},{9,1... | collective-permute-start | bytes 2359304 | tf_op jit(solution)/shard_map/ppermute | solution.py:1015
  249.6 16.8 %collective-permute-start.29 = (bf16[4,3,128,128]{3,2,1,0:T(8,128)(2,1)S(1)}, bf16[4,3,128,128]{3,2,1,0:T(8,128)(2,1)S(1)}, u32[]{:S(2)}, u32[]{:S(2)}) collective-permute-start(bf16[4,3,128,128]{3,2,1,0:T(8,128)(2,1)S(1)} %slice_bitcast_fusion.12), channel_id=1, source_target_pairs={{0,4},{4,0},{1,5},{5,1},{2,6},{6,2},{3,7},{7,3},{8,12},{12,8},{9,1... | collective-permute-start | bytes 1179656 | tf_op jit(solution)/shard_map/ppermute | solution.py:1015
  249.9 16.6 %collective-permute-start.28 = (bf16[4,3,128,128]{3,2,1,0:T(8,128)(2,1)S(1)}, bf16[4,3,128,128]{3,2,1,0:T(8,128)(2,1)S(1)}, u32[]{:S(2)}, u32[]{:S(2)}) collective-permute-start(bf16[4,3,128,128]{3,2,1,0:T(8,128)(2,1)S(1)} %slice_bitcast_fusion.13), channel_id=1, source_target_pairs={{0,2},{2,0},{1,3},{3,1},{4,6},{6,4},{5,7},{7,5},{8,10},{10,8},{9,1... | collective-permute-start | bytes 1179656 | tf_op jit(solution)/shard_map/ppermute | solution.py:1015
  266.7 25.6 %collective-permute-start.30 = (bf16[128,128,128]{2,1,0:T(8,128)(2,1)}, bf16[128,128,128]{2,1,0:T(8,128)(2,1)}, u32[]{:S(2)}, u32[]{:S(2)}) collective-permute-start(bf16[128,128,128]{2,1,0:T(8,128)(2,1)} %get-tuple-element.210), channel_id=1, source_target_pairs={{0,1},{1,0},{2,3},{3,2},{4,5},{5,4},{6,7},{7,6},{8,9},{9,8},{10,11... | collective-permute-start | bytes 12582920 | tf_op jit(solution)/shard_map/ppermute | solution.py:1015
  268.9 19.6 %collective-permute-start.31 = (bf16[6,128,128]{2,1,0:T(8,128)(2,1)}, bf16[6,128,128]{2,1,0:T(8,128)(2,1)S(1)}, u32[]{:S(2)}, u32[]{:S(2)}) collective-permute-start(bf16[6,128,128]{2,1,0:T(8,128)(2,1)} %get-tuple-element.310), channel_id=1, source_target_pairs={{0,8},{8,16},{16,24},{24,0},{1,9},{9,17},{17,25},{25,1},{2,10},{10... | collective-permute-start | bytes 589832 | tf_op jit(solution)/shard_map/ppermute | solution.py:1015
  270.5 18.0 %collective-permute-start.32 = (bf16[6,128,128]{2,1,0:T(8,128)(2,1)S(1)}, bf16[6,128,128]{2,1,0:T(8,128)(2,1)S(1)}, u32[]{:S(2)}, u32[]{:S(2)}) collective-permute-start(bf16[6,128,128]{2,1,0:T(8,128)(2,1)S(1)} %get-tuple-element.312), channel_id=1, source_target_pairs={{0,16},{8,24},{16,0},{24,8},{1,17},{9,25},{17,1},{25,9},{2,18},{10... | collective-permute-start | bytes 589832 | tf_op jit(solution)/shard_map/ppermute | solution.py:1015
  274.2 16.9 %collective-permute-start.33 = (bf16[6,128,128]{2,1,0:T(8,128)(2,1)S(1)}, bf16[6,128,128]{2,1,0:T(8,128)(2,1)}, u32[]{:S(2)}, u32[]{:S(2)}) collective-permute-start(bf16[6,128,128]{2,1,0:T(8,128)(2,1)S(1)} %get-tuple-element.311), channel_id=1, source_target_pairs={{0,24},{8,0},{16,8},{24,16},{1,25},{9,1},{17,9},{25,17},{2,26},{10... | collective-permute-start | bytes 589832 | tf_op jit(solution)/shard_map/ppermute | solution.py:1015
  302.7 6.8 %collective-permute-start.36 = (f32[2,2,4,2176]{3,1,0,2:T(2,128)}, f32[2,2,4,2176]{3,1,0,2:T(2,128)}, u32[]{:S(2)}, u32[]{:S(2)}) collective-permute-start(f32[2,2,4,2176]{3,1,0,2:T(2,128)} %bitcast.203), channel_id=1, source_target_pairs={{0,1},{1,0},{2,3},{3,2},{4,5},{5,4},{6,7},{7,6},{8,9},{9,8},{10,11... | collective-permute-start | bytes 417800 | tf_op jit(solution)/shard_map/ppermute | solution.py:1015
  304.6 25.0 %collective-permute-start.35 = (bf16[2,4,4,128,128]{4,3,2,1,0:T(8,128)(2,1)}, bf16[2,4,4,128,128]{4,3,2,1,0:T(8,128)(2,1)S(1)}, u32[]{:S(2)}, u32[]{:S(2)}) collective-permute-start(bf16[2,4,4,128,128]{4,3,2,1,0:T(8,128)(2,1)} %slice_bitcast_fusion.6), channel_id=1, source_target_pairs={{0,2},{2,0},{1,3},{3,1},{4,6},{6,4},{5,7},{7,5},{8,10},{10,8},{9,1... | collective-permute-start | bytes 3145736 | tf_op jit(solution)/shard_map/ppermute | solution.py:1015
  306.2 24.7 %collective-permute-start.34 = (bf16[2,4,4,128,128]{4,3,2,1,0:T(8,128)(2,1)}, bf16[2,4,4,128,128]{4,3,2,1,0:T(8,128)(2,1)S(1)}, u32[]{:S(2)}, u32[]{:S(2)}) collective-permute-start(bf16[2,4,4,128,128]{4,3,2,1,0:T(8,128)(2,1)} %slice_bitcast_fusion.7), channel_id=1, source_target_pairs={{0,4},{4,0},{1,5},{5,1},{2,6},{6,2},{3,7},{7,3},{8,12},{12,8},{9,1... | collective-permute-start | bytes 3145736 | tf_op jit(solution)/shard_map/ppermute | solution.py:1015
  332.6 13.6 %collective-permute-start.38 = (bf16[4,4,128,128]{3,2,1,0:T(8,128)(2,1)S(1)}, bf16[4,4,128,128]{3,2,1,0:T(8,128)(2,1)S(1)}, u32[]{:S(2)}, u32[]{:S(2)}) collective-permute-start(bf16[4,4,128,128]{3,2,1,0:T(8,128)(2,1)S(1)} %slice_bitcast_fusion.10), channel_id=1, source_target_pairs={{0,4},{4,0},{1,5},{5,1},{2,6},{6,2},{3,7},{7,3},{8,12},{12,8},{9,1... | collective-permute-start | bytes 1572872 | tf_op jit(solution)/shard_map/ppermute | solution.py:1015
  333.0 13.4 %collective-permute-start.37 = (bf16[4,4,128,128]{3,2,1,0:T(8,128)(2,1)S(1)}, bf16[4,4,128,128]{3,2,1,0:T(8,128)(2,1)S(1)}, u32[]{:S(2)}, u32[]{:S(2)}) collective-permute-start(bf16[4,4,128,128]{3,2,1,0:T(8,128)(2,1)S(1)} %slice_bitcast_fusion.11), channel_id=1, source_target_pairs={{0,2},{2,0},{1,3},{3,1},{4,6},{6,4},{5,7},{7,5},{8,10},{10,8},{9,1... | collective-permute-start | bytes 1572872 | tf_op jit(solution)/shard_map/ppermute | solution.py:1015
  346.6 31.5 %collective-permute-start.47 = (bf16[4,208,768]{2,1,0:T(8,128)(2,1)S(1)}, bf16[4,208,768]{2,1,0:T(8,128)(2,1)S(1)}, u32[]{:S(2)}, u32[]{:S(2)}) collective-permute-start(bf16[4,208,768]{2,1,0:T(8,128)(2,1)S(1)} %slice_bitcast_fusion.4), channel_id=1, source_target_pairs={{0,4},{4,0},{1,5},{5,1},{2,6},{6,2},{3,7},{7,3},{8,12},{12,8},{9,1... | collective-permute-start | bytes 3833864 | tf_op jit(solution)/shard_map/ppermute | solution.py:1015
  349.9 4.0 collective-permute-start.44
  350.0 4.0 collective-permute-start.45
  351.2 26.8 %collective-permute-start.40 = (bf16[8,128,128]{2,1,0:T(8,128)(2,1)S(1)}, bf16[8,128,128]{2,1,0:T(8,128)(2,1)S(1)}, u32[]{:S(2)}, u32[]{:S(2)}) collective-permute-start(bf16[8,128,128]{2,1,0:T(8,128)(2,1)S(1)} %get-tuple-element.301), channel_id=1, source_target_pairs={{0,8},{8,16},{16,24},{24,0},{1,9},{9,17},{17,25},{25,1},{2,10},{10... | collective-permute-start | bytes 786440 | tf_op jit(solution)/shard_map/ppermute | solution.py:1015
  352.7 25.3 %collective-permute-start.41 = (bf16[8,128,128]{2,1,0:T(8,128)(2,1)S(1)}, bf16[8,128,128]{2,1,0:T(8,128)(2,1)S(1)}, u32[]{:S(2)}, u32[]{:S(2)}) collective-permute-start(bf16[8,128,128]{2,1,0:T(8,128)(2,1)S(1)} %get-tuple-element.303), channel_id=1, source_target_pairs={{0,16},{8,24},{16,0},{24,8},{1,17},{9,25},{17,1},{25,9},{2,18},{10... | collective-permute-start | bytes 786440 | tf_op jit(solution)/shard_map/ppermute | solution.py:1015
  354.0 24.1 %collective-permute-start.42 = (bf16[8,128,128]{2,1,0:T(8,128)(2,1)S(1)}, bf16[8,128,128]{2,1,0:T(8,128)(2,1)S(1)}, u32[]{:S(2)}, u32[]{:S(2)}) collective-permute-start(bf16[8,128,128]{2,1,0:T(8,128)(2,1)S(1)} %get-tuple-element.302), channel_id=1, source_target_pairs={{0,24},{8,0},{16,8},{24,16},{1,25},{9,1},{17,9},{25,17},{2,26},{10... | collective-permute-start | bytes 786440 | tf_op jit(solution)/shard_map/ppermute | solution.py:1015
  354.0 24.0 %collective-permute-start.46 = (f32[2176]{0:T(1024)S(1)}, f32[2176]{0:T(1024)S(1)}, u32[]{:S(2)}, u32[]{:S(2)}) collective-permute-start(f32[2176]{0:T(1024)S(1)} %get-tuple-element.267), channel_id=1, source_target_pairs={{0,24},{8,0},{16,8},{24,16},{1,25},{9,1},{17,9},{25,17},{2,26},{10... | collective-permute-start | bytes 26120 | tf_op jit(solution)/shard_map/ppermute | solution.py:1015
  382.1 3.5 collective-permute-start.49
  382.3 3.7 collective-permute-start.48
  389.0 9.9 %collective-permute-start.52 = (f32[2,4,2304]{2,0,1:T(2,128)S(1)}, f32[2,4,2304]{2,0,1:T(2,128)S(1)}, u32[]{:S(2)}, u32[]{:S(2)}) collective-permute-start(f32[2,4,2304]{2,0,1:T(2,128)S(1)} %get-tuple-element.322), channel_id=1, source_target_pairs={{0,2},{2,0},{1,3},{3,1},{4,6},{6,4},{5,7},{7,5},{8,10},{10,8},{9,1... | collective-permute-start | bytes 221192 | tf_op jit(solution)/shard_map/ppermute | solution.py:1015
  399.1 4.8 %collective-permute-start.53 = (f32[2,2,4,2304]{3,0,1,2:T(2,128)S(1)}, f32[2,2,4,2304]{3,0,1,2:T(2,128)S(1)}, u32[]{:S(2)}, u32[]{:S(2)}) collective-permute-start(f32[2,2,4,2304]{3,0,1,2:T(2,128)S(1)} %pad_maximum_fusion.7), channel_id=1, source_target_pairs={{0,1},{1,0},{2,3},{3,2},{4,5},{5,4},{6,7},{7,6},{8,9},{9,8},{10,11... | collective-permute-start | bytes 442376 | tf_op jit(solution)/shard_map/ppermute | solution.py:1015
  407.1 41.2 %collective-permute-start.54 = (bf16[208,768]{1,0:T(8,128)(2,1)S(1)}, bf16[208,768]{1,0:T(8,128)(2,1)S(1)}, u32[]{:S(2)}, u32[]{:S(2)}) collective-permute-start(bf16[208,768]{1,0:T(8,128)(2,1)S(1)} %get-tuple-element.298), channel_id=1, source_target_pairs={{0,8},{8,16},{16,24},{24,0},{1,9},{9,17},{17,25},{25,1},{2,10},{10... | collective-permute-start | bytes 958472 | tf_op jit(solution)/shard_map/ppermute | solution.py:1015
  408.9 39.4 %collective-permute-start.55 = (bf16[208,768]{1,0:T(8,128)(2,1)S(1)}, bf16[208,768]{1,0:T(8,128)(2,1)S(1)}, u32[]{:S(2)}, u32[]{:S(2)}) collective-permute-start(bf16[208,768]{1,0:T(8,128)(2,1)S(1)} %get-tuple-element.300), channel_id=1, source_target_pairs={{0,16},{8,24},{16,0},{24,8},{1,17},{9,25},{17,1},{25,9},{2,18},{10... | collective-permute-start | bytes 958472 | tf_op jit(solution)/shard_map/ppermute | solution.py:1015
  410.9 37.4 %collective-permute-start.56 = (bf16[208,768]{1,0:T(8,128)(2,1)S(1)}, bf16[208,768]{1,0:T(8,128)(2,1)S(1)}, u32[]{:S(2)}, u32[]{:S(2)}) collective-permute-start(bf16[208,768]{1,0:T(8,128)(2,1)S(1)} %get-tuple-element.299), channel_id=1, source_target_pairs={{0,24},{8,0},{16,8},{24,16},{1,25},{9,1},{17,9},{25,17},{2,26},{10... | collective-permute-start | bytes 958472 | tf_op jit(solution)/shard_map/ppermute | solution.py:1015
  412.0 35.2 %collective-permute-start.57 = (bf16[208,768]{1,0:T(8,128)(2,1)S(1)}, bf16[208,768]{1,0:T(8,128)(2,1)S(1)}, u32[]{:S(2)}, u32[]{:S(2)}) collective-permute-start(bf16[208,768]{1,0:T(8,128)(2,1)S(1)} %get-tuple-element.246), channel_id=1, source_target_pairs={{4,0},{8,4},{12,8},{16,12},{20,16},{24,20},{28,24},{0,28},{5,1},{9... | collective-permute-start | bytes 958472 | tf_op jit(solution)/shard_map/ppermute | solution.py:1445
  413.3 33.9 %collective-permute-start.58 = (bf16[208,768]{1,0:T(8,128)(2,1)S(1)}, bf16[208,768]{1,0:T(8,128)(2,1)S(1)}, u32[]{:S(2)}, u32[]{:S(2)}) collective-permute-start(bf16[208,768]{1,0:T(8,128)(2,1)S(1)} %get-tuple-element.247), channel_id=1, source_target_pairs={{0,4},{4,8},{8,12},{12,16},{16,20},{20,24},{24,28},{28,0},{1,5},{5... | collective-permute-start | bytes 958472 | tf_op jit(solution)/shard_map/ppermute | solution.py:1446
  (48 other events, 648.9 us)
Sparse Core Ops, SparseCore 0:
  11.5 110.3 all-gather.1

commit v5 on v4

--- a/solution.py
+++ b/solution.py
@@ -1029,6 +1029,21 @@
 
 def gather_axis(value, axis, size):
     return jnp.stack([value] + [moved(value, axis, size, -step) for step in range(1, size)])
+
+
+def line_step(state, axis, size):
+    onward, backward = state
+    up = [(i, i + 1) for i in range(size - 1)]
+    down = [(i + 1, i) for i in range(size - 1)]
+    return lax.ppermute(onward, axis, down), lax.ppermute(backward, axis, up)
+
+
+def line_pieces(value, steps, axis, size):
+    coord = lax.axis_index(axis)
+    pieces = [value]
+    for step in range(1, size):
+        pieces.append(jnp.where(coord + step < size, steps[step - 1][0], steps[size - step - 1][1]))
+    return pieces
 
 
 def rolled(value, axis, size, step):
@@ -1126,27 +1141,42 @@
 
 def reduce_core(kept, sent, chunks, sizes):
     size_of = dict(zip(ALL_AXES, sizes))
-    total = (kept.astype(F32) + moved(sent, "core", 2, 1).astype(F32)).astype(BF)
+    received = moved(sent, "core", 2, 1)
     parts = []
     start = 0
     for first, count, axes in chunks:
-        shape = [size_of[name] for name in axes] + [count, BLOCK_SIDE, BLOCK_SIDE]
-        stop = start + math.prod(shape[:-2])
-        parts.append(total[start:stop].reshape(shape))
-        start = stop
+        shape = [size_of[name] for name in axes[1:]] + [count, BLOCK_SIDE, BLOCK_SIDE]
+        length = math.prod(shape[:-2])
+        terms = []
+        for _ in range(size_of[axes[0]]):
+            stop = start + length
+            total = kept[start:stop].astype(F32) + received[start:stop].astype(F32)
+            terms.append(total.astype(BF).reshape(shape))
+            start = stop
+        parts.append(terms)
     return parts
 
 
 def reduce_stage(parts, chunks, stage, sizes):
     results = []
-    for part, (first, count, axes) in zip(parts, chunks):
-        name = axes[stage]
-        results.append(reduce_axis(part, name, sizes[ALL_AXES.index(name)]).astype(BF))
+    for terms, (first, count, axes) in zip(parts, chunks):
+        received = [moved(terms[step], axes[stage], len(terms), step) for step in range(1, len(terms))]
+        following = []
+        for index in range(terms[0].shape[0]):
+            total = terms[0][index].astype(F32)
+            for term in received:
+                total = total + term[index].astype(F32)
+            following.append(total.astype(BF))
+        results.append(following)
     return results
 
 
 def reduce_last(parts, sizes):
-    return reduce_axis(jnp.concatenate(parts, axis=1), "fz", sizes[0])
+    terms = [jnp.concatenate(pieces) for pieces in zip(*parts)]
+    total = terms[0].astype(F32)
+    for step in range(1, len(terms)):
+        total = total + moved(terms[step], "fz", sizes[0], step).astype(F32)
+    return total
 
 
 def gather_stage(shard, axes, stage, sizes):
@@ -1300,23 +1330,6 @@
     long_frame, short_frame = own_frames[0], own_frames[1]
     frame_perm = [(i, (i + 1) % frame_count) for i in range(frame_count)]
     back_perm = [(j, i) for i, j in frame_perm]
-    def gather_early(shard):
-        return lax.all_gather(shard, ALL_AXES, axis=0, tiled=True)
-
-    weights = [gather_early(shards[0])] if early else []
-    long_pair = gather_axis(long_frame, "fx", nx)
-    from_previous = lax.ppermute(short_frame, FRAME_AXES, frame_perm)
-    from_next = lax.ppermute(short_frame, FRAME_AXES, back_perm)
-    long_pair, late_shards, from_previous, from_next = lax.optimization_barrier(
-        (long_pair, late_shards, from_previous, from_next)
-    )
-    late_shards = [late_shards[:, : chunks[2][1]], late_shards[:, chunks[2][1] :]]
-    late_shards = [gather_stage(part, orders[2 + i], 1, sizes) for i, part in enumerate(late_shards)]
-    long_frames = [long_pair] + [moved(long_pair, "fz", nz, -step) for step in range(1, nz)]
-    late_shards, long_frames[1:-1] = lax.optimization_barrier((late_shards, long_frames[1:-1]))
-    late_pieces = gather_last(late_shards, orders[2:], sizes)
-    partner = jnp.where(with_next, from_next, from_previous)
-
     frames_seen = frame_count + 2
     own = own_frames.reshape(OWN_ROWS, D)
     row_ids = jnp.arange(frames_seen * PAD_ROWS, dtype=jnp.int32)
@@ -1339,19 +1352,44 @@
     arriving = cotangent[0].reshape(2, NT, D)
     arriving = jnp.where(swap, arriving[::-1], arriving).reshape(2 * NT, D)
 
+    early_looked = jnp.where(late_fits, 0, device_count * early).astype(jnp.int32).reshape(1)
     stat_parts = stat_products(stat_left, stat_right, basis_left, basis_right)
-    early_looked = jnp.where(late_fits, 0, device_count * early).astype(jnp.int32).reshape(1)
-
+
+    def gather_early(shard):
+        return lax.all_gather(shard, ALL_AXES, axis=0, tiled=True)
+
+    weights = [gather_early(shards[0])] if early else []
+    long_pair = gather_axis(long_frame, "fx", nx)
+    from_previous = lax.ppermute(short_frame, FRAME_AXES, frame_perm)
+    from_next = lax.ppermute(short_frame, FRAME_AXES, back_perm)
     (
-        late_pieces, long_frames, partner, stat_parts, key_bias, targets, qkv_tiles, held_tiles, sent_tiles, own_ranks,
-        early_looked, rows14, conv_t, taps_forward, taps_backward, tail_bias, arriving,
+        long_pair, late_shards, from_previous, from_next, targets, qkv_tiles, held_tiles, sent_tiles, own_ranks, early_looked,
     ) = lax.optimization_barrier(
         (
-            late_pieces, long_frames, partner, stat_parts, key_bias, targets, qkv_tiles, held_tiles, sent_tiles, own_ranks,
-            early_looked, rows14, conv_t, taps_forward, taps_backward, tail_bias, arriving,
+            long_pair, late_shards, from_previous, from_next, targets, qkv_tiles, held_tiles, sent_tiles, own_ranks,
+            early_looked,
         )
     )
+    late_shards = [late_shards[:, : chunks[2][1]], late_shards[:, chunks[2][1] :]]
+    late_shards = [gather_stage(part, orders[2 + i], 1, sizes) for i, part in enumerate(late_shards)]
+    line = [line_step((long_pair, long_pair), "fz", nz)]
+    partner = jnp.where(with_next, from_next, from_previous)
+    (
+        late_shards, line[0], partner, stat_parts, key_bias, rows14, conv_t, taps_forward, taps_backward, tail_bias, arriving,
+    ) = lax.optimization_barrier(
+        (
+            late_shards, line[0], partner, stat_parts, key_bias, rows14, conv_t, taps_forward, taps_backward, tail_bias,
+            arriving,
+        )
+    )
+    late_pieces = gather_last(late_shards, orders[2:], sizes)
+    line.append(line_step(line[-1], "fz", nz))
+
+
     weights = weights + late_pieces + [moved(piece, "core", nc, 1) for piece in late_pieces]
+    for _ in range(nz - 3):
+        line.append(line_step(line[-1], "fz", nz))
+    long_frames = line_pieces(long_pair, line, "fz", nz)
     seen = jnp.concatenate(
         [frames.reshape(-1, D) for frames in long_frames] + [short_frame, partner]
     )
@@ -1389,12 +1427,6 @@
     grad_seen, grad_own, sums = input_grads(seen, own, grad_query, grad_key, grad_value, w_qkv)
     late_parts, reduced, grad_seen, sums = lax.optimization_barrier((late_parts, reduced, grad_seen, sums))
 
-    seen_frames = grad_seen.reshape(frames_seen, PAD_ROWS, D)
-    long_terms = seen_frames[:frame_count].reshape(nz, nx, PAD_ROWS, D)
-    partner_term = seen_frames[frame_count + 1]
-    nothing = jnp.zeros_like(partner_term)
-    to_previous = jnp.where(with_previous, partner_term, nothing)
-    to_next = jnp.where(with_next, partner_term, nothing)
     late_parts = reduce_stage(late_parts, chunks[2:], 0, sizes)
     small_local = jnp.concatenate(
         [
@@ -1411,10 +1443,18 @@
     )
     small_total = small_local.shape[0]
     small = small_step(small_shares(small_local, sizes, coords), 3, sizes)
-    late_parts, small = lax.optimization_barrier((late_parts, small))
+    late_parts, small, grad_seen = lax.optimization_barrier((late_parts, small, grad_seen))
+    seen_frames = grad_seen.reshape(frames_seen, PAD_ROWS, D)
+    long_terms = seen_frames[:frame_count].reshape(nz, nx, PAD_ROWS, D)
+    partner_term = seen_frames[frame_count + 1]
+    nothing = jnp.zeros_like(partner_term)
+    to_previous = jnp.where(with_previous, partner_term, nothing)
+    to_next = jnp.where(with_next, partner_term, nothing)
     late_parts = reduce_stage(late_parts, chunks[2:], 1, sizes)
     small = small_step(small, 1, sizes)
-    late_parts, small, long_terms = lax.optimization_barrier((late_parts, small, long_terms))
+    late_parts, small, long_terms, to_previous, to_next = lax.optimization_barrier(
+        (late_parts, small, long_terms, to_previous, to_next)
+    )
     late_total = reduce_last(late_parts, sizes)
     small = small_step(small_step(small, 2, sizes), 0, sizes)
     long_terms = reduce_axis(long_terms, "fx", nx, 1).astype(BF)

time: 470 us -> 460 us (0.979)
  local copies, waits for them, and re-layouts: 43.7 us -> 26.4 us
  waiting for transfers between devices: 136 us -> 121 us
  starting transfers between devices: 61.3 us -> 76.1 us
  Pallas kernels: 155 us -> 166 us
    ppermute x47 -> x44, waiting for transfers between devices: 127 us -> 74.9 us  [moved(): lax.ppermute(value, axis, [(i, (i + step) % size) for i in range(size)])]
    ppermute x0 -> x6, waiting for transfers between devices: none -> 38.7 us  [line_step(): return (lax.ppermute(onward, axis, down), lax.ppermute(backward, axis, up))]
    ppermute x0 -> x6, starting transfers between devices: none -> 19.2 us  [line_step(): return (lax.ppermute(onward, axis, down), lax.ppermute(backward, axis, up))]
    pallas_call x1, Pallas kernels: 32 us -> 43.5 us  [middle(): pl.pallas_call(kernel, grid_spec=pltpu.PrefetchScalarGridSpec(num_scalar_...]
    ppermute x47 -> x44, starting transfers between devices: 57.2 us -> 52.8 us  [moved(): lax.ppermute(value, axis, [(i, (i + step) % size) for i in range(size)])]
    unnamed x97 -> x69, local copies, waits for them, and re-layouts: 12.6 us -> 8.92 us
  transfers between devices with their start and end apart: 52 -> 55, of which waited for: 19 -> 19; matrix products, arithmetic and copies ran while one was open for 12% -> 10% of each run, Pallas kernels for 20% -> 20%
where the time goes in v5:
time: 460 us; the launch traced here: 454 us
  Pallas kernels  166 us (36%)
  waiting for transfers between devices  121 us (26%)
  starting transfers between devices  76.1 us (17%)
  other arithmetic  43.1 us (9%)
  local copies, waits for them, and re-layouts  26.4 us (6%)
  between operations  21.9 us (5%)
    ppermute x44, waiting for transfers between devices, moved(): lax.ppermute(value, axis, [(i, (i + step) % size) for i in range(size)])  74.9 us
    ppermute x44, starting transfers between devices, moved(): lax.ppermute(value, axis, [(i, (i + step) % size) for i in range(size)])  52.8 us
    pallas_call x1, Pallas kernels, middle(): pl.pallas_call(kernel, grid_spec=pltpu.PrefetchScalarGridSpec(num_scalar_...  43.5 us
    ppermute x6, waiting for transfers between devices, line_step(): return (lax.ppermute(onward, axis, down), lax.ppermute(backward, axis, up))  38.7 us
    pallas_call x1, Pallas kernels, finish(): pl.pallas_call(finish_kernel, in_specs=[pl.BlockSpec(memory_space=pltpu.S...  28.3 us
    pallas_call x2, Pallas kernels, attend_back(): pl.pallas_call(kernel, grid=(count,), in_specs=[spec(OWN_ROWS), spec(keys...  23.2 us
    ppermute x6, starting transfers between devices, line_step(): return (lax.ppermute(onward, axis, down), lax.ppermute(backward, axis, up))  19.2 us
    pallas_call x1, Pallas kernels, project(): pl.pallas_call(kernel, grid_spec=pltpu.PrefetchScalarGridSpec(num_scalar_...  15.7 us
  transfers between devices with their start and end apart: 55, of which 19 were waited for; matrix products, arithmetic and copies ran while one was open for 10% of the time, Pallas kernels for 20%

profile of v5, /device:TPU:15, one launch (start us, length us, event | category | flops | bytes accessed | tf_op | source)
XLA Modules:
  0.0 454.5 jit_solution(2550039013191252054)
XLA Ops:
  7.2 3.0 shard_map.255
  10.5 2.3 collective-permute-start.10
  12.8 2.2 collective-permute-start.11
  32.1 7.0 %collective-permute-done.11 = bf16[8,128,128]{2,1,0:T(8,128)(2,1)} collective-permute-done((bf16[8,128,128]{2,1,0:T(8,128)(2,1)}, bf16[8,128,128]{2,1,0:T(8,128)(2,1)}, u32[]{:S(2)}, u32[]{:S(2)}) %collective-permute-start.11) | collective-permute-done | bytes 262176 | tf_op jit(solution)/shard_map/ppermute | solution.py:1015
  40.3 5.9 %collective-permute-done.12 = bf16[208,768]{1,0:T(8,128)(2,1)S(1)} collective-permute-done((bf16[208,768]{1,0:T(8,128)(2,1)S(1)}, bf16[208,768]{1,0:T(8,128)(2,1)S(1)}, u32[]{:S(2)}, u32[]{:S(2)}) %collective-permute-start.12) | collective-permute-done | bytes 319520 | tf_op jit(solution)/shard_map/ppermute | solution.py:1363
  53.5 2.2 collective-permute-start.16
  55.7 3.8 collective-permute-start.17
  63.5 3.6 shard_map.256
  70.6 6.0 %collective-permute-done.16 = bf16[2,208,768]{2,1,0:T(8,128)(2,1)} collective-permute-done((bf16[2,208,768]{2,1,0:T(8,128)(2,1)S(1)}, bf16[2,208,768]{2,1,0:T(8,128)(2,1)}, u32[]{:S(2)}, u32[]{:S(2)}) %collective-permute-start.16) | collective-permute-done | bytes 639008 | tf_op jit(solution)/shard_map/ppermute | solution.py:1038
  76.6 3.4 collective-permute-start.24
  81.9 2.8 collective-permute-start.26
  84.7 23.9 %collective-permute-done.24 = bf16[2,208,768]{2,1,0:T(8,128)(2,1)} collective-permute-done((bf16[2,208,768]{2,1,0:T(8,128)(2,1)}, bf16[2,208,768]{2,1,0:T(8,128)(2,1)}, u32[]{:S(2)}, u32[]{:S(2)}) %collective-permute-start.24) | collective-permute-done | bytes 639008 | tf_op jit(solution)/shard_map/ppermute | solution.py:1038
  108.7 4.5 collective-permute-start.25
  116.2 2.5 collective-permute-start.27
  120.5 5.4 %collective-permute-done.25 = bf16[2,208,768]{2,1,0:T(8,128)(2,1)} collective-permute-done((bf16[2,208,768]{2,1,0:T(8,128)(2,1)}, bf16[2,208,768]{2,1,0:T(8,128)(2,1)}, u32[]{:S(2)}, u32[]{:S(2)}) %collective-permute-start.25) | collective-permute-done | bytes 639008 | tf_op jit(solution)/shard_map/ppermute | solution.py:1038
  125.9 2.2 collective-permute-start.23
  131.0 3.3 collective-permute-done.27
  140.9 15.7 %shard_map.257 = (bf16[416,768]{1,0:T(8,128)(2,1)}, bf16[2080,1536]{1,0:T(8,128)(2,1)}, bf16[2080,768]{1,0:T(8,128)(2,1)}, bf16[416,768]{1,0:T(8,128)(2,1)}, bf16[768,2304]{1,0:T(8,128)(2,1)}) custom-call(s32[448]{0:T(512)} %get-tuple-element.175.tiles, s32[1]{0:T(128)} %bitcast.42.early, ...), custom_call_target="tpu_custom_call" | custom-call | bytes 45000000 | tf_op jit(solution)/shard_map/pallas_call | solution.py:541
  156.6 14.5 %shard_map.258 = (bf16[416,768]{1,0:T(8,128)(2,1)}, f32[416,768]{1,0:T(8,128)}) custom-call(bf16[416,768]{1,0:T(8,128)(2,1)} %get-tuple-element.181.refs_0_, bf16[2080,1536]{1,0:T(8,128)(2,1)} %get-tuple-element.182.refs_1_.refs_2_, bf16[2080,1536]{1,0:T(8,128)(2,1)} %get-tuple-element.182.refs_1_.refs_2_, f32[1,2080]{1,0:T(1,128)} %reshape.482.refs_3_), custom_call_target="tpu_custom_call" | custom-call | bytes 36000000 | tf_op jit(solution)/shard_map/pallas_call | solution.py:628
  171.1 43.5 %shard_map.259 = (f32[16,768]{1,0:T(8,128)}, f32[416,768]{1,0:T(8,128)}, bf16[416,768]{1,0:T(8,128)(2,1)}, f32[8,768]{1,0:T(8,128)}, f32[4,768]{1,0:T(4,128)}, /...) custom-call(s32[448]{0:T(512)} %get-tuple-element.163.refs_0_, ...), custom_call_target="tpu_custom_call" | custom-call | bytes 120000000 | tf_op jit(solution)/shard_map/pallas_call | solution.py:880
  215.5 11.7 %shard_map.260 = (bf16[416,768]{1,0:T(8,128)(2,1)}, bf16[2080,768]{1,0:T(8,128)(2,1)}, bf16[2080,768]{1,0:T(8,128)(2,1)}) custom-call(bf16[416,768]{1,0:T(8,128)(2,1)} %get-tuple-element.181.refs_0_, bf16[2080,1536]{1,0:T(8,128)(2,1)} %get-tuple-element.182.refs_1_.refs_2_, bf16[2080,1536]{1,0:T(8,128)(2,1)} %get-tuple-element.182.refs_1_.refs_2_, ...), custom_call_target="tpu_custom_call" | custom-call | bytes 36000000 | tf_op jit(solution)/shard_map/pallas_call | solution.py:656
  227.2 4.6 %add_convert_fusion.16 = (bf16[24,128,128]{2,1,0:T(8,128)(2,1)}, bf16[24,128,128]{2,1,0:T(8,128)(2,1)S(1)}, bf16[24,128,128]{2,1,0:T(8,128)(2,1)S(1)}, bf16[24,128,128]{2,1,0:T(8,128)(2,1)S(1)}) fusion(bf16[96,128,128]{2,1,0:T(8,128)(2,1)} %collective-permute-done.28, bf16[96,128,128]{2,1,0:T(8,128)(2,1)S(1)} %copy-done.10), kind=kLoop, calls=%fused_computation.46 | loop fusion | flops 6291456 | bytes 9437184 | tf_op jit(solution)/shard_map/convert_element_type | solution.py:1154
  232.2 11.5 %shard_map.261 = (bf16[416,768]{1,0:T(8,128)(2,1)}, bf16[2080,768]{1,0:T(8,128)(2,1)}, bf16[2080,768]{1,0:T(8,128)(2,1)}) custom-call(bf16[416,768]{1,0:T(8,128)(2,1)} %get-tuple-element.181.refs_0_, bf16[2080,1536]{1,0:T(8,128)(2,1)} %get-tuple-element.182.refs_1_.refs_2_, ...), custom_call_target="tpu_custom_call", output_to_operand_aliasing={{0}: (7, {}), {1}: (8, {}), {2}: (9, {})} | custom-call | bytes 36000000 | tf_op jit(solution)/shard_map/pallas_call | solution.py:656
  243.7 7.4 %collective-permute-done.30 = bf16[2,4,3,128,128]{4,3,2,1,0:T(8,128)(2,1)S(1)} collective-permute-done((bf16[2,4,3,128,128]{4,3,2,1,0:T(8,128)(2,1)}, bf16[2,4,3,128,128]{4,3,2,1,0:T(8,128)(2,1)S(1)}, u32[]{:S(2)}, u32[]{:S(2)}) %collective-permute-start.30) | collective-permute-done | bytes 786464 | tf_op jit(solution)/shard_map/ppermute | solution.py:1015
  252.7 15.1 %shard_map.262 = (bf16[128,128,128]{2,1,0:T(8,128)(2,1)}, bf16[128,128,128]{2,1,0:T(8,128)(2,1)}, bf16[768,2304]{1,0:T(8,128)(2,1)}) custom-call(s32[448]{0:T(512)S(1)} %select_reduce_fusion.3.refs_2_.targets, bf16[2080,768]{1,0:T(8,128)(2,1)} %get-tuple-element.208.low, ...), custom_call_target="tpu_custom_call", output_to_operand_aliasing={{0}: (6, {}), {1}: (7, {})} | custom-call | bytes 42000000 | tf_op jit(solution)/shard_map/pallas_call | solution.py:952
  268.2 1.8 collective-permute-start.33
  273.5 12.4 %shard_map.263 = (bf16[2080,768]{1,0:T(8,128)(2,1)}, f32[416,768]{1,0:T(8,128)}, f32[8,768]{1,0:T(8,128)}) custom-call(bf16[2080,768]{1,0:T(8,128)(2,1)} %constant_dynamic-update-slice_fusion.3.refs_9_.seen, bf16[416,768]{1,0:T(8,128)(2,1)} %bitcast.213, bf16[416,768]{1,0:T(8,128)(2,1)} %get-tuple-element.230.dq, bf16[2080,768]{1,0:T(8,128)(2,1)} %get-tuple-element.210.dk, ...), custom_call_target="tpu_custom_call" | custom-call | bytes 36000000 | tf_op jit(solution)/shard_map/pallas_call | solution.py:999
  285.9 2.3 collective-permute-done.35
  289.6 4.4 add_convert_fusion.12
  294.0 1.7 concatenate.80
  300.3 20.2 %collective-permute-done.38 = bf16[2,4,4,128,128]{4,3,2,1,0:T(8,128)(2,1)} collective-permute-done((bf16[2,4,4,128,128]{4,3,2,1,0:T(8,128)(2,1)}, bf16[2,4,4,128,128]{4,3,2,1,0:T(8,128)(2,1)}, u32[]{:S(2)}, u32[]{:S(2)}) %collective-permute-start.38) | collective-permute-done | bytes 1048608 | tf_op jit(solution)/shard_map/ppermute | solution.py:1015
  320.5 1.6 fusion.21
  322.1 1.6 collective-permute-done.37
  327.6 11.3 %collective-permute-done.41 = bf16[4,4,128,128]{3,2,1,0:T(8,128)(2,1)S(1)} collective-permute-done((bf16[4,4,128,128]{3,2,1,0:T(8,128)(2,1)S(1)}, bf16[4,4,128,128]{3,2,1,0:T(8,128)(2,1)S(1)}, u32[]{:S(2)}, u32[]{:S(2)}) %collective-permute-start.41) | collective-permute-done | bytes 524320 | tf_op jit(solution)/shard_map/ppermute | solution.py:1015
  341.9 2.3 collective-permute-start.44
  344.8 3.2 collective-permute-start.48
  348.0 14.5 %collective-permute-done.47 = f32[2176]{0:T(1024)S(1)} collective-permute-done((f32[2176]{0:T(1024)S(1)}, f32[2176]{0:T(1024)S(1)}, u32[]{:S(2)}, u32[]{:S(2)}) %collective-permute-start.47) | collective-permute-done | bytes 8736 | tf_op jit(solution)/shard_map/ppermute | solution.py:1015
  362.9 1.6 collective-permute-start.49
  364.5 4.5 collective-permute-done.49
  370.1 1.7 pad_maximum_fusion.6
  373.1 1.8 collective-permute-start.52
  377.9 2.5 collective-permute-done.54
  381.9 7.1 %shard_map.264 = (f32[14,128,128]{2,1,0:T(8,128)}, f32[14,128,128]{2,1,0:T(8,128)}, f32[14,128,128]{2,1,0:T(8,128)}, f32[14,128,128]{2,1,0:T(8,128)}, f32[14,128,128]{2,1,0:T(8,128)}) custom-call(s32[14]{0:T(128)} %fusion.106.ranks, f32[14,128,128]{2,1,0:T(8,128)} %get-tuple-element.370.refs_0_.refs_1_.refs_2_.refs_3_.refs_4_.refs_5_.refs_6_, ...), custom_call_target="tpu_custom_call" | custom-call | bytes 24000000 | tf_op jit(solution)/shard_map/pallas_call | solution.py:224
  389.3 7.7 %collective-permute-start.56 = (f32[2,2,4,2304]{3,0,1,2:T(2,128)S(1)}, f32[2,2,4,2304]{3,0,1,2:T(2,128)S(1)}, u32[]{:S(2)}, u32[]{:S(2)}) collective-permute-start(f32[2,2,4,2304]{3,0,1,2:T(2,128)S(1)} %pad_maximum_fusion.15), channel_id=1, source_target_pairs={{0,1},{1,0},{2,3},{3,2},{4,5},{5,4},{6,7},{7,6},{8,9},{9,8},{10,11... | collective-permute-start | bytes 442376 | tf_op jit(solution)/shard_map/ppermute | solution.py:1015
  402.9 3.2 collective-permute-start.58
  407.6 2.5 collective-permute-start.61
  410.0 2.0 multiply_subtract_fusion
  412.1 28.3 %shard_map.265 = (f32[14,128,128]{2,1,0:T(8,128)}, f32[14,128,128]{2,1,0:T(8,128)}, f32[14,128,128]{2,1,0:T(8,128)}, f32[14,128,128]{2,1,0:T(8,128)}, f32[14,128...) custom-call(f32[1]{0:T(128)} %bitcast.117.factor, f32[14,128,128]{2,1,0:T(8,128)} %get-tuple-element.280.refs_0_, ...), custom_call_target="tpu_custom_call" | custom-call | bytes 90000000 | tf_op jit(solution)/shard_map/pallas_call | solution.py:369
  (300 shorter events, 84.5 us)
Async XLA Ops:
  7.2 133.7 %all-gather.2.cloned.1.call-start = ((), (), s32[]{:S(2)}) async-start(), calls=%async_computation | async-start | bytes 6488064 | tf_op jit(solution)/shard_map/all_gather | solution.py:1359
  10.3 18.1 %collective-permute-start.9 = (bf16[8,128,128]{2,1,0:T(8,128)(2,1)}, bf16[8,128,128]{2,1,0:T(8,128)(2,1)S(1)}, u32[]{:S(2)}, u32[]{:S(2)}) collective-permute-start(bf16[8,128,128]{2,1,0:T(8,128)(2,1)} %get-tuple-element.162), channel_id=1, source_target_pairs={{0,24},{8,0},{16,8},{24,16},{1,25},{9,1},{17,9},{25,17},{2,26},{10... | collective-permute-start | bytes 786440 | tf_op jit(solution)/shard_map/ppermute | solution.py:1015
  10.5 21.6 %collective-permute-start.10 = (bf16[8,128,128]{2,1,0:T(8,128)(2,1)}, bf16[8,128,128]{2,1,0:T(8,128)(2,1)S(1)}, u32[]{:S(2)}, u32[]{:S(2)}) collective-permute-start(bf16[8,128,128]{2,1,0:T(8,128)(2,1)} %get-tuple-element.162), channel_id=1, source_target_pairs={{0,16},{8,24},{16,0},{24,8},{1,17},{9,25},{17,1},{25,9},{2,18},{10... | collective-permute-start | bytes 786440 | tf_op jit(solution)/shard_map/ppermute | solution.py:1015
  12.8 26.4 %collective-permute-start.11 = (bf16[8,128,128]{2,1,0:T(8,128)(2,1)}, bf16[8,128,128]{2,1,0:T(8,128)(2,1)}, u32[]{:S(2)}, u32[]{:S(2)}) collective-permute-start(bf16[8,128,128]{2,1,0:T(8,128)(2,1)} %get-tuple-element.162), channel_id=1, source_target_pairs={{0,8},{8,16},{16,24},{24,0},{1,9},{9,17},{17,25},{25,1},{2,10},{10... | collective-permute-start | bytes 786440 | tf_op jit(solution)/shard_map/ppermute | solution.py:1015
  21.5 18.7 %collective-permute-start.8 = (bf16[208,768]{1,0:T(8,128)(2,1)S(1)}, bf16[208,768]{1,0:T(8,128)(2,1)S(1)}, u32[]{:S(2)}, u32[]{:S(2)}) collective-permute-start(bf16[208,768]{1,0:T(8,128)(2,1)S(1)} %get-tuple-element.381), channel_id=1, source_target_pairs={{0,4},{4,0},{1,5},{5,1},{2,6},{6,2},{3,7},{7,3},{8,12},{12,8},{9,1... | collective-permute-start | bytes 958472 | tf_op jit(solution)/shard_map/ppermute | solution.py:1015
  21.8 24.4 %collective-permute-start.12 = (bf16[208,768]{1,0:T(8,128)(2,1)S(1)}, bf16[208,768]{1,0:T(8,128)(2,1)S(1)}, u32[]{:S(2)}, u32[]{:S(2)}) collective-permute-start(bf16[208,768]{1,0:T(8,128)(2,1)S(1)} %get-tuple-element.380), channel_id=1, source_target_pairs={{0,4},{4,8},{8,12},{12,16},{16,20},{20,24},{24,28},{28,0},{1,5},{5... | collective-permute-start | bytes 958472 | tf_op jit(solution)/shard_map/ppermute | solution.py:1363
  28.3 17.9 %collective-permute-start.13 = (bf16[208,768]{1,0:T(8,128)(2,1)S(1)}, bf16[208,768]{1,0:T(8,128)(2,1)}, u32[]{:S(2)}, u32[]{:S(2)}) collective-permute-start(bf16[208,768]{1,0:T(8,128)(2,1)S(1)} %get-tuple-element.380), channel_id=1, source_target_pairs={{4,0},{8,4},{12,8},{16,12},{20,16},{24,20},{28,24},{0,28},{5,1},{9... | collective-permute-start | bytes 958472 | tf_op jit(solution)/shard_map/ppermute | solution.py:1364
  48.4 19.5 %collective-permute-start.15 = (bf16[4,4,128,128]{3,2,1,0:T(8,128)(2,1)S(1)}, bf16[4,4,128,128]{3,2,1,0:T(8,128)(2,1)}, u32[]{:S(2)}, u32[]{:S(2)}) collective-permute-start(bf16[4,4,128,128]{3,2,1,0:T(8,128)(2,1)S(1)} %get-tuple-element.368), channel_id=1, source_target_pairs={{0,4},{4,0},{1,5},{5,1},{2,6},{6,2},{3,7},{7,3},{8,12},{12,8},{9,1... | collective-permute-start | bytes 1572872 | tf_op jit(solution)/shard_map/ppermute | solution.py:1015
  50.0 19.1 %collective-permute-start.14 = (bf16[4,4,128,128]{3,2,1,0:T(8,128)(2,1)}, bf16[4,4,128,128]{3,2,1,0:T(8,128)(2,1)}, u32[]{:S(2)}, u32[]{:S(2)}) collective-permute-start(bf16[4,4,128,128]{3,2,1,0:T(8,128)(2,1)} %get-tuple-element.369), channel_id=1, source_target_pairs={{0,2},{2,0},{1,3},{3,1},{4,6},{6,4},{5,7},{7,5},{8,10},{10,8},{9,1... | collective-permute-start | bytes 1572872 | tf_op jit(solution)/shard_map/ppermute | solution.py:1015
  53.5 23.1 %collective-permute-start.16 = (bf16[2,208,768]{2,1,0:T(8,128)(2,1)S(1)}, bf16[2,208,768]{2,1,0:T(8,128)(2,1)}, u32[]{:S(2)}, u32[]{:S(2)}) collective-permute-start(bf16[2,208,768]{2,1,0:T(8,128)(2,1)S(1)} %pad_maximum_fusion.7), channel_id=1, source_target_pairs={{8,0},{16,8},{24,16},{9,1},{17,9},{25,17},{10,2},{18,10},{26,18},{... | collective-permute-start | bytes 1916936 | tf_op jit(solution)/shard_map/ppermute | solution.py:1038
  55.7 20.9 %collective-permute-start.17 = (bf16[2,208,768]{2,1,0:T(8,128)(2,1)S(1)}, bf16[2,208,768]{2,1,0:T(8,128)(2,1)}, u32[]{:S(2)}, u32[]{:S(2)}) collective-permute-start(bf16[2,208,768]{2,1,0:T(8,128)(2,1)S(1)} %pad_maximum_fusion.7), channel_id=1, source_target_pairs={{0,8},{8,16},{16,24},{1,9},{9,17},{17,25},{2,10},{10,18},{18,26},{... | collective-permute-start | bytes 1916936 | tf_op jit(solution)/shard_map/ppermute | solution.py:1038
  76.6 32.1 %collective-permute-start.24 = (bf16[2,208,768]{2,1,0:T(8,128)(2,1)}, bf16[2,208,768]{2,1,0:T(8,128)(2,1)}, u32[]{:S(2)}, u32[]{:S(2)}) collective-permute-start(bf16[2,208,768]{2,1,0:T(8,128)(2,1)} %collective-permute-done.17), channel_id=1, source_target_pairs={{0,8},{8,16},{16,24},{1,9},{9,17},{17,25},{2,10},{10,18},{18,26},{... | collective-permute-start | bytes 1916936 | tf_op jit(solution)/shard_map/ppermute | solution.py:1038
  80.0 39.9 %collective-permute-start.18 = (bf16[2,4,4,128,128]{4,3,2,1,0:T(8,128)(2,1)S(1)}, bf16[2,4,4,128,128]{4,3,2,1,0:T(8,128)(2,1)}, u32[]{:S(2)}, u32[]{:S(2)}) collective-permute-start(bf16[2,4,4,128,128]{4,3,2,1,0:T(8,128)(2,1)S(1)} %pad_maximum_fusion.4), channel_id=1, source_target_pairs={{0,4},{4,0},{1,5},{5,1},{2,6},{6,2},{3,7},{7,3},{8,12},{12,8},{9,1... | collective-permute-start | bytes 3145736 | tf_op jit(solution)/shard_map/ppermute | solution.py:1015
  80.8 39.5 %collective-permute-start.19 = (bf16[2,4,4,128,128]{4,3,2,1,0:T(8,128)(2,1)S(1)}, bf16[2,4,4,128,128]{4,3,2,1,0:T(8,128)(2,1)}, u32[]{:S(2)}, u32[]{:S(2)}) collective-permute-start(bf16[2,4,4,128,128]{4,3,2,1,0:T(8,128)(2,1)S(1)} %pad_maximum_fusion.5), channel_id=1, source_target_pairs={{0,2},{2,0},{1,3},{3,1},{4,6},{6,4},{5,7},{7,5},{8,10},{10,8},{9,1... | collective-permute-start | bytes 3145736 | tf_op jit(solution)/shard_map/ppermute | solution.py:1015
  81.9 34.3 %collective-permute-start.26 = (bf16[2,208,768]{2,1,0:T(8,128)(2,1)}, bf16[2,208,768]{2,1,0:T(8,128)(2,1)}, u32[]{:S(2)}, u32[]{:S(2)}) collective-permute-start(bf16[2,208,768]{2,1,0:T(8,128)(2,1)} %collective-permute-done.16), channel_id=1, source_target_pairs={{8,0},{16,8},{24,16},{9,1},{17,9},{25,17},{10,2},{18,10},{26,18},{... | collective-permute-start | bytes 1916936 | tf_op jit(solution)/shard_map/ppermute | solution.py:1038
  108.7 17.2 %collective-permute-start.25 = (bf16[2,208,768]{2,1,0:T(8,128)(2,1)}, bf16[2,208,768]{2,1,0:T(8,128)(2,1)}, u32[]{:S(2)}, u32[]{:S(2)}) collective-permute-start(bf16[2,208,768]{2,1,0:T(8,128)(2,1)} %collective-permute-done.24), channel_id=1, source_target_pairs={{0,8},{8,16},{16,24},{1,9},{9,17},{17,25},{2,10},{10,18},{18,26},{... | collective-permute-start | bytes 1916936 | tf_op jit(solution)/shard_map/ppermute | solution.py:1038
  114.1 23.8 %collective-permute-start.20 = (bf16[32,128,128]{2,1,0:T(8,128)(2,1)S(1)}, bf16[32,128,128]{2,1,0:T(8,128)(2,1)S(1)}, u32[]{:S(2)}, u32[]{:S(2)}) collective-permute-start(bf16[32,128,128]{2,1,0:T(8,128)(2,1)S(1)} %bitcast.220), channel_id=1, source_target_pairs={{0,1},{1,0},{2,3},{3,2},{4,5},{5,4},{6,7},{7,6},{8,9},{9,8},{10,11... | collective-permute-start | bytes 3145736 | tf_op jit(solution)/shard_map/ppermute | solution.py:1015
  116.2 18.1 %collective-permute-start.27 = (bf16[2,208,768]{2,1,0:T(8,128)(2,1)}, bf16[2,208,768]{2,1,0:T(8,128)(2,1)S(1)}, u32[]{:S(2)}, u32[]{:S(2)}) collective-permute-start(bf16[2,208,768]{2,1,0:T(8,128)(2,1)} %collective-permute-done.26), channel_id=1, source_target_pairs={{8,0},{16,8},{24,16},{9,1},{17,9},{25,17},{10,2},{18,10},{26,18},{... | collective-permute-start | bytes 1916936 | tf_op jit(solution)/shard_map/ppermute | solution.py:1038
  119.9 18.0 %collective-permute-start.22 = (bf16[32,128,128]{2,1,0:T(8,128)(2,1)S(1)}, bf16[32,128,128]{2,1,0:T(8,128)(2,1)S(1)}, u32[]{:S(2)}, u32[]{:S(2)}) collective-permute-start(bf16[32,128,128]{2,1,0:T(8,128)(2,1)S(1)} %bitcast.217), channel_id=1, source_target_pairs={{0,1},{1,0},{2,3},{3,2},{4,5},{5,4},{6,7},{7,6},{8,9},{9,8},{10,11... | collective-permute-start | bytes 3145736 | tf_op jit(solution)/shard_map/ppermute | solution.py:1015
  120.3 18.6 %collective-permute-start.21 = (bf16[32,128,128]{2,1,0:T(8,128)(2,1)}, bf16[32,128,128]{2,1,0:T(8,128)(2,1)S(1)}, u32[]{:S(2)}, u32[]{:S(2)}) collective-permute-start(bf16[32,128,128]{2,1,0:T(8,128)(2,1)} %bitcast.57.refs_2_.refs_5_), channel_id=1, source_target_pairs={{0,1},{1,0},{2,3},{3,2},{4,5},{5,4},{6,7},{7,6},{8,9},{9,8},{10,11... | collective-permute-start | bytes 3145736 | tf_op jit(solution)/shard_map/ppermute | solution.py:1015
  125.9 15.0 %collective-permute-start.23 = (bf16[32,128,128]{2,1,0:T(8,128)(2,1)}, bf16[32,128,128]{2,1,0:T(8,128)(2,1)}, u32[]{:S(2)}, u32[]{:S(2)}) collective-permute-start(bf16[32,128,128]{2,1,0:T(8,128)(2,1)} %bitcast.59.refs_4_.refs_7_), channel_id=1, source_target_pairs={{0,1},{1,0},{2,3},{3,2},{4,5},{5,4},{6,7},{7,6},{8,9},{9,8},{10,11... | collective-permute-start | bytes 3145736 | tf_op jit(solution)/shard_map/ppermute | solution.py:1015
  214.6 12.6 %collective-permute-start.28 = (bf16[96,128,128]{2,1,0:T(8,128)(2,1)}, bf16[96,128,128]{2,1,0:T(8,128)(2,1)}, u32[]{:S(2)}, u32[]{:S(2)}) collective-permute-start(bf16[96,128,128]{2,1,0:T(8,128)(2,1)} %get-tuple-element.198), channel_id=1, source_target_pairs={{0,1},{1,0},{2,3},{3,2},{4,5},{5,4},{6,7},{7,6},{8,9},{9,8},{10,11... | collective-permute-start | bytes 9437192 | tf_op jit(solution)/shard_map/ppermute | solution.py:1015
  231.8 19.3 %collective-permute-start.30 = (bf16[2,4,3,128,128]{4,3,2,1,0:T(8,128)(2,1)}, bf16[2,4,3,128,128]{4,3,2,1,0:T(8,128)(2,1)S(1)}, u32[]{:S(2)}, u32[]{:S(2)}) collective-permute-start(bf16[2,4,3,128,128]{4,3,2,1,0:T(8,128)(2,1)} %bitcast.70), channel_id=1, source_target_pairs={{0,2},{2,0},{1,3},{3,1},{4,6},{6,4},{5,7},{7,5},{8,10},{10,8},{9,1... | collective-permute-start | bytes 2359304 | tf_op jit(solution)/shard_map/ppermute | solution.py:1015
  232.2 19.3 %collective-permute-start.29 = (bf16[2,4,3,128,128]{4,3,2,1,0:T(8,128)(2,1)S(1)}, bf16[2,4,3,128,128]{4,3,2,1,0:T(8,128)(2,1)S(1)}, u32[]{:S(2)}, u32[]{:S(2)}) collective-permute-start(bf16[2,4,3,128,128]{4,3,2,1,0:T(8,128)(2,1)S(1)} %bitcast.238), channel_id=1, source_target_pairs={{0,4},{4,0},{1,5},{5,1},{2,6},{6,2},{3,7},{7,3},{8,12},{12,8},{9,1... | collective-permute-start | bytes 2359304 | tf_op jit(solution)/shard_map/ppermute | solution.py:1015
  251.8 16.2 %collective-permute-start.32 = (bf16[4,3,128,128]{3,2,1,0:T(8,128)(2,1)S(1)}, bf16[4,3,128,128]{3,2,1,0:T(8,128)(2,1)S(1)}, u32[]{:S(2)}, u32[]{:S(2)}) collective-permute-start(bf16[4,3,128,128]{3,2,1,0:T(8,128)(2,1)S(1)} %get-tuple-element.219), channel_id=1, source_target_pairs={{0,4},{4,0},{1,5},{5,1},{2,6},{6,2},{3,7},{7,3},{8,12},{12,8},{9,1... | collective-permute-start | bytes 1179656 | tf_op jit(solution)/shard_map/ppermute | solution.py:1015
  252.1 16.0 %collective-permute-start.31 = (bf16[4,3,128,128]{3,2,1,0:T(8,128)(2,1)S(1)}, bf16[4,3,128,128]{3,2,1,0:T(8,128)(2,1)S(1)}, u32[]{:S(2)}, u32[]{:S(2)}) collective-permute-start(bf16[4,3,128,128]{3,2,1,0:T(8,128)(2,1)S(1)} %get-tuple-element.217), channel_id=1, source_target_pairs={{0,2},{2,0},{1,3},{3,1},{4,6},{6,4},{5,7},{7,5},{8,10},{10,8},{9,1... | collective-permute-start | bytes 1179656 | tf_op jit(solution)/shard_map/ppermute | solution.py:1015
  268.2 21.3 %collective-permute-start.33 = (bf16[128,128,128]{2,1,0:T(8,128)(2,1)}, bf16[128,128,128]{2,1,0:T(8,128)(2,1)}, u32[]{:S(2)}, u32[]{:S(2)}) collective-permute-start(bf16[128,128,128]{2,1,0:T(8,128)(2,1)} %get-tuple-element.221), channel_id=1, source_target_pairs={{0,1},{1,0},{2,3},{3,2},{4,5},{5,4},{6,7},{7,6},{8,9},{9,8},{10,11... | collective-permute-start | bytes 12582920 | tf_op jit(solution)/shard_map/ppermute | solution.py:1015
  270.0 15.9 %collective-permute-start.34 = (bf16[6,128,128]{2,1,0:T(8,128)(2,1)S(1)}, bf16[6,128,128]{2,1,0:T(8,128)(2,1)S(1)}, u32[]{:S(2)}, u32[]{:S(2)}) collective-permute-start(bf16[6,128,128]{2,1,0:T(8,128)(2,1)S(1)} %pad_maximum_fusion.12), channel_id=1, source_target_pairs={{0,8},{8,16},{16,24},{24,0},{1,9},{9,17},{17,25},{25,1},{2,10},{10... | collective-permute-start | bytes 589832 | tf_op jit(solution)/shard_map/ppermute | solution.py:1015
  271.2 16.9 %collective-permute-start.35 = (bf16[6,128,128]{2,1,0:T(8,128)(2,1)S(1)}, bf16[6,128,128]{2,1,0:T(8,128)(2,1)S(1)}, u32[]{:S(2)}, u32[]{:S(2)}) collective-permute-start(bf16[6,128,128]{2,1,0:T(8,128)(2,1)S(1)} %pad_maximum_fusion.13), channel_id=1, source_target_pairs={{0,16},{8,24},{16,0},{24,8},{1,17},{9,25},{17,1},{25,9},{2,18},{10... | collective-permute-start | bytes 589832 | tf_op jit(solution)/shard_map/ppermute | solution.py:1015
  271.5 18.0 %collective-permute-start.36 = (bf16[6,128,128]{2,1,0:T(8,128)(2,1)S(1)}, bf16[6,128,128]{2,1,0:T(8,128)(2,1)S(1)}, u32[]{:S(2)}, u32[]{:S(2)}) collective-permute-start(bf16[6,128,128]{2,1,0:T(8,128)(2,1)S(1)} %pad_maximum_fusion.14), channel_id=1, source_target_pairs={{0,24},{8,0},{16,8},{24,16},{1,25},{9,1},{17,9},{25,17},{2,26},{10... | collective-permute-start | bytes 589832 | tf_op jit(solution)/shard_map/ppermute | solution.py:1015
  295.9 24.6 %collective-permute-start.38 = (bf16[2,4,4,128,128]{4,3,2,1,0:T(8,128)(2,1)}, bf16[2,4,4,128,128]{4,3,2,1,0:T(8,128)(2,1)}, u32[]{:S(2)}, u32[]{:S(2)}) collective-permute-start(bf16[2,4,4,128,128]{4,3,2,1,0:T(8,128)(2,1)} %bitcast.237), channel_id=1, source_target_pairs={{0,2},{2,0},{1,3},{3,1},{4,6},{6,4},{5,7},{7,5},{8,10},{10,8},{9,1... | collective-permute-start | bytes 3145736 | tf_op jit(solution)/shard_map/ppermute | solution.py:1015
  298.7 25.0 %collective-permute-start.37 = (bf16[2,4,4,128,128]{4,3,2,1,0:T(8,128)(2,1)}, bf16[2,4,4,128,128]{4,3,2,1,0:T(8,128)(2,1)S(1)}, u32[]{:S(2)}, u32[]{:S(2)}) collective-permute-start(bf16[2,4,4,128,128]{4,3,2,1,0:T(8,128)(2,1)} %bitcast.236), channel_id=1, source_target_pairs={{0,4},{4,0},{1,5},{5,1},{2,6},{6,2},{3,7},{7,3},{8,12},{12,8},{9,1... | collective-permute-start | bytes 3145736 | tf_op jit(solution)/shard_map/ppermute | solution.py:1015
  326.5 12.3 %collective-permute-start.41 = (bf16[4,4,128,128]{3,2,1,0:T(8,128)(2,1)S(1)}, bf16[4,4,128,128]{3,2,1,0:T(8,128)(2,1)S(1)}, u32[]{:S(2)}, u32[]{:S(2)}) collective-permute-start(bf16[4,4,128,128]{3,2,1,0:T(8,128)(2,1)S(1)} %get-tuple-element.248), channel_id=1, source_target_pairs={{0,4},{4,0},{1,5},{5,1},{2,6},{6,2},{3,7},{7,3},{8,12},{12,8},{9,1... | collective-permute-start | bytes 1572872 | tf_op jit(solution)/shard_map/ppermute | solution.py:1015
  326.6 12.4 %collective-permute-start.40 = (bf16[4,4,128,128]{3,2,1,0:T(8,128)(2,1)S(1)}, bf16[4,4,128,128]{3,2,1,0:T(8,128)(2,1)S(1)}, u32[]{:S(2)}, u32[]{:S(2)}) collective-permute-start(bf16[4,4,128,128]{3,2,1,0:T(8,128)(2,1)S(1)} %get-tuple-element.246), channel_id=1, source_target_pairs={{0,2},{2,0},{1,3},{3,1},{4,6},{6,4},{5,7},{7,5},{8,10},{10,8},{9,1... | collective-permute-start | bytes 1572872 | tf_op jit(solution)/shard_map/ppermute | solution.py:1015
  339.4 29.8 %collective-permute-start.50 = (bf16[4,208,768]{2,1,0:T(8,128)(2,1)S(1)}, bf16[4,208,768]{2,1,0:T(8,128)(2,1)S(1)}, u32[]{:S(2)}, u32[]{:S(2)}) collective-permute-start(bf16[4,208,768]{2,1,0:T(8,128)(2,1)S(1)} %slice_bitcast_fusion.4), channel_id=1, source_target_pairs={{0,4},{4,0},{1,5},{5,1},{2,6},{6,2},{3,7},{7,3},{8,12},{12,8},{9,1... | collective-permute-start | bytes 3833864 | tf_op jit(solution)/shard_map/ppermute | solution.py:1015
  341.8 27.2 %collective-permute-start.43 = (bf16[8,128,128]{2,1,0:T(8,128)(2,1)S(1)}, bf16[8,128,128]{2,1,0:T(8,128)(2,1)S(1)}, u32[]{:S(2)}, u32[]{:S(2)}) collective-permute-start(bf16[8,128,128]{2,1,0:T(8,128)(2,1)S(1)} %pad_maximum_fusion.9), channel_id=1, source_target_pairs={{0,8},{8,16},{16,24},{24,0},{1,9},{9,17},{17,25},{25,1},{2,10},{10... | collective-permute-start | bytes 786440 | tf_op jit(solution)/shard_map/ppermute | solution.py:1015
  341.9 27.1 %collective-permute-start.44 = (bf16[8,128,128]{2,1,0:T(8,128)(2,1)S(1)}, bf16[8,128,128]{2,1,0:T(8,128)(2,1)S(1)}, u32[]{:S(2)}, u32[]{:S(2)}) collective-permute-start(bf16[8,128,128]{2,1,0:T(8,128)(2,1)S(1)} %pad_maximum_fusion.10), channel_id=1, source_target_pairs={{0,16},{8,24},{16,0},{24,8},{1,17},{9,25},{17,1},{25,9},{2,18},{10... | collective-permute-start | bytes 786440 | tf_op jit(solution)/shard_map/ppermute | solution.py:1015
  344.4 18.1 %collective-permute-start.47 = (f32[2176]{0:T(1024)S(1)}, f32[2176]{0:T(1024)S(1)}, u32[]{:S(2)}, u32[]{:S(2)}) collective-permute-start(f32[2176]{0:T(1024)S(1)} %get-tuple-element.296), channel_id=1, source_target_pairs={{0,8},{8,16},{16,24},{24,0},{1,9},{9,17},{17,25},{25,1},{2,10},{10... | collective-permute-start | bytes 26120 | tf_op jit(solution)/shard_map/ppermute | solution.py:1015
  344.8 18.1 %collective-permute-start.48 = (f32[2176]{0:T(1024)S(1)}, f32[2176]{0:T(1024)S(1)}, u32[]{:S(2)}, u32[]{:S(2)}) collective-permute-start(f32[2176]{0:T(1024)S(1)} %get-tuple-element.298), channel_id=1, source_target_pairs={{0,16},{8,24},{16,0},{24,8},{1,17},{9,25},{17,1},{25,9},{2,18},{10... | collective-permute-start | bytes 26120 | tf_op jit(solution)/shard_map/ppermute | solution.py:1015
  362.5 6.5 %collective-permute-start.45 = (bf16[8,128,128]{2,1,0:T(8,128)(2,1)S(1)}, bf16[8,128,128]{2,1,0:T(8,128)(2,1)S(1)}, u32[]{:S(2)}, u32[]{:S(2)}) collective-permute-start(bf16[8,128,128]{2,1,0:T(8,128)(2,1)S(1)} %pad_maximum_fusion.11), channel_id=1, source_target_pairs={{0,24},{8,0},{16,8},{24,16},{1,25},{9,1},{17,9},{25,17},{2,26},{10... | collective-permute-start | bytes 786440 | tf_op jit(solution)/shard_map/ppermute | solution.py:1015
  362.9 6.1 %collective-permute-start.49 = (f32[2176]{0:T(1024)S(1)}, f32[2176]{0:T(1024)S(1)}, u32[]{:S(2)}, u32[]{:S(2)}) collective-permute-start(f32[2176]{0:T(1024)S(1)} %get-tuple-element.297), channel_id=1, source_target_pairs={{0,24},{8,0},{16,8},{24,16},{1,25},{9,1},{17,9},{25,17},{2,26},{10... | collective-permute-start | bytes 26120 | tf_op jit(solution)/shard_map/ppermute | solution.py:1015
  380.5 8.6 %collective-permute-start.55 = (f32[2,4,2304]{2,0,1:T(2,128)S(1)}, f32[2,4,2304]{2,0,1:T(2,128)S(1)}, u32[]{:S(2)}, u32[]{:S(2)}) collective-permute-start(f32[2,4,2304]{2,0,1:T(2,128)S(1)} %get-tuple-element.389), channel_id=1, source_target_pairs={{0,2},{2,0},{1,3},{3,1},{4,6},{6,4},{5,7},{7,5},{8,10},{10,8},{9,1... | collective-permute-start | bytes 221192 | tf_op jit(solution)/shard_map/ppermute | solution.py:1015
  389.3 9.1 %collective-permute-start.56 = (f32[2,2,4,2304]{3,0,1,2:T(2,128)S(1)}, f32[2,2,4,2304]{3,0,1,2:T(2,128)S(1)}, u32[]{:S(2)}, u32[]{:S(2)}) collective-permute-start(f32[2,2,4,2304]{3,0,1,2:T(2,128)S(1)} %pad_maximum_fusion.15), channel_id=1, source_target_pairs={{0,1},{1,0},{2,3},{3,2},{4,5},{5,4},{6,7},{7,6},{8,9},{9,8},{10,11... | collective-permute-start | bytes 442376 | tf_op jit(solution)/shard_map/ppermute | solution.py:1015
  401.5 40.9 %collective-permute-start.57 = (bf16[208,768]{1,0:T(8,128)(2,1)S(1)}, bf16[208,768]{1,0:T(8,128)(2,1)S(1)}, u32[]{:S(2)}, u32[]{:S(2)}) collective-permute-start(bf16[208,768]{1,0:T(8,128)(2,1)S(1)} %get-tuple-element.355), channel_id=1, source_target_pairs={{0,8},{8,16},{16,24},{24,0},{1,9},{9,17},{17,25},{25,1},{2,10},{10... | collective-permute-start | bytes 958472 | tf_op jit(solution)/shard_map/ppermute | solution.py:1015
  402.9 39.5 %collective-permute-start.58 = (bf16[208,768]{1,0:T(8,128)(2,1)S(1)}, bf16[208,768]{1,0:T(8,128)(2,1)S(1)}, u32[]{:S(2)}, u32[]{:S(2)}) collective-permute-start(bf16[208,768]{1,0:T(8,128)(2,1)S(1)} %get-tuple-element.357), channel_id=1, source_target_pairs={{0,16},{8,24},{16,0},{24,8},{1,17},{9,25},{17,1},{25,9},{2,18},{10... | collective-permute-start | bytes 958472 | tf_op jit(solution)/shard_map/ppermute | solution.py:1015
  406.1 36.3 %collective-permute-start.59 = (bf16[208,768]{1,0:T(8,128)(2,1)S(1)}, bf16[208,768]{1,0:T(8,128)(2,1)S(1)}, u32[]{:S(2)}, u32[]{:S(2)}) collective-permute-start(bf16[208,768]{1,0:T(8,128)(2,1)S(1)} %get-tuple-element.356), channel_id=1, source_target_pairs={{0,24},{8,0},{16,8},{24,16},{1,25},{9,1},{17,9},{25,17},{2,26},{10... | collective-permute-start | bytes 958472 | tf_op jit(solution)/shard_map/ppermute | solution.py:1015
  407.5 33.8 %collective-permute-start.60 = (bf16[208,768]{1,0:T(8,128)(2,1)}, bf16[208,768]{1,0:T(8,128)(2,1)S(1)}, u32[]{:S(2)}, u32[]{:S(2)}) collective-permute-start(bf16[208,768]{1,0:T(8,128)(2,1)} %get-tuple-element.276), channel_id=1, source_target_pairs={{4,0},{8,4},{12,8},{16,12},{20,16},{24,20},{28,24},{0,28},{5,1},{9... | collective-permute-start | bytes 958472 | tf_op jit(solution)/shard_map/ppermute | solution.py:1485
  407.6 33.8 %collective-permute-start.61 = (bf16[208,768]{1,0:T(8,128)(2,1)S(1)}, bf16[208,768]{1,0:T(8,128)(2,1)S(1)}, u32[]{:S(2)}, u32[]{:S(2)}) collective-permute-start(bf16[208,768]{1,0:T(8,128)(2,1)S(1)} %get-tuple-element.277), channel_id=1, source_target_pairs={{0,4},{4,8},{8,12},{12,16},{16,20},{20,24},{24,28},{28,0},{1,5},{5... | collective-permute-start | bytes 958472 | tf_op jit(solution)/shard_map/ppermute | solution.py:1486
  (38 other events, 424.6 us)
Sparse Core Ops, SparseCore 0:
  11.5 102.8 all-gather.1

commit v6 on v5

--- a/solution.py
+++ b/solution.py
@@ -1056,7 +1056,7 @@
     shares = jnp.pad(vector, (0, device_count * share - vector.shape[0])).reshape(sizes + (share,))
     for axis, size in enumerate(sizes):
         shares = rolled(shares, axis, size, coords[axis])
-    return shares.transpose(3, 1, 2, 0, 4)
+    return shares.transpose(3, 0, 1, 2, 4)
 
 
 def small_step(shares, axis, sizes):
@@ -1410,11 +1410,11 @@
     learned = jnp.where(swap, learned[::-1], learned).reshape(2 * NT, D)
 
     halfway = reduce_core(*buffers[:2], chunks[:2], sizes) if early else []
-    back = attend_back((0, PAIRS // 2), [], query, key_value, key_bias, attended, logs, grad_att)
+    back = attend_back((0, PAIRS // 3), [], query, key_value, key_bias, attended, logs, grad_att)
     back, halfway = lax.optimization_barrier((back, halfway))
     halfway = reduce_stage(halfway, chunks, 0, sizes)
     grad_query, grad_key, grad_value = attend_back(
-        (PAIRS // 2, PAIRS - PAIRS // 2), back, query, key_value, key_bias, attended, logs, grad_att
+        (PAIRS // 3, PAIRS - PAIRS // 3), back, query, key_value, key_bias, attended, logs, grad_att
     )
     grad_query, halfway = lax.optimization_barrier((grad_query, halfway))
     halfway = reduce_stage(halfway, chunks, 1, sizes)
@@ -1442,7 +1442,7 @@
         ]
     )
     small_total = small_local.shape[0]
-    small = small_step(small_shares(small_local, sizes, coords), 3, sizes)
+    small = small_step(small_step(small_shares(small_local, sizes, coords), 3, sizes), 0, sizes)
     late_parts, small, grad_seen = lax.optimization_barrier((late_parts, small, grad_seen))
     seen_frames = grad_seen.reshape(frames_seen, PAD_ROWS, D)
     long_terms = seen_frames[:frame_count].reshape(nz, nx, PAD_ROWS, D)
@@ -1456,7 +1456,7 @@
         (late_parts, small, long_terms, to_previous, to_next)
     )
     late_total = reduce_last(late_parts, sizes)
-    small = small_step(small_step(small, 2, sizes), 0, sizes)
+    small = small_step(small, 2, sizes)
     long_terms = reduce_axis(long_terms, "fx", nx, 1).astype(BF)
     late_total, small, long_terms = lax.optimization_barrier((late_total, small, long_terms))
     if early:

time: 460 us -> 456 us (level)
  waiting for transfers between devices: 121 us -> 115 us
    ppermute x44, waiting for transfers between devices: 74.9 us -> 67.9 us  [moved(): lax.ppermute(value, axis, [(i, (i + step) % size) for i in range(size)])]
  transfers between devices with their start and end apart: 55 -> 55, of which waited for: 19 -> 21; matrix products, arithmetic and copies ran while one was open for 10% -> 10% of each run, Pallas kernels for 20% -> 20%
where the time goes in v6:
time: 456 us; the launch traced here: 451 us
  Pallas kernels  167 us (37%)
  waiting for transfers between devices  115 us (25%)
  starting transfers between devices  73 us (16%)
  other arithmetic  47.1 us (10%)
  local copies, waits for them, and re-layouts  27.3 us (6%)
  between operations  21.9 us (5%)
    ppermute x44, waiting for transfers between devices, moved(): lax.ppermute(value, axis, [(i, (i + step) % size) for i in range(size)])  67.9 us
    ppermute x44, starting transfers between devices, moved(): lax.ppermute(value, axis, [(i, (i + step) % size) for i in range(size)])  49.8 us
    pallas_call x1, Pallas kernels, middle(): pl.pallas_call(kernel, grid_spec=pltpu.PrefetchScalarGridSpec(num_scalar_...  43.6 us
    ppermute x6, waiting for transfers between devices, line_step(): return (lax.ppermute(onward, axis, down), lax.ppermute(backward, axis, up))  38.6 us
    pallas_call x1, Pallas kernels, finish(): pl.pallas_call(finish_kernel, in_specs=[pl.BlockSpec(memory_space=pltpu.S...  28.3 us
    pallas_call x2, Pallas kernels, attend_back(): pl.pallas_call(kernel, grid=(count,), in_specs=[spec(OWN_ROWS), spec(keys...  23.2 us
    ppermute x6, starting transfers between devices, line_step(): return (lax.ppermute(onward, axis, down), lax.ppermute(backward, axis, up))  19.1 us
    pallas_call x1, Pallas kernels, project(): pl.pallas_call(kernel, grid_spec=pltpu.PrefetchScalarGridSpec(num_scalar_...  15.8 us
  transfers between devices with their start and end apart: 55, of which 21 were waited for; matrix products, arithmetic and copies ran while one was open for 10% of the time, Pallas kernels for 20%

profile of v6, /device:TPU:15, one launch (start us, length us, event | category | flops | bytes accessed | tf_op | source)
XLA Modules:
  0.0 451.3 jit_solution(16782810096926669255)
XLA Ops:
  7.2 3.0 shard_map.255
  10.5 2.3 collective-permute-start.10
  12.8 2.2 collective-permute-start.11
  32.1 7.0 %collective-permute-done.11 = bf16[8,128,128]{2,1,0:T(8,128)(2,1)} collective-permute-done((bf16[8,128,128]{2,1,0:T(8,128)(2,1)}, bf16[8,128,128]{2,1,0:T(8,128)(2,1)}, u32[]{:S(2)}, u32[]{:S(2)}) %collective-permute-start.11) | collective-permute-done | bytes 262176 | tf_op jit(solution)/shard_map/ppermute | solution.py:1015
  40.3 5.9 %collective-permute-done.12 = bf16[208,768]{1,0:T(8,128)(2,1)S(1)} collective-permute-done((bf16[208,768]{1,0:T(8,128)(2,1)S(1)}, bf16[208,768]{1,0:T(8,128)(2,1)S(1)}, u32[]{:S(2)}, u32[]{:S(2)}) %collective-permute-start.12) | collective-permute-done | bytes 319520 | tf_op jit(solution)/shard_map/ppermute | solution.py:1363
  53.5 2.2 collective-permute-start.16
  55.7 3.8 collective-permute-start.17
  63.5 3.6 shard_map.256
  70.6 6.0 %collective-permute-done.16 = bf16[2,208,768]{2,1,0:T(8,128)(2,1)} collective-permute-done((bf16[2,208,768]{2,1,0:T(8,128)(2,1)S(1)}, bf16[2,208,768]{2,1,0:T(8,128)(2,1)}, u32[]{:S(2)}, u32[]{:S(2)}) %collective-permute-start.16) | collective-permute-done | bytes 639008 | tf_op jit(solution)/shard_map/ppermute | solution.py:1038
  76.6 3.4 collective-permute-start.24
  82.0 2.7 collective-permute-start.26
  84.7 23.9 %collective-permute-done.24 = bf16[2,208,768]{2,1,0:T(8,128)(2,1)} collective-permute-done((bf16[2,208,768]{2,1,0:T(8,128)(2,1)}, bf16[2,208,768]{2,1,0:T(8,128)(2,1)}, u32[]{:S(2)}, u32[]{:S(2)}) %collective-permute-start.24) | collective-permute-done | bytes 639008 | tf_op jit(solution)/shard_map/ppermute | solution.py:1038
  108.6 4.5 collective-permute-start.25
  116.2 2.5 collective-permute-start.27
  120.5 5.3 %collective-permute-done.25 = bf16[2,208,768]{2,1,0:T(8,128)(2,1)} collective-permute-done((bf16[2,208,768]{2,1,0:T(8,128)(2,1)}, bf16[2,208,768]{2,1,0:T(8,128)(2,1)}, u32[]{:S(2)}, u32[]{:S(2)}) %collective-permute-start.25) | collective-permute-done | bytes 639008 | tf_op jit(solution)/shard_map/ppermute | solution.py:1038
  125.9 2.2 collective-permute-start.23
  130.9 3.3 collective-permute-done.27
  140.9 15.8 %shard_map.257 = (bf16[416,768]{1,0:T(8,128)(2,1)}, bf16[2080,1536]{1,0:T(8,128)(2,1)}, bf16[2080,768]{1,0:T(8,128)(2,1)}, bf16[416,768]{1,0:T(8,128)(2,1)}, bf16[768,2304]{1,0:T(8,128)(2,1)}) custom-call(s32[448]{0:T(512)} %get-tuple-element.175.tiles, s32[1]{0:T(128)} %bitcast.42.early, ...), custom_call_target="tpu_custom_call" | custom-call | bytes 45000000 | tf_op jit(solution)/shard_map/pallas_call | solution.py:541
  156.7 14.5 %shard_map.258 = (bf16[416,768]{1,0:T(8,128)(2,1)}, f32[416,768]{1,0:T(8,128)}) custom-call(bf16[416,768]{1,0:T(8,128)(2,1)} %get-tuple-element.181.refs_0_, bf16[2080,1536]{1,0:T(8,128)(2,1)} %get-tuple-element.182.refs_1_.refs_2_, bf16[2080,1536]{1,0:T(8,128)(2,1)} %get-tuple-element.182.refs_1_.refs_2_, f32[1,2080]{1,0:T(1,128)} %reshape.482.refs_3_), custom_call_target="tpu_custom_call" | custom-call | bytes 36000000 | tf_op jit(solution)/shard_map/pallas_call | solution.py:628
  171.1 43.6 %shard_map.259 = (f32[16,768]{1,0:T(8,128)}, f32[416,768]{1,0:T(8,128)}, bf16[416,768]{1,0:T(8,128)(2,1)}, f32[8,768]{1,0:T(8,128)}, f32[4,768]{1,0:T(4,128)}, /...) custom-call(s32[448]{0:T(512)} %get-tuple-element.163.refs_0_, ...), custom_call_target="tpu_custom_call" | custom-call | bytes 120000000 | tf_op jit(solution)/shard_map/pallas_call | solution.py:880
  215.5 8.7 %shard_map.260 = (bf16[416,768]{1,0:T(8,128)(2,1)}, bf16[2080,768]{1,0:T(8,128)(2,1)}, bf16[2080,768]{1,0:T(8,128)(2,1)}) custom-call(bf16[416,768]{1,0:T(8,128)(2,1)} %get-tuple-element.181.refs_0_, bf16[2080,1536]{1,0:T(8,128)(2,1)} %get-tuple-element.182.refs_1_.refs_2_, bf16[2080,1536]{1,0:T(8,128)(2,1)} %get-tuple-element.182.refs_1_.refs_2_, ...), custom_call_target="tpu_custom_call" | custom-call | bytes 24000000 | tf_op jit(solution)/shard_map/pallas_call | solution.py:656
  224.2 4.6 %add_convert_fusion.16 = (bf16[24,128,128]{2,1,0:T(8,128)(2,1)}, bf16[24,128,128]{2,1,0:T(8,128)(2,1)S(1)}, bf16[24,128,128]{2,1,0:T(8,128)(2,1)S(1)}, bf16[24,128,128]{2,1,0:T(8,128)(2,1)S(1)}) fusion(bf16[96,128,128]{2,1,0:T(8,128)(2,1)} %collective-permute-done.28, bf16[96,128,128]{2,1,0:T(8,128)(2,1)S(1)} %copy-done.11), kind=kLoop, calls=%fused_computation.46 | loop fusion | flops 6291456 | bytes 9437184 | tf_op jit(solution)/shard_map/convert_element_type | solution.py:1154
  229.1 14.5 %shard_map.261 = (bf16[416,768]{1,0:T(8,128)(2,1)}, bf16[2080,768]{1,0:T(8,128)(2,1)}, bf16[2080,768]{1,0:T(8,128)(2,1)}) custom-call(bf16[416,768]{1,0:T(8,128)(2,1)} %get-tuple-element.181.refs_0_, bf16[2080,1536]{1,0:T(8,128)(2,1)} %get-tuple-element.182.refs_1_.refs_2_, ...), custom_call_target="tpu_custom_call", output_to_operand_aliasing={{0}: (7, {}), {1}: (8, {}), {2}: (9, {})} | custom-call | bytes 48000000 | tf_op jit(solution)/shard_map/pallas_call | solution.py:656
  243.6 4.5 collective-permute-done.30
  249.7 15.2 %shard_map.262 = (bf16[128,128,128]{2,1,0:T(8,128)(2,1)}, bf16[128,128,128]{2,1,0:T(8,128)(2,1)}, bf16[768,2304]{1,0:T(8,128)(2,1)}) custom-call(s32[448]{0:T(512)S(1)} %select_reduce_fusion.3.refs_2_.targets, bf16[2080,768]{1,0:T(8,128)(2,1)} %get-tuple-element.208.low, ...), custom_call_target="tpu_custom_call", output_to_operand_aliasing={{0}: (6, {}), {1}: (7, {})} | custom-call | bytes 42000000 | tf_op jit(solution)/shard_map/pallas_call | solution.py:952
  265.2 1.8 collective-permute-start.33
  270.5 12.4 %shard_map.263 = (bf16[2080,768]{1,0:T(8,128)(2,1)}, f32[416,768]{1,0:T(8,128)}, f32[8,768]{1,0:T(8,128)}) custom-call(bf16[2080,768]{1,0:T(8,128)(2,1)} %constant_dynamic-update-slice_fusion.3.refs_9_.seen, bf16[416,768]{1,0:T(8,128)(2,1)} %bitcast.218, bf16[416,768]{1,0:T(8,128)(2,1)} %get-tuple-element.230.dq, bf16[2080,768]{1,0:T(8,128)(2,1)} %get-tuple-element.210.dk, ...), custom_call_target="tpu_custom_call" | custom-call | bytes 36000000 | tf_op jit(solution)/shard_map/pallas_call | solution.py:999
  283.0 2.3 collective-permute-done.35
  286.6 4.3 add_convert_fusion.12
  291.0 1.7 concatenate.80
  297.1 2.0 collective-permute-start.41
  300.9 1.9 collective-permute-done.42
  302.9 16.7 %collective-permute-done.38 = bf16[2,4,4,128,128]{4,3,2,1,0:T(8,128)(2,1)S(1)} collective-permute-done((bf16[2,4,4,128,128]{4,3,2,1,0:T(8,128)(2,1)S(1)}, bf16[2,4,4,128,128]{4,3,2,1,0:T(8,128)(2,1)S(1)}, u32[]{:S(2)}, u32[]{:S(2)}) %collective-permute-start.38) | collective-permute-done | bytes 1048608 | tf_op jit(solution)/shard_map/ppermute | solution.py:1015
  320.4 1.6 collective-permute-start.45
  324.6 10.6 %collective-permute-done.44 = bf16[4,4,128,128]{3,2,1,0:T(8,128)(2,1)S(1)} collective-permute-done((bf16[4,4,128,128]{3,2,1,0:T(8,128)(2,1)S(1)}, bf16[4,4,128,128]{3,2,1,0:T(8,128)(2,1)S(1)}, u32[]{:S(2)}, u32[]{:S(2)}) %collective-permute-start.44) | collective-permute-done | bytes 524320 | tf_op jit(solution)/shard_map/ppermute | solution.py:1015
  341.5 2.0 collective-permute-start.47
  344.3 1.9 collective-permute-start.48
  346.9 2.5 collective-permute-done.49
  349.3 11.9 %collective-permute-done.47 = bf16[8,128,128]{2,1,0:T(8,128)(2,1)S(1)} collective-permute-done((bf16[8,128,128]{2,1,0:T(8,128)(2,1)S(1)}, bf16[8,128,128]{2,1,0:T(8,128)(2,1)S(1)}, u32[]{:S(2)}, u32[]{:S(2)}) %collective-permute-start.47) | collective-permute-done | bytes 262176 | tf_op jit(solution)/shard_map/ppermute | solution.py:1015
  361.2 5.0 %collective-permute-done.48 = bf16[8,128,128]{2,1,0:T(8,128)(2,1)S(1)} collective-permute-done((bf16[8,128,128]{2,1,0:T(8,128)(2,1)S(1)}, bf16[8,128,128]{2,1,0:T(8,128)(2,1)S(1)}, u32[]{:S(2)}, u32[]{:S(2)}) %collective-permute-start.48) | collective-permute-done | bytes 262176 | tf_op jit(solution)/shard_map/ppermute | solution.py:1015
  366.3 2.7 fusion.12
  369.6 1.7 pad_maximum_fusion.6
  372.6 1.8 collective-permute-start.52
  381.3 7.1 %shard_map.264 = (f32[14,128,128]{2,1,0:T(8,128)}, f32[14,128,128]{2,1,0:T(8,128)}, f32[14,128,128]{2,1,0:T(8,128)}, f32[14,128,128]{2,1,0:T(8,128)}, f32[14,128,128]{2,1,0:T(8,128)}) custom-call(s32[14]{0:T(128)} %fusion.107.ranks, f32[14,128,128]{2,1,0:T(8,128)} %get-tuple-element.368.refs_0_.refs_1_.refs_2_.refs_3_.refs_4_.refs_5_.refs_6_, ...), custom_call_target="tpu_custom_call" | custom-call | bytes 24000000 | tf_op jit(solution)/shard_map/pallas_call | solution.py:224
  388.7 6.0 %collective-permute-start.56 = (f32[2,2,4,2304]{3,0,1,2:T(2,128)S(1)}, f32[2,2,4,2304]{3,0,1,2:T(2,128)S(1)}, u32[]{:S(2)}, u32[]{:S(2)}) collective-permute-start(f32[2,2,4,2304]{3,0,1,2:T(2,128)S(1)} %pad_maximum_fusion.15), channel_id=1, source_target_pairs={{0,1},{1,0},{2,3},{3,2},{4,5},{5,4},{6,7},{7,6},{8,9},{9,8},{10,11... | collective-permute-start | bytes 442376 | tf_op jit(solution)/shard_map/ppermute | solution.py:1015
  400.3 2.8 collective-permute-start.58
  407.0 28.3 %shard_map.265 = (f32[14,128,128]{2,1,0:T(8,128)}, f32[14,128,128]{2,1,0:T(8,128)}, f32[14,128,128]{2,1,0:T(8,128)}, f32[14,128,128]{2,1,0:T(8,128)}, f32[14,128...) custom-call(f32[1]{0:T(128)} %bitcast.120.factor, f32[14,128,128]{2,1,0:T(8,128)} %get-tuple-element.280.refs_0_, ...), custom_call_target="tpu_custom_call" | custom-call | bytes 90000000 | tf_op jit(solution)/shard_map/pallas_call | solution.py:369
  435.3 2.9 collective-permute-done.60
  (312 shorter events, 92.5 us)
Async XLA Ops:
  7.2 133.7 %all-gather.2.cloned.1.call-start = ((), (), s32[]{:S(2)}) async-start(), calls=%async_computation | async-start | bytes 6488064 | tf_op jit(solution)/shard_map/all_gather | solution.py:1359
  10.2 17.9 %collective-permute-start.9 = (bf16[8,128,128]{2,1,0:T(8,128)(2,1)}, bf16[8,128,128]{2,1,0:T(8,128)(2,1)S(1)}, u32[]{:S(2)}, u32[]{:S(2)}) collective-permute-start(bf16[8,128,128]{2,1,0:T(8,128)(2,1)} %get-tuple-element.162), channel_id=1, source_target_pairs={{0,24},{8,0},{16,8},{24,16},{1,25},{9,1},{17,9},{25,17},{2,26},{10... | collective-permute-start | bytes 786440 | tf_op jit(solution)/shard_map/ppermute | solution.py:1015
  10.5 21.6 %collective-permute-start.10 = (bf16[8,128,128]{2,1,0:T(8,128)(2,1)}, bf16[8,128,128]{2,1,0:T(8,128)(2,1)S(1)}, u32[]{:S(2)}, u32[]{:S(2)}) collective-permute-start(bf16[8,128,128]{2,1,0:T(8,128)(2,1)} %get-tuple-element.162), channel_id=1, source_target_pairs={{0,16},{8,24},{16,0},{24,8},{1,17},{9,25},{17,1},{25,9},{2,18},{10... | collective-permute-start | bytes 786440 | tf_op jit(solution)/shard_map/ppermute | solution.py:1015
  12.8 26.4 %collective-permute-start.11 = (bf16[8,128,128]{2,1,0:T(8,128)(2,1)}, bf16[8,128,128]{2,1,0:T(8,128)(2,1)}, u32[]{:S(2)}, u32[]{:S(2)}) collective-permute-start(bf16[8,128,128]{2,1,0:T(8,128)(2,1)} %get-tuple-element.162), channel_id=1, source_target_pairs={{0,8},{8,16},{16,24},{24,0},{1,9},{9,17},{17,25},{25,1},{2,10},{10... | collective-permute-start | bytes 786440 | tf_op jit(solution)/shard_map/ppermute | solution.py:1015
  21.4 18.9 %collective-permute-start.8 = (bf16[208,768]{1,0:T(8,128)(2,1)S(1)}, bf16[208,768]{1,0:T(8,128)(2,1)S(1)}, u32[]{:S(2)}, u32[]{:S(2)}) collective-permute-start(bf16[208,768]{1,0:T(8,128)(2,1)S(1)} %get-tuple-element.379), channel_id=1, source_target_pairs={{0,4},{4,0},{1,5},{5,1},{2,6},{6,2},{3,7},{7,3},{8,12},{12,8},{9,1... | collective-permute-start | bytes 958472 | tf_op jit(solution)/shard_map/ppermute | solution.py:1015
  21.7 24.5 %collective-permute-start.12 = (bf16[208,768]{1,0:T(8,128)(2,1)S(1)}, bf16[208,768]{1,0:T(8,128)(2,1)S(1)}, u32[]{:S(2)}, u32[]{:S(2)}) collective-permute-start(bf16[208,768]{1,0:T(8,128)(2,1)S(1)} %get-tuple-element.378), channel_id=1, source_target_pairs={{0,4},{4,8},{8,12},{12,16},{16,20},{20,24},{24,28},{28,0},{1,5},{5... | collective-permute-start | bytes 958472 | tf_op jit(solution)/shard_map/ppermute | solution.py:1363
  28.1 18.1 %collective-permute-start.13 = (bf16[208,768]{1,0:T(8,128)(2,1)S(1)}, bf16[208,768]{1,0:T(8,128)(2,1)}, u32[]{:S(2)}, u32[]{:S(2)}) collective-permute-start(bf16[208,768]{1,0:T(8,128)(2,1)S(1)} %get-tuple-element.378), channel_id=1, source_target_pairs={{4,0},{8,4},{12,8},{16,12},{20,16},{24,20},{28,24},{0,28},{5,1},{9... | collective-permute-start | bytes 958472 | tf_op jit(solution)/shard_map/ppermute | solution.py:1364
  48.4 19.5 %collective-permute-start.15 = (bf16[4,4,128,128]{3,2,1,0:T(8,128)(2,1)S(1)}, bf16[4,4,128,128]{3,2,1,0:T(8,128)(2,1)}, u32[]{:S(2)}, u32[]{:S(2)}) collective-permute-start(bf16[4,4,128,128]{3,2,1,0:T(8,128)(2,1)S(1)} %get-tuple-element.366), channel_id=1, source_target_pairs={{0,4},{4,0},{1,5},{5,1},{2,6},{6,2},{3,7},{7,3},{8,12},{12,8},{9,1... | collective-permute-start | bytes 1572872 | tf_op jit(solution)/shard_map/ppermute | solution.py:1015
  50.0 19.1 %collective-permute-start.14 = (bf16[4,4,128,128]{3,2,1,0:T(8,128)(2,1)}, bf16[4,4,128,128]{3,2,1,0:T(8,128)(2,1)}, u32[]{:S(2)}, u32[]{:S(2)}) collective-permute-start(bf16[4,4,128,128]{3,2,1,0:T(8,128)(2,1)} %get-tuple-element.367), channel_id=1, source_target_pairs={{0,2},{2,0},{1,3},{3,1},{4,6},{6,4},{5,7},{7,5},{8,10},{10,8},{9,1... | collective-permute-start | bytes 1572872 | tf_op jit(solution)/shard_map/ppermute | solution.py:1015
  53.5 23.1 %collective-permute-start.16 = (bf16[2,208,768]{2,1,0:T(8,128)(2,1)S(1)}, bf16[2,208,768]{2,1,0:T(8,128)(2,1)}, u32[]{:S(2)}, u32[]{:S(2)}) collective-permute-start(bf16[2,208,768]{2,1,0:T(8,128)(2,1)S(1)} %pad_maximum_fusion.7), channel_id=1, source_target_pairs={{8,0},{16,8},{24,16},{9,1},{17,9},{25,17},{10,2},{18,10},{26,18},{... | collective-permute-start | bytes 1916936 | tf_op jit(solution)/shard_map/ppermute | solution.py:1038
  55.7 20.8 %collective-permute-start.17 = (bf16[2,208,768]{2,1,0:T(8,128)(2,1)S(1)}, bf16[2,208,768]{2,1,0:T(8,128)(2,1)}, u32[]{:S(2)}, u32[]{:S(2)}) collective-permute-start(bf16[2,208,768]{2,1,0:T(8,128)(2,1)S(1)} %pad_maximum_fusion.7), channel_id=1, source_target_pairs={{0,8},{8,16},{16,24},{1,9},{9,17},{17,25},{2,10},{10,18},{18,26},{... | collective-permute-start | bytes 1916936 | tf_op jit(solution)/shard_map/ppermute | solution.py:1038
  76.6 32.1 %collective-permute-start.24 = (bf16[2,208,768]{2,1,0:T(8,128)(2,1)}, bf16[2,208,768]{2,1,0:T(8,128)(2,1)}, u32[]{:S(2)}, u32[]{:S(2)}) collective-permute-start(bf16[2,208,768]{2,1,0:T(8,128)(2,1)} %collective-permute-done.17), channel_id=1, source_target_pairs={{0,8},{8,16},{16,24},{1,9},{9,17},{17,25},{2,10},{10,18},{18,26},{... | collective-permute-start | bytes 1916936 | tf_op jit(solution)/shard_map/ppermute | solution.py:1038
  79.9 40.0 %collective-permute-start.18 = (bf16[2,4,4,128,128]{4,3,2,1,0:T(8,128)(2,1)S(1)}, bf16[2,4,4,128,128]{4,3,2,1,0:T(8,128)(2,1)}, u32[]{:S(2)}, u32[]{:S(2)}) collective-permute-start(bf16[2,4,4,128,128]{4,3,2,1,0:T(8,128)(2,1)S(1)} %pad_maximum_fusion.4), channel_id=1, source_target_pairs={{0,4},{4,0},{1,5},{5,1},{2,6},{6,2},{3,7},{7,3},{8,12},{12,8},{9,1... | collective-permute-start | bytes 3145736 | tf_op jit(solution)/shard_map/ppermute | solution.py:1015
  80.9 39.4 %collective-permute-start.19 = (bf16[2,4,4,128,128]{4,3,2,1,0:T(8,128)(2,1)S(1)}, bf16[2,4,4,128,128]{4,3,2,1,0:T(8,128)(2,1)}, u32[]{:S(2)}, u32[]{:S(2)}) collective-permute-start(bf16[2,4,4,128,128]{4,3,2,1,0:T(8,128)(2,1)S(1)} %pad_maximum_fusion.5), channel_id=1, source_target_pairs={{0,2},{2,0},{1,3},{3,1},{4,6},{6,4},{5,7},{7,5},{8,10},{10,8},{9,1... | collective-permute-start | bytes 3145736 | tf_op jit(solution)/shard_map/ppermute | solution.py:1015
  82.0 34.2 %collective-permute-start.26 = (bf16[2,208,768]{2,1,0:T(8,128)(2,1)}, bf16[2,208,768]{2,1,0:T(8,128)(2,1)}, u32[]{:S(2)}, u32[]{:S(2)}) collective-permute-start(bf16[2,208,768]{2,1,0:T(8,128)(2,1)} %collective-permute-done.16), channel_id=1, source_target_pairs={{8,0},{16,8},{24,16},{9,1},{17,9},{25,17},{10,2},{18,10},{26,18},{... | collective-permute-start | bytes 1916936 | tf_op jit(solution)/shard_map/ppermute | solution.py:1038
  108.6 17.2 %collective-permute-start.25 = (bf16[2,208,768]{2,1,0:T(8,128)(2,1)}, bf16[2,208,768]{2,1,0:T(8,128)(2,1)}, u32[]{:S(2)}, u32[]{:S(2)}) collective-permute-start(bf16[2,208,768]{2,1,0:T(8,128)(2,1)} %collective-permute-done.24), channel_id=1, source_target_pairs={{0,8},{8,16},{16,24},{1,9},{9,17},{17,25},{2,10},{10,18},{18,26},{... | collective-permute-start | bytes 1916936 | tf_op jit(solution)/shard_map/ppermute | solution.py:1038
  114.0 23.8 %collective-permute-start.20 = (bf16[32,128,128]{2,1,0:T(8,128)(2,1)S(1)}, bf16[32,128,128]{2,1,0:T(8,128)(2,1)S(1)}, u32[]{:S(2)}, u32[]{:S(2)}) collective-permute-start(bf16[32,128,128]{2,1,0:T(8,128)(2,1)S(1)} %bitcast.225), channel_id=1, source_target_pairs={{0,1},{1,0},{2,3},{3,2},{4,5},{5,4},{6,7},{7,6},{8,9},{9,8},{10,11... | collective-permute-start | bytes 3145736 | tf_op jit(solution)/shard_map/ppermute | solution.py:1015
  116.2 18.1 %collective-permute-start.27 = (bf16[2,208,768]{2,1,0:T(8,128)(2,1)}, bf16[2,208,768]{2,1,0:T(8,128)(2,1)S(1)}, u32[]{:S(2)}, u32[]{:S(2)}) collective-permute-start(bf16[2,208,768]{2,1,0:T(8,128)(2,1)} %collective-permute-done.26), channel_id=1, source_target_pairs={{8,0},{16,8},{24,16},{9,1},{17,9},{25,17},{10,2},{18,10},{26,18},{... | collective-permute-start | bytes 1916936 | tf_op jit(solution)/shard_map/ppermute | solution.py:1038
  119.9 17.9 %collective-permute-start.22 = (bf16[32,128,128]{2,1,0:T(8,128)(2,1)S(1)}, bf16[32,128,128]{2,1,0:T(8,128)(2,1)S(1)}, u32[]{:S(2)}, u32[]{:S(2)}) collective-permute-start(bf16[32,128,128]{2,1,0:T(8,128)(2,1)S(1)} %bitcast.222), channel_id=1, source_target_pairs={{0,1},{1,0},{2,3},{3,2},{4,5},{5,4},{6,7},{7,6},{8,9},{9,8},{10,11... | collective-permute-start | bytes 3145736 | tf_op jit(solution)/shard_map/ppermute | solution.py:1015
  120.3 18.6 %collective-permute-start.21 = (bf16[32,128,128]{2,1,0:T(8,128)(2,1)}, bf16[32,128,128]{2,1,0:T(8,128)(2,1)S(1)}, u32[]{:S(2)}, u32[]{:S(2)}) collective-permute-start(bf16[32,128,128]{2,1,0:T(8,128)(2,1)} %bitcast.57.refs_2_.refs_5_), channel_id=1, source_target_pairs={{0,1},{1,0},{2,3},{3,2},{4,5},{5,4},{6,7},{7,6},{8,9},{9,8},{10,11... | collective-permute-start | bytes 3145736 | tf_op jit(solution)/shard_map/ppermute | solution.py:1015
  125.9 15.0 %collective-permute-start.23 = (bf16[32,128,128]{2,1,0:T(8,128)(2,1)}, bf16[32,128,128]{2,1,0:T(8,128)(2,1)}, u32[]{:S(2)}, u32[]{:S(2)}) collective-permute-start(bf16[32,128,128]{2,1,0:T(8,128)(2,1)} %bitcast.59.refs_4_.refs_7_), channel_id=1, source_target_pairs={{0,1},{1,0},{2,3},{3,2},{4,5},{5,4},{6,7},{7,6},{8,9},{9,8},{10,11... | collective-permute-start | bytes 3145736 | tf_op jit(solution)/shard_map/ppermute | solution.py:1015
  214.7 9.4 %collective-permute-start.28 = (bf16[96,128,128]{2,1,0:T(8,128)(2,1)}, bf16[96,128,128]{2,1,0:T(8,128)(2,1)}, u32[]{:S(2)}, u32[]{:S(2)}) collective-permute-start(bf16[96,128,128]{2,1,0:T(8,128)(2,1)} %get-tuple-element.198), channel_id=1, source_target_pairs={{0,1},{1,0},{2,3},{3,2},{4,5},{5,4},{6,7},{7,6},{8,9},{9,8},{10,11... | collective-permute-start | bytes 9437192 | tf_op jit(solution)/shard_map/ppermute | solution.py:1015
  228.8 19.3 %collective-permute-start.30 = (bf16[2,4,3,128,128]{4,3,2,1,0:T(8,128)(2,1)}, bf16[2,4,3,128,128]{4,3,2,1,0:T(8,128)(2,1)S(1)}, u32[]{:S(2)}, u32[]{:S(2)}) collective-permute-start(bf16[2,4,3,128,128]{4,3,2,1,0:T(8,128)(2,1)} %bitcast.70), channel_id=1, source_target_pairs={{0,2},{2,0},{1,3},{3,1},{4,6},{6,4},{5,7},{7,5},{8,10},{10,8},{9,1... | collective-permute-start | bytes 2359304 | tf_op jit(solution)/shard_map/ppermute | solution.py:1015
  229.0 19.4 %collective-permute-start.29 = (bf16[2,4,3,128,128]{4,3,2,1,0:T(8,128)(2,1)S(1)}, bf16[2,4,3,128,128]{4,3,2,1,0:T(8,128)(2,1)S(1)}, u32[]{:S(2)}, u32[]{:S(2)}) collective-permute-start(bf16[2,4,3,128,128]{4,3,2,1,0:T(8,128)(2,1)S(1)} %bitcast.243), channel_id=1, source_target_pairs={{0,4},{4,0},{1,5},{5,1},{2,6},{6,2},{3,7},{7,3},{8,12},{12,8},{9,1... | collective-permute-start | bytes 2359304 | tf_op jit(solution)/shard_map/ppermute | solution.py:1015
  248.7 16.2 %collective-permute-start.32 = (bf16[4,3,128,128]{3,2,1,0:T(8,128)(2,1)S(1)}, bf16[4,3,128,128]{3,2,1,0:T(8,128)(2,1)S(1)}, u32[]{:S(2)}, u32[]{:S(2)}) collective-permute-start(bf16[4,3,128,128]{3,2,1,0:T(8,128)(2,1)S(1)} %get-tuple-element.219), channel_id=1, source_target_pairs={{0,4},{4,0},{1,5},{5,1},{2,6},{6,2},{3,7},{7,3},{8,12},{12,8},{9,1... | collective-permute-start | bytes 1179656 | tf_op jit(solution)/shard_map/ppermute | solution.py:1015
  249.1 16.0 %collective-permute-start.31 = (bf16[4,3,128,128]{3,2,1,0:T(8,128)(2,1)S(1)}, bf16[4,3,128,128]{3,2,1,0:T(8,128)(2,1)S(1)}, u32[]{:S(2)}, u32[]{:S(2)}) collective-permute-start(bf16[4,3,128,128]{3,2,1,0:T(8,128)(2,1)S(1)} %get-tuple-element.217), channel_id=1, source_target_pairs={{0,2},{2,0},{1,3},{3,1},{4,6},{6,4},{5,7},{7,5},{8,10},{10,8},{9,1... | collective-permute-start | bytes 1179656 | tf_op jit(solution)/shard_map/ppermute | solution.py:1015
  265.2 21.4 %collective-permute-start.33 = (bf16[128,128,128]{2,1,0:T(8,128)(2,1)}, bf16[128,128,128]{2,1,0:T(8,128)(2,1)}, u32[]{:S(2)}, u32[]{:S(2)}) collective-permute-start(bf16[128,128,128]{2,1,0:T(8,128)(2,1)} %get-tuple-element.221), channel_id=1, source_target_pairs={{0,1},{1,0},{2,3},{3,2},{4,5},{5,4},{6,7},{7,6},{8,9},{9,8},{10,11... | collective-permute-start | bytes 12582920 | tf_op jit(solution)/shard_map/ppermute | solution.py:1015
  267.0 16.0 %collective-permute-start.34 = (bf16[6,128,128]{2,1,0:T(8,128)(2,1)S(1)}, bf16[6,128,128]{2,1,0:T(8,128)(2,1)S(1)}, u32[]{:S(2)}, u32[]{:S(2)}) collective-permute-start(bf16[6,128,128]{2,1,0:T(8,128)(2,1)S(1)} %pad_maximum_fusion.12), channel_id=1, source_target_pairs={{0,8},{8,16},{16,24},{24,0},{1,9},{9,17},{17,25},{25,1},{2,10},{10... | collective-permute-start | bytes 589832 | tf_op jit(solution)/shard_map/ppermute | solution.py:1015
  268.3 16.9 %collective-permute-start.35 = (bf16[6,128,128]{2,1,0:T(8,128)(2,1)S(1)}, bf16[6,128,128]{2,1,0:T(8,128)(2,1)S(1)}, u32[]{:S(2)}, u32[]{:S(2)}) collective-permute-start(bf16[6,128,128]{2,1,0:T(8,128)(2,1)S(1)} %pad_maximum_fusion.13), channel_id=1, source_target_pairs={{0,16},{8,24},{16,0},{24,8},{1,17},{9,25},{17,1},{25,9},{2,18},{10... | collective-permute-start | bytes 589832 | tf_op jit(solution)/shard_map/ppermute | solution.py:1015
  268.5 18.0 %collective-permute-start.36 = (bf16[6,128,128]{2,1,0:T(8,128)(2,1)S(1)}, bf16[6,128,128]{2,1,0:T(8,128)(2,1)S(1)}, u32[]{:S(2)}, u32[]{:S(2)}) collective-permute-start(bf16[6,128,128]{2,1,0:T(8,128)(2,1)S(1)} %pad_maximum_fusion.14), channel_id=1, source_target_pairs={{0,24},{8,0},{16,8},{24,16},{1,25},{9,1},{17,9},{25,17},{2,26},{10... | collective-permute-start | bytes 589832 | tf_op jit(solution)/shard_map/ppermute | solution.py:1015
  294.8 24.7 %collective-permute-start.38 = (bf16[2,4,4,128,128]{4,3,2,1,0:T(8,128)(2,1)S(1)}, bf16[2,4,4,128,128]{4,3,2,1,0:T(8,128)(2,1)S(1)}, u32[]{:S(2)}, u32[]{:S(2)}) collective-permute-start(bf16[2,4,4,128,128]{4,3,2,1,0:T(8,128)(2,1)S(1)} %bitcast.242), channel_id=1, source_target_pairs={{0,2},{2,0},{1,3},{3,1},{4,6},{6,4},{5,7},{7,5},{8,10},{10,8},{9,1... | collective-permute-start | bytes 3145736 | tf_op jit(solution)/shard_map/ppermute | solution.py:1015
  295.3 24.7 %collective-permute-start.37 = (bf16[2,4,4,128,128]{4,3,2,1,0:T(8,128)(2,1)S(1)}, bf16[2,4,4,128,128]{4,3,2,1,0:T(8,128)(2,1)S(1)}, u32[]{:S(2)}, u32[]{:S(2)}) collective-permute-start(bf16[2,4,4,128,128]{4,3,2,1,0:T(8,128)(2,1)S(1)} %bitcast.241), channel_id=1, source_target_pairs={{0,4},{4,0},{1,5},{5,1},{2,6},{6,2},{3,7},{7,3},{8,12},{12,8},{9,1... | collective-permute-start | bytes 3145736 | tf_op jit(solution)/shard_map/ppermute | solution.py:1015
  297.1 3.8 collective-permute-start.41
  299.1 3.8 collective-permute-start.42
  320.4 4.2 collective-permute-start.45
  323.0 12.2 %collective-permute-start.44 = (bf16[4,4,128,128]{3,2,1,0:T(8,128)(2,1)S(1)}, bf16[4,4,128,128]{3,2,1,0:T(8,128)(2,1)S(1)}, u32[]{:S(2)}, u32[]{:S(2)}) collective-permute-start(bf16[4,4,128,128]{3,2,1,0:T(8,128)(2,1)S(1)} %get-tuple-element.248), channel_id=1, source_target_pairs={{0,4},{4,0},{1,5},{5,1},{2,6},{6,2},{3,7},{7,3},{8,12},{12,8},{9,1... | collective-permute-start | bytes 1572872 | tf_op jit(solution)/shard_map/ppermute | solution.py:1015
  324.1 12.3 %collective-permute-start.43 = (bf16[4,4,128,128]{3,2,1,0:T(8,128)(2,1)S(1)}, bf16[4,4,128,128]{3,2,1,0:T(8,128)(2,1)S(1)}, u32[]{:S(2)}, u32[]{:S(2)}) collective-permute-start(bf16[4,4,128,128]{3,2,1,0:T(8,128)(2,1)S(1)} %get-tuple-element.246), channel_id=1, source_target_pairs={{0,2},{2,0},{1,3},{3,1},{4,6},{6,4},{5,7},{7,5},{8,10},{10,8},{9,1... | collective-permute-start | bytes 1572872 | tf_op jit(solution)/shard_map/ppermute | solution.py:1015
  338.3 28.0 %collective-permute-start.50 = (bf16[4,208,768]{2,1,0:T(8,128)(2,1)}, bf16[4,208,768]{2,1,0:T(8,128)(2,1)}, u32[]{:S(2)}, u32[]{:S(2)}) collective-permute-start(bf16[4,208,768]{2,1,0:T(8,128)(2,1)} %slice_bitcast_fusion.4), channel_id=1, source_target_pairs={{0,4},{4,0},{1,5},{5,1},{2,6},{6,2},{3,7},{7,3},{8,12},{12,8},{9,1... | collective-permute-start | bytes 3833864 | tf_op jit(solution)/shard_map/ppermute | solution.py:1015
  340.5 8.9 %collective-permute-start.46 = (bf16[8,128,128]{2,1,0:T(8,128)(2,1)S(1)}, bf16[8,128,128]{2,1,0:T(8,128)(2,1)S(1)}, u32[]{:S(2)}, u32[]{:S(2)}) collective-permute-start(bf16[8,128,128]{2,1,0:T(8,128)(2,1)S(1)} %pad_maximum_fusion.9), channel_id=1, source_target_pairs={{0,8},{8,16},{16,24},{24,0},{1,9},{9,17},{17,25},{25,1},{2,10},{10... | collective-permute-start | bytes 786440 | tf_op jit(solution)/shard_map/ppermute | solution.py:1015
  341.5 19.7 %collective-permute-start.47 = (bf16[8,128,128]{2,1,0:T(8,128)(2,1)S(1)}, bf16[8,128,128]{2,1,0:T(8,128)(2,1)S(1)}, u32[]{:S(2)}, u32[]{:S(2)}) collective-permute-start(bf16[8,128,128]{2,1,0:T(8,128)(2,1)S(1)} %pad_maximum_fusion.10), channel_id=1, source_target_pairs={{0,16},{8,24},{16,0},{24,8},{1,17},{9,25},{17,1},{25,9},{2,18},{10... | collective-permute-start | bytes 786440 | tf_op jit(solution)/shard_map/ppermute | solution.py:1015
  344.3 21.8 %collective-permute-start.48 = (bf16[8,128,128]{2,1,0:T(8,128)(2,1)S(1)}, bf16[8,128,128]{2,1,0:T(8,128)(2,1)S(1)}, u32[]{:S(2)}, u32[]{:S(2)}) collective-permute-start(bf16[8,128,128]{2,1,0:T(8,128)(2,1)S(1)} %pad_maximum_fusion.11), channel_id=1, source_target_pairs={{0,24},{8,0},{16,8},{24,16},{1,25},{9,1},{17,9},{25,17},{2,26},{10... | collective-permute-start | bytes 786440 | tf_op jit(solution)/shard_map/ppermute | solution.py:1015
  380.1 8.4 %collective-permute-start.55 = (f32[2,4,2304]{2,0,1:T(2,128)S(1)}, f32[2,4,2304]{2,0,1:T(2,128)S(1)}, u32[]{:S(2)}, u32[]{:S(2)}) collective-permute-start(f32[2,4,2304]{2,0,1:T(2,128)S(1)} %get-tuple-element.390), channel_id=1, source_target_pairs={{0,2},{2,0},{1,3},{3,1},{4,6},{6,4},{5,7},{7,5},{8,10},{10,8},{9,1... | collective-permute-start | bytes 221192 | tf_op jit(solution)/shard_map/ppermute | solution.py:1015
  388.7 7.3 %collective-permute-start.56 = (f32[2,2,4,2304]{3,0,1,2:T(2,128)S(1)}, f32[2,2,4,2304]{3,0,1,2:T(2,128)S(1)}, u32[]{:S(2)}, u32[]{:S(2)}) collective-permute-start(f32[2,2,4,2304]{3,0,1,2:T(2,128)S(1)} %pad_maximum_fusion.15), channel_id=1, source_target_pairs={{0,1},{1,0},{2,3},{3,2},{4,5},{5,4},{6,7},{7,6},{8,9},{9,8},{10,11... | collective-permute-start | bytes 442376 | tf_op jit(solution)/shard_map/ppermute | solution.py:1015
  399.2 40.1 %collective-permute-start.57 = (bf16[208,768]{1,0:T(8,128)(2,1)S(1)}, bf16[208,768]{1,0:T(8,128)(2,1)S(1)}, u32[]{:S(2)}, u32[]{:S(2)}) collective-permute-start(bf16[208,768]{1,0:T(8,128)(2,1)S(1)} %get-tuple-element.353), channel_id=1, source_target_pairs={{0,8},{8,16},{16,24},{24,0},{1,9},{9,17},{17,25},{25,1},{2,10},{10... | collective-permute-start | bytes 958472 | tf_op jit(solution)/shard_map/ppermute | solution.py:1015
  400.3 39.0 %collective-permute-start.58 = (bf16[208,768]{1,0:T(8,128)(2,1)S(1)}, bf16[208,768]{1,0:T(8,128)(2,1)S(1)}, u32[]{:S(2)}, u32[]{:S(2)}) collective-permute-start(bf16[208,768]{1,0:T(8,128)(2,1)S(1)} %get-tuple-element.355), channel_id=1, source_target_pairs={{0,16},{8,24},{16,0},{24,8},{1,17},{9,25},{17,1},{25,9},{2,18},{10... | collective-permute-start | bytes 958472 | tf_op jit(solution)/shard_map/ppermute | solution.py:1015
  403.1 36.3 %collective-permute-start.59 = (bf16[208,768]{1,0:T(8,128)(2,1)S(1)}, bf16[208,768]{1,0:T(8,128)(2,1)S(1)}, u32[]{:S(2)}, u32[]{:S(2)}) collective-permute-start(bf16[208,768]{1,0:T(8,128)(2,1)S(1)} %get-tuple-element.354), channel_id=1, source_target_pairs={{0,24},{8,0},{16,8},{24,16},{1,25},{9,1},{17,9},{25,17},{2,26},{10... | collective-permute-start | bytes 958472 | tf_op jit(solution)/shard_map/ppermute | solution.py:1015
  403.4 34.8 %collective-permute-start.60 = (bf16[208,768]{1,0:T(8,128)(2,1)S(1)}, bf16[208,768]{1,0:T(8,128)(2,1)S(1)}, u32[]{:S(2)}, u32[]{:S(2)}) collective-permute-start(bf16[208,768]{1,0:T(8,128)(2,1)S(1)} %copy-done.24), channel_id=1, source_target_pairs={{4,0},{8,4},{12,8},{16,12},{20,16},{24,20},{28,24},{0,28},{5,1},{9... | collective-permute-start | bytes 958472 | tf_op jit(solution)/shard_map/ppermute | solution.py:1485
  404.5 33.7 %collective-permute-start.61 = (bf16[208,768]{1,0:T(8,128)(2,1)S(1)}, bf16[208,768]{1,0:T(8,128)(2,1)S(1)}, u32[]{:S(2)}, u32[]{:S(2)}) collective-permute-start(bf16[208,768]{1,0:T(8,128)(2,1)S(1)} %copy-done.23), channel_id=1, source_target_pairs={{0,4},{4,8},{8,12},{12,16},{16,20},{20,24},{24,28},{28,0},{1,5},{5... | collective-permute-start | bytes 958472 | tf_op jit(solution)/shard_map/ppermute | solution.py:1486
  (45 other events, 458.1 us)
Sparse Core Ops, SparseCore 0:
  11.5 102.8 all-gather.1
